TPU v7x, 32 devices: a whole 2x2x4 slice. The times are simulated.
32 devices in a mesh: runs: 2 (over y), tm: 4 (over z), grp: 2 (over x), state: 2 (over core).
Axes of the slice: x: 2, y: 2, z: 4, core: 2. Of those that a mesh axis runs over, the one named last changes fastest.
Arguments:
- rows_h: bfloat16 [4, 64, 128, 512], P(('runs', 'grp'), 'tm', None, 'state'), parts along dimension 0, may hold values from -0.27 to 0.27
- rows_y: bfloat16 [4, 64, 128], P(('runs', 'grp'), 'tm'), parts along dimension 0, may hold values from -6 to 6
- tile_block: int32 [4, 64, 1], P(('runs', 'grp'), 'tm'), parts along dimension 0, may hold values from 0 to 3; in each aligned block of 16 rows (0 to 15, 16 to 31, ..., all dimensions but the last counted through in order) at most 16 rows name the same one
- tile_count: int32 [4, 64], P(('runs', 'grp'), 'tm'), parts along dimension 0, may hold values from 1 to 128
- kappa: float32 [4, 4, 512], P(('runs', 'grp'), 'tm'), parts along dimension 0, may hold values from 0.02 to 0.2
- rate: float32 [4, 4, 512], P(('runs', 'grp'), 'tm'), parts along dimension 0, may hold values from 0.0001 to 0.05
- smooth_gain: float32 [4, 4, 512], P(('runs', 'grp'), 'tm'), parts along dimension 0, may hold values from 0.3 to 0.995
- start_state: float32 [1024], P('runs'), parts along dimension 0, may hold values from -6 to 6
Outputs:
- filtered: float32 [4, 4, 512], P(('runs', 'grp'), 'tm', 'state'), parts along dimension 0
- smoothed: float32 [4, 4, 512], P(('runs', 'grp'), 'tm', 'state'), parts along dimension 0
There are 2 independent parts, one for each index of `runs`. A program takes and returns all parts, laid end to end along the dimension named above; each array names one. Nothing has to cross between parts.
Inputs may be any that keep to these rules, and one draw needn't show every extreme that they name: `tile_block`: among the 16 tiles of one device, at most 16 project to the same time block.
All inputs are finite; a program needn't handle non-finite values.
Results may differ from a plain program's by a relative error of at most 0.0023.
Values may be sent and summed in bfloat16 or wider, within the bound.
No kernel may reach another device: no remote copies, remote signals or barrier semaphores. Data moves between devices by JAX's collectives and lax.ppermute only.
A program may use at most 128 MiB of HBM per device.

v0:
```python
import jax
import jax.numpy as jnp
from jax import lax
from jax.sharding import PartitionSpec as P

STEPS = 4


def prefix_2(value, axis, join, neutral, backward):
    count, mine = (lax.axis_size(axis), lax.axis_index(axis))
    pieces = jax.tree.map(lambda part: lax.all_gather(part, axis), value)
    if backward:
        pieces = jax.tree.map(lambda part: part[::-1], pieces)
        mine = count - 1 - mine
    so_far = jax.tree.map(
        lambda part, zero: jnp.full_like(part, 0) + jnp.asarray(zero, part.dtype), value, neutral
    )

    def lap(position, so_far):
        longer = join(so_far, jax.tree.map(lambda part: part[position], pieces))
        return jax.tree.map(lambda new, old: jnp.where(position < mine, new, old), longer, so_far)

    return lax.fori_loop(0, count - 1, lap, so_far)


def broadcast(array, axis, root):
    mine = lax.axis_index(axis) == root
    return lax.psum(jnp.where(mine, array, jnp.zeros_like(array)), axis)


def stencil(field, coeff, decay):
    for step_index in range(STEPS):
        zero_row = jnp.zeros_like(field[:1])
        upper_cell = jnp.concatenate([zero_row, field[:-1]], axis=0)
        lower_cell = jnp.concatenate([field[1:], zero_row], axis=0)
        field = field + coeff * (upper_cell + lower_cell - 2.0 * field) - decay * field
    return field


def matmul_high(left, right):
    return jnp.dot(left, right, precision=lax.Precision.HIGHEST)


def compose(earlier, later):
    return (matmul_high(later[0], earlier[0]), matmul_high(later[0], earlier[1]) + later[1])


def chain_back(earlier, later):
    return (later[0] * earlier[0], later[0] * earlier[1] + later[1])


def contract_rows(left, right):
    return lax.dot_general(
        left, right, (((0,), (0,)), ((), ())), preferred_element_type=jnp.float32
    )


def shards(rows_h, rows_y, tile_block, tile_count, kappa, rate, smooth_gain, start_state):
    tm_size = lax.axis_size("tm")
    state_size = lax.axis_size("state")
    tile_num = rows_h.shape[1]
    row_num = rows_h.shape[2]
    half_width = rows_h.shape[3]
    full_width = kappa.shape[2]
    capacity = 4 * tile_num // tm_size
    slot_num = tm_size * capacity
    part_index = lax.axis_index("state")
    live_rows = jnp.arange(row_num, dtype=jnp.int32)[None, :] < tile_count[0][:, None]
    h_masked = jnp.where(live_rows[:, :, None], rows_h[0], jnp.zeros((), jnp.bfloat16))
    y_masked = jnp.where(live_rows, rows_y[0], jnp.zeros((), jnp.bfloat16))
    owner_index = tile_block[0, :, 0]
    onehot = (owner_index[:, None] == jnp.arange(tm_size, dtype=jnp.int32)[None, :]).astype(
        jnp.int32
    )
    earlier_same = jnp.sum((jnp.cumsum(onehot, axis=0) - onehot) * onehot, axis=1)
    slot_index = owner_index * capacity + earlier_same
    send_h = jnp.zeros((slot_num, row_num, half_width), jnp.bfloat16).at[slot_index].set(h_masked)
    send_y = jnp.zeros((slot_num, row_num), jnp.bfloat16).at[slot_index].set(y_masked)
    recv_h, recv_y = (
        lax.all_to_all(
            send_h.reshape(tm_size, capacity, row_num, half_width),
            "tm",
            split_axis=0,
            concat_axis=0,
            tiled=True,
        ),
        lax.all_to_all(
            send_y.reshape(tm_size, capacity, row_num),
            "tm",
            split_axis=0,
            concat_axis=0,
            tiled=True,
        ),
    )
    share = slot_num // state_size
    swapped = lax.all_to_all(
        recv_h.reshape(slot_num, row_num, half_width),
        "state",
        split_axis=0,
        concat_axis=2,
        tiled=True,
    )
    values_half = lax.dynamic_slice_in_dim(
        recv_y.reshape(slot_num, row_num), part_index * share, share, 0
    )
    flat_rows = swapped.reshape(share * row_num, full_width)
    gram_part = contract_rows(flat_rows, flat_rows)
    info_part = contract_rows(flat_rows, values_half.reshape(share * row_num))
    trace_part = jnp.sum(jnp.square(flat_rows.astype(jnp.float32)))
    gram_cols = lax.psum_scatter(
        gram_part.astype(jnp.bfloat16), "state", scatter_dimension=1, tiled=True
    ).astype(jnp.float32)
    info_vec, trace_val = lax.psum((info_part, trace_part), "state")
    kappa_row = kappa[0, 0]
    rate_row = rate[0, 0]
    lam_val = full_width / (2.0 * (full_width + trace_val))
    eye_cols = (
        jnp.arange(full_width, dtype=jnp.int32)[:, None]
        == part_index * half_width + jnp.arange(half_width, dtype=jnp.int32)[None, :]
    ).astype(jnp.float32)
    trans_cols = stencil(eye_cols - lam_val * gram_cols, kappa_row[:, None], rate_row[:, None])
    forcing = lam_val * stencil(info_vec, kappa_row, rate_row)
    transition = lax.all_gather(trans_cols, "state", axis=1, tiled=True)
    identity_pair = (jnp.eye(full_width, dtype=jnp.float32), jnp.zeros((full_width,), jnp.float32))
    prefix = prefix_2((transition, forcing), "tm", compose, identity_pair, False)
    inclusive = compose(prefix, (transition, forcing))
    totals_pair = (
        broadcast(inclusive[0], "tm", tm_size - 1),
        broadcast(inclusive[1], "tm", tm_size - 1),
    )
    before_pair = prefix_2(totals_pair, "grp", compose, identity_pair, False)
    entry_state = matmul_high(before_pair[0], start_state) + before_pair[1]
    incoming = matmul_high(prefix[0], entry_state) + prefix[1]
    updated = matmul_high(transition, incoming) + forcing
    innovation = updated - stencil(incoming, kappa_row, rate_row)
    gain_vec = smooth_gain[0, 0]
    own_pair = (gain_vec, gain_vec * innovation)
    unit_pair = (jnp.ones((full_width,), jnp.float32), jnp.zeros((full_width,), jnp.float32))
    suffix = prefix_2(own_pair, "tm", chain_back, unit_pair, True)
    whole_pair = chain_back(suffix, own_pair)
    head_pair = (broadcast(whole_pair[0], "tm", 0), broadcast(whole_pair[1], "tm", 0))
    after_groups = prefix_2(head_pair, "grp", chain_back, unit_pair, True)
    residual = suffix[0] * after_groups[1] + suffix[1]
    smoothed = updated + residual
    filtered_part = lax.dynamic_slice_in_dim(updated, part_index * half_width, half_width, 0)
    smoothed_part = lax.dynamic_slice_in_dim(smoothed, part_index * half_width, half_width, 0)
    return (filtered_part.reshape(1, 1, half_width), smoothed_part.reshape(1, 1, half_width))


def solution(mesh):
    return jax.shard_map(
        shards,
        mesh=mesh,
        in_specs=(
            P(("runs", "grp"), "tm", None, "state"),
            P(("runs", "grp"), "tm", None),
            P(("runs", "grp"), "tm", None),
            P(("runs", "grp"), "tm"),
            P(("runs", "grp"), "tm", None),
            P(("runs", "grp"), "tm", None),
            P(("runs", "grp"), "tm", None),
            P("runs"),
        ),
        out_specs=(P(("runs", "grp"), "tm", "state"), P(("runs", "grp"), "tm", "state")),
        check_vma=False,
    )
```

profile of v0, /device:TPU:0, one launch (start us, length us, event | category | flops | bytes accessed | tf_op | source)
XLA Modules:
  0.0 406.8 jit_solution(9971076858261453375)
XLA Ops:
  17.2 99.5 %all_to_all.25 = bf16[4,16,128,256]{3,2,1,0:T(8,128)(2,1)S(1)} all-to-all(bf16[4,16,128,256]{3,2,1,0:T(8,128)(2,1)} %bitcast.121), channel_id=1, replica_groups=mesh['runs'=2,'tm'=4,'grp'=2,'state'=2] {'tm'}, dimensions={0} | all-to-all | bytes 8388608 | tf_op jit(solution)/shard_map/all_to_all | solution.py:80
  116.7 8.2 %all_to_all.26 = bf16[64,128,256]{2,1,0:T(8,128)(2,1)} all-to-all(bf16[64,128,256]{2,1,0:T(8,128)(2,1)S(1)} %bitcast.122), channel_id=1, replica_groups=mesh['runs'=2,'tm'=4,'grp'=2,'state'=2] {'state'}, dimensions={0} | all-to-all | bytes 8388608 | tf_op jit(solution)/shard_map/all_to_all | solution.py:96
  124.8 7.9 %copy.14 = bf16[32,128,2,256]{1,0,3,2:T(8,128)(2,1)} copy(bf16[32,128,2,256]{3,1,0,2:T(8,128)(2,1)} %bitcast.118) | data formatting | bytes 8388608 | tf_op jit(solution)/shard_map/all_to_all | solution.py:96
  132.8 6.8 %fusion.14 = bf16[512,512]{1,0:T(8,128)(2,1)} fusion(bf16[64,8,32,128]{3,2,1,0:T(8,128)(2,1)} %bitcast.123), kind=kOutput, calls=%fused_computation.27 | convolution fusion | flops 2147745792 | bytes 4718592 | tf_op jit(solution)/shard_map/dot_general | solution.py:53
  140.8 3.2 all-to-all-start.2
  144.1 5.5 %all-to-all-done.2 = bf16[4,16,128]{2,1,0:T(8,128)(2,1)S(1)} async-done(((bf16[4,16,128]{2,1,0:T(8,128)(2,1)}), bf16[4,16,128]{2,1,0:T(8,128)(2,1)S(1)}, u32[]{:S(2)}, u32[]{:S(2)}) %all-to-all-start.2) | async-done | bytes 16416 | tf_op jit(solution)/shard_map/all_to_all | solution.py:87
  149.7 4.4 %fusion.7 = f32[1,512]{1,0:T(1,128)S(1)} fusion(bf16[4096,1]{0,1:T(2,128)(2,1)S(1)} %reshape.148, bf16[64,8,32,128]{3,2,1,0:T(8,128)(2,1)} %bitcast.124), kind=kOutput, calls=%fused_computation.18 | convolution fusion | flops 4194304 | bytes 4204544 | tf_op jit(solution)/shard_map/dot_general | solution.py:53
  156.9 3.1 all-reduce.9
  164.8 7.4 %all-gather.13.cloned.1.call-done = f32[512,512]{1,0:T(8,128)} async-done(((f32[512,256]{1,0:T(8,128)}), f32[512,512]{1,0:T(8,128)}) %all-gather.13.cloned.1.call-update) | async-done | bytes 1048592 | tf_op jit(solution)/shard_map/all_gather | solution.py:123
  173.1 12.3 %all-gather.4 = f32[4,1,512]{2,1,0:T(1,128)S(1)} all-gather(f32[1,1,512]{2,1,0:T(1,128)S(1)} %bitcast.160), channel_id=3, replica_groups=mesh['runs'=2,'tm'=4,'grp'=2,'state'=2] {'tm'}, dimensions={0}, use_global_device_ids=true | all-gather | bytes 10240 | tf_op jit(solution)/shard_map/all_gather | solution.py:11
  185.4 70.4 %all-gather.17.cloned.1.call-done = f32[2048,512]{1,0:T(8,128)} async-done(((f32[512,512]{1,0:T(8,128)}), f32[2048,512]{1,0:T(8,128)}) %all-gather.17.cloned.1.call-update) | async-done | bytes 4194320 | tf_op jit(solution)/shard_map/all_gather | solution.py:11
  255.8 16.4 %while.20 = (s32[]{:T(128)}, f32[512,512]{1,0:T(8,128)S(1)}, f32[512]{0:T(512)S(1)}, s32[]{:T(128)}, f32[4,512,512]{2,1,0:T(8,128)}, /*index=5*/f32[4,512]{1,0:T(4,128)S(1)}, s32[]{:T(128)}, s32[]{:T(128)}) while((s32[]{:T(128)}, f32[512,512]{1,0:T(8,128)S(1)}, f32[512]{0:T(512)S(1)}, s32[]{:T(128)}, f32[4,512,512]{2,1,0:T(8,128)}, ...), condition=%wide.region_9.10_spmd.clone, body=%wide.region_8.9_spmd.clone.sunk | while | flops 1614022656 | bytes 7361647 | solution.py:23
  258.2 3.1 convolution_select_fusion.4
  263.7 3.1 convolution_select_fusion.4
  269.1 3.1 convolution_select_fusion.4
  275.1 50.5 %all-reduce.12.cloned.1.call-done = f32[1,512,512]{2,1,0:T(8,128)} async-done(((f32[1,512,512]{2,1,0:T(8,128)}), f32[1,512,512]{2,1,0:T(8,128)}) %all-reduce.12.cloned.1.call-update) | async-done | bytes 1048592 | tf_op jit(solution)/shard_map/psum | solution.py:28
  325.7 11.9 %all-gather.2 = f32[4,1,512]{2,1,0:T(1,128)S(1)} all-gather(f32[1,1,512]{2,1,0:T(1,128)S(1)} %copy-done.5), channel_id=4, replica_groups=mesh['runs'=2,'tm'=4,'grp'=2,'state'=2] {'tm'}, dimensions={0}, use_global_device_ids=true | all-gather | bytes 10240 | tf_op jit(solution)/shard_map/all_gather | solution.py:11
  338.7 8.9 %psum.45 = f32[1,512]{1,0:T(1,128)S(1)} all-reduce(f32[1,512]{1,0:T(1,128)S(1)} %bitcast.175), channel_id=1, replica_groups=mesh['runs'=2,'tm'=4,'grp'=2,'state'=2] {'tm'}, use_global_device_ids=true, to_apply=%region_11.12 | all-reduce | flops 512 | bytes 4096 | tf_op jit(solution)/shard_map/psum | solution.py:28
  347.6 4.3 %all-gather.5 = f32[2,1,512]{2,1,0:T(1,128)S(1)} all-gather(f32[1,1,512]{2,1,0:T(1,128)S(1)} %bitcast.174), channel_id=1, replica_groups=mesh['runs'=2,'tm'=4,'grp'=2,'state'=2] {'grp'}, dimensions={0}, use_global_device_ids=true | all-gather | bytes 6144 | tf_op jit(solution)/shard_map/all_gather | solution.py:11
  351.9 7.7 %all-gather.15.cloned.1.call-done = f32[2,512,512]{2,1,0:T(8,128)} async-done(((f32[1,512,512]{2,1,0:T(8,128)}), f32[2,512,512]{2,1,0:T(8,128)}) %all-gather.15.cloned.1.call-update) | async-done | bytes 2097168 | tf_op jit(solution)/shard_map/all_gather | solution.py:11
  367.7 11.9 %all-gather.6 = f32[4,1,512]{2,1,0:T(1,128)S(1)} all-gather(f32[1,1,512]{2,1,0:T(1,128)S(1)} %bitcast.163), channel_id=5, replica_groups=mesh['runs'=2,'tm'=4,'grp'=2,'state'=2] {'tm'}, dimensions={0}, use_global_device_ids=true | all-gather | bytes 10240 | tf_op jit(solution)/shard_map/all_gather | solution.py:11
  379.9 10.4 %all-reduce.8 = (f32[1,512]{1,0:T(1,128)S(1)}, f32[1,512]{1,0:T(1,128)S(1)}) all-reduce(f32[1,512]{1,0:T(1,128)S(1)} %bitcast.172, f32[1,512]{1,0:T(1,128)S(1)} %bitcast.171), channel_id=1, replica_groups=mesh['runs'=2,'tm'=4,'grp'=2,'state'=2] {'tm'}, use_global_device_ids=true, to_apply=%region_15.16 | all-reduce | flops 1024 | bytes 8192 | tf_op jit(solution)/shard_map/psum | solution.py:28
  390.3 4.3 %all-gather.7 = f32[2,1,512]{2,1,0:T(1,128)S(1)} all-gather(f32[1,1,512]{2,1,0:T(1,128)S(1)} %bitcast.177), channel_id=1, replica_groups=mesh['runs'=2,'tm'=4,'grp'=2,'state'=2] {'grp'}, dimensions={0}, use_global_device_ids=true | all-gather | bytes 6144 | tf_op jit(solution)/shard_map/all_gather | solution.py:11
  394.6 4.3 %all-gather.8 = f32[2,1,512]{2,1,0:T(1,128)S(1)} all-gather(f32[1,1,512]{2,1,0:T(1,128)S(1)} %bitcast.176), channel_id=1, replica_groups=mesh['runs'=2,'tm'=4,'grp'=2,'state'=2] {'grp'}, dimensions={0}, use_global_device_ids=true | all-gather | bytes 6144 | tf_op jit(solution)/shard_map/all_gather | solution.py:11
  (112 shorter events, 39.7 us)
Async XLA Ops:
  7.2 354.6 %copy-start = (f32[512]{0:T(512)S(1)}, f32[512]{0:T(512)}, u32[]{:S(2)}) copy-start(f32[512]{0:T(512)} %param.19) | copy-start | bytes 6148
  7.2 153.5 %reduce-scatter.2.cloned.1.call-start = ((), (), s32[]{:S(2)}) async-start(), calls=%async_computation.4 | async-start | bytes 786432 | tf_op jit(solution)/shard_map/reduce_scatter | solution.py:110
  132.7 6.8 %copy-start.6 = (bf16[1,16,128]{2,1,0:T(8,128)(2,1)S(1)}, bf16[1,16,128]{2,1,0:T(8,128)(2,1)}, u32[]{:S(2)}) copy-start(bf16[1,16,128]{2,1,0:T(8,128)(2,1)} %param.13) | copy-start | bytes 12292
  132.7 6.8 %copy-start.7 = (s32[1,16]{1,0:T(1,128)S(1)}, s32[1,16]{1,0:T(1,128)}, u32[]{:S(2)}) copy-start(s32[1,16]{1,0:T(1,128)} %param.15) | copy-start | bytes 196
  140.8 8.8 %all-to-all-start.2 = ((bf16[4,16,128]{2,1,0:T(8,128)(2,1)}), bf16[4,16,128]{2,1,0:T(8,128)(2,1)S(1)}, u32[]{:S(2)}, u32[]{:S(2)}) async-start(bf16[4,16,128]{2,1,0:T(8,128)(2,1)} %bitcast.15), calls=%async_computation.3 | async-start | bytes 32768 | tf_op jit(solution)/shard_map/all_to_all | solution.py:87
  144.1 28.2 %all-gather.13.cloned.1.call-start = ((), (), s32[]{:S(2)}) async-start(), calls=%async_computation.5 | async-start | bytes 1572864 | tf_op jit(solution)/shard_map/all_gather | solution.py:123
  149.6 4.5 %copy-start.1 = (bf16[64,128,256]{2,1,0:T(8,128)(2,1)S(1)}, bf16[64,128,256]{2,1,0:T(8,128)(2,1)}, u32[]{:S(2)}) copy-start(bf16[64,128,256]{2,1,0:T(8,128)(2,1)} %all_to_all.26) | copy-start | bytes 12582916
  154.1 7.7 %copy-start.3 = (f32[1,1,512]{2,1,0:T(1,128)S(1)}, f32[1,1,512]{2,1,0:T(1,128)}, u32[]{:S(2)}) copy-start(f32[1,1,512]{2,1,0:T(1,128)} %param.17) | copy-start | bytes 6148
  154.1 7.7 %copy-start.4 = (f32[1,1,512]{2,1,0:T(1,128)S(1)}, f32[1,1,512]{2,1,0:T(1,128)}, u32[]{:S(2)}) copy-start(f32[1,1,512]{2,1,0:T(1,128)} %param.16) | copy-start | bytes 6148
  164.8 91.1 %all-gather.17.cloned.1.call-start = ((), (), s32[]{:S(2)}) async-start(), calls=%async_computation.8 | async-start | bytes 5242880 | tf_op jit(solution)/shard_map/all_gather | solution.py:11
  172.2 153.4 %all-reduce.12.cloned.1.call-start = ((), (), s32[]{:S(2)}) async-start(), calls=%async_computation.6 | async-start | bytes 2097152 | tf_op jit(solution)/shard_map/psum | solution.py:28
  255.8 16.4 %copy-start.2 = (f32[512,512]{1,0:T(8,128)S(1)}, f32[512,512]{1,0:T(8,128)}, u32[]{:S(2)}) copy-start(f32[512,512]{1,0:T(8,128)} %all-gather.13.cloned.1.call-done) | copy-start | bytes 3145732
  272.2 53.4 %copy-start.5 = (f32[1,1,512]{2,1,0:T(1,128)S(1)}, f32[1,1,512]{2,1,0:T(1,128)}, u32[]{:S(2)}) copy-start(f32[1,1,512]{2,1,0:T(1,128)} %param.18) | copy-start | bytes 6148
  275.1 84.5 %all-gather.15.cloned.1.call-start = ((), (), s32[]{:S(2)}) async-start(), calls=%async_computation.7 | async-start | bytes 3145728 | tf_op jit(solution)/shard_map/all_gather | solution.py:11
Sparse Core Ops, SparseCore 0:
  139.7 7.2 reduce-scatter.1
  164.9 7.2 all-gather.12
  173.9 81.9 all-gather.16
  275.2 50.3 all-reduce.11
  327.0 32.5 all-gather.14
where the time goes:
time: 408 us; the launch traced here: 407 us
  blocking collectives  179 us (44%)
  waiting for transfers between devices  142 us (35%)
  matrix products  38.3 us (9%)
  local copies, waits for them, and re-layouts  16.2 us (4%)
  between operations  14.8 us (4%)
  other arithmetic  13.1 us (3%)
    all_to_all x1, blocking collectives, shards(): lax.all_to_all(send_h.reshape(tm_size, capacity, row_num, half_width), 't...  99.5 us
    all_gather x2, waiting for transfers between devices, prefix_2(): pieces = jax.tree.map(lambda part: lax.all_gather(part, axis), value)  78.1 us
    psum x1, waiting for transfers between devices, broadcast(): return lax.psum(jnp.where(mine, array, jnp.zeros_like(array)), axis)  50.5 us
    all_gather x6, blocking collectives, prefix_2(): pieces = jax.tree.map(lambda part: lax.all_gather(part, axis), value)  49.1 us
    dot_general x13, matrix products, matmul_high(): return jnp.dot(left, right, precision=lax.Precision.HIGHEST)  27.1 us
    psum x2, blocking collectives, broadcast(): return lax.psum(jnp.where(mine, array, jnp.zeros_like(array)), axis)  19.3 us
    dot_general x2, matrix products, contract_rows(): lax.dot_general(left, right, (((0,), (0,)), ((), ())), preferred_element_...  11.2 us
  transfers between devices with their start and end apart: 6, of which 5 were waited for; matrix products, arithmetic and copies ran while one was open for 3% of the time, Pallas kernels for 0%

commit v1 on v0

v1 whole, which is shorter than its diff:
```python
import functools

import jax
import jax.numpy as jnp
from jax import lax
from jax.experimental import pallas as pl
from jax.experimental.pallas import tpu as pltpu
from jax.sharding import PartitionSpec as P

STEPS = 4
LANES = 128
GROUP_ROWS = 16
DIRECT_TM = 4

VMEM = pl.BlockSpec(memory_space=pltpu.VMEM)
SMEM = pl.BlockSpec(memory_space=pltpu.SMEM)


def stencil(field, coeff, decay):
    width = field.shape[1]
    cell = lax.broadcasted_iota(jnp.int32, field.shape, 1)
    for _ in range(STEPS):
        upper_cell = jnp.where(cell == 0, 0.0, pltpu.roll(field, 1, 1))
        lower_cell = jnp.where(cell == width - 1, 0.0, pltpu.roll(field, width - 1, 1))
        field = field + coeff * (upper_cell + lower_cell - 2.0 * field) - decay * field
    return field


def row_pass(block, state, meta, y_ref, own_ref, other_ref, acc, part_ref):
    tile_num, row_num, half = own_ref.shape
    core = meta[2 * tile_num]
    own_at = pl.multiple_of(core * half, half)
    other_at = pl.multiple_of((1 - core) * half, half)
    state_own = state[:, pl.ds(own_at, half)]
    state_other = state[:, pl.ds(other_at, half)]
    lane = lax.broadcasted_iota(jnp.int32, (GROUP_ROWS, LANES), 1)
    row = lax.broadcasted_iota(jnp.int32, (GROUP_ROWS, LANES), 0)
    acc[...] = jnp.zeros_like(acc)

    def fold(values):
        total = values[:, :LANES]
        for start in range(LANES, half, LANES):
            total = total + values[:, start : start + LANES]
        return total

    def tile(index, carry):
        @pl.when(meta[index] == block)
        def _():
            live = meta[tile_num + index]
            readings = y_ref[pl.ds(index, 1), :]
            sum_own = jnp.zeros((GROUP_ROWS, half), jnp.float32)
            sum_other = jnp.zeros((GROUP_ROWS, half), jnp.float32)
            squares = jnp.zeros((GROUP_ROWS, LANES), jnp.float32)
            for start in range(0, row_num, GROUP_ROWS):
                own = own_ref[index, start : start + GROUP_ROWS, :].astype(jnp.float32)
                other = other_ref[index, start : start + GROUP_ROWS, :].astype(jnp.float32)
                valid = row + start < live
                product = fold(own * state_own) + fold(other * state_other)
                product = product - jnp.where(lane == row + start, readings, 0.0)
                weight = jnp.sum(product, axis=1, keepdims=True)
                weight = jnp.where(valid[:, :1], weight, 0.0)
                sum_own = sum_own + own * weight
                sum_other = sum_other + other * weight
                squares = squares + jnp.where(valid, fold(own * own) + fold(other * other), 0.0)
            acc[:, :half] += sum_own
            acc[:, half : 2 * half] += sum_other
            acc[:, 2 * half :] += squares

        return carry

    lax.fori_loop(0, tile_num, tile, 0)
    totals = jnp.sum(acc[...], axis=0, keepdims=True)
    part_ref[:, pl.ds(own_at, half)] = totals[:, :half]
    part_ref[:, pl.ds(other_at, half)] = totals[:, half : 2 * half]
    part_ref[:, 2 * half :] = totals[:, 2 * half :]


def first_kernel(block, meta, y_ref, own_ref, other_ref, state_ref, part_ref, acc):
    row_pass(block, state_ref, meta, y_ref, own_ref, other_ref, acc, part_ref)


def advance(parts, state, kappa_ref, rate_ref):
    total = parts[0][...]
    for part in parts[1:]:
        total = total + part[...]
    width = state.shape[1]
    trace_val = jnp.sum(total[:, width:], axis=1, keepdims=True)
    lam_val = width / (2.0 * (width + trace_val))
    innovation = -lam_val * stencil(total[:, :width], kappa_ref, rate_ref)
    return stencil(state, kappa_ref, rate_ref) + innovation, innovation


def step_kernel(block, number, *refs):
    parts, rest = refs[:number], refs[number:]
    meta, y_ref, own_ref, other_ref, state_ref, kappa_ref, rate_ref = rest[:7]
    next_ref, innovation_ref, part_ref, acc = rest[7:]
    updated, innovation = advance(parts, state_ref[...], kappa_ref[...], rate_ref[...])
    next_ref[...] = updated
    innovation_ref[...] = innovation
    if block is None:
        block = meta[2 * y_ref.shape[0] + 1]
    row_pass(block, next_ref, meta, y_ref, own_ref, other_ref, acc, part_ref)


def last_kernel(number, *refs):
    parts, (state_ref, kappa_ref, rate_ref, next_ref, innovation_ref) = refs[:number], refs[number:]
    updated, innovation = advance(parts, state_ref[...], kappa_ref[...], rate_ref[...])
    next_ref[...] = updated
    innovation_ref[...] = innovation


def shards(rows_h, rows_y, tile_block, tile_count, kappa, rate, smooth_gain, start_state):
    tm_size, grp_size = lax.axis_size("tm"), lax.axis_size("grp")
    state_size = lax.axis_size("state")
    tm_index, grp_index, core = (lax.axis_index(name) for name in ("tm", "grp", "state"))
    tile_num, half = rows_h.shape[1], rows_h.shape[3]
    width = kappa.shape[2]
    own = rows_h[0]
    other = lax.ppermute(own, "state", [(i, (i + 1) % state_size) for i in range(state_size)])
    readings = rows_y[0].astype(jnp.float32)
    meta = jnp.concatenate([tile_block[0, :, 0], tile_count[0], core[None].astype(jnp.int32)])
    state = start_state.reshape(1, width)
    direct = tm_size <= DIRECT_TM

    params = jnp.concatenate([kappa[0], rate[0], smooth_gain[0]], axis=0)
    if direct:
        gathered = jnp.zeros((tm_size,) + params.shape, params.dtype)
        gathered = lax.dynamic_update_slice_in_dim(gathered, params[None], tm_index, 0)
        for shift in range(1, tm_size):
            moved = lax.ppermute(params, "tm", [(i, (i + shift) % tm_size) for i in range(tm_size)])
            gathered = lax.dynamic_update_slice_in_dim(
                gathered, moved[None], (tm_index - shift) % tm_size, 0
            )
    else:
        gathered = lax.all_gather(params, "tm")

    vector = jax.ShapeDtypeStruct((1, width), jnp.float32)
    partial = jax.ShapeDtypeStruct((1, width + LANES), jnp.float32)
    acc = pltpu.VMEM((GROUP_ROWS, width + LANES), jnp.float32)

    def first(block, state):
        return pl.pallas_call(
            functools.partial(first_kernel, block),
            out_shape=partial,
            in_specs=[SMEM] + [VMEM] * 4,
            out_specs=VMEM,
            scratch_shapes=[acc],
        )(meta, readings, own, other, state)

    def step(block, parts, state, coeff, decay, meta=meta):
        return pl.pallas_call(
            functools.partial(step_kernel, block, len(parts)),
            out_shape=(vector, vector, partial),
            in_specs=[VMEM] * len(parts) + [SMEM] + [VMEM] * 6,
            out_specs=(VMEM, VMEM, VMEM),
            scratch_shapes=[acc],
        )(*parts, meta, readings, own, other, state, coeff, decay)

    def last(parts, state, coeff, decay):
        return pl.pallas_call(
            functools.partial(last_kernel, len(parts)),
            out_shape=(vector, vector),
            in_specs=[VMEM] * (len(parts) + 3),
            out_specs=(VMEM, VMEM),
        )(*parts, state, coeff, decay)

    def exchange(part, group):
        parts = [part]
        for shift in range(1, tm_size):
            pairs = [
                (i * grp_size + group, (i + shift) % tm_size * grp_size + group)
                for i in range(tm_size)
            ]
            parts.append(lax.ppermute(part, ("tm", "grp"), pairs))
        return parts

    def coefficients(position):
        return gathered[position][0:1], gathered[position][1:2]

    def group_direct(state, group):
        states, innovations = [], []
        part = first(0, state)
        for block in range(tm_size):
            parts = exchange(part, group)
            if block < tm_size - 1:
                state, innovation, part = step(block + 1, parts, state, *coefficients(block))
            else:
                state, innovation = last(parts, state, *coefficients(block))
            states.append(state)
            innovations.append(innovation)
        return jnp.concatenate(states, 0), jnp.concatenate(innovations, 0)

    def group_loop(state, group):
        part = first(0, state)

        def lap(block, carry):
            state, part, states, innovations = carry
            here = lax.dynamic_index_in_dim(gathered, block, 0, False)
            own_meta = jnp.concatenate([meta, (block + 1)[None].astype(jnp.int32)])
            state, innovation, part = step(
                None, [lax.psum(part, "tm")], state, here[0:1], here[1:2], own_meta
            )
            states = lax.dynamic_update_slice_in_dim(states, state, block, 0)
            innovations = lax.dynamic_update_slice_in_dim(innovations, innovation, block, 0)
            return state, part, states, innovations

        empty = jnp.zeros((tm_size, width), jnp.float32)
        return lax.fori_loop(0, tm_size, lap, (state, part, empty, empty))[2:]

    states = innovations = jnp.zeros((tm_size, width), jnp.float32)
    for group in range(grp_size):
        new_states, new_innovations = (group_direct if direct else group_loop)(state, group)
        mine = grp_index == group
        states = jnp.where(mine, new_states, states)
        innovations = jnp.where(mine, new_innovations, innovations)
        if group < grp_size - 1:
            state = lax.ppermute(new_states[-1:], "grp", [(group, group + 1)])

    gains = gathered[:, 2]
    residual = jnp.zeros((1, width), jnp.float32)
    residuals = [None] * tm_size
    for group in reversed(range(grp_size)):
        running = residual
        for block in reversed(range(tm_size)):
            residuals[block] = running
            running = gains[block][None] * (running + innovations[block][None])
        if group > 0:
            arrived = lax.ppermute(running, "grp", [(group, group - 1)])
            residual = jnp.where(grp_index == group - 1, arrived, residual)
    smoothed = states + jnp.concatenate(residuals, 0)

    def out(values):
        piece = lax.dynamic_slice(values, (tm_index, core * half), (1, half))
        return piece.reshape(1, 1, half)

    return out(states), out(smoothed)


def solution(mesh):
    return jax.shard_map(
        shards,
        mesh=mesh,
        in_specs=(
            P(("runs", "grp"), "tm", None, "state"),
            P(("runs", "grp"), "tm", None),
            P(("runs", "grp"), "tm", None),
            P(("runs", "grp"), "tm"),
            P(("runs", "grp"), "tm", None),
            P(("runs", "grp"), "tm", None),
            P(("runs", "grp"), "tm", None),
            P("runs"),
        ),
        out_specs=(P(("runs", "grp"), "tm", "state"), P(("runs", "grp"), "tm", "state")),
        check_vma=False,
    )
```

time: 408 us -> 160 us (0.39)
  blocking collectives: 179 us -> 0 us
  waiting for transfers between devices: 142 us -> 59.3 us
  starting transfers between devices: 3.44 us -> 57.1 us
  matrix products: 38.3 us -> 0 us
  Pallas kernels: 0 us -> 28.3 us
  between operations: 14.8 us -> 1.41 us
  other arithmetic: 13.1 us -> 2.64 us
  local copies, waits for them, and re-layouts: 16.2 us -> 10.8 us
    all_to_all x2 -> x0, blocking collectives: 108 us -> none  [the longest x1 99.5 us: shards(): lax.all_to_all(send_h.reshape(tm_size, capacity, row_num, half_width), 't...]
    all_gather x3 -> x0, waiting for transfers between devices: 85.5 us -> none  [the longest x2 78.1 us: prefix_2(): pieces = jax.tree.map(lambda part: lax.all_gather(part, axis), value)]
    ppermute x0 -> x30, waiting for transfers between devices: none -> 59.3 us  [the longest x1 46.6 us: shards(): arrived = lax.ppermute(running, 'grp', [(group, group - 1)])]
    ppermute x0 -> x30, starting transfers between devices: none -> 57.1 us  [the longest x24 47.5 us: exchange(): parts.append(lax.ppermute(part, ('tm', 'grp'), pairs))]
    psum x1 -> x0, waiting for transfers between devices: 50.5 us -> none  [broadcast(): return lax.psum(jnp.where(mine, array, jnp.zeros_like(array)), axis)]
    all_gather x6 -> x0, blocking collectives: 49.1 us -> none  [prefix_2(): pieces = jax.tree.map(lambda part: lax.all_gather(part, axis), value)]
    dot_general x15 -> x0, matrix products: 38.3 us -> none  [the longest x13 27.1 us: matmul_high(): return jnp.dot(left, right, precision=lax.Precision.HIGHEST)]
    pallas_call x0 -> x10, Pallas kernels: none -> 28.3 us  [the longest x6 16.7 us: step(): pl.pallas_call(functools.partial(step_kernel, block, len(parts)), out_sha...]
  transfers between devices with their start and end apart: 6 -> 30, of which waited for: 5 -> 8; matrix products, arithmetic and copies ran while one was open for 3% -> 1% of each run, Pallas kernels for 0% -> 0%
where the time goes in v1:
time: 160 us
  waiting for transfers between devices  59.3 us (37%)
  starting transfers between devices  57.1 us (36%)
  Pallas kernels  28.3 us (18%)
  local copies, waits for them, and re-layouts  10.8 us (7%)
  other arithmetic  2.64 us (2%)
    ppermute x24, starting transfers between devices, exchange(): parts.append(lax.ppermute(part, ('tm', 'grp'), pairs))  47.5 us
    ppermute x1, waiting for transfers between devices, shards(): arrived = lax.ppermute(running, 'grp', [(group, group - 1)])  46.6 us
    pallas_call x6, Pallas kernels, step(): pl.pallas_call(functools.partial(step_kernel, block, len(parts)), out_sha...  16.7 us
    ppermute x24, waiting for transfers between devices, exchange(): parts.append(lax.ppermute(part, ('tm', 'grp'), pairs))  11.2 us
    unnamed x96, local copies, waits for them, and re-layouts  10.1 us
    pallas_call x2, Pallas kernels, first(): pl.pallas_call(functools.partial(first_kernel, block), out_shape=partial,...  8.22 us
    ppermute x3, starting transfers between devices, shards(): lax.ppermute(params, 'tm', [(i, (i + shift) % tm_size) for i in range(tm_...  7.01 us
    pallas_call x2, Pallas kernels, last(): pl.pallas_call(functools.partial(last_kernel, len(parts)), out_shape=(vec...  3.38 us
  transfers between devices with their start and end apart: 30, of which 8 were waited for; matrix products, arithmetic and copies ran while one was open for 1% of the time, Pallas kernels for 0%

profile of v1, /device:TPU:0, one launch (start us, length us, event | category | flops | bytes accessed | tf_op | source)
XLA Modules:
  0.0 159.6 jit_solution(3582203731127152803)
XLA Ops:
  2.0 3.1 %collective-permute-start.4 = (f32[3,512]{1,0:T(4,128)S(1)}, f32[3,512]{1,0:T(4,128)S(1)}, u32[]{:S(2)}, u32[]{:S(2)}) collective-permute-start(f32[3,512]{1,0:T(4,128)S(1)} %pad_maximum_fusion), channel_id=1, source_target_pairs={{0,4},{4,8},{8,12},{12,0},{1,5},{5,9},{9,13},{13,1},{2,6},{6,10},{... | collective-permute-start | bytes 18440 | tf_op jit(solution)/shard_map/ppermute | solution.py:130
  5.1 2.6 %collective-permute-start.5 = (f32[3,512]{1,0:T(4,128)S(1)}, f32[3,512]{1,0:T(4,128)S(1)}, u32[]{:S(2)}, u32[]{:S(2)}) collective-permute-start(f32[3,512]{1,0:T(4,128)S(1)} %pad_maximum_fusion), channel_id=1, source_target_pairs={{0,8},{4,12},{8,0},{12,4},{1,9},{5,13},{9,1},{13,5},{2,10},{6,14},... | collective-permute-start | bytes 18440 | tf_op jit(solution)/shard_map/ppermute | solution.py:130
  13.3 4.1 %shard_map.95.refs_0_ = f32[1,640]{1,0:T(1,128)} custom-call(s32[33]{0:T(128)} %pad_add_fusion.meta.refs_4_, f32[16,128]{1,0:T(8,128)} %bitcast_convert_fusion.y_ref.refs_5_, bf16[16,128,256]{2,1,0:T(8,128)(2,1)} %bitcast.64, bf16[16,128,256]{2,1,0:T(8,128)(2,1)} %copy-done, f32[1,512]{1,0:T(1,128)} %bitcast.78), custom_call_target="tpu_custom_call" | custom-call | tf_op jit(solution)/shard_map/pallas_call | solution.py:142
  19.3 3.7 %collective-permute-start.2 = (f32[1,640]{1,0:T(1,128)}, f32[1,640]{1,0:T(1,128)S(1)}, u32[]{:S(2)}, u32[]{:S(2)}) collective-permute-start(f32[1,640]{1,0:T(1,128)} %shard_map.95.refs_0_), channel_id=1, source_target_pairs={{0,8},{4,12},{8,0},{12,4},{1,9},{5,13},{9,1},{13,5},{16,24},{20,28... | collective-permute-start | bytes 7688 | tf_op jit(solution)/shard_map/ppermute | solution.py:174
  23.0 4.0 %collective-permute-start.3 = (f32[1,640]{1,0:T(1,128)}, f32[1,640]{1,0:T(1,128)S(1)}, u32[]{:S(2)}, u32[]{:S(2)}) collective-permute-start(f32[1,640]{1,0:T(1,128)} %shard_map.95.refs_0_), channel_id=1, source_target_pairs={{0,12},{4,0},{8,4},{12,8},{1,13},{5,1},{9,5},{13,9},{16,28},{20,16... | collective-permute-start | bytes 7688 | tf_op jit(solution)/shard_map/ppermute | solution.py:174
  29.9 2.8 %shard_map.96 = (f32[1,512]{1,0:T(1,128)}, f32[1,512]{1,0:T(1,128)}, f32[1,640]{1,0:T(1,128)}) custom-call(f32[1,640]{1,0:T(1,128)} %shard_map.95.refs_0_, f32[1,640]{1,0:T(1,128)} %copy-done.12, f32[1,640]{1,0:T(1,128)} %copy-done.13, f32[1,640]{1,0:T(1,128)} %copy-done.15, s32[33]{0:T(128)} %pad_add_fusion.meta.refs_4_, ...), custom_call_target="tpu_custom_call" | custom-call | tf_op jit(solution)/shard_map/pallas_call | solution.py:151
  32.7 4.1 %collective-permute-start.7 = (f32[1,640]{1,0:T(1,128)}, f32[1,640]{1,0:T(1,128)S(1)}, u32[]{:S(2)}, u32[]{:S(2)}) collective-permute-start(f32[1,640]{1,0:T(1,128)} %get-tuple-element.24.refs_0_), channel_id=1, source_target_pairs={{0,4},{4,8},{8,12},{12,0},{1,5},{5,9},{9,13},{13,1},{16,20},{20,24... | collective-permute-start | bytes 7688 | tf_op jit(solution)/shard_map/ppermute | solution.py:174
  36.8 3.7 %collective-permute-start.8 = (f32[1,640]{1,0:T(1,128)}, f32[1,640]{1,0:T(1,128)S(1)}, u32[]{:S(2)}, u32[]{:S(2)}) collective-permute-start(f32[1,640]{1,0:T(1,128)} %get-tuple-element.24.refs_0_), channel_id=1, source_target_pairs={{0,8},{4,12},{8,0},{12,4},{1,9},{5,13},{9,1},{13,5},{16,24},{20,28... | collective-permute-start | bytes 7688 | tf_op jit(solution)/shard_map/ppermute | solution.py:174
  40.6 2.5 %collective-permute-start.9 = (f32[1,640]{1,0:T(1,128)}, f32[1,640]{1,0:T(1,128)S(1)}, u32[]{:S(2)}, u32[]{:S(2)}) collective-permute-start(f32[1,640]{1,0:T(1,128)} %get-tuple-element.24.refs_0_), channel_id=1, source_target_pairs={{0,12},{4,0},{8,4},{12,8},{1,13},{5,1},{9,5},{13,9},{16,28},{20,16... | collective-permute-start | bytes 7688 | tf_op jit(solution)/shard_map/ppermute | solution.py:174
  43.4 2.8 %collective-permute-done.9.refs_3_ = f32[1,640]{1,0:T(1,128)S(1)} collective-permute-done((f32[1,640]{1,0:T(1,128)}, f32[1,640]{1,0:T(1,128)S(1)}, u32[]{:S(2)}, u32[]{:S(2)}) %collective-permute-start.9) | collective-permute-done | bytes 2592 | tf_op jit(solution)/shard_map/ppermute | solution.py:174
  46.8 2.8 %shard_map.97 = (f32[1,512]{1,0:T(1,128)}, f32[1,512]{1,0:T(1,128)}, f32[1,640]{1,0:T(1,128)}) custom-call(f32[1,640]{1,0:T(1,128)} %get-tuple-element.24.refs_0_, f32[1,640]{1,0:T(1,128)} %copy-done.19, f32[1,640]{1,0:T(1,128)} %copy-done.24, f32[1,640]{1,0:T(1,128)} %copy-done.28, s32[33]{0:T(128)} %pad_add_fusion.meta.refs_4_, ...), custom_call_target="tpu_custom_call" | custom-call | tf_op jit(solution)/shard_map/pallas_call | solution.py:151
  49.6 2.6 %collective-permute-start.10 = (f32[1,640]{1,0:T(1,128)}, f32[1,640]{1,0:T(1,128)S(1)}, u32[]{:S(2)}, u32[]{:S(2)}) collective-permute-start(f32[1,640]{1,0:T(1,128)} %get-tuple-element.26.refs_0_), channel_id=1, source_target_pairs={{0,4},{4,8},{8,12},{12,0},{1,5},{5,9},{9,13},{13,1},{16,20},{20,24... | collective-permute-start | bytes 7688 | tf_op jit(solution)/shard_map/ppermute | solution.py:174
  52.2 4.5 %collective-permute-start.11 = (f32[1,640]{1,0:T(1,128)}, f32[1,640]{1,0:T(1,128)S(1)}, u32[]{:S(2)}, u32[]{:S(2)}) collective-permute-start(f32[1,640]{1,0:T(1,128)} %get-tuple-element.26.refs_0_), channel_id=1, source_target_pairs={{0,8},{4,12},{8,0},{12,4},{1,9},{5,13},{9,1},{13,5},{16,24},{20,28... | collective-permute-start | bytes 7688 | tf_op jit(solution)/shard_map/ppermute | solution.py:174
  56.7 3.0 %collective-permute-start.12 = (f32[1,640]{1,0:T(1,128)}, f32[1,640]{1,0:T(1,128)S(1)}, u32[]{:S(2)}, u32[]{:S(2)}) collective-permute-start(f32[1,640]{1,0:T(1,128)} %get-tuple-element.26.refs_0_), channel_id=1, source_target_pairs={{0,12},{4,0},{8,4},{12,8},{1,13},{5,1},{9,5},{13,9},{16,28},{20,16... | collective-permute-start | bytes 7688 | tf_op jit(solution)/shard_map/ppermute | solution.py:174
  59.8 2.6 %collective-permute-done.12.refs_3_ = f32[1,640]{1,0:T(1,128)S(1)} collective-permute-done((f32[1,640]{1,0:T(1,128)}, f32[1,640]{1,0:T(1,128)S(1)}, u32[]{:S(2)}, u32[]{:S(2)}) %collective-permute-start.12) | collective-permute-done | bytes 2592 | tf_op jit(solution)/shard_map/ppermute | solution.py:174
  62.9 2.8 %shard_map.98 = (f32[1,512]{1,0:T(1,128)}, f32[1,512]{1,0:T(1,128)}, f32[1,640]{1,0:T(1,128)}) custom-call(f32[1,640]{1,0:T(1,128)} %get-tuple-element.26.refs_0_, f32[1,640]{1,0:T(1,128)} %copy-done.20, f32[1,640]{1,0:T(1,128)} %copy-done.25, f32[1,640]{1,0:T(1,128)} %copy-done.29, s32[33]{0:T(128)} %pad_add_fusion.meta.refs_4_, ...), custom_call_target="tpu_custom_call" | custom-call | tf_op jit(solution)/shard_map/pallas_call | solution.py:151
  65.7 3.5 %collective-permute-start.13 = (f32[1,640]{1,0:T(1,128)}, f32[1,640]{1,0:T(1,128)S(1)}, u32[]{:S(2)}, u32[]{:S(2)}) collective-permute-start(f32[1,640]{1,0:T(1,128)} %get-tuple-element.28.refs_0_), channel_id=1, source_target_pairs={{0,4},{4,8},{8,12},{12,0},{1,5},{5,9},{9,13},{13,1},{16,20},{20,24... | collective-permute-start | bytes 7688 | tf_op jit(solution)/shard_map/ppermute | solution.py:174
  69.2 4.2 %collective-permute-start.14 = (f32[1,640]{1,0:T(1,128)}, f32[1,640]{1,0:T(1,128)S(1)}, u32[]{:S(2)}, u32[]{:S(2)}) collective-permute-start(f32[1,640]{1,0:T(1,128)} %get-tuple-element.28.refs_0_), channel_id=1, source_target_pairs={{0,8},{4,12},{8,0},{12,4},{1,9},{5,13},{9,1},{13,5},{16,24},{20,28... | collective-permute-start | bytes 7688 | tf_op jit(solution)/shard_map/ppermute | solution.py:174
  75.8 3.4 %collective-permute-done.15.refs_3_ = f32[1,640]{1,0:T(1,128)S(1)} collective-permute-done((f32[1,640]{1,0:T(1,128)}, f32[1,640]{1,0:T(1,128)S(1)}, u32[]{:S(2)}, u32[]{:S(2)}) %collective-permute-start.15) | collective-permute-done | bytes 2592 | tf_op jit(solution)/shard_map/ppermute | solution.py:174
  84.8 4.1 %shard_map.100.refs_0_ = f32[1,640]{1,0:T(1,128)} custom-call(s32[33]{0:T(128)} %pad_add_fusion.meta.refs_4_, f32[16,128]{1,0:T(8,128)} %bitcast_convert_fusion.y_ref.refs_5_, bf16[16,128,256]{2,1,0:T(8,128)(2,1)} %bitcast.68, bf16[16,128,256]{2,1,0:T(8,128)(2,1)} %copy-done, f32[1,512]{1,0:T(1,128)} %copy-done.10), custom_call_target="tpu_custom_call" | custom-call | tf_op jit(solution)/shard_map/pallas_call | solution.py:142
  92.1 2.8 %shard_map.101 = (f32[1,512]{1,0:T(1,128)}, f32[1,512]{1,0:T(1,128)}, f32[1,640]{1,0:T(1,128)}) custom-call(f32[1,640]{1,0:T(1,128)} %shard_map.100.refs_0_, f32[1,640]{1,0:T(1,128)} %copy-done.16, f32[1,640]{1,0:T(1,128)} %copy-done.21, f32[1,640]{1,0:T(1,128)} %copy-done.26, s32[33]{0:T(128)} %pad_add_fusion.meta.refs_4_, ...), custom_call_target="tpu_custom_call" | custom-call | tf_op jit(solution)/shard_map/pallas_call | solution.py:151
  97.5 2.8 %shard_map.102 = (f32[1,512]{1,0:T(1,128)}, f32[1,512]{1,0:T(1,128)}, f32[1,640]{1,0:T(1,128)}) custom-call(f32[1,640]{1,0:T(1,128)} %get-tuple-element.32.refs_0_, f32[1,640]{1,0:T(1,128)} %copy-done.17, f32[1,640]{1,0:T(1,128)} %copy-done.22, f32[1,640]{1,0:T(1,128)} %copy-done.27, s32[33]{0:T(128)} %pad_add_fusion.meta.refs_4_, ...), custom_call_target="tpu_custom_call" | custom-call | tf_op jit(solution)/shard_map/pallas_call | solution.py:151
  102.9 2.8 %shard_map.103 = (f32[1,512]{1,0:T(1,128)}, f32[1,512]{1,0:T(1,128)}, f32[1,640]{1,0:T(1,128)}) custom-call(f32[1,640]{1,0:T(1,128)} %get-tuple-element.34.refs_0_, f32[1,640]{1,0:T(1,128)} %copy-done.14, f32[1,640]{1,0:T(1,128)} %copy-done.18, f32[1,640]{1,0:T(1,128)} %copy-done.23, s32[33]{0:T(128)} %pad_add_fusion.meta.refs_4_, ...), custom_call_target="tpu_custom_call" | custom-call | tf_op jit(solution)/shard_map/pallas_call | solution.py:151
  112.3 46.6 %collective-permute-done.29 = f32[1,512]{1,0:T(1,128)S(1)} collective-permute-done((f32[1,512]{1,0:T(1,128)S(1)}, f32[1,512]{1,0:T(1,128)S(1)}, u32[]{:S(2)}, u32[]{:S(2)}) %collective-permute-start.29) | collective-permute-done | bytes 2080 | tf_op jit(solution)/shard_map/ppermute | solution.py:228
  (156 shorter events, 36.4 us)
Async XLA Ops:
  2.0 10.2 %collective-permute-start.4 = (f32[3,512]{1,0:T(4,128)S(1)}, f32[3,512]{1,0:T(4,128)S(1)}, u32[]{:S(2)}, u32[]{:S(2)}) collective-permute-start(f32[3,512]{1,0:T(4,128)S(1)} %pad_maximum_fusion), channel_id=1, source_target_pairs={{0,4},{4,8},{8,12},{12,0},{1,5},{5,9},{9,13},{13,1},{2,6},{6,10},{... | collective-permute-start | bytes 18440 | tf_op jit(solution)/shard_map/ppermute | solution.py:130
  5.1 7.2 %collective-permute-start.5 = (f32[3,512]{1,0:T(4,128)S(1)}, f32[3,512]{1,0:T(4,128)S(1)}, u32[]{:S(2)}, u32[]{:S(2)}) collective-permute-start(f32[3,512]{1,0:T(4,128)S(1)} %pad_maximum_fusion), channel_id=1, source_target_pairs={{0,8},{4,12},{8,0},{12,4},{1,9},{5,13},{9,1},{13,5},{2,10},{6,14},... | collective-permute-start | bytes 18440 | tf_op jit(solution)/shard_map/ppermute | solution.py:130
  7.7 4.6 %collective-permute-start.6 = (f32[3,512]{1,0:T(4,128)S(1)}, f32[3,512]{1,0:T(4,128)S(1)}, u32[]{:S(2)}, u32[]{:S(2)}) collective-permute-start(f32[3,512]{1,0:T(4,128)S(1)} %pad_maximum_fusion), channel_id=1, source_target_pairs={{0,12},{4,0},{8,4},{12,8},{1,13},{5,1},{9,5},{13,9},{2,14},{6,2},{... | collective-permute-start | bytes 18440 | tf_op jit(solution)/shard_map/ppermute | solution.py:130
  9.0 3.3 %collective-permute-start = (bf16[16,128,256]{2,1,0:T(8,128)(2,1)}, bf16[16,128,256]{2,1,0:T(8,128)(2,1)S(1)}, u32[]{:S(2)}, u32[]{:S(2)}) collective-permute-start(bf16[16,128,256]{2,1,0:T(8,128)(2,1)} %bitcast.63), channel_id=1, source_target_pairs={{0,1},{1,0},{2,3},{3,2},{4,5},{5,4},{6,7},{7,6},{8,9},{9,8},{10,11... | collective-permute-start | bytes 3145736 | tf_op jit(solution)/shard_map/ppermute | solution.py:119
  17.4 10.2 %collective-permute-start.1 = (f32[1,640]{1,0:T(1,128)}, f32[1,640]{1,0:T(1,128)S(1)}, u32[]{:S(2)}, u32[]{:S(2)}) collective-permute-start(f32[1,640]{1,0:T(1,128)} %shard_map.95.refs_0_), channel_id=1, source_target_pairs={{0,4},{4,8},{8,12},{12,0},{1,5},{5,9},{9,13},{13,1},{16,20},{20,24... | collective-permute-start | bytes 7688 | tf_op jit(solution)/shard_map/ppermute | solution.py:174
  19.3 8.3 %collective-permute-start.2 = (f32[1,640]{1,0:T(1,128)}, f32[1,640]{1,0:T(1,128)S(1)}, u32[]{:S(2)}, u32[]{:S(2)}) collective-permute-start(f32[1,640]{1,0:T(1,128)} %shard_map.95.refs_0_), channel_id=1, source_target_pairs={{0,8},{4,12},{8,0},{12,4},{1,9},{5,13},{9,1},{13,5},{16,24},{20,28... | collective-permute-start | bytes 7688 | tf_op jit(solution)/shard_map/ppermute | solution.py:174
  23.0 6.3 %collective-permute-start.3 = (f32[1,640]{1,0:T(1,128)}, f32[1,640]{1,0:T(1,128)S(1)}, u32[]{:S(2)}, u32[]{:S(2)}) collective-permute-start(f32[1,640]{1,0:T(1,128)} %shard_map.95.refs_0_), channel_id=1, source_target_pairs={{0,12},{4,0},{8,4},{12,8},{1,13},{5,1},{9,5},{13,9},{16,28},{20,16... | collective-permute-start | bytes 7688 | tf_op jit(solution)/shard_map/ppermute | solution.py:174
  32.7 10.3 %collective-permute-start.7 = (f32[1,640]{1,0:T(1,128)}, f32[1,640]{1,0:T(1,128)S(1)}, u32[]{:S(2)}, u32[]{:S(2)}) collective-permute-start(f32[1,640]{1,0:T(1,128)} %get-tuple-element.24.refs_0_), channel_id=1, source_target_pairs={{0,4},{4,8},{8,12},{12,0},{1,5},{5,9},{9,13},{13,1},{16,20},{20,24... | collective-permute-start | bytes 7688 | tf_op jit(solution)/shard_map/ppermute | solution.py:174
  36.8 6.6 %collective-permute-start.8 = (f32[1,640]{1,0:T(1,128)}, f32[1,640]{1,0:T(1,128)S(1)}, u32[]{:S(2)}, u32[]{:S(2)}) collective-permute-start(f32[1,640]{1,0:T(1,128)} %get-tuple-element.24.refs_0_), channel_id=1, source_target_pairs={{0,8},{4,12},{8,0},{12,4},{1,9},{5,13},{9,1},{13,5},{16,24},{20,28... | collective-permute-start | bytes 7688 | tf_op jit(solution)/shard_map/ppermute | solution.py:174
  40.6 5.7 %collective-permute-start.9 = (f32[1,640]{1,0:T(1,128)}, f32[1,640]{1,0:T(1,128)S(1)}, u32[]{:S(2)}, u32[]{:S(2)}) collective-permute-start(f32[1,640]{1,0:T(1,128)} %get-tuple-element.24.refs_0_), channel_id=1, source_target_pairs={{0,12},{4,0},{8,4},{12,8},{1,13},{5,1},{9,5},{13,9},{16,28},{20,16... | collective-permute-start | bytes 7688 | tf_op jit(solution)/shard_map/ppermute | solution.py:174
  49.6 10.1 %collective-permute-start.10 = (f32[1,640]{1,0:T(1,128)}, f32[1,640]{1,0:T(1,128)S(1)}, u32[]{:S(2)}, u32[]{:S(2)}) collective-permute-start(f32[1,640]{1,0:T(1,128)} %get-tuple-element.26.refs_0_), channel_id=1, source_target_pairs={{0,4},{4,8},{8,12},{12,0},{1,5},{5,9},{9,13},{13,1},{16,20},{20,24... | collective-permute-start | bytes 7688 | tf_op jit(solution)/shard_map/ppermute | solution.py:174
  52.2 7.6 %collective-permute-start.11 = (f32[1,640]{1,0:T(1,128)}, f32[1,640]{1,0:T(1,128)S(1)}, u32[]{:S(2)}, u32[]{:S(2)}) collective-permute-start(f32[1,640]{1,0:T(1,128)} %get-tuple-element.26.refs_0_), channel_id=1, source_target_pairs={{0,8},{4,12},{8,0},{12,4},{1,9},{5,13},{9,1},{13,5},{16,24},{20,28... | collective-permute-start | bytes 7688 | tf_op jit(solution)/shard_map/ppermute | solution.py:174
  56.7 5.7 %collective-permute-start.12 = (f32[1,640]{1,0:T(1,128)}, f32[1,640]{1,0:T(1,128)S(1)}, u32[]{:S(2)}, u32[]{:S(2)}) collective-permute-start(f32[1,640]{1,0:T(1,128)} %get-tuple-element.26.refs_0_), channel_id=1, source_target_pairs={{0,12},{4,0},{8,4},{12,8},{1,13},{5,1},{9,5},{13,9},{16,28},{20,16... | collective-permute-start | bytes 7688 | tf_op jit(solution)/shard_map/ppermute | solution.py:174
  65.7 9.7 %collective-permute-start.13 = (f32[1,640]{1,0:T(1,128)}, f32[1,640]{1,0:T(1,128)S(1)}, u32[]{:S(2)}, u32[]{:S(2)}) collective-permute-start(f32[1,640]{1,0:T(1,128)} %get-tuple-element.28.refs_0_), channel_id=1, source_target_pairs={{0,4},{4,8},{8,12},{12,0},{1,5},{5,9},{9,13},{13,1},{16,20},{20,24... | collective-permute-start | bytes 7688 | tf_op jit(solution)/shard_map/ppermute | solution.py:174
  69.2 6.6 %collective-permute-start.14 = (f32[1,640]{1,0:T(1,128)}, f32[1,640]{1,0:T(1,128)S(1)}, u32[]{:S(2)}, u32[]{:S(2)}) collective-permute-start(f32[1,640]{1,0:T(1,128)} %get-tuple-element.28.refs_0_), channel_id=1, source_target_pairs={{0,8},{4,12},{8,0},{12,4},{1,9},{5,13},{9,1},{13,5},{16,24},{20,28... | collective-permute-start | bytes 7688 | tf_op jit(solution)/shard_map/ppermute | solution.py:174
  73.5 5.7 %collective-permute-start.15 = (f32[1,640]{1,0:T(1,128)}, f32[1,640]{1,0:T(1,128)S(1)}, u32[]{:S(2)}, u32[]{:S(2)}) collective-permute-start(f32[1,640]{1,0:T(1,128)} %get-tuple-element.28.refs_0_), channel_id=1, source_target_pairs={{0,12},{4,0},{8,4},{12,8},{1,13},{5,1},{9,5},{13,9},{16,28},{20,16... | collective-permute-start | bytes 7688 | tf_op jit(solution)/shard_map/ppermute | solution.py:174
  81.4 2.8 %collective-permute-start.16 = (f32[1,512]{1,0:T(1,128)}, f32[1,512]{1,0:T(1,128)S(1)}, u32[]{:S(2)}, u32[]{:S(2)}) collective-permute-start(f32[1,512]{1,0:T(1,128)} %get-tuple-element.30), channel_id=1, source_target_pairs={{0,2},{1,3},{4,6},{5,7},{8,10},{9,11},{12,14},{13,15},{16,18},{17,... | collective-permute-start | bytes 6152 | tf_op jit(solution)/shard_map/ppermute | solution.py:217
  88.9 2.0 %collective-permute-start.17 = (f32[1,640]{1,0:T(1,128)}, f32[1,640]{1,0:T(1,128)S(1)}, u32[]{:S(2)}, u32[]{:S(2)}) collective-permute-start(f32[1,640]{1,0:T(1,128)} %shard_map.100.refs_0_), channel_id=1, source_target_pairs={{2,6},{6,10},{10,14},{14,2},{3,7},{7,11},{11,15},{15,3},{18,22},{2... | collective-permute-start | bytes 7688 | tf_op jit(solution)/shard_map/ppermute | solution.py:174
  89.6 1.4 collective-permute-start.18
  94.9 2.0 %collective-permute-start.20 = (f32[1,640]{1,0:T(1,128)}, f32[1,640]{1,0:T(1,128)S(1)}, u32[]{:S(2)}, u32[]{:S(2)}) collective-permute-start(f32[1,640]{1,0:T(1,128)} %get-tuple-element.32.refs_0_), channel_id=1, source_target_pairs={{2,6},{6,10},{10,14},{14,2},{3,7},{7,11},{11,15},{15,3},{18,22},{2... | collective-permute-start | bytes 7688 | tf_op jit(solution)/shard_map/ppermute | solution.py:174
  100.3 2.0 %collective-permute-start.23 = (f32[1,640]{1,0:T(1,128)}, f32[1,640]{1,0:T(1,128)S(1)}, u32[]{:S(2)}, u32[]{:S(2)}) collective-permute-start(f32[1,640]{1,0:T(1,128)} %get-tuple-element.34.refs_0_), channel_id=1, source_target_pairs={{2,6},{6,10},{10,14},{14,2},{3,7},{7,11},{11,15},{15,3},{18,22},{2... | collective-permute-start | bytes 7688 | tf_op jit(solution)/shard_map/ppermute | solution.py:174
  105.7 2.0 %collective-permute-start.26 = (f32[1,640]{1,0:T(1,128)}, f32[1,640]{1,0:T(1,128)S(1)}, u32[]{:S(2)}, u32[]{:S(2)}) collective-permute-start(f32[1,640]{1,0:T(1,128)} %get-tuple-element.36.refs_0_), channel_id=1, source_target_pairs={{2,6},{6,10},{10,14},{14,2},{3,7},{7,11},{11,15},{15,3},{18,22},{2... | collective-permute-start | bytes 7688 | tf_op jit(solution)/shard_map/ppermute | solution.py:174
  106.4 1.4 collective-permute-start.27
  110.9 48.0 %collective-permute-start.29 = (f32[1,512]{1,0:T(1,128)S(1)}, f32[1,512]{1,0:T(1,128)S(1)}, u32[]{:S(2)}, u32[]{:S(2)}) collective-permute-start(f32[1,512]{1,0:T(1,128)S(1)} %fusion), channel_id=1, source_target_pairs={{2,0},{3,1},{6,4},{7,5},{10,8},{11,9},{14,12},{15,13},{18,16},{19,... | collective-permute-start | bytes 6152 | tf_op jit(solution)/shard_map/ppermute | solution.py:228
  (54 other events, 74.8 us)

commit v2 on v1

--- a/solution.py
+++ b/solution.py
@@ -13,6 +13,7 @@
 DIRECT_TM = 4
 
 VMEM = pl.BlockSpec(memory_space=pltpu.VMEM)
+KERNEL = pltpu.CompilerParams(vmem_limit_bytes=8 * 2**20)
 SMEM = pl.BlockSpec(memory_space=pltpu.SMEM)
 
 
@@ -120,17 +121,18 @@
     readings = rows_y[0].astype(jnp.float32)
     meta = jnp.concatenate([tile_block[0, :, 0], tile_count[0], core[None].astype(jnp.int32)])
     state = start_state.reshape(1, width)
-    direct = tm_size <= DIRECT_TM
+    direct = tm_size <= DIRECT_TM and tm_size & (tm_size - 1) == 0
+
+    def exchange(part):
+        parts = [part]
+        for flip in range(1, tm_size):
+            parts.append(lax.ppermute(part, "tm", [(i, i ^ flip) for i in range(tm_size)]))
+        return parts
 
     params = jnp.concatenate([kappa[0], rate[0], smooth_gain[0]], axis=0)
     if direct:
-        gathered = jnp.zeros((tm_size,) + params.shape, params.dtype)
-        gathered = lax.dynamic_update_slice_in_dim(gathered, params[None], tm_index, 0)
-        for shift in range(1, tm_size):
-            moved = lax.ppermute(params, "tm", [(i, (i + shift) % tm_size) for i in range(tm_size)])
-            gathered = lax.dynamic_update_slice_in_dim(
-                gathered, moved[None], (tm_index - shift) % tm_size, 0
-            )
+        pieces = jnp.stack(exchange(params))
+        gathered = pieces[jnp.arange(tm_size) ^ tm_index]
     else:
         gathered = lax.all_gather(params, "tm")
 
@@ -145,6 +147,7 @@
             in_specs=[SMEM] + [VMEM] * 4,
             out_specs=VMEM,
             scratch_shapes=[acc],
+            compiler_params=KERNEL,
         )(meta, readings, own, other, state)
 
     def step(block, parts, state, coeff, decay, meta=meta):
@@ -154,6 +157,7 @@
             in_specs=[VMEM] * len(parts) + [SMEM] + [VMEM] * 6,
             out_specs=(VMEM, VMEM, VMEM),
             scratch_shapes=[acc],
+            compiler_params=KERNEL,
         )(*parts, meta, readings, own, other, state, coeff, decay)
 
     def last(parts, state, coeff, decay):
@@ -162,26 +166,17 @@
             out_shape=(vector, vector),
             in_specs=[VMEM] * (len(parts) + 3),
             out_specs=(VMEM, VMEM),
+            compiler_params=KERNEL,
         )(*parts, state, coeff, decay)
-
-    def exchange(part, group):
-        parts = [part]
-        for shift in range(1, tm_size):
-            pairs = [
-                (i * grp_size + group, (i + shift) % tm_size * grp_size + group)
-                for i in range(tm_size)
-            ]
-            parts.append(lax.ppermute(part, ("tm", "grp"), pairs))
-        return parts
 
     def coefficients(position):
         return gathered[position][0:1], gathered[position][1:2]
 
-    def group_direct(state, group):
+    def group_direct(state):
         states, innovations = [], []
         part = first(0, state)
         for block in range(tm_size):
-            parts = exchange(part, group)
+            parts = exchange(part)
             if block < tm_size - 1:
                 state, innovation, part = step(block + 1, parts, state, *coefficients(block))
             else:
@@ -190,7 +185,7 @@
             innovations.append(innovation)
         return jnp.concatenate(states, 0), jnp.concatenate(innovations, 0)
 
-    def group_loop(state, group):
+    def group_loop(state):
         part = first(0, state)
 
         def lap(block, carry):
@@ -209,7 +204,7 @@
 
     states = innovations = jnp.zeros((tm_size, width), jnp.float32)
     for group in range(grp_size):
-        new_states, new_innovations = (group_direct if direct else group_loop)(state, group)
+        new_states, new_innovations = (group_direct if direct else group_loop)(state)
         mine = grp_index == group
         states = jnp.where(mine, new_states, states)
         innovations = jnp.where(mine, new_innovations, innovations)

time: 160 us -> 102 us (0.64)
  waiting for transfers between devices: 59.3 us -> 37.2 us
  Pallas kernels: 28.3 us -> 12.8 us
  starting transfers between devices: 57.1 us -> 45.2 us
  local copies, waits for them, and re-layouts: 10.8 us -> 3.94 us
  other arithmetic: 2.64 us -> 0.87 us
    ppermute x1, waiting for transfers between devices: 46.6 us -> 4.15 us  [shards(): arrived = lax.ppermute(running, 'grp', [(group, group - 1)])]
    ppermute x27, waiting for transfers between devices: 11.2 us -> 31.8 us  [exchange(): lax.ppermute(part, 'tm', [(i, i ^ flip) for i in range(tm_size)])]
    ppermute x27, starting transfers between devices: 54.5 us -> 40.8 us  [exchange(): lax.ppermute(part, 'tm', [(i, i ^ flip) for i in range(tm_size)])]
    pallas_call x6, Pallas kernels: 16.7 us -> 9.8 us  [step(): pl.pallas_call(functools.partial(step_kernel, block, len(parts)), out_sha...]
    unnamed x96 -> x18, local copies, waits for them, and re-layouts: 10.1 us -> 3.35 us
    pallas_call x2, Pallas kernels: 8.22 us -> 2.2 us  [first(): pl.pallas_call(functools.partial(first_kernel, block), out_shape=partial,...]
    pallas_call x2, Pallas kernels: 3.38 us -> 0.77 us  [last(): pl.pallas_call(functools.partial(last_kernel, len(parts)), out_shape=(vec...]
  transfers between devices with their start and end apart: 30 -> 30, of which waited for: 8 -> 20; matrix products, arithmetic and copies ran while one was open for 1% -> 1% of each run, Pallas kernels for 0% -> 0%
where the time goes in v2:
time: 102 us; the launch traced here: 101 us
  starting transfers between devices  45.2 us (44%)
  waiting for transfers between devices  37.2 us (36%)
  Pallas kernels  12.8 us (13%)
  local copies, waits for them, and re-layouts  3.94 us (4%)
    ppermute x27, starting transfers between devices, exchange(): lax.ppermute(part, 'tm', [(i, i ^ flip) for i in range(tm_size)])  40.8 us
    ppermute x27, waiting for transfers between devices, exchange(): lax.ppermute(part, 'tm', [(i, i ^ flip) for i in range(tm_size)])  31.8 us
    pallas_call x6, Pallas kernels, step(): pl.pallas_call(functools.partial(step_kernel, block, len(parts)), out_sha...  9.8 us
    ppermute x1, waiting for transfers between devices, shards(): arrived = lax.ppermute(running, 'grp', [(group, group - 1)])  4.15 us
    unnamed x18, local copies, waits for them, and re-layouts  3.35 us
    ppermute x1, starting transfers between devices, shards(): state = lax.ppermute(new_states[-1:], 'grp', [(group, group + 1)])  2.62 us
    pallas_call x2, Pallas kernels, first(): pl.pallas_call(functools.partial(first_kernel, block), out_shape=partial,...  2.2 us
  transfers between devices with their start and end apart: 30, of which 20 were waited for; matrix products, arithmetic and copies ran while one was open for 1% of the time, Pallas kernels for 0%

profile of v2, /device:TPU:0, one launch (start us, length us, event | category | flops | bytes accessed | tf_op | source)
XLA Modules:
  0.0 100.9 jit_solution(13607156325615395434)
XLA Ops:
  1.9 2.7 %collective-permute-start.4 = (f32[3,512]{1,0:T(4,128)S(1)}, f32[3,512]{1,0:T(4,128)S(1)}, u32[]{:S(2)}, u32[]{:S(2)}) collective-permute-start(f32[3,512]{1,0:T(4,128)S(1)} %get-tuple-element.61), channel_id=1, source_target_pairs={{0,4},{4,0},{8,12},{12,8},{1,5},{5,1},{9,13},{13,9},{2,6},{6,2},{1... | collective-permute-start | bytes 18440 | tf_op jit(solution)/shard_map/ppermute | solution.py:129
  4.5 2.6 %collective-permute-start.5 = (f32[3,512]{1,0:T(4,128)S(1)}, f32[3,512]{1,0:T(4,128)S(1)}, u32[]{:S(2)}, u32[]{:S(2)}) collective-permute-start(f32[3,512]{1,0:T(4,128)S(1)} %get-tuple-element.61), channel_id=1, source_target_pairs={{0,8},{4,12},{8,0},{12,4},{1,9},{5,13},{9,1},{13,5},{2,10},{6,14},... | collective-permute-start | bytes 18440 | tf_op jit(solution)/shard_map/ppermute | solution.py:129
  9.1 3.5 %collective-permute-done.6 = f32[3,512]{1,0:T(4,128)S(1)} collective-permute-done((f32[3,512]{1,0:T(4,128)S(1)}, f32[3,512]{1,0:T(4,128)S(1)}, u32[]{:S(2)}, u32[]{:S(2)}) %collective-permute-start.6) | collective-permute-done | bytes 6176 | tf_op jit(solution)/shard_map/ppermute | solution.py:129
  16.3 3.7 %collective-permute-start.3 = (f32[1,640]{1,0:T(1,128)S(1)}, f32[1,640]{1,0:T(1,128)S(1)}, u32[]{:S(2)}, u32[]{:S(2)}) collective-permute-start(f32[1,640]{1,0:T(1,128)S(1)} %shard_map.95.refs_0_), channel_id=1, source_target_pairs={{0,12},{4,8},{8,4},{12,0},{1,13},{5,9},{9,5},{13,1},{2,14},{6,10},... | collective-permute-start | bytes 7688 | tf_op jit(solution)/shard_map/ppermute | solution.py:129
  21.7 1.9 %shard_map.96 = (f32[1,512]{1,0:T(1,128)S(1)}, f32[1,512]{1,0:T(1,128)S(1)}, f32[1,640]{1,0:T(1,128)S(1)}) custom-call(f32[1,640]{1,0:T(1,128)S(1)} %shard_map.95.refs_0_, f32[1,640]{1,0:T(1,128)S(1)} %collective-permute-done.1.refs_1_, f32[1,640]{1,0:T(1,128)S(1)} %collective-permute-done.2.refs_2_, f32[1,640]{1,0:T(1,128)S(1)} %collective-permute-done.3.refs_3_, ...), custom_call_target="tpu_custom_call" | custom-call | tf_op jit(solution)/shard_map/pallas_call | solution.py:154
  24.2 3.8 %collective-permute-start.8 = (f32[1,640]{1,0:T(1,128)S(1)}, f32[1,640]{1,0:T(1,128)S(1)}, u32[]{:S(2)}, u32[]{:S(2)}) collective-permute-start(f32[1,640]{1,0:T(1,128)S(1)} %get-tuple-element.24.refs_0_), channel_id=1, source_target_pairs={{0,8},{4,12},{8,0},{12,4},{1,9},{5,13},{9,1},{13,5},{2,10},{6,14},... | collective-permute-start | bytes 7688 | tf_op jit(solution)/shard_map/ppermute | solution.py:129
  29.6 3.8 %collective-permute-done.9.refs_3_ = f32[1,640]{1,0:T(1,128)S(1)} collective-permute-done((f32[1,640]{1,0:T(1,128)S(1)}, f32[1,640]{1,0:T(1,128)S(1)}, u32[]{:S(2)}, u32[]{:S(2)}) %collective-permute-start.9) | collective-permute-done | bytes 2592 | tf_op jit(solution)/shard_map/ppermute | solution.py:129
  35.7 3.7 %collective-permute-start.12 = (f32[1,640]{1,0:T(1,128)S(1)}, f32[1,640]{1,0:T(1,128)S(1)}, u32[]{:S(2)}, u32[]{:S(2)}) collective-permute-start(f32[1,640]{1,0:T(1,128)S(1)} %get-tuple-element.26.refs_0_), channel_id=1, source_target_pairs={{0,12},{4,8},{8,4},{12,0},{1,13},{5,9},{9,5},{13,1},{2,14},{6,10},... | collective-permute-start | bytes 7688 | tf_op jit(solution)/shard_map/ppermute | solution.py:129
  43.0 3.8 %collective-permute-start.14 = (f32[1,640]{1,0:T(1,128)S(1)}, f32[1,640]{1,0:T(1,128)S(1)}, u32[]{:S(2)}, u32[]{:S(2)}) collective-permute-start(f32[1,640]{1,0:T(1,128)S(1)} %get-tuple-element.28.refs_0_), channel_id=1, source_target_pairs={{0,8},{4,12},{8,0},{12,4},{1,9},{5,13},{9,1},{13,5},{2,10},{6,14},... | collective-permute-start | bytes 7688 | tf_op jit(solution)/shard_map/ppermute | solution.py:129
  48.4 3.8 %collective-permute-done.15.refs_3_ = f32[1,640]{1,0:T(1,128)S(1)} collective-permute-done((f32[1,640]{1,0:T(1,128)S(1)}, f32[1,640]{1,0:T(1,128)S(1)}, u32[]{:S(2)}, u32[]{:S(2)}) %collective-permute-start.15) | collective-permute-done | bytes 2592 | tf_op jit(solution)/shard_map/ppermute | solution.py:129
  52.6 2.6 %collective-permute-start.16 = (f32[1,512]{1,0:T(1,128)S(1)}, f32[1,512]{1,0:T(1,128)S(1)}, u32[]{:S(2)}, u32[]{:S(2)}) collective-permute-start(f32[1,512]{1,0:T(1,128)S(1)} %get-tuple-element.30), channel_id=1, source_target_pairs={{0,2},{1,3},{4,6},{5,7},{8,10},{9,11},{12,14},{13,15},{16,18},{17,... | collective-permute-start | bytes 6152 | tf_op jit(solution)/shard_map/ppermute | solution.py:212
  57.7 2.3 %collective-permute-start.18 = (f32[1,640]{1,0:T(1,128)S(1)}, f32[1,640]{1,0:T(1,128)S(1)}, u32[]{:S(2)}, u32[]{:S(2)}) collective-permute-start(f32[1,640]{1,0:T(1,128)S(1)} %shard_map.100.refs_0_), channel_id=1, source_target_pairs={{0,8},{4,12},{8,0},{12,4},{1,9},{5,13},{9,1},{13,5},{2,10},{6,14},... | collective-permute-start | bytes 7688 | tf_op jit(solution)/shard_map/ppermute | solution.py:129
  60.1 2.1 %collective-permute-start.19 = (f32[1,640]{1,0:T(1,128)S(1)}, f32[1,640]{1,0:T(1,128)S(1)}, u32[]{:S(2)}, u32[]{:S(2)}) collective-permute-start(f32[1,640]{1,0:T(1,128)S(1)} %shard_map.100.refs_0_), channel_id=1, source_target_pairs={{0,12},{4,8},{8,4},{12,0},{1,13},{5,9},{9,5},{13,1},{2,14},{6,10},... | collective-permute-start | bytes 7688 | tf_op jit(solution)/shard_map/ppermute | solution.py:129
  62.3 3.2 %collective-permute-done.19.refs_3_ = f32[1,640]{1,0:T(1,128)S(1)} collective-permute-done((f32[1,640]{1,0:T(1,128)S(1)}, f32[1,640]{1,0:T(1,128)S(1)}, u32[]{:S(2)}, u32[]{:S(2)}) %collective-permute-start.19) | collective-permute-done | bytes 2592 | tf_op jit(solution)/shard_map/ppermute | solution.py:129
  65.5 1.9 %shard_map.101 = (f32[1,512]{1,0:T(1,128)S(1)}, f32[1,512]{1,0:T(1,128)S(1)}, f32[1,640]{1,0:T(1,128)S(1)}) custom-call(f32[1,640]{1,0:T(1,128)S(1)} %shard_map.100.refs_0_, f32[1,640]{1,0:T(1,128)S(1)} %collective-permute-done.17.refs_1_, f32[1,640]{1,0:T(1,128)S(1)} %collective-permute-done.18.refs_2_, f32[1,640]{1,0:T(1,128)S(1)} %collective-permute-done.19.refs_3_, ...), custom_call_target="tpu_custom_call" | custom-call | tf_op jit(solution)/shard_map/pallas_call | solution.py:154
  67.5 2.6 %collective-permute-start.21 = (f32[1,640]{1,0:T(1,128)S(1)}, f32[1,640]{1,0:T(1,128)S(1)}, u32[]{:S(2)}, u32[]{:S(2)}) collective-permute-start(f32[1,640]{1,0:T(1,128)S(1)} %get-tuple-element.32.refs_0_), channel_id=1, source_target_pairs={{0,8},{4,12},{8,0},{12,4},{1,9},{5,13},{9,1},{13,5},{2,10},{6,14},... | collective-permute-start | bytes 7688 | tf_op jit(solution)/shard_map/ppermute | solution.py:129
  72.0 3.4 %collective-permute-done.22.refs_3_ = f32[1,640]{1,0:T(1,128)S(1)} collective-permute-done((f32[1,640]{1,0:T(1,128)S(1)}, f32[1,640]{1,0:T(1,128)S(1)}, u32[]{:S(2)}, u32[]{:S(2)}) %collective-permute-start.22) | collective-permute-done | bytes 2592 | tf_op jit(solution)/shard_map/ppermute | solution.py:129
  77.1 2.3 %collective-permute-start.24 = (f32[1,640]{1,0:T(1,128)S(1)}, f32[1,640]{1,0:T(1,128)S(1)}, u32[]{:S(2)}, u32[]{:S(2)}) collective-permute-start(f32[1,640]{1,0:T(1,128)S(1)} %get-tuple-element.34.refs_0_), channel_id=1, source_target_pairs={{0,8},{4,12},{8,0},{12,4},{1,9},{5,13},{9,1},{13,5},{2,10},{6,14},... | collective-permute-start | bytes 7688 | tf_op jit(solution)/shard_map/ppermute | solution.py:129
  79.5 2.1 %collective-permute-start.25 = (f32[1,640]{1,0:T(1,128)S(1)}, f32[1,640]{1,0:T(1,128)S(1)}, u32[]{:S(2)}, u32[]{:S(2)}) collective-permute-start(f32[1,640]{1,0:T(1,128)S(1)} %get-tuple-element.34.refs_0_), channel_id=1, source_target_pairs={{0,12},{4,8},{8,4},{12,0},{1,13},{5,9},{9,5},{13,1},{2,14},{6,10},... | collective-permute-start | bytes 7688 | tf_op jit(solution)/shard_map/ppermute | solution.py:129
  81.7 3.1 %collective-permute-done.25.refs_3_ = f32[1,640]{1,0:T(1,128)S(1)} collective-permute-done((f32[1,640]{1,0:T(1,128)S(1)}, f32[1,640]{1,0:T(1,128)S(1)}, u32[]{:S(2)}, u32[]{:S(2)}) %collective-permute-start.25) | collective-permute-done | bytes 2592 | tf_op jit(solution)/shard_map/ppermute | solution.py:129
  86.3 2.6 %collective-permute-start.27 = (f32[1,640]{1,0:T(1,128)S(1)}, f32[1,640]{1,0:T(1,128)S(1)}, u32[]{:S(2)}, u32[]{:S(2)}) collective-permute-start(f32[1,640]{1,0:T(1,128)S(1)} %get-tuple-element.36.refs_0_), channel_id=1, source_target_pairs={{0,8},{4,12},{8,0},{12,4},{1,9},{5,13},{9,1},{13,5},{2,10},{6,14},... | collective-permute-start | bytes 7688 | tf_op jit(solution)/shard_map/ppermute | solution.py:129
  88.9 1.8 %collective-permute-start.28 = (f32[1,640]{1,0:T(1,128)S(1)}, f32[1,640]{1,0:T(1,128)S(1)}, u32[]{:S(2)}, u32[]{:S(2)}) collective-permute-start(f32[1,640]{1,0:T(1,128)S(1)} %get-tuple-element.36.refs_0_), channel_id=1, source_target_pairs={{0,12},{4,8},{8,4},{12,0},{1,13},{5,9},{9,5},{13,1},{2,14},{6,10},... | collective-permute-start | bytes 7688 | tf_op jit(solution)/shard_map/ppermute | solution.py:129
  90.9 3.4 %collective-permute-done.28.refs_3_ = f32[1,640]{1,0:T(1,128)S(1)} collective-permute-done((f32[1,640]{1,0:T(1,128)S(1)}, f32[1,640]{1,0:T(1,128)S(1)}, u32[]{:S(2)}, u32[]{:S(2)}) %collective-permute-start.28) | collective-permute-done | bytes 2592 | tf_op jit(solution)/shard_map/ppermute | solution.py:129
  96.1 4.1 %collective-permute-done.29 = f32[1,512]{1,0:T(1,128)S(1)} collective-permute-done((f32[1,512]{1,0:T(1,128)S(1)}, f32[1,512]{1,0:T(1,128)S(1)}, u32[]{:S(2)}, u32[]{:S(2)}) %collective-permute-start.29) | collective-permute-done | bytes 2080 | tf_op jit(solution)/shard_map/ppermute | solution.py:223
  (77 shorter events, 29.0 us)
Async XLA Ops:
  0.6 12.5 %collective-permute-start = (bf16[16,128,256]{2,1,0:T(8,128)(2,1)}, bf16[16,128,256]{2,1,0:T(8,128)(2,1)S(1)}, u32[]{:S(2)}, u32[]{:S(2)}) collective-permute-start(bf16[16,128,256]{2,1,0:T(8,128)(2,1)} %bitcast.62), channel_id=1, source_target_pairs={{0,1},{1,0},{2,3},{3,2},{4,5},{5,4},{6,7},{7,6},{8,9},{9,8},{10,11... | collective-permute-start | bytes 3145736 | tf_op jit(solution)/shard_map/ppermute | solution.py:120
  1.9 6.7 %collective-permute-start.4 = (f32[3,512]{1,0:T(4,128)S(1)}, f32[3,512]{1,0:T(4,128)S(1)}, u32[]{:S(2)}, u32[]{:S(2)}) collective-permute-start(f32[3,512]{1,0:T(4,128)S(1)} %get-tuple-element.61), channel_id=1, source_target_pairs={{0,4},{4,0},{8,12},{12,8},{1,5},{5,1},{9,13},{13,9},{2,6},{6,2},{1... | collective-permute-start | bytes 18440 | tf_op jit(solution)/shard_map/ppermute | solution.py:129
  4.5 4.5 %collective-permute-start.5 = (f32[3,512]{1,0:T(4,128)S(1)}, f32[3,512]{1,0:T(4,128)S(1)}, u32[]{:S(2)}, u32[]{:S(2)}) collective-permute-start(f32[3,512]{1,0:T(4,128)S(1)} %get-tuple-element.61), channel_id=1, source_target_pairs={{0,8},{4,12},{8,0},{12,4},{1,9},{5,13},{9,1},{13,5},{2,10},{6,14},... | collective-permute-start | bytes 18440 | tf_op jit(solution)/shard_map/ppermute | solution.py:129
  7.1 5.4 %collective-permute-start.6 = (f32[3,512]{1,0:T(4,128)S(1)}, f32[3,512]{1,0:T(4,128)S(1)}, u32[]{:S(2)}, u32[]{:S(2)}) collective-permute-start(f32[3,512]{1,0:T(4,128)S(1)} %get-tuple-element.61), channel_id=1, source_target_pairs={{0,12},{4,8},{8,4},{12,0},{1,13},{5,9},{9,5},{13,1},{2,14},{6,10},... | collective-permute-start | bytes 18440 | tf_op jit(solution)/shard_map/ppermute | solution.py:129
  15.6 4.5 %collective-permute-start.1 = (f32[1,640]{1,0:T(1,128)S(1)}, f32[1,640]{1,0:T(1,128)S(1)}, u32[]{:S(2)}, u32[]{:S(2)}) collective-permute-start(f32[1,640]{1,0:T(1,128)S(1)} %shard_map.95.refs_0_), channel_id=1, source_target_pairs={{0,4},{4,0},{8,12},{12,8},{1,5},{5,1},{9,13},{13,9},{2,6},{6,2},{1... | collective-permute-start | bytes 7688 | tf_op jit(solution)/shard_map/ppermute | solution.py:129
  15.7 4.6 %collective-permute-start.2 = (f32[1,640]{1,0:T(1,128)S(1)}, f32[1,640]{1,0:T(1,128)S(1)}, u32[]{:S(2)}, u32[]{:S(2)}) collective-permute-start(f32[1,640]{1,0:T(1,128)S(1)} %shard_map.95.refs_0_), channel_id=1, source_target_pairs={{0,8},{4,12},{8,0},{12,4},{1,9},{5,13},{9,1},{13,5},{2,10},{6,14},... | collective-permute-start | bytes 7688 | tf_op jit(solution)/shard_map/ppermute | solution.py:129
  16.3 5.4 %collective-permute-start.3 = (f32[1,640]{1,0:T(1,128)S(1)}, f32[1,640]{1,0:T(1,128)S(1)}, u32[]{:S(2)}, u32[]{:S(2)}) collective-permute-start(f32[1,640]{1,0:T(1,128)S(1)} %shard_map.95.refs_0_), channel_id=1, source_target_pairs={{0,12},{4,8},{8,4},{12,0},{1,13},{5,9},{9,5},{13,1},{2,14},{6,10},... | collective-permute-start | bytes 7688 | tf_op jit(solution)/shard_map/ppermute | solution.py:129
  23.6 4.5 %collective-permute-start.7 = (f32[1,640]{1,0:T(1,128)S(1)}, f32[1,640]{1,0:T(1,128)S(1)}, u32[]{:S(2)}, u32[]{:S(2)}) collective-permute-start(f32[1,640]{1,0:T(1,128)S(1)} %get-tuple-element.24.refs_0_), channel_id=1, source_target_pairs={{0,4},{4,0},{8,12},{12,8},{1,5},{5,1},{9,13},{13,9},{2,6},{6,2},{1... | collective-permute-start | bytes 7688 | tf_op jit(solution)/shard_map/ppermute | solution.py:129
  24.2 5.4 %collective-permute-start.8 = (f32[1,640]{1,0:T(1,128)S(1)}, f32[1,640]{1,0:T(1,128)S(1)}, u32[]{:S(2)}, u32[]{:S(2)}) collective-permute-start(f32[1,640]{1,0:T(1,128)S(1)} %get-tuple-element.24.refs_0_), channel_id=1, source_target_pairs={{0,8},{4,12},{8,0},{12,4},{1,9},{5,13},{9,1},{13,5},{2,10},{6,14},... | collective-permute-start | bytes 7688 | tf_op jit(solution)/shard_map/ppermute | solution.py:129
  28.0 5.4 %collective-permute-start.9 = (f32[1,640]{1,0:T(1,128)S(1)}, f32[1,640]{1,0:T(1,128)S(1)}, u32[]{:S(2)}, u32[]{:S(2)}) collective-permute-start(f32[1,640]{1,0:T(1,128)S(1)} %get-tuple-element.24.refs_0_), channel_id=1, source_target_pairs={{0,12},{4,8},{8,4},{12,0},{1,13},{5,9},{9,5},{13,1},{2,14},{6,10},... | collective-permute-start | bytes 7688 | tf_op jit(solution)/shard_map/ppermute | solution.py:129
  35.0 4.5 %collective-permute-start.10 = (f32[1,640]{1,0:T(1,128)S(1)}, f32[1,640]{1,0:T(1,128)S(1)}, u32[]{:S(2)}, u32[]{:S(2)}) collective-permute-start(f32[1,640]{1,0:T(1,128)S(1)} %get-tuple-element.26.refs_0_), channel_id=1, source_target_pairs={{0,4},{4,0},{8,12},{12,8},{1,5},{5,1},{9,13},{13,9},{2,6},{6,2},{1... | collective-permute-start | bytes 7688 | tf_op jit(solution)/shard_map/ppermute | solution.py:129
  35.1 4.6 %collective-permute-start.11 = (f32[1,640]{1,0:T(1,128)S(1)}, f32[1,640]{1,0:T(1,128)S(1)}, u32[]{:S(2)}, u32[]{:S(2)}) collective-permute-start(f32[1,640]{1,0:T(1,128)S(1)} %get-tuple-element.26.refs_0_), channel_id=1, source_target_pairs={{0,8},{4,12},{8,0},{12,4},{1,9},{5,13},{9,1},{13,5},{2,10},{6,14},... | collective-permute-start | bytes 7688 | tf_op jit(solution)/shard_map/ppermute | solution.py:129
  35.7 5.4 %collective-permute-start.12 = (f32[1,640]{1,0:T(1,128)S(1)}, f32[1,640]{1,0:T(1,128)S(1)}, u32[]{:S(2)}, u32[]{:S(2)}) collective-permute-start(f32[1,640]{1,0:T(1,128)S(1)} %get-tuple-element.26.refs_0_), channel_id=1, source_target_pairs={{0,12},{4,8},{8,4},{12,0},{1,13},{5,9},{9,5},{13,1},{2,14},{6,10},... | collective-permute-start | bytes 7688 | tf_op jit(solution)/shard_map/ppermute | solution.py:129
  43.0 5.4 %collective-permute-start.14 = (f32[1,640]{1,0:T(1,128)S(1)}, f32[1,640]{1,0:T(1,128)S(1)}, u32[]{:S(2)}, u32[]{:S(2)}) collective-permute-start(f32[1,640]{1,0:T(1,128)S(1)} %get-tuple-element.28.refs_0_), channel_id=1, source_target_pairs={{0,8},{4,12},{8,0},{12,4},{1,9},{5,13},{9,1},{13,5},{2,10},{6,14},... | collective-permute-start | bytes 7688 | tf_op jit(solution)/shard_map/ppermute | solution.py:129
  46.9 5.4 %collective-permute-start.15 = (f32[1,640]{1,0:T(1,128)S(1)}, f32[1,640]{1,0:T(1,128)S(1)}, u32[]{:S(2)}, u32[]{:S(2)}) collective-permute-start(f32[1,640]{1,0:T(1,128)S(1)} %get-tuple-element.28.refs_0_), channel_id=1, source_target_pairs={{0,12},{4,8},{8,4},{12,0},{1,13},{5,9},{9,5},{13,1},{2,14},{6,10},... | collective-permute-start | bytes 7688 | tf_op jit(solution)/shard_map/ppermute | solution.py:129
  57.7 4.6 %collective-permute-start.18 = (f32[1,640]{1,0:T(1,128)S(1)}, f32[1,640]{1,0:T(1,128)S(1)}, u32[]{:S(2)}, u32[]{:S(2)}) collective-permute-start(f32[1,640]{1,0:T(1,128)S(1)} %shard_map.100.refs_0_), channel_id=1, source_target_pairs={{0,8},{4,12},{8,0},{12,4},{1,9},{5,13},{9,1},{13,5},{2,10},{6,14},... | collective-permute-start | bytes 7688 | tf_op jit(solution)/shard_map/ppermute | solution.py:129
  60.1 5.4 %collective-permute-start.19 = (f32[1,640]{1,0:T(1,128)S(1)}, f32[1,640]{1,0:T(1,128)S(1)}, u32[]{:S(2)}, u32[]{:S(2)}) collective-permute-start(f32[1,640]{1,0:T(1,128)S(1)} %shard_map.100.refs_0_), channel_id=1, source_target_pairs={{0,12},{4,8},{8,4},{12,0},{1,13},{5,9},{9,5},{13,1},{2,14},{6,10},... | collective-permute-start | bytes 7688 | tf_op jit(solution)/shard_map/ppermute | solution.py:129
  67.5 4.6 %collective-permute-start.21 = (f32[1,640]{1,0:T(1,128)S(1)}, f32[1,640]{1,0:T(1,128)S(1)}, u32[]{:S(2)}, u32[]{:S(2)}) collective-permute-start(f32[1,640]{1,0:T(1,128)S(1)} %get-tuple-element.32.refs_0_), channel_id=1, source_target_pairs={{0,8},{4,12},{8,0},{12,4},{1,9},{5,13},{9,1},{13,5},{2,10},{6,14},... | collective-permute-start | bytes 7688 | tf_op jit(solution)/shard_map/ppermute | solution.py:129
  70.1 5.4 %collective-permute-start.22 = (f32[1,640]{1,0:T(1,128)S(1)}, f32[1,640]{1,0:T(1,128)S(1)}, u32[]{:S(2)}, u32[]{:S(2)}) collective-permute-start(f32[1,640]{1,0:T(1,128)S(1)} %get-tuple-element.32.refs_0_), channel_id=1, source_target_pairs={{0,12},{4,8},{8,4},{12,0},{1,13},{5,9},{9,5},{13,1},{2,14},{6,10},... | collective-permute-start | bytes 7688 | tf_op jit(solution)/shard_map/ppermute | solution.py:129
  77.1 4.6 %collective-permute-start.24 = (f32[1,640]{1,0:T(1,128)S(1)}, f32[1,640]{1,0:T(1,128)S(1)}, u32[]{:S(2)}, u32[]{:S(2)}) collective-permute-start(f32[1,640]{1,0:T(1,128)S(1)} %get-tuple-element.34.refs_0_), channel_id=1, source_target_pairs={{0,8},{4,12},{8,0},{12,4},{1,9},{5,13},{9,1},{13,5},{2,10},{6,14},... | collective-permute-start | bytes 7688 | tf_op jit(solution)/shard_map/ppermute | solution.py:129
  79.5 5.4 %collective-permute-start.25 = (f32[1,640]{1,0:T(1,128)S(1)}, f32[1,640]{1,0:T(1,128)S(1)}, u32[]{:S(2)}, u32[]{:S(2)}) collective-permute-start(f32[1,640]{1,0:T(1,128)S(1)} %get-tuple-element.34.refs_0_), channel_id=1, source_target_pairs={{0,12},{4,8},{8,4},{12,0},{1,13},{5,9},{9,5},{13,1},{2,14},{6,10},... | collective-permute-start | bytes 7688 | tf_op jit(solution)/shard_map/ppermute | solution.py:129
  86.3 4.6 %collective-permute-start.27 = (f32[1,640]{1,0:T(1,128)S(1)}, f32[1,640]{1,0:T(1,128)S(1)}, u32[]{:S(2)}, u32[]{:S(2)}) collective-permute-start(f32[1,640]{1,0:T(1,128)S(1)} %get-tuple-element.36.refs_0_), channel_id=1, source_target_pairs={{0,8},{4,12},{8,0},{12,4},{1,9},{5,13},{9,1},{13,5},{2,10},{6,14},... | collective-permute-start | bytes 7688 | tf_op jit(solution)/shard_map/ppermute | solution.py:129
  88.9 5.4 %collective-permute-start.28 = (f32[1,640]{1,0:T(1,128)S(1)}, f32[1,640]{1,0:T(1,128)S(1)}, u32[]{:S(2)}, u32[]{:S(2)}) collective-permute-start(f32[1,640]{1,0:T(1,128)S(1)} %get-tuple-element.36.refs_0_), channel_id=1, source_target_pairs={{0,12},{4,8},{8,4},{12,0},{1,13},{5,9},{9,5},{13,1},{2,14},{6,10},... | collective-permute-start | bytes 7688 | tf_op jit(solution)/shard_map/ppermute | solution.py:129
  94.8 5.5 %collective-permute-start.29 = (f32[1,512]{1,0:T(1,128)S(1)}, f32[1,512]{1,0:T(1,128)S(1)}, u32[]{:S(2)}, u32[]{:S(2)}) collective-permute-start(f32[1,512]{1,0:T(1,128)S(1)} %fusion), channel_id=1, source_target_pairs={{2,0},{3,1},{6,4},{7,5},{10,8},{11,9},{14,12},{15,13},{18,16},{19,... | collective-permute-start | bytes 6152 | tf_op jit(solution)/shard_map/ppermute | solution.py:223
  (15 other events, 39.4 us)

commit v3 on v2

v3 whole, which is shorter than its diff:
```python
import functools

import jax
import jax.numpy as jnp
from jax import lax
from jax.experimental import pallas as pl
from jax.experimental.pallas import tpu as pltpu
from jax.sharding import PartitionSpec as P

STEPS = 4
LANES = 128
GROUP_ROWS = 16
DIRECT_TM = 4

VMEM = pl.BlockSpec(memory_space=pltpu.VMEM)
KERNEL = pltpu.CompilerParams(vmem_limit_bytes=16 * 2**20)
SMEM = pl.BlockSpec(memory_space=pltpu.SMEM)


def stencil(field, coeff, decay):
    width = field.shape[1]
    cell = lax.broadcasted_iota(jnp.int32, field.shape, 1)
    for _ in range(STEPS):
        upper_cell = jnp.where(cell == 0, 0.0, pltpu.roll(field, 1, 1))
        lower_cell = jnp.where(cell == width - 1, 0.0, pltpu.roll(field, width - 1, 1))
        field = field + coeff * (upper_cell + lower_cell - 2.0 * field) - decay * field
    return field


def row_pass(block, state, meta, y_ref, own_ref, other_ref, acc, part_ref):
    tile_num, row_num, half = own_ref.shape
    core = meta[2 * tile_num]
    own_at = pl.multiple_of(core * half, half)
    other_at = pl.multiple_of((1 - core) * half, half)
    state_own = state[:, pl.ds(own_at, half)]
    state_other = state[:, pl.ds(other_at, half)]
    lane = lax.broadcasted_iota(jnp.int32, (GROUP_ROWS, LANES), 1)
    row = lax.broadcasted_iota(jnp.int32, (GROUP_ROWS, LANES), 0)
    acc[...] = jnp.zeros_like(acc)

    def fold(values):
        total = values[:, :LANES]
        for start in range(LANES, half, LANES):
            total = total + values[:, start : start + LANES]
        return total

    def tile(index, carry):
        @pl.when(meta[index] == block)
        def _():
            live = meta[tile_num + index]
            readings = y_ref[pl.ds(index, 1), :]
            sum_own = jnp.zeros((GROUP_ROWS, half), jnp.float32)
            sum_other = jnp.zeros((GROUP_ROWS, half), jnp.float32)
            squares = jnp.zeros((GROUP_ROWS, LANES), jnp.float32)
            for start in range(0, row_num, GROUP_ROWS):
                own = own_ref[index, start : start + GROUP_ROWS, :].astype(jnp.float32)
                other = other_ref[index, start : start + GROUP_ROWS, :].astype(jnp.float32)
                valid = row + start < live
                product = fold(own * state_own) + fold(other * state_other)
                product = product - jnp.where(lane == row + start, readings, 0.0)
                weight = jnp.sum(product, axis=1, keepdims=True)
                weight = jnp.where(valid[:, :1], weight, 0.0)
                sum_own = sum_own + own * weight
                sum_other = sum_other + other * weight
                squares = squares + jnp.where(valid, fold(own * own) + fold(other * other), 0.0)
            acc[:, :half] += sum_own
            acc[:, half : 2 * half] += sum_other
            acc[:, 2 * half :] += squares

        return carry

    lax.fori_loop(0, tile_num, tile, 0)
    totals = jnp.sum(acc[...], axis=0, keepdims=True)
    part_ref[:, pl.ds(own_at, half)] = totals[:, :half]
    part_ref[:, pl.ds(other_at, half)] = totals[:, half : 2 * half]
    part_ref[:, 2 * half :] = totals[:, 2 * half :]


def first_kernel(block, meta, y_ref, own_ref, other_ref, state_ref, part_ref, acc):
    row_pass(block, state_ref, meta, y_ref, own_ref, other_ref, acc, part_ref)


def step_kernel(
    total_ref, meta, y_ref, own_ref, other_ref, state_ref, kappa_ref, rate_ref,
    next_ref, innovation_ref, part_ref, acc,
):
    width = state_ref.shape[1]
    trace_val = jnp.sum(total_ref[:, width:], axis=1, keepdims=True)
    lam_val = width / (2.0 * (width + trace_val))
    coeff, decay = kappa_ref[...], rate_ref[...]
    innovation = -lam_val * stencil(total_ref[:, :width], coeff, decay)
    next_ref[...] = stencil(state_ref[...], coeff, decay) + innovation
    innovation_ref[...] = innovation
    block = meta[2 * y_ref.shape[0] + 1]
    row_pass(block, next_ref, meta, y_ref, own_ref, other_ref, acc, part_ref)


def gram_kernel(meta, y_ref, own_ref, other_ref, params_ref, *refs):
    outs, side_ref, acc, vec = refs[:-3], refs[-3], refs[-2], refs[-1]
    tile_num, row_num, half = own_ref.shape
    block_num = len(outs)
    core, position = meta[2 * tile_num], meta[2 * tile_num + 1]
    acc[...] = jnp.zeros_like(acc)
    vec[...] = jnp.zeros_like(vec)
    row = lax.broadcasted_iota(jnp.int32, (row_num, half), 0)
    over_rows = (((0,), (0,)), ((), ()))

    def tile(index, carry):
        block = meta[index]
        live = meta[tile_num + index]
        rows = own_ref[index].astype(jnp.float32)
        rows = jnp.where(row < live, rows, 0.0).astype(jnp.bfloat16)
        readings = jnp.broadcast_to(y_ref[pl.ds(index, 1), :], (8, row_num)).astype(jnp.bfloat16)
        square = lax.dot_general(rows, rows, over_rows, preferred_element_type=jnp.float32)
        acc[block, 0:LANES] += square[:LANES, :LANES]
        acc[block, LANES : 2 * LANES] += square[:LANES, LANES:]
        acc[block, 2 * LANES : 3 * LANES] += square[LANES:, LANES:]
        for piece in range(2):
            at = pl.multiple_of((piece ^ core) * LANES, LANES)
            acc[block, (3 + piece) * LANES : (4 + piece) * LANES] += lax.dot_general(
                rows[:, piece * LANES : (piece + 1) * LANES],
                other_ref[index, :, pl.ds(at, LANES)],
                over_rows,
                preferred_element_type=jnp.float32,
            )
        vec[block] += jnp.dot(readings, rows, preferred_element_type=jnp.float32)
        return carry

    lax.fori_loop(0, tile_num, tile, 0, unroll=2)
    on_diagonal = lax.broadcasted_iota(jnp.int32, (LANES, LANES), 0) == lax.broadcasted_iota(
        jnp.int32, (LANES, LANES), 1
    )
    for flip, out_ref in enumerate(outs):
        block = position ^ flip
        for piece in range(5):
            values = acc[block, piece * LANES : (piece + 1) * LANES]
            if piece in (0, 2):
                side_ref[block, 0:1, (piece // 2) * LANES : (piece // 2 + 1) * LANES] = jnp.sum(
                    jnp.where(on_diagonal, values, 0.0), axis=0, keepdims=True
                )
                values = jnp.where(on_diagonal, 0.0, values)
            out_ref[piece * LANES : (piece + 1) * LANES] = values.astype(jnp.bfloat16)
    for block in range(block_num):
        side_ref[block, 1:2, :] = vec[block, 0:1, :]
    for which in range(3):
        for piece in range(2):
            side_ref[block_num + which, piece : piece + 1, :] = params_ref[
                which : which + 1, piece * half : (piece + 1) * half
            ]


def sum_kernel(*refs):
    total = refs[0][...].astype(jnp.float32)
    for part in refs[1:-1]:
        total = total + part[...].astype(jnp.float32)
    refs[-1][...] = total.astype(jnp.bfloat16)


def chain(grams, diag, info, kappa, rate, state, states_ref, innovations_ref):
    width = state.shape[1]
    line = lax.broadcasted_iota(jnp.int32, (16, width), 0)
    for block in range(grams.shape[0]):
        high = state.astype(jnp.bfloat16).astype(jnp.float32)
        middle = (state - high).astype(jnp.bfloat16).astype(jnp.float32)
        low = state - high - middle
        split = jnp.where(line == 0, high, jnp.where(line == 1, middle, jnp.where(line == 2, low, 0.0)))
        product = jnp.dot(
            split.astype(jnp.bfloat16), grams[block], preferred_element_type=jnp.float32
        )
        diagonal = diag[block : block + 1, :]
        product = jnp.sum(product, axis=0, keepdims=True) + diagonal * state
        trace_val = jnp.sum(diagonal, axis=1, keepdims=True)
        lam_val = width / (2.0 * (width + trace_val))
        coeff, decay = kappa[block : block + 1, :], rate[block : block + 1, :]
        innovation = -lam_val * stencil(product - info[block : block + 1, :], coeff, decay)
        state = stencil(state, coeff, decay) + innovation
        states_ref[block : block + 1, :] = state
        innovations_ref[block : block + 1, :] = innovation


def assemble_kernel(number, *refs):
    own, other, rest = refs[:number], refs[number : 2 * number], refs[2 * number :]
    where, diag, info, kappa, rate, state_ref, grams, states_ref, innovations_ref = rest
    core, position = where[0], where[1]
    half = 2 * LANES
    for flip in range(number):
        block = position ^ flip
        for pieces, side in ((own[flip], core), (other[flip], 1 - core)):
            def piece(index):
                return pieces[index * LANES : (index + 1) * LANES, :]

            def put(row, column, values):
                row, column = pl.multiple_of(row, LANES), pl.multiple_of(column, LANES)
                grams[block, pl.ds(row, LANES), pl.ds(column, LANES)] = values

            here, there = side * half, (1 - side) * half
            put(here, here, piece(0))
            put(here, here + LANES, piece(1))
            put(here + LANES, here, piece(1).T)
            put(here + LANES, here + LANES, piece(2))
            for index in range(2):
                across = there + (index ^ side) * LANES
                put(here + index * LANES, across, piece(3 + index))
                put(across, here + index * LANES, piece(3 + index).T)
    chain(grams, diag, info, kappa, rate, state_ref[...], states_ref, innovations_ref)


def chain_kernel(grams, diag, info, kappa, rate, state_ref, states_ref, innovations_ref):
    chain(grams, diag, info, kappa, rate, state_ref[...], states_ref, innovations_ref)


def shards(rows_h, rows_y, tile_block, tile_count, kappa, rate, smooth_gain, start_state):
    tm_size, grp_size = lax.axis_size("tm"), lax.axis_size("grp")
    state_size = lax.axis_size("state")
    tm_index, grp_index, core = (lax.axis_index(name) for name in ("tm", "grp", "state"))
    tile_num, half = rows_h.shape[1], rows_h.shape[3]
    width = kappa.shape[2]
    own = rows_h[0]
    other = lax.ppermute(own, "state", [(i, (i + 1) % state_size) for i in range(state_size)])
    readings = rows_y[0].astype(jnp.float32)
    state = start_state.reshape(1, width)
    meta = jnp.concatenate(
        [tile_block[0, :, 0], tile_count[0], jnp.stack([core, tm_index]).astype(jnp.int32)]
    )
    params = jnp.concatenate([kappa[0], rate[0], smooth_gain[0]], axis=0)
    direct = tm_size <= DIRECT_TM and tm_size & (tm_size - 1) == 0
    states_shape = jax.ShapeDtypeStruct((tm_size, width), jnp.float32)

    def flip_over(array, flip):
        return lax.ppermute(array, "tm", [(i, i ^ flip) for i in range(tm_size)])

    def across(array):
        return lax.ppermute(array, "state", [(i, (i + 1) % state_size) for i in range(state_size)])

    if direct:
        packed = jax.ShapeDtypeStruct((5 * LANES, LANES), jnp.bfloat16)
        *pieces, side = pl.pallas_call(
            gram_kernel,
            out_shape=[packed] * tm_size
            + [jax.ShapeDtypeStruct((tm_size + 3, 2, half), jnp.float32)],
            in_specs=[SMEM] + [VMEM] * 4,
            out_specs=[VMEM] * (tm_size + 1),
            scratch_shapes=[
                pltpu.VMEM((tm_size, 5 * LANES, LANES), jnp.float32),
                pltpu.VMEM((tm_size, 8, half), jnp.float32),
            ],
            compiler_params=KERNEL,
        )(meta, readings, own, other, params)
        parts = pieces[:1] + [flip_over(pieces[flip], flip) for flip in range(1, tm_size)]

        sides = [side] + [flip_over(side, flip) for flip in range(1, tm_size)]
        side_sum = sum(values[:tm_size] for values in sides)
        side_other = across(side_sum)
        low = jnp.where(core == 0, side_sum, side_other)
        high = jnp.where(core == 0, side_other, side_sum)
        vectors = jnp.concatenate([low, high], axis=2)
        diag, info = vectors[:, 0], vectors[:, 1]
        order = jnp.arange(tm_size) ^ tm_index
        gathered = jnp.stack([values[tm_size:].reshape(3, width) for values in sides])[order]

        own_sum = pl.pallas_call(
            sum_kernel,
            out_shape=packed,
            in_specs=[VMEM] * tm_size,
            out_specs=VMEM,
            compiler_params=KERNEL,
        )(*parts)
        own_sums = [own_sum] + [flip_over(own_sum, flip) for flip in range(1, tm_size)]
        other_sums = [across(values) for values in own_sums]
        coefficients = (diag, info, gathered[:, 0], gathered[:, 1])
        grams, new_states, new_innovations = pl.pallas_call(
            functools.partial(assemble_kernel, tm_size),
            out_shape=(
                jax.ShapeDtypeStruct((tm_size, width, width), jnp.bfloat16),
                states_shape,
                states_shape,
            ),
            in_specs=[VMEM] * (2 * tm_size) + [SMEM] + [VMEM] * 5,
            out_specs=(VMEM, VMEM, VMEM),
            compiler_params=KERNEL,
        )(*own_sums, *other_sums, meta[2 * tile_num :], *coefficients, state)

        def run_group(state, group):
            if group == 0:
                return new_states, new_innovations
            return pl.pallas_call(
                chain_kernel,
                out_shape=(states_shape, states_shape),
                in_specs=[VMEM] * 6,
                out_specs=(VMEM, VMEM),
                compiler_params=KERNEL,
            )(grams, *coefficients, state)
    else:
        gathered = lax.all_gather(params, "tm")
        vector = jax.ShapeDtypeStruct((1, width), jnp.float32)
        partial = jax.ShapeDtypeStruct((1, width + LANES), jnp.float32)
        acc = pltpu.VMEM((GROUP_ROWS, width + LANES), jnp.float32)

        def run_group(state, group):
            part = pl.pallas_call(
                functools.partial(first_kernel, 0),
                out_shape=partial,
                in_specs=[SMEM] + [VMEM] * 4,
                out_specs=VMEM,
                scratch_shapes=[acc],
                compiler_params=KERNEL,
            )(meta, readings, own, other, state)

            def lap(block, carry):
                state, part, states, innovations = carry
                here = lax.dynamic_index_in_dim(gathered, block, 0, False)
                own_meta = meta.at[2 * tile_num + 1].set((block + 1).astype(jnp.int32))
                state, innovation, part = pl.pallas_call(
                    step_kernel,
                    out_shape=(vector, vector, partial),
                    in_specs=[VMEM, SMEM] + [VMEM] * 6,
                    out_specs=(VMEM, VMEM, VMEM),
                    scratch_shapes=[acc],
                    compiler_params=KERNEL,
                )(lax.psum(part, "tm"), own_meta, readings, own, other, state, here[0:1], here[1:2])
                states = lax.dynamic_update_slice_in_dim(states, state, block, 0)
                innovations = lax.dynamic_update_slice_in_dim(innovations, innovation, block, 0)
                return state, part, states, innovations

            empty = jnp.zeros((tm_size, width), jnp.float32)
            return lax.fori_loop(0, tm_size, lap, (state, part, empty, empty))[2:]

    states = innovations = jnp.zeros((tm_size, width), jnp.float32)
    for group in range(grp_size):
        new_states, new_innovations = run_group(state, group)
        mine = grp_index == group
        states = jnp.where(mine, new_states, states)
        innovations = jnp.where(mine, new_innovations, innovations)
        if group < grp_size - 1:
            state = lax.ppermute(new_states[-1:], "grp", [(group, group + 1)])

    gains = gathered[:, 2]
    residual = jnp.zeros((1, width), jnp.float32)
    residuals = [None] * tm_size
    for group in reversed(range(grp_size)):
        running = residual
        for block in reversed(range(tm_size)):
            residuals[block] = running
            running = gains[block][None] * (running + innovations[block][None])
        if group > 0:
            arrived = lax.ppermute(running, "grp", [(group, group - 1)])
            residual = jnp.where(grp_index == group - 1, arrived, residual)
    smoothed = states + jnp.concatenate(residuals, 0)

    def out(values):
        piece = lax.dynamic_slice(values, (tm_index, core * half), (1, half))
        return piece.reshape(1, 1, half)

    return out(states), out(smoothed)


def solution(mesh):
    return jax.shard_map(
        shards,
        mesh=mesh,
        in_specs=(
            P(("runs", "grp"), "tm", None, "state"),
            P(("runs", "grp"), "tm", None),
            P(("runs", "grp"), "tm", None),
            P(("runs", "grp"), "tm"),
            P(("runs", "grp"), "tm", None),
            P(("runs", "grp"), "tm", None),
            P(("runs", "grp"), "tm", None),
            P("runs"),
        ),
        out_specs=(P(("runs", "grp"), "tm", "state"), P(("runs", "grp"), "tm", "state")),
        check_vma=False,
    )
```

time: 102 us -> 64.7 us (0.63)
  starting transfers between devices: 45.2 us -> 21.4 us
  waiting for transfers between devices: 37.2 us -> 28.4 us
  Pallas kernels: 12.8 us -> 8.87 us
  other arithmetic: 0.87 us -> 3 us
  local copies, waits for them, and re-layouts: 3.94 us -> 1.87 us
    ppermute x27 -> x14, starting transfers between devices: 40.8 us -> 16.2 us  [the longest x9 16.2 us: flip_over(): return lax.ppermute(array, 'tm', [(i, i ^ flip) for i in range(tm_size)])]
    ppermute x27 -> x14, waiting for transfers between devices: 31.8 us -> 22.7 us  [the longest x9 21.3 us: flip_over(): return lax.ppermute(array, 'tm', [(i, i ^ flip) for i in range(tm_size)])]
    pallas_call x10 -> x4, Pallas kernels: 12.8 us -> 8.87 us  [the longest x1 3.29 us: shards(): pl.pallas_call(gram_kernel, out_shape=[packed] * tm_size + [jax.ShapeDtyp...]
    unnamed x18 -> x4, local copies, waits for them, and re-layouts: 3.35 us -> 1.23 us
    concatenate x1 -> x2, other arithmetic: 0.08 us -> 1.48 us  [the longest x1 0.75 us: shards(): jnp.concatenate([tile_block[0, :, 0], tile_count[0], jnp.stack([core, tm_...]
  transfers between devices with their start and end apart: 30 -> 17, of which waited for: 20 -> 10; matrix products, arithmetic and copies ran while one was open for 1% -> 5% of each run, Pallas kernels for 0% -> 0%
where the time goes in v3:
time: 64.7 us; the launch traced here: 64.4 us
  waiting for transfers between devices  28.4 us (44%)
  starting transfers between devices  21.4 us (33%)
  Pallas kernels  8.87 us (14%)
  other arithmetic  3 us (5%)
  local copies, waits for them, and re-layouts  1.87 us (3%)
  between operations  0.83 us (1%)
    ppermute x9, waiting for transfers between devices, flip_over(): return lax.ppermute(array, 'tm', [(i, i ^ flip) for i in range(tm_size)])  21.3 us
    ppermute x9, starting transfers between devices, flip_over(): return lax.ppermute(array, 'tm', [(i, i ^ flip) for i in range(tm_size)])  16.2 us
    ppermute x1, waiting for transfers between devices, shards(): arrived = lax.ppermute(running, 'grp', [(group, group - 1)])  4.16 us
    ppermute x1, starting transfers between devices, shards(): state = lax.ppermute(new_states[-1:], 'grp', [(group, group + 1)])  3.39 us
    pallas_call x1, Pallas kernels, shards(): pl.pallas_call(gram_kernel, out_shape=[packed] * tm_size + [jax.ShapeDtyp...  3.29 us
    pallas_call x1, Pallas kernels, shards(): pl.pallas_call(functools.partial(assemble_kernel, tm_size), out_shape=(ja...  3.23 us
    pallas_call x1, Pallas kernels, run_group(): pl.pallas_call(chain_kernel, out_shape=(states_shape, states_shape), in_s...  2.27 us
    ppermute x5, waiting for transfers between devices, across(): lax.ppermute(array, 'state', [(i, (i + 1) % state_size) for i in range(st...  1.35 us
  transfers between devices with their start and end apart: 17, of which 10 were waited for; matrix products, arithmetic and copies ran while one was open for 5% of the time, Pallas kernels for 0%

profile of v3, /device:TPU:0, one launch (start us, length us, event | category | flops | bytes accessed | tf_op | source)
XLA Modules:
  0.0 64.4 jit_solution(9122490143829190489)
XLA Ops:
  1.2 0.7 %pad_add_fusion.meta = s32[34]{0:T(128)S(1)} fusion(s32[1]{0:T(128)} %bitcast.3, s32[1]{0:T(128)} %bitcast.2, s32[16]{0:T(128)} %bitcast.70, s32[16]{0:T(128)} %bitcast.71), kind=kLoop, calls=%fused_computation.40 | loop fusion | flops 102 | bytes 272 | tf_op jit(solution)/shard_map/concatenate | solution.py:222
  1.9 0.7 %pad_maximum_fusion.2.params_ref = f32[3,512]{1,0:T(4,128)S(1)} fusion(f32[1,512]{1,0:T(1,128)} %bitcast.67, f32[1,512]{1,0:T(1,128)} %bitcast.68, f32[1,512]{1,0:T(1,128)} %bitcast.69), kind=kLoop, calls=%fused_computation.11 | loop fusion | flops 3072 | bytes 12288 | tf_op jit(solution)/shard_map/concatenate | solution.py:225
  2.7 0.7 %bitcast_convert_fusion.y_ref = f32[16,128]{1,0:T(8,128)S(1)} fusion(bf16[1,16,128]{2,1,0:T(8,128)(2,1)} %param.9), kind=kLoop, calls=%fused_computation.21 | loop fusion | flops 2048 | bytes 12288 | tf_op jit(solution)/shard_map/convert_element_type | solution.py:220
  3.7 1.2 %copy-done = bf16[1,16,128,256]{3,2,1,0:T(8,128)(2,1)S(1)} copy-done((bf16[1,16,128,256]{3,2,1,0:T(8,128)(2,1)S(1)}, bf16[1,16,128,256]{3,2,1,0:T(8,128)(2,1)}, u32[]{:S(2)}) %copy-start) | copy-done | bytes 1048600
  4.9 3.3 %shard_map.95 = (bf16[640,128]{1,0:T(8,128)(2,1)S(1)}, bf16[640,128]{1,0:T(8,128)(2,1)S(1)}, bf16[640,128]{1,0:T(8,128)(2,1)S(1)}, bf16[640,128]{1,0:T(8,128)(2,1)S(1)}, f32[7,2,256]{2,1,0:T(2,128)S(1)}) custom-call(s32[34]{0:T(128)S(1)} %pad_add_fusion.meta, f32[16,128]{1,0:T(8,128)S(1)} %bitcast_convert_fusion.y_ref, bf16[16,128,256]{2,1,0:T(8,128)(2,1)S(1)} %bitcast.58, ...), custom_call_target="tpu_custom_call" | custom-call | tf_op jit(solution)/shard_map/pallas_call | solution.py:237
  8.2 3.0 %collective-permute-start.11 = (f32[7,2,256]{2,0,1:T(8,128)S(1)}, f32[7,2,256]{2,0,1:T(8,128)S(1)}, u32[]{:S(2)}, u32[]{:S(2)}) collective-permute-start(f32[7,2,256]{2,0,1:T(8,128)S(1)} %copy.14), channel_id=1, source_target_pairs={{0,4},{4,0},{8,12},{12,8},{1,5},{5,1},{9,13},{13,9},{2,6},{6,2},{1... | collective-permute-start | bytes 43016 | tf_op jit(solution)/shard_map/ppermute | solution.py:230
  11.2 2.6 %collective-permute-start.12 = (f32[7,2,256]{2,0,1:T(8,128)S(1)}, f32[7,2,256]{2,0,1:T(8,128)S(1)}, u32[]{:S(2)}, u32[]{:S(2)}) collective-permute-start(f32[7,2,256]{2,0,1:T(8,128)S(1)} %copy.14), channel_id=1, source_target_pairs={{0,8},{4,12},{8,0},{12,4},{1,9},{5,13},{9,1},{13,5},{2,10},{6,14},... | collective-permute-start | bytes 43016 | tf_op jit(solution)/shard_map/ppermute | solution.py:230
  13.9 1.0 %collective-permute-start.1 = (bf16[640,128]{1,0:T(8,128)(2,1)S(1)}, bf16[640,128]{1,0:T(8,128)(2,1)S(1)}, u32[]{:S(2)}, u32[]{:S(2)}) collective-permute-start(bf16[640,128]{1,0:T(8,128)(2,1)S(1)} %get-tuple-element.13), channel_id=1, source_target_pairs={{0,4},{4,0},{8,12},{12,8},{1,5},{5,1},{9,13},{13,9},{2,6},{6,2},{1... | collective-permute-start | bytes 491528 | tf_op jit(solution)/shard_map/ppermute | solution.py:230
  14.8 3.5 %collective-permute-start.2 = (bf16[640,128]{1,0:T(8,128)(2,1)S(1)}, bf16[640,128]{1,0:T(8,128)(2,1)S(1)}, u32[]{:S(2)}, u32[]{:S(2)}) collective-permute-start(bf16[640,128]{1,0:T(8,128)(2,1)S(1)} %get-tuple-element.14), channel_id=1, source_target_pairs={{0,8},{4,12},{8,0},{12,4},{1,9},{5,13},{9,1},{13,5},{2,10},{6,14},... | collective-permute-start | bytes 491528 | tf_op jit(solution)/shard_map/ppermute | solution.py:230
  18.3 1.3 %collective-permute-done.13 = f32[7,2,256]{2,0,1:T(8,128)S(1)} collective-permute-done((f32[7,2,256]{2,0,1:T(8,128)S(1)}, f32[7,2,256]{2,0,1:T(8,128)S(1)}, u32[]{:S(2)}, u32[]{:S(2)}) %collective-permute-start.13) | collective-permute-done | bytes 14368 | tf_op jit(solution)/shard_map/ppermute | solution.py:230
  20.3 2.1 %collective-permute-done.1.refs_1_ = bf16[640,128]{1,0:T(8,128)(2,1)S(1)} collective-permute-done((bf16[640,128]{1,0:T(8,128)(2,1)S(1)}, bf16[640,128]{1,0:T(8,128)(2,1)S(1)}, u32[]{:S(2)}, u32[]{:S(2)}) %collective-permute-start.1) | collective-permute-done | bytes 163872 | tf_op jit(solution)/shard_map/ppermute | solution.py:230
  22.4 8.0 %collective-permute-done.2.refs_2_ = bf16[640,128]{1,0:T(8,128)(2,1)S(1)} collective-permute-done((bf16[640,128]{1,0:T(8,128)(2,1)S(1)}, bf16[640,128]{1,0:T(8,128)(2,1)S(1)}, u32[]{:S(2)}, u32[]{:S(2)}) %collective-permute-start.2) | collective-permute-done | bytes 163872 | tf_op jit(solution)/shard_map/ppermute | solution.py:230
  30.6 2.3 %collective-permute-start.6 = (bf16[640,128]{1,0:T(8,128)(2,1)S(1)}, bf16[640,128]{1,0:T(8,128)(2,1)S(1)}, u32[]{:S(2)}, u32[]{:S(2)}) collective-permute-start(bf16[640,128]{1,0:T(8,128)(2,1)S(1)} %shard_map.96.refs_0_), channel_id=1, source_target_pairs={{0,12},{4,8},{8,4},{12,0},{1,13},{5,9},{9,5},{13,1},{2,14},{6,10},... | collective-permute-start | bytes 491528 | tf_op jit(solution)/shard_map/ppermute | solution.py:230
  32.8 3.6 %collective-permute-start.4 = (bf16[640,128]{1,0:T(8,128)(2,1)S(1)}, bf16[640,128]{1,0:T(8,128)(2,1)S(1)}, u32[]{:S(2)}, u32[]{:S(2)}) collective-permute-start(bf16[640,128]{1,0:T(8,128)(2,1)S(1)} %shard_map.96.refs_0_), channel_id=1, source_target_pairs={{0,4},{4,0},{8,12},{12,8},{1,5},{5,1},{9,13},{13,9},{2,6},{6,2},{1... | collective-permute-start | bytes 491528 | tf_op jit(solution)/shard_map/ppermute | solution.py:230
  36.7 2.9 %collective-permute-done.6.refs_3_ = bf16[640,128]{1,0:T(8,128)(2,1)S(1)} collective-permute-done((bf16[640,128]{1,0:T(8,128)(2,1)S(1)}, bf16[640,128]{1,0:T(8,128)(2,1)S(1)}, u32[]{:S(2)}, u32[]{:S(2)}) %collective-permute-start.6) | collective-permute-done | bytes 163872 | tf_op jit(solution)/shard_map/ppermute | solution.py:230
  39.6 1.3 %collective-permute-done.4.refs_1_ = bf16[640,128]{1,0:T(8,128)(2,1)S(1)} collective-permute-done((bf16[640,128]{1,0:T(8,128)(2,1)S(1)}, bf16[640,128]{1,0:T(8,128)(2,1)S(1)}, u32[]{:S(2)}, u32[]{:S(2)}) %collective-permute-start.4) | collective-permute-done | bytes 163872 | tf_op jit(solution)/shard_map/ppermute | solution.py:230
  40.9 5.7 %collective-permute-done.5.refs_2_ = bf16[640,128]{1,0:T(8,128)(2,1)S(1)} collective-permute-done((bf16[640,128]{1,0:T(8,128)(2,1)S(1)}, bf16[640,128]{1,0:T(8,128)(2,1)S(1)}, u32[]{:S(2)}, u32[]{:S(2)}) %collective-permute-start.5) | collective-permute-done | bytes 163872 | tf_op jit(solution)/shard_map/ppermute | solution.py:230
  46.7 1.3 %collective-permute-done.9.refs_6_ = bf16[640,128]{1,0:T(8,128)(2,1)S(1)} collective-permute-done((bf16[640,128]{1,0:T(8,128)(2,1)S(1)}, bf16[640,128]{1,0:T(8,128)(2,1)S(1)}, u32[]{:S(2)}, u32[]{:S(2)}) %collective-permute-start.9) | collective-permute-done | bytes 163872 | tf_op jit(solution)/shard_map/ppermute | solution.py:233
  48.0 3.2 %shard_map.97 = (bf16[4,512,512]{2,1,0:T(8,128)(2,1)S(1)}, f32[4,512]{1,0:T(4,128)S(1)}, f32[4,512]{1,0:T(4,128)S(1)}) custom-call(bf16[640,128]{1,0:T(8,128)(2,1)S(1)} %shard_map.96.refs_0_, bf16[640,128]{1,0:T(8,128)(2,1)S(1)} %collective-permute-done.4.refs_1_, bf16[640,128]{1,0:T(8,128)(2,1)S(1)} %collective-permute-done.5.refs_2_, ...), custom_call_target="tpu_custom_call" | custom-call | tf_op jit(solution)/shard_map/pallas_call | solution.py:271
  51.3 3.4 %collective-permute-start.15 = (f32[1,512]{1,0:T(1,128)S(1)}, f32[1,512]{1,0:T(1,128)S(1)}, u32[]{:S(2)}, u32[]{:S(2)}) collective-permute-start(f32[1,512]{1,0:T(1,128)S(1)} %slice.98), channel_id=1, source_target_pairs={{0,2},{1,3},{4,6},{5,7},{8,10},{9,11},{12,14},{13,15},{16,18},{17,... | collective-permute-start | bytes 6152 | tf_op jit(solution)/shard_map/ppermute | solution.py:335
  54.7 1.3 %collective-permute-done.15.state_ref = f32[1,512]{1,0:T(1,128)S(1)} collective-permute-done((f32[1,512]{1,0:T(1,128)S(1)}, f32[1,512]{1,0:T(1,128)S(1)}, u32[]{:S(2)}, u32[]{:S(2)}) %collective-permute-start.15) | collective-permute-done | bytes 2080 | tf_op jit(solution)/shard_map/ppermute | solution.py:335
  55.9 2.3 %shard_map.98 = (f32[4,512]{1,0:T(4,128)S(1)}, f32[4,512]{1,0:T(4,128)S(1)}) custom-call(bf16[4,512,512]{2,1,0:T(8,128)(2,1)S(1)} %get-tuple-element.17.grams, f32[4,512]{1,0:T(4,128)S(1)} %get-tuple-element.29.refs_9_.diag, f32[4,512]{1,0:T(4,128)S(1)} %get-tuple-element.28.refs_10_.info, f32[4,512]{1,0:T(4,128)S(1)} %get-tuple-element.35.refs_11_.kappa, ...), custom_call_target="tpu_custom_call" | custom-call | tf_op jit(solution)/shard_map/pallas_call | solution.py:286
  58.3 1.3 %collective-permute-start.16 = (f32[1,512]{1,0:T(1,128)S(1)}, f32[1,512]{1,0:T(1,128)S(1)}, u32[]{:S(2)}, u32[]{:S(2)}) collective-permute-start(f32[1,512]{1,0:T(1,128)S(1)} %fusion.3), channel_id=1, source_target_pairs={{2,0},{3,1},{6,4},{7,5},{10,8},{11,9},{14,12},{15,13},{18,16},{19,... | collective-permute-start | bytes 6152 | tf_op jit(solution)/shard_map/ppermute | solution.py:346
  59.6 4.2 %collective-permute-done.16 = f32[1,512]{1,0:T(1,128)S(1)} collective-permute-done((f32[1,512]{1,0:T(1,128)S(1)}, f32[1,512]{1,0:T(1,128)S(1)}, u32[]{:S(2)}, u32[]{:S(2)}) %collective-permute-start.16) | collective-permute-done | bytes 2080 | tf_op jit(solution)/shard_map/ppermute | solution.py:346
  (43 shorter events, 2.7 us)
Async XLA Ops:
  0.6 47.4 %copy-start.1 = (f32[512]{0:T(512)S(1)}, f32[512]{0:T(512)}, u32[]{:S(2)}) copy-start(f32[512]{0:T(512)} %param.15) | copy-start | bytes 6148
  0.6 3.0 %collective-permute-start = (bf16[16,128,256]{2,1,0:T(8,128)(2,1)}, bf16[16,128,256]{2,1,0:T(8,128)(2,1)S(1)}, u32[]{:S(2)}, u32[]{:S(2)}) collective-permute-start(bf16[16,128,256]{2,1,0:T(8,128)(2,1)} %bitcast.57), channel_id=1, source_target_pairs={{0,1},{1,0},{2,3},{3,2},{4,5},{5,4},{6,7},{7,6},{8,9},{9,8},{10,11... | collective-permute-start | bytes 3145736 | tf_op jit(solution)/shard_map/ppermute | solution.py:219
  3.7 1.2 %copy-start = (bf16[1,16,128,256]{3,2,1,0:T(8,128)(2,1)S(1)}, bf16[1,16,128,256]{3,2,1,0:T(8,128)(2,1)}, u32[]{:S(2)}) copy-start(bf16[1,16,128,256]{3,2,1,0:T(8,128)(2,1)} %param.8) | copy-start | bytes 3145732
  8.2 10.1 %collective-permute-start.11 = (f32[7,2,256]{2,0,1:T(8,128)S(1)}, f32[7,2,256]{2,0,1:T(8,128)S(1)}, u32[]{:S(2)}, u32[]{:S(2)}) collective-permute-start(f32[7,2,256]{2,0,1:T(8,128)S(1)} %copy.14), channel_id=1, source_target_pairs={{0,4},{4,0},{8,12},{12,8},{1,5},{5,1},{9,13},{13,9},{2,6},{6,2},{1... | collective-permute-start | bytes 43016 | tf_op jit(solution)/shard_map/ppermute | solution.py:230
  11.2 7.1 %collective-permute-start.12 = (f32[7,2,256]{2,0,1:T(8,128)S(1)}, f32[7,2,256]{2,0,1:T(8,128)S(1)}, u32[]{:S(2)}, u32[]{:S(2)}) collective-permute-start(f32[7,2,256]{2,0,1:T(8,128)S(1)} %copy.14), channel_id=1, source_target_pairs={{0,8},{4,12},{8,0},{12,4},{1,9},{5,13},{9,1},{13,5},{2,10},{6,14},... | collective-permute-start | bytes 43016 | tf_op jit(solution)/shard_map/ppermute | solution.py:230
  13.8 5.8 %collective-permute-start.13 = (f32[7,2,256]{2,0,1:T(8,128)S(1)}, f32[7,2,256]{2,0,1:T(8,128)S(1)}, u32[]{:S(2)}, u32[]{:S(2)}) collective-permute-start(f32[7,2,256]{2,0,1:T(8,128)S(1)} %copy.14), channel_id=1, source_target_pairs={{0,12},{4,8},{8,4},{12,0},{1,13},{5,9},{9,5},{13,1},{2,14},{6,10},... | collective-permute-start | bytes 43016 | tf_op jit(solution)/shard_map/ppermute | solution.py:230
  13.9 8.5 %collective-permute-start.1 = (bf16[640,128]{1,0:T(8,128)(2,1)S(1)}, bf16[640,128]{1,0:T(8,128)(2,1)S(1)}, u32[]{:S(2)}, u32[]{:S(2)}) collective-permute-start(bf16[640,128]{1,0:T(8,128)(2,1)S(1)} %get-tuple-element.13), channel_id=1, source_target_pairs={{0,4},{4,0},{8,12},{12,8},{1,5},{5,1},{9,13},{13,9},{2,6},{6,2},{1... | collective-permute-start | bytes 491528 | tf_op jit(solution)/shard_map/ppermute | solution.py:230
  14.8 15.6 %collective-permute-start.2 = (bf16[640,128]{1,0:T(8,128)(2,1)S(1)}, bf16[640,128]{1,0:T(8,128)(2,1)S(1)}, u32[]{:S(2)}, u32[]{:S(2)}) collective-permute-start(bf16[640,128]{1,0:T(8,128)(2,1)S(1)} %get-tuple-element.14), channel_id=1, source_target_pairs={{0,8},{4,12},{8,0},{12,4},{1,9},{5,13},{9,1},{13,5},{2,10},{6,14},... | collective-permute-start | bytes 491528 | tf_op jit(solution)/shard_map/ppermute | solution.py:230
  18.3 12.1 %collective-permute-start.3 = (bf16[640,128]{1,0:T(8,128)(2,1)S(1)}, bf16[640,128]{1,0:T(8,128)(2,1)S(1)}, u32[]{:S(2)}, u32[]{:S(2)}) collective-permute-start(bf16[640,128]{1,0:T(8,128)(2,1)S(1)} %get-tuple-element.15), channel_id=1, source_target_pairs={{0,12},{4,8},{8,4},{12,0},{1,13},{5,9},{9,5},{13,1},{2,14},{6,10},... | collective-permute-start | bytes 491528 | tf_op jit(solution)/shard_map/ppermute | solution.py:230
  19.6 27.0 %collective-permute-start.14 = (f32[4,2,256]{2,0,1:T(4,128)S(1)}, f32[4,2,256]{2,0,1:T(4,128)S(1)}, u32[]{:S(2)}, u32[]{:S(2)}) collective-permute-start(f32[4,2,256]{2,0,1:T(4,128)S(1)} %slice_add_fusion), channel_id=1, source_target_pairs={{0,1},{1,0},{2,3},{3,2},{4,5},{5,4},{6,7},{7,6},{8,9},{9,8},{10,11... | collective-permute-start | bytes 24584 | tf_op jit(solution)/shard_map/ppermute | solution.py:233
  30.6 9.0 %collective-permute-start.6 = (bf16[640,128]{1,0:T(8,128)(2,1)S(1)}, bf16[640,128]{1,0:T(8,128)(2,1)S(1)}, u32[]{:S(2)}, u32[]{:S(2)}) collective-permute-start(bf16[640,128]{1,0:T(8,128)(2,1)S(1)} %shard_map.96.refs_0_), channel_id=1, source_target_pairs={{0,12},{4,8},{8,4},{12,0},{1,13},{5,9},{9,5},{13,1},{2,14},{6,10},... | collective-permute-start | bytes 491528 | tf_op jit(solution)/shard_map/ppermute | solution.py:230
  32.8 8.1 %collective-permute-start.4 = (bf16[640,128]{1,0:T(8,128)(2,1)S(1)}, bf16[640,128]{1,0:T(8,128)(2,1)S(1)}, u32[]{:S(2)}, u32[]{:S(2)}) collective-permute-start(bf16[640,128]{1,0:T(8,128)(2,1)S(1)} %shard_map.96.refs_0_), channel_id=1, source_target_pairs={{0,4},{4,0},{8,12},{12,8},{1,5},{5,1},{9,13},{13,9},{2,6},{6,2},{1... | collective-permute-start | bytes 491528 | tf_op jit(solution)/shard_map/ppermute | solution.py:230
  36.4 10.2 %collective-permute-start.5 = (bf16[640,128]{1,0:T(8,128)(2,1)S(1)}, bf16[640,128]{1,0:T(8,128)(2,1)S(1)}, u32[]{:S(2)}, u32[]{:S(2)}) collective-permute-start(bf16[640,128]{1,0:T(8,128)(2,1)S(1)} %shard_map.96.refs_0_), channel_id=1, source_target_pairs={{0,8},{4,12},{8,0},{12,4},{1,9},{5,13},{9,1},{13,5},{2,10},{6,14},... | collective-permute-start | bytes 491528 | tf_op jit(solution)/shard_map/ppermute | solution.py:230
  36.7 9.9 %collective-permute-start.7 = (bf16[640,128]{1,0:T(8,128)(2,1)S(1)}, bf16[640,128]{1,0:T(8,128)(2,1)S(1)}, u32[]{:S(2)}, u32[]{:S(2)}) collective-permute-start(bf16[640,128]{1,0:T(8,128)(2,1)S(1)} %shard_map.96.refs_0_), channel_id=1, source_target_pairs={{0,1},{1,0},{2,3},{3,2},{4,5},{5,4},{6,7},{7,6},{8,9},{9,8},{10,11... | collective-permute-start | bytes 491528 | tf_op jit(solution)/shard_map/ppermute | solution.py:233
  39.6 7.0 %collective-permute-start.10 = (bf16[640,128]{1,0:T(8,128)(2,1)S(1)}, bf16[640,128]{1,0:T(8,128)(2,1)S(1)}, u32[]{:S(2)}, u32[]{:S(2)}) collective-permute-start(bf16[640,128]{1,0:T(8,128)(2,1)S(1)} %collective-permute-done.6.refs_3_), channel_id=1, source_target_pairs={{0,1},{1,0},{2,3},{3,2},{4,5},{5,4},{6,7},{7,6},{8,9},{9,8},{10,11... | collective-permute-start | bytes 491528 | tf_op jit(solution)/shard_map/ppermute | solution.py:233
  40.9 5.8 %collective-permute-start.8 = (bf16[640,128]{1,0:T(8,128)(2,1)S(1)}, bf16[640,128]{1,0:T(8,128)(2,1)S(1)}, u32[]{:S(2)}, u32[]{:S(2)}) collective-permute-start(bf16[640,128]{1,0:T(8,128)(2,1)S(1)} %collective-permute-done.4.refs_1_), channel_id=1, source_target_pairs={{0,1},{1,0},{2,3},{3,2},{4,5},{5,4},{6,7},{7,6},{8,9},{9,8},{10,11... | collective-permute-start | bytes 491528 | tf_op jit(solution)/shard_map/ppermute | solution.py:233
  46.6 1.4 %collective-permute-start.9 = (bf16[640,128]{1,0:T(8,128)(2,1)S(1)}, bf16[640,128]{1,0:T(8,128)(2,1)S(1)}, u32[]{:S(2)}, u32[]{:S(2)}) collective-permute-start(bf16[640,128]{1,0:T(8,128)(2,1)S(1)} %collective-permute-done.5.refs_2_), channel_id=1, source_target_pairs={{0,1},{1,0},{2,3},{3,2},{4,5},{5,4},{6,7},{7,6},{8,9},{9,8},{10,11... | collective-permute-start | bytes 491528 | tf_op jit(solution)/shard_map/ppermute | solution.py:233
  51.3 4.7 %collective-permute-start.15 = (f32[1,512]{1,0:T(1,128)S(1)}, f32[1,512]{1,0:T(1,128)S(1)}, u32[]{:S(2)}, u32[]{:S(2)}) collective-permute-start(f32[1,512]{1,0:T(1,128)S(1)} %slice.98), channel_id=1, source_target_pairs={{0,2},{1,3},{4,6},{5,7},{8,10},{9,11},{12,14},{13,15},{16,18},{17,... | collective-permute-start | bytes 6152 | tf_op jit(solution)/shard_map/ppermute | solution.py:335
  58.3 5.5 %collective-permute-start.16 = (f32[1,512]{1,0:T(1,128)S(1)}, f32[1,512]{1,0:T(1,128)S(1)}, u32[]{:S(2)}, u32[]{:S(2)}) collective-permute-start(f32[1,512]{1,0:T(1,128)S(1)} %fusion.3), channel_id=1, source_target_pairs={{2,0},{3,1},{6,4},{7,5},{10,8},{11,9},{14,12},{15,13},{18,16},{19,... | collective-permute-start | bytes 6152 | tf_op jit(solution)/shard_map/ppermute | solution.py:346

commit v4 on v3

--- a/solution.py
+++ b/solution.py
@@ -10,6 +10,7 @@
 STEPS = 4
 LANES = 128
 GROUP_ROWS = 16
+VECTORS = 10
 DIRECT_TM = 4
 
 VMEM = pl.BlockSpec(memory_space=pltpu.VMEM)
@@ -95,13 +96,19 @@
     row_pass(block, next_ref, meta, y_ref, own_ref, other_ref, acc, part_ref)
 
 
-def gram_kernel(meta, y_ref, own_ref, other_ref, params_ref, *refs):
-    outs, side_ref, acc, vec = refs[:-3], refs[-3], refs[-2], refs[-1]
+def pieces_of(values):
+    high = values.astype(jnp.bfloat16).astype(jnp.float32)
+    middle = (values - high).astype(jnp.bfloat16).astype(jnp.float32)
+    return high, middle, values - high - middle
+
+
+def gram_kernel(meta, y_ref, own_ref, other_ref, *refs):
+    outs, acc, vec, side = refs[:-3], refs[-3], refs[-2], refs[-1]
     tile_num, row_num, half = own_ref.shape
-    block_num = len(outs)
     core, position = meta[2 * tile_num], meta[2 * tile_num + 1]
     acc[...] = jnp.zeros_like(acc)
     vec[...] = jnp.zeros_like(vec)
+    side[...] = jnp.zeros_like(side)
     row = lax.broadcasted_iota(jnp.int32, (row_num, half), 0)
     over_rows = (((0,), (0,)), ((), ()))
 
@@ -127,86 +134,107 @@
         return carry
 
     lax.fori_loop(0, tile_num, tile, 0, unroll=2)
-    on_diagonal = lax.broadcasted_iota(jnp.int32, (LANES, LANES), 0) == lax.broadcasted_iota(
-        jnp.int32, (LANES, LANES), 1
-    )
+    line = lax.broadcasted_iota(jnp.int32, (LANES, LANES), 0)
+    column = lax.broadcasted_iota(jnp.int32, (LANES, LANES), 1)
     for flip, out_ref in enumerate(outs):
         block = position ^ flip
-        for piece in range(5):
-            values = acc[block, piece * LANES : (piece + 1) * LANES]
-            if piece in (0, 2):
-                side_ref[block, 0:1, (piece // 2) * LANES : (piece // 2 + 1) * LANES] = jnp.sum(
-                    jnp.where(on_diagonal, values, 0.0), axis=0, keepdims=True
-                )
-                values = jnp.where(on_diagonal, 0.0, values)
-            out_ref[piece * LANES : (piece + 1) * LANES] = values.astype(jnp.bfloat16)
-    for block in range(block_num):
-        side_ref[block, 1:2, :] = vec[block, 0:1, :]
+
+        def take(piece):
+            return acc[block, piece * LANES : (piece + 1) * LANES]
+
+        packed = jnp.where(line < column, take(0), jnp.where(line > column, take(2), 0.0))
+        out_ref[0:LANES] = packed.astype(jnp.bfloat16)
+        for at, piece in ((1, 1), (2, 3), (3, 4)):
+            out_ref[at * LANES : (at + 1) * LANES] = take(piece).astype(jnp.bfloat16)
+        values = [vec[block, 0:1, :LANES], vec[block, 0:1, LANES:]]
+        for piece in (0, 2):
+            values.append(
+                jnp.sum(jnp.where(line == column, take(piece), 0.0), axis=0, keepdims=True)
+            )
+        for at, value in enumerate(values):
+            for which, part in enumerate(pieces_of(value)):
+                side[which * 4 + at : which * 4 + at + 1, :] = part
+        out_ref[4 * LANES :] = side[...].astype(jnp.bfloat16)
+
+
+def sum_kernel(meta, params_ref, *refs):
+    parts, out_ref, side = refs[:-2], refs[-2], refs[-1]
+    core = meta[meta.shape[0] - 2]
+    total = parts[0][...].astype(jnp.float32)
+    for part in parts[1:]:
+        total = total + part[...].astype(jnp.float32)
+    out_ref[: 4 * LANES] = total[: 4 * LANES].astype(jnp.bfloat16)
+    below = total[4 * LANES :]
+    values = [below[at : at + 1] + below[at + 4 : at + 5] + below[at + 8 : at + 9] for at in range(4)]
     for which in range(3):
         for piece in range(2):
-            side_ref[block_num + which, piece : piece + 1, :] = params_ref[
-                which : which + 1, piece * half : (piece + 1) * half
-            ]
-
-
-def sum_kernel(*refs):
-    total = refs[0][...].astype(jnp.float32)
-    for part in refs[1:-1]:
-        total = total + part[...].astype(jnp.float32)
-    refs[-1][...] = total.astype(jnp.bfloat16)
-
-
-def chain(grams, diag, info, kappa, rate, state, states_ref, innovations_ref):
+            at = pl.multiple_of((2 * core + piece) * LANES, LANES)
+            values.append(params_ref[which : which + 1, pl.ds(at, LANES)])
+    side[...] = jnp.zeros_like(side)
+    for at, value in enumerate(values):
+        for which, part in enumerate(pieces_of(value)):
+            side[which * VECTORS + at : which * VECTORS + at + 1, :] = part
+    out_ref[4 * LANES :] = side[...].astype(jnp.bfloat16)
+
+
+def chain(grams, vectors, state, states_ref, innovations_ref):
     width = state.shape[1]
     line = lax.broadcasted_iota(jnp.int32, (16, width), 0)
     for block in range(grams.shape[0]):
-        high = state.astype(jnp.bfloat16).astype(jnp.float32)
-        middle = (state - high).astype(jnp.bfloat16).astype(jnp.float32)
-        low = state - high - middle
+        info, diagonal, coeff, decay = (vectors[block, which : which + 1, :] for which in range(4))
+        high, middle, low = pieces_of(state)
         split = jnp.where(line == 0, high, jnp.where(line == 1, middle, jnp.where(line == 2, low, 0.0)))
         product = jnp.dot(
             split.astype(jnp.bfloat16), grams[block], preferred_element_type=jnp.float32
         )
-        diagonal = diag[block : block + 1, :]
         product = jnp.sum(product, axis=0, keepdims=True) + diagonal * state
         trace_val = jnp.sum(diagonal, axis=1, keepdims=True)
         lam_val = width / (2.0 * (width + trace_val))
-        coeff, decay = kappa[block : block + 1, :], rate[block : block + 1, :]
-        innovation = -lam_val * stencil(product - info[block : block + 1, :], coeff, decay)
+        innovation = -lam_val * stencil(product - info, coeff, decay)
         state = stencil(state, coeff, decay) + innovation
         states_ref[block : block + 1, :] = state
         innovations_ref[block : block + 1, :] = innovation
 
 
-def assemble_kernel(number, *refs):
+def assemble_kernel(number, meta, *refs):
     own, other, rest = refs[:number], refs[number : 2 * number], refs[2 * number :]
-    where, diag, info, kappa, rate, state_ref, grams, states_ref, innovations_ref = rest
-    core, position = where[0], where[1]
+    state_ref, grams, vectors, states_ref, innovations_ref = rest
+    core, position = meta[meta.shape[0] - 2], meta[meta.shape[0] - 1]
     half = 2 * LANES
+    line = lax.broadcasted_iota(jnp.int32, (LANES, LANES), 0)
+    column = lax.broadcasted_iota(jnp.int32, (LANES, LANES), 1)
     for flip in range(number):
         block = position ^ flip
         for pieces, side in ((own[flip], core), (other[flip], 1 - core)):
+
             def piece(index):
                 return pieces[index * LANES : (index + 1) * LANES, :]
 
             def put(row, column, values):
                 row, column = pl.multiple_of(row, LANES), pl.multiple_of(column, LANES)
-                grams[block, pl.ds(row, LANES), pl.ds(column, LANES)] = values
+                grams[block, pl.ds(row, LANES), pl.ds(column, LANES)] = values.astype(jnp.bfloat16)
 
             here, there = side * half, (1 - side) * half
-            put(here, here, piece(0))
+            packed = piece(0).astype(jnp.float32)
+            turned = packed.T
+            put(here, here, jnp.where(line < column, packed, turned))
+            put(here + LANES, here + LANES, jnp.where(line > column, packed, turned))
             put(here, here + LANES, piece(1))
             put(here + LANES, here, piece(1).T)
-            put(here + LANES, here + LANES, piece(2))
             for index in range(2):
-                across = there + (index ^ side) * LANES
-                put(here + index * LANES, across, piece(3 + index))
-                put(across, here + index * LANES, piece(3 + index).T)
-    chain(grams, diag, info, kappa, rate, state_ref[...], states_ref, innovations_ref)
-
-
-def chain_kernel(grams, diag, info, kappa, rate, state_ref, states_ref, innovations_ref):
-    chain(grams, diag, info, kappa, rate, state_ref[...], states_ref, innovations_ref)
+                beyond = there + (index ^ side) * LANES
+                put(here + index * LANES, beyond, piece(2 + index))
+                put(beyond, here + index * LANES, piece(2 + index).T)
+            below = pieces[4 * LANES :, :].astype(jnp.float32)
+            below = below[:VECTORS] + below[VECTORS : 2 * VECTORS] + below[2 * VECTORS : 3 * VECTORS]
+            for at in range(VECTORS):
+                lanes = pl.ds(pl.multiple_of(here + (at % 2) * LANES, LANES), LANES)
+                vectors[block, at // 2 : at // 2 + 1, lanes] = below[at : at + 1]
+    chain(grams, vectors, state_ref[...], states_ref, innovations_ref)
+
+
+def chain_kernel(grams, vectors, state_ref, states_ref, innovations_ref):
+    chain(grams, vectors, state_ref[...], states_ref, innovations_ref)
 
 
 def shards(rows_h, rows_y, tile_block, tile_count, kappa, rate, smooth_gain, start_state):
@@ -233,52 +261,43 @@
         return lax.ppermute(array, "state", [(i, (i + 1) % state_size) for i in range(state_size)])
 
     if direct:
-        packed = jax.ShapeDtypeStruct((5 * LANES, LANES), jnp.bfloat16)
-        *pieces, side = pl.pallas_call(
+        sent = jax.ShapeDtypeStruct((4 * LANES + 16, LANES), jnp.bfloat16)
+        pieces = pl.pallas_call(
             gram_kernel,
-            out_shape=[packed] * tm_size
-            + [jax.ShapeDtypeStruct((tm_size + 3, 2, half), jnp.float32)],
-            in_specs=[SMEM] + [VMEM] * 4,
-            out_specs=[VMEM] * (tm_size + 1),
+            out_shape=[sent] * tm_size,
+            in_specs=[SMEM] + [VMEM] * 3,
+            out_specs=[VMEM] * tm_size,
             scratch_shapes=[
                 pltpu.VMEM((tm_size, 5 * LANES, LANES), jnp.float32),
                 pltpu.VMEM((tm_size, 8, half), jnp.float32),
+                pltpu.VMEM((16, LANES), jnp.float32),
             ],
             compiler_params=KERNEL,
-        )(meta, readings, own, other, params)
-        parts = pieces[:1] + [flip_over(pieces[flip], flip) for flip in range(1, tm_size)]
-
-        sides = [side] + [flip_over(side, flip) for flip in range(1, tm_size)]
-        side_sum = sum(values[:tm_size] for values in sides)
-        side_other = across(side_sum)
-        low = jnp.where(core == 0, side_sum, side_other)
-        high = jnp.where(core == 0, side_other, side_sum)
-        vectors = jnp.concatenate([low, high], axis=2)
-        diag, info = vectors[:, 0], vectors[:, 1]
-        order = jnp.arange(tm_size) ^ tm_index
-        gathered = jnp.stack([values[tm_size:].reshape(3, width) for values in sides])[order]
-
+        )(meta, readings, own, other)
+        parts = [pieces[0]] + [flip_over(pieces[flip], flip) for flip in range(1, tm_size)]
         own_sum = pl.pallas_call(
             sum_kernel,
-            out_shape=packed,
-            in_specs=[VMEM] * tm_size,
+            out_shape=jax.ShapeDtypeStruct((4 * LANES + 32, LANES), jnp.bfloat16),
+            in_specs=[SMEM] + [VMEM] * (tm_size + 1),
             out_specs=VMEM,
+            scratch_shapes=[pltpu.VMEM((32, LANES), jnp.float32)],
             compiler_params=KERNEL,
-        )(*parts)
+        )(meta, params, *parts)
         own_sums = [own_sum] + [flip_over(own_sum, flip) for flip in range(1, tm_size)]
         other_sums = [across(values) for values in own_sums]
-        coefficients = (diag, info, gathered[:, 0], gathered[:, 1])
-        grams, new_states, new_innovations = pl.pallas_call(
+        grams, vectors, new_states, new_innovations = pl.pallas_call(
             functools.partial(assemble_kernel, tm_size),
             out_shape=(
                 jax.ShapeDtypeStruct((tm_size, width, width), jnp.bfloat16),
+                jax.ShapeDtypeStruct((tm_size, VECTORS // 2, width), jnp.float32),
                 states_shape,
                 states_shape,
             ),
-            in_specs=[VMEM] * (2 * tm_size) + [SMEM] + [VMEM] * 5,
-            out_specs=(VMEM, VMEM, VMEM),
+            in_specs=[SMEM] + [VMEM] * (2 * tm_size + 1),
+            out_specs=[VMEM] * 4,
             compiler_params=KERNEL,
-        )(*own_sums, *other_sums, meta[2 * tile_num :], *coefficients, state)
+        )(meta, *own_sums, *other_sums, state)
+        gains = vectors[:, 4]
 
         def run_group(state, group):
             if group == 0:
@@ -286,12 +305,13 @@
             return pl.pallas_call(
                 chain_kernel,
                 out_shape=(states_shape, states_shape),
-                in_specs=[VMEM] * 6,
+                in_specs=[VMEM] * 3,
                 out_specs=(VMEM, VMEM),
                 compiler_params=KERNEL,
-            )(grams, *coefficients, state)
+            )(grams, vectors, state)
     else:
         gathered = lax.all_gather(params, "tm")
+        gains = gathered[:, 2]
         vector = jax.ShapeDtypeStruct((1, width), jnp.float32)
         partial = jax.ShapeDtypeStruct((1, width + LANES), jnp.float32)
         acc = pltpu.VMEM((GROUP_ROWS, width + LANES), jnp.float32)
@@ -334,7 +354,6 @@
         if group < grp_size - 1:
             state = lax.ppermute(new_states[-1:], "grp", [(group, group + 1)])
 
-    gains = gathered[:, 2]
     residual = jnp.zeros((1, width), jnp.float32)
     residuals = [None] * tm_size
     for group in reversed(range(grp_size)):

time: 64.7 us -> 57.6 us (0.89)
  starting transfers between devices: 21.4 us -> 15.3 us
  other arithmetic: 3 us -> 2.17 us
  Pallas kernels: 8.87 us -> 9.58 us
    ppermute x9 -> x6, starting transfers between devices: 16.2 us -> 10.1 us  [flip_over(): return lax.ppermute(array, 'tm', [(i, i ^ flip) for i in range(tm_size)])]
    ppermute x9 -> x6, waiting for transfers between devices: 21.3 us -> 20.5 us  [flip_over(): return lax.ppermute(array, 'tm', [(i, i ^ flip) for i in range(tm_size)])]
    ppermute x1, waiting for transfers between devices: 0.31 us -> 1.06 us  [shards(): lax.ppermute(own, 'state', [(i, (i + 1) % state_size) for i in range(stat...]
    concatenate x1, other arithmetic: 0.73 us -> 0.01 us  [shards(): params = jnp.concatenate([kappa[0], rate[0], smooth_gain[0]], axis=0)]
    ppermute x5 -> x4, waiting for transfers between devices: 1.35 us -> 1.34 us  [across(): lax.ppermute(array, 'state', [(i, (i + 1) % state_size) for i in range(st...]
  transfers between devices with their start and end apart: 17 -> 13, of which waited for: 10 -> 9; matrix products, arithmetic and copies ran while one was open for 5% -> 3% of each run, Pallas kernels for 0% -> 0%
where the time goes in v4:
time: 57.6 us; the launch traced here: 57.4 us
  waiting for transfers between devices  28.4 us (49%)
  starting transfers between devices  15.3 us (27%)
  Pallas kernels  9.58 us (17%)
  other arithmetic  2.17 us (4%)
  local copies, waits for them, and re-layouts  1.25 us (2%)
  between operations  0.78 us (1%)
    ppermute x6, waiting for transfers between devices, flip_over(): return lax.ppermute(array, 'tm', [(i, i ^ flip) for i in range(tm_size)])  20.5 us
    ppermute x6, starting transfers between devices, flip_over(): return lax.ppermute(array, 'tm', [(i, i ^ flip) for i in range(tm_size)])  10.1 us
    ppermute x1, waiting for transfers between devices, shards(): arrived = lax.ppermute(running, 'grp', [(group, group - 1)])  4.16 us
    ppermute x1, starting transfers between devices, shards(): state = lax.ppermute(new_states[-1:], 'grp', [(group, group + 1)])  3.4 us
    pallas_call x1, Pallas kernels, shards(): pl.pallas_call(gram_kernel, out_shape=[sent] * tm_size, in_specs=[SMEM] +...  3.33 us
    pallas_call x1, Pallas kernels, shards(): pl.pallas_call(functools.partial(assemble_kernel, tm_size), out_shape=(ja...  3.33 us
    pallas_call x1, Pallas kernels, run_group(): pl.pallas_call(chain_kernel, out_shape=(states_shape, states_shape), in_s...  2.27 us
    ppermute x4, waiting for transfers between devices, across(): lax.ppermute(array, 'state', [(i, (i + 1) % state_size) for i in range(st...  1.34 us
  transfers between devices with their start and end apart: 13, of which 9 were waited for; matrix products, arithmetic and copies ran while one was open for 3% of the time, Pallas kernels for 0%

profile of v4, /device:TPU:0, one launch (start us, length us, event | category | flops | bytes accessed | tf_op | source)
XLA Modules:
  0.0 57.4 jit_solution(12714850735636008291)
XLA Ops:
  0.7 0.5 collective-permute-start
  1.2 0.7 %pad_add_fusion.meta = s32[34]{0:T(128)S(1)} fusion(s32[1]{0:T(128)} %bitcast.3, s32[1]{0:T(128)} %bitcast.2, s32[16]{0:T(128)} %bitcast.47, s32[16]{0:T(128)} %bitcast.48), kind=kLoop, calls=%fused_computation.23 | loop fusion | flops 102 | bytes 272 | tf_op jit(solution)/shard_map/concatenate | solution.py:250
  1.9 0.7 %bitcast_convert_fusion.y_ref = f32[16,128]{1,0:T(8,128)S(1)} fusion(bf16[1,16,128]{2,1,0:T(8,128)(2,1)} %param.9), kind=kLoop, calls=%fused_computation.7 | loop fusion | flops 2048 | bytes 12288 | tf_op jit(solution)/shard_map/convert_element_type | solution.py:248
  2.6 1.1 %collective-permute-done.other_ref = bf16[16,128,256]{2,1,0:T(8,128)(2,1)S(1)} collective-permute-done((bf16[16,128,256]{2,1,0:T(8,128)(2,1)}, bf16[16,128,256]{2,1,0:T(8,128)(2,1)S(1)}, u32[]{:S(2)}, u32[]{:S(2)}) %collective-permute-start) | collective-permute-done | bytes 1048608 | tf_op jit(solution)/shard_map/ppermute | solution.py:247
  3.7 1.2 %copy-done = bf16[1,16,128,256]{3,2,1,0:T(8,128)(2,1)S(1)} copy-done((bf16[1,16,128,256]{3,2,1,0:T(8,128)(2,1)S(1)}, bf16[1,16,128,256]{3,2,1,0:T(8,128)(2,1)}, u32[]{:S(2)}) %copy-start) | copy-done | bytes 1048600
  4.9 3.3 %shard_map.95 = (bf16[528,128]{1,0:T(8,128)(2,1)S(1)}, bf16[528,128]{1,0:T(8,128)(2,1)S(1)}, bf16[528,128]{1,0:T(8,128)(2,1)S(1)}, bf16[528,128]{1,0:T(8,128)(2,1)S(1)}) custom-call(s32[34]{0:T(128)S(1)} %pad_add_fusion.meta, f32[16,128]{1,0:T(8,128)S(1)} %bitcast_convert_fusion.y_ref, bf16[16,128,256]{2,1,0:T(8,128)(2,1)S(1)} %bitcast.42, ...), custom_call_target="tpu_custom_call" | custom-call | tf_op jit(solution)/shard_map/pallas_call | solution.py:265
  8.2 3.0 %collective-permute-start.1 = (bf16[528,128]{1,0:T(8,128)(2,1)S(1)}, bf16[528,128]{1,0:T(8,128)(2,1)S(1)}, u32[]{:S(2)}, u32[]{:S(2)}) collective-permute-start(bf16[528,128]{1,0:T(8,128)(2,1)S(1)} %get-tuple-element.13), channel_id=1, source_target_pairs={{0,4},{4,0},{8,12},{12,8},{1,5},{5,1},{9,13},{13,9},{2,6},{6,2},{1... | collective-permute-start | bytes 405512 | tf_op jit(solution)/shard_map/ppermute | solution.py:258
  11.3 2.6 %collective-permute-start.2 = (bf16[528,128]{1,0:T(8,128)(2,1)S(1)}, bf16[528,128]{1,0:T(8,128)(2,1)S(1)}, u32[]{:S(2)}, u32[]{:S(2)}) collective-permute-start(bf16[528,128]{1,0:T(8,128)(2,1)S(1)} %get-tuple-element.14), channel_id=1, source_target_pairs={{0,8},{4,12},{8,0},{12,4},{1,9},{5,13},{9,1},{13,5},{2,10},{6,14},... | collective-permute-start | bytes 405512 | tf_op jit(solution)/shard_map/ppermute | solution.py:258
  13.9 3.3 %collective-permute-done.1.refs_1_ = bf16[528,128]{1,0:T(8,128)(2,1)S(1)} collective-permute-done((bf16[528,128]{1,0:T(8,128)(2,1)S(1)}, bf16[528,128]{1,0:T(8,128)(2,1)S(1)}, u32[]{:S(2)}, u32[]{:S(2)}) %collective-permute-start.1) | collective-permute-done | bytes 135200 | tf_op jit(solution)/shard_map/ppermute | solution.py:258
  17.1 7.3 %collective-permute-done.2.refs_2_ = bf16[528,128]{1,0:T(8,128)(2,1)S(1)} collective-permute-done((bf16[528,128]{1,0:T(8,128)(2,1)S(1)}, bf16[528,128]{1,0:T(8,128)(2,1)S(1)}, u32[]{:S(2)}, u32[]{:S(2)}) %collective-permute-start.2) | collective-permute-done | bytes 135200 | tf_op jit(solution)/shard_map/ppermute | solution.py:258
  24.4 0.7 %shard_map.96.refs_0_ = bf16[544,128]{1,0:T(8,128)(2,1)S(1)} custom-call(s32[34]{0:T(128)S(1)} %pad_add_fusion.meta, f32[3,512]{1,0:T(4,128)S(1)} %pad_maximum_fusion.params_ref, bf16[528,128]{1,0:T(8,128)(2,1)S(1)} %get-tuple-element.12.refs_0_, bf16[528,128]{1,0:T(8,128)(2,1)S(1)} %collective-permute-done.1.refs_1_, ...), custom_call_target="tpu_custom_call" | custom-call | tf_op jit(solution)/shard_map/pallas_call | solution.py:278
  25.1 2.5 %collective-permute-start.6 = (bf16[544,128]{1,0:T(8,128)(2,1)S(1)}, bf16[544,128]{1,0:T(8,128)(2,1)S(1)}, u32[]{:S(2)}, u32[]{:S(2)}) collective-permute-start(bf16[544,128]{1,0:T(8,128)(2,1)S(1)} %shard_map.96.refs_0_), channel_id=1, source_target_pairs={{0,12},{4,8},{8,4},{12,0},{1,13},{5,9},{9,5},{13,1},{2,14},{6,10},... | collective-permute-start | bytes 417800 | tf_op jit(solution)/shard_map/ppermute | solution.py:258
  27.6 1.5 %collective-permute-start.4 = (bf16[544,128]{1,0:T(8,128)(2,1)S(1)}, bf16[544,128]{1,0:T(8,128)(2,1)S(1)}, u32[]{:S(2)}, u32[]{:S(2)}) collective-permute-start(bf16[544,128]{1,0:T(8,128)(2,1)S(1)} %shard_map.96.refs_0_), channel_id=1, source_target_pairs={{0,4},{4,0},{8,12},{12,8},{1,5},{5,1},{9,13},{13,9},{2,6},{6,2},{1... | collective-permute-start | bytes 417800 | tf_op jit(solution)/shard_map/ppermute | solution.py:258
  29.5 3.9 %collective-permute-done.6.refs_3_ = bf16[544,128]{1,0:T(8,128)(2,1)S(1)} collective-permute-done((bf16[544,128]{1,0:T(8,128)(2,1)S(1)}, bf16[544,128]{1,0:T(8,128)(2,1)S(1)}, u32[]{:S(2)}, u32[]{:S(2)}) %collective-permute-start.6) | collective-permute-done | bytes 139296 | tf_op jit(solution)/shard_map/ppermute | solution.py:258
  33.4 0.8 %collective-permute-done.4.refs_1_ = bf16[544,128]{1,0:T(8,128)(2,1)S(1)} collective-permute-done((bf16[544,128]{1,0:T(8,128)(2,1)S(1)}, bf16[544,128]{1,0:T(8,128)(2,1)S(1)}, u32[]{:S(2)}, u32[]{:S(2)}) %collective-permute-start.4) | collective-permute-done | bytes 139296 | tf_op jit(solution)/shard_map/ppermute | solution.py:258
  34.2 5.3 %collective-permute-done.5.refs_2_ = bf16[544,128]{1,0:T(8,128)(2,1)S(1)} collective-permute-done((bf16[544,128]{1,0:T(8,128)(2,1)S(1)}, bf16[544,128]{1,0:T(8,128)(2,1)S(1)}, u32[]{:S(2)}, u32[]{:S(2)}) %collective-permute-start.5) | collective-permute-done | bytes 139296 | tf_op jit(solution)/shard_map/ppermute | solution.py:258
  39.5 1.3 %collective-permute-done.9.refs_6_ = bf16[544,128]{1,0:T(8,128)(2,1)S(1)} collective-permute-done((bf16[544,128]{1,0:T(8,128)(2,1)S(1)}, bf16[544,128]{1,0:T(8,128)(2,1)S(1)}, u32[]{:S(2)}, u32[]{:S(2)}) %collective-permute-start.9) | collective-permute-done | bytes 139296 | tf_op jit(solution)/shard_map/ppermute | solution.py:261
  40.9 3.3 %shard_map.97 = (bf16[4,512,512]{2,1,0:T(8,128)(2,1)S(1)}, f32[4,5,512]{2,1,0:T(8,128)S(1)}, f32[4,512]{1,0:T(4,128)S(1)}, f32[4,512]{1,0:T(4,128)S(1)}) custom-call(s32[34]{0:T(128)S(1)} %pad_add_fusion.meta, bf16[544,128]{1,0:T(8,128)(2,1)S(1)} %shard_map.96.refs_0_, bf16[544,128]{1,0:T(8,128)(2,1)S(1)} %collective-permute-done.4.refs_1_, ...), custom_call_target="tpu_custom_call" | custom-call | tf_op jit(solution)/shard_map/pallas_call | solution.py:288
  44.2 3.4 %collective-permute-start.11 = (f32[1,512]{1,0:T(1,128)S(1)}, f32[1,512]{1,0:T(1,128)S(1)}, u32[]{:S(2)}, u32[]{:S(2)}) collective-permute-start(f32[1,512]{1,0:T(1,128)S(1)} %slice.50), channel_id=1, source_target_pairs={{0,2},{1,3},{4,6},{5,7},{8,10},{9,11},{12,14},{13,15},{16,18},{17,... | collective-permute-start | bytes 6152 | tf_op jit(solution)/shard_map/ppermute | solution.py:355
  47.6 1.3 %collective-permute-done.11.state_ref = f32[1,512]{1,0:T(1,128)S(1)} collective-permute-done((f32[1,512]{1,0:T(1,128)S(1)}, f32[1,512]{1,0:T(1,128)S(1)}, u32[]{:S(2)}, u32[]{:S(2)}) %collective-permute-start.11) | collective-permute-done | bytes 2080 | tf_op jit(solution)/shard_map/ppermute | solution.py:355
  48.9 2.3 %shard_map.98 = (f32[4,512]{1,0:T(4,128)S(1)}, f32[4,512]{1,0:T(4,128)S(1)}) custom-call(bf16[4,512,512]{2,1,0:T(8,128)(2,1)S(1)} %get-tuple-element.16.grams, f32[4,5,512]{2,1,0:T(8,128)S(1)} %get-tuple-element.17.vectors, f32[1,512]{1,0:T(1,128)S(1)} %collective-permute-done.11.state_ref), custom_call_target="tpu_custom_call" | custom-call | tf_op jit(solution)/shard_map/pallas_call | solution.py:305
  51.2 1.3 %collective-permute-start.12 = (f32[1,512]{1,0:T(1,128)S(1)}, f32[1,512]{1,0:T(1,128)S(1)}, u32[]{:S(2)}, u32[]{:S(2)}) collective-permute-start(f32[1,512]{1,0:T(1,128)S(1)} %fusion), channel_id=1, source_target_pairs={{2,0},{3,1},{6,4},{7,5},{10,8},{11,9},{14,12},{15,13},{18,16},{19,... | collective-permute-start | bytes 6152 | tf_op jit(solution)/shard_map/ppermute | solution.py:365
  52.6 4.2 %collective-permute-done.12 = f32[1,512]{1,0:T(1,128)S(1)} collective-permute-done((f32[1,512]{1,0:T(1,128)S(1)}, f32[1,512]{1,0:T(1,128)S(1)}, u32[]{:S(2)}, u32[]{:S(2)}) %collective-permute-start.12) | collective-permute-done | bytes 2080 | tf_op jit(solution)/shard_map/ppermute | solution.py:365
  56.7 0.7 %add_bitcast_fusion = (f32[1,1,256]{2,1,0:T(1,128)}, f32[1,1,256]{2,1,0:T(1,128)}) fusion(s32[]{:T(128)S(6)} %select_n.42, s32[]{:T(128)S(6)} %select_n.43, f32[1,512]{1,0:T(1,128)S(1)} %get-tuple-element.25, f32[1,512]{1,0:T(1,128)S(1)} %get-tuple-element.24, f32[1,512]{1,0:T(1,128)S(1)} %get-tuple-element.23, f32[1,512]{1,0:T(1,128)S(1)} %get-tuple-element.22, ...), kind=kLoop, calls=%fused_computation.22 | loop fusion | flops 1024 | bytes 11272 | tf_op jit(solution)/shard_map/reshape | solution.py:371
  (25 shorter events, 0.5 us)
Async XLA Ops:
  0.6 13.2 %copy-start.4 = (f32[1,1,512]{2,1,0:T(1,128)S(1)}, f32[1,1,512]{2,1,0:T(1,128)}, u32[]{:S(2)}) copy-start(f32[1,1,512]{2,1,0:T(1,128)} %param.12) | copy-start | bytes 6148
  0.6 13.2 %copy-start.3 = (f32[1,1,512]{2,1,0:T(1,128)S(1)}, f32[1,1,512]{2,1,0:T(1,128)}, u32[]{:S(2)}) copy-start(f32[1,1,512]{2,1,0:T(1,128)} %param.13) | copy-start | bytes 6148
  0.7 13.2 %copy-start.2 = (f32[1,1,512]{2,1,0:T(1,128)S(1)}, f32[1,1,512]{2,1,0:T(1,128)}, u32[]{:S(2)}) copy-start(f32[1,1,512]{2,1,0:T(1,128)} %param.14) | copy-start | bytes 6148
  0.7 40.2 %copy-start.1 = (f32[512]{0:T(512)S(1)}, f32[512]{0:T(512)}, u32[]{:S(2)}) copy-start(f32[512]{0:T(512)} %param.15) | copy-start | bytes 6148
  0.7 3.0 %collective-permute-start = (bf16[16,128,256]{2,1,0:T(8,128)(2,1)}, bf16[16,128,256]{2,1,0:T(8,128)(2,1)S(1)}, u32[]{:S(2)}, u32[]{:S(2)}) collective-permute-start(bf16[16,128,256]{2,1,0:T(8,128)(2,1)} %bitcast.41), channel_id=1, source_target_pairs={{0,1},{1,0},{2,3},{3,2},{4,5},{5,4},{6,7},{7,6},{8,9},{9,8},{10,11... | collective-permute-start | bytes 3145736 | tf_op jit(solution)/shard_map/ppermute | solution.py:247
  3.7 1.2 %copy-start = (bf16[1,16,128,256]{3,2,1,0:T(8,128)(2,1)S(1)}, bf16[1,16,128,256]{3,2,1,0:T(8,128)(2,1)}, u32[]{:S(2)}) copy-start(bf16[1,16,128,256]{3,2,1,0:T(8,128)(2,1)} %param.8) | copy-start | bytes 3145732
  8.2 8.9 %collective-permute-start.1 = (bf16[528,128]{1,0:T(8,128)(2,1)S(1)}, bf16[528,128]{1,0:T(8,128)(2,1)S(1)}, u32[]{:S(2)}, u32[]{:S(2)}) collective-permute-start(bf16[528,128]{1,0:T(8,128)(2,1)S(1)} %get-tuple-element.13), channel_id=1, source_target_pairs={{0,4},{4,0},{8,12},{12,8},{1,5},{5,1},{9,13},{13,9},{2,6},{6,2},{1... | collective-permute-start | bytes 405512 | tf_op jit(solution)/shard_map/ppermute | solution.py:258
  11.3 13.2 %collective-permute-start.2 = (bf16[528,128]{1,0:T(8,128)(2,1)S(1)}, bf16[528,128]{1,0:T(8,128)(2,1)S(1)}, u32[]{:S(2)}, u32[]{:S(2)}) collective-permute-start(bf16[528,128]{1,0:T(8,128)(2,1)S(1)} %get-tuple-element.14), channel_id=1, source_target_pairs={{0,8},{4,12},{8,0},{12,4},{1,9},{5,13},{9,1},{13,5},{2,10},{6,14},... | collective-permute-start | bytes 405512 | tf_op jit(solution)/shard_map/ppermute | solution.py:258
  13.8 10.6 %collective-permute-start.3 = (bf16[528,128]{1,0:T(8,128)(2,1)S(1)}, bf16[528,128]{1,0:T(8,128)(2,1)S(1)}, u32[]{:S(2)}, u32[]{:S(2)}) collective-permute-start(bf16[528,128]{1,0:T(8,128)(2,1)S(1)} %get-tuple-element.15), channel_id=1, source_target_pairs={{0,12},{4,8},{8,4},{12,0},{1,13},{5,9},{9,5},{13,1},{2,14},{6,10},... | collective-permute-start | bytes 405512 | tf_op jit(solution)/shard_map/ppermute | solution.py:258
  25.1 8.4 %collective-permute-start.6 = (bf16[544,128]{1,0:T(8,128)(2,1)S(1)}, bf16[544,128]{1,0:T(8,128)(2,1)S(1)}, u32[]{:S(2)}, u32[]{:S(2)}) collective-permute-start(bf16[544,128]{1,0:T(8,128)(2,1)S(1)} %shard_map.96.refs_0_), channel_id=1, source_target_pairs={{0,12},{4,8},{8,4},{12,0},{1,13},{5,9},{9,5},{13,1},{2,14},{6,10},... | collective-permute-start | bytes 417800 | tf_op jit(solution)/shard_map/ppermute | solution.py:258
  27.6 6.6 %collective-permute-start.4 = (bf16[544,128]{1,0:T(8,128)(2,1)S(1)}, bf16[544,128]{1,0:T(8,128)(2,1)S(1)}, u32[]{:S(2)}, u32[]{:S(2)}) collective-permute-start(bf16[544,128]{1,0:T(8,128)(2,1)S(1)} %shard_map.96.refs_0_), channel_id=1, source_target_pairs={{0,4},{4,0},{8,12},{12,8},{1,5},{5,1},{9,13},{13,9},{2,6},{6,2},{1... | collective-permute-start | bytes 417800 | tf_op jit(solution)/shard_map/ppermute | solution.py:258
  29.1 10.4 %collective-permute-start.5 = (bf16[544,128]{1,0:T(8,128)(2,1)S(1)}, bf16[544,128]{1,0:T(8,128)(2,1)S(1)}, u32[]{:S(2)}, u32[]{:S(2)}) collective-permute-start(bf16[544,128]{1,0:T(8,128)(2,1)S(1)} %shard_map.96.refs_0_), channel_id=1, source_target_pairs={{0,8},{4,12},{8,0},{12,4},{1,9},{5,13},{9,1},{13,5},{2,10},{6,14},... | collective-permute-start | bytes 417800 | tf_op jit(solution)/shard_map/ppermute | solution.py:258
  29.5 10.0 %collective-permute-start.7 = (bf16[544,128]{1,0:T(8,128)(2,1)S(1)}, bf16[544,128]{1,0:T(8,128)(2,1)S(1)}, u32[]{:S(2)}, u32[]{:S(2)}) collective-permute-start(bf16[544,128]{1,0:T(8,128)(2,1)S(1)} %shard_map.96.refs_0_), channel_id=1, source_target_pairs={{0,1},{1,0},{2,3},{3,2},{4,5},{5,4},{6,7},{7,6},{8,9},{9,8},{10,11... | collective-permute-start | bytes 417800 | tf_op jit(solution)/shard_map/ppermute | solution.py:261
  33.4 6.1 %collective-permute-start.10 = (bf16[544,128]{1,0:T(8,128)(2,1)S(1)}, bf16[544,128]{1,0:T(8,128)(2,1)S(1)}, u32[]{:S(2)}, u32[]{:S(2)}) collective-permute-start(bf16[544,128]{1,0:T(8,128)(2,1)S(1)} %collective-permute-done.6.refs_3_), channel_id=1, source_target_pairs={{0,1},{1,0},{2,3},{3,2},{4,5},{5,4},{6,7},{7,6},{8,9},{9,8},{10,11... | collective-permute-start | bytes 417800 | tf_op jit(solution)/shard_map/ppermute | solution.py:261
  34.2 5.3 %collective-permute-start.8 = (bf16[544,128]{1,0:T(8,128)(2,1)S(1)}, bf16[544,128]{1,0:T(8,128)(2,1)S(1)}, u32[]{:S(2)}, u32[]{:S(2)}) collective-permute-start(bf16[544,128]{1,0:T(8,128)(2,1)S(1)} %collective-permute-done.4.refs_1_), channel_id=1, source_target_pairs={{0,1},{1,0},{2,3},{3,2},{4,5},{5,4},{6,7},{7,6},{8,9},{9,8},{10,11... | collective-permute-start | bytes 417800 | tf_op jit(solution)/shard_map/ppermute | solution.py:261
  39.5 1.4 %collective-permute-start.9 = (bf16[544,128]{1,0:T(8,128)(2,1)S(1)}, bf16[544,128]{1,0:T(8,128)(2,1)S(1)}, u32[]{:S(2)}, u32[]{:S(2)}) collective-permute-start(bf16[544,128]{1,0:T(8,128)(2,1)S(1)} %collective-permute-done.5.refs_2_), channel_id=1, source_target_pairs={{0,1},{1,0},{2,3},{3,2},{4,5},{5,4},{6,7},{7,6},{8,9},{9,8},{10,11... | collective-permute-start | bytes 417800 | tf_op jit(solution)/shard_map/ppermute | solution.py:261
  44.2 4.7 %collective-permute-start.11 = (f32[1,512]{1,0:T(1,128)S(1)}, f32[1,512]{1,0:T(1,128)S(1)}, u32[]{:S(2)}, u32[]{:S(2)}) collective-permute-start(f32[1,512]{1,0:T(1,128)S(1)} %slice.50), channel_id=1, source_target_pairs={{0,2},{1,3},{4,6},{5,7},{8,10},{9,11},{12,14},{13,15},{16,18},{17,... | collective-permute-start | bytes 6152 | tf_op jit(solution)/shard_map/ppermute | solution.py:355
  51.2 5.5 %collective-permute-start.12 = (f32[1,512]{1,0:T(1,128)S(1)}, f32[1,512]{1,0:T(1,128)S(1)}, u32[]{:S(2)}, u32[]{:S(2)}) collective-permute-start(f32[1,512]{1,0:T(1,128)S(1)} %fusion), channel_id=1, source_target_pairs={{2,0},{3,1},{6,4},{7,5},{10,8},{11,9},{14,12},{15,13},{18,16},{19,... | collective-permute-start | bytes 6152 | tf_op jit(solution)/shard_map/ppermute | solution.py:365

commit v5 on v4

--- a/solution.py
+++ b/solution.py
@@ -102,74 +102,95 @@
     return high, middle, values - high - middle
 
 
-def gram_kernel(meta, y_ref, own_ref, other_ref, *refs):
-    outs, acc, vec, side = refs[:-3], refs[-3], refs[-2], refs[-1]
-    tile_num, row_num, half = own_ref.shape
-    core, position = meta[2 * tile_num], meta[2 * tile_num + 1]
+OVER_ROWS = (((0,), (0,)), ((), ()))
+
+
+def valid_rows(index, counts, own_ref):
+    rows = own_ref[index].astype(jnp.float32)
+    row = lax.broadcasted_iota(jnp.int32, rows.shape, 0)
+    return jnp.where(row < counts[0, index], rows, 0.0).astype(jnp.bfloat16)
+
+
+def half_kernel(blocks, counts, y_ref, own_ref, out_ref, acc, vec, side, readings):
+    tile_num = own_ref.shape[0]
+    readings[...] = y_ref[...].astype(jnp.float32)
     acc[...] = jnp.zeros_like(acc)
     vec[...] = jnp.zeros_like(vec)
     side[...] = jnp.zeros_like(side)
-    row = lax.broadcasted_iota(jnp.int32, (row_num, half), 0)
-    over_rows = (((0,), (0,)), ((), ()))
 
     def tile(index, carry):
-        block = meta[index]
-        live = meta[tile_num + index]
-        rows = own_ref[index].astype(jnp.float32)
-        rows = jnp.where(row < live, rows, 0.0).astype(jnp.bfloat16)
-        readings = jnp.broadcast_to(y_ref[pl.ds(index, 1), :], (8, row_num)).astype(jnp.bfloat16)
-        square = lax.dot_general(rows, rows, over_rows, preferred_element_type=jnp.float32)
+        block = blocks[index, 0]
+        rows = valid_rows(index, counts, own_ref)
+        values = jnp.broadcast_to(readings[pl.ds(index, 1), :], (8, rows.shape[0]))
+        square = lax.dot_general(rows, rows, OVER_ROWS, preferred_element_type=jnp.float32)
         acc[block, 0:LANES] += square[:LANES, :LANES]
         acc[block, LANES : 2 * LANES] += square[:LANES, LANES:]
         acc[block, 2 * LANES : 3 * LANES] += square[LANES:, LANES:]
-        for piece in range(2):
-            at = pl.multiple_of((piece ^ core) * LANES, LANES)
-            acc[block, (3 + piece) * LANES : (4 + piece) * LANES] += lax.dot_general(
-                rows[:, piece * LANES : (piece + 1) * LANES],
-                other_ref[index, :, pl.ds(at, LANES)],
-                over_rows,
-                preferred_element_type=jnp.float32,
-            )
-        vec[block] += jnp.dot(readings, rows, preferred_element_type=jnp.float32)
+        vec[block] += jnp.dot(
+            values.astype(jnp.bfloat16), rows, preferred_element_type=jnp.float32
+        )
         return carry
 
     lax.fori_loop(0, tile_num, tile, 0, unroll=2)
     line = lax.broadcasted_iota(jnp.int32, (LANES, LANES), 0)
     column = lax.broadcasted_iota(jnp.int32, (LANES, LANES), 1)
-    for flip, out_ref in enumerate(outs):
-        block = position ^ flip
-
-        def take(piece):
-            return acc[block, piece * LANES : (piece + 1) * LANES]
-
-        packed = jnp.where(line < column, take(0), jnp.where(line > column, take(2), 0.0))
-        out_ref[0:LANES] = packed.astype(jnp.bfloat16)
-        for at, piece in ((1, 1), (2, 3), (3, 4)):
-            out_ref[at * LANES : (at + 1) * LANES] = take(piece).astype(jnp.bfloat16)
+    for block in range(out_ref.shape[0]):
+        first, between, second = (acc[block, at * LANES : (at + 1) * LANES] for at in range(3))
+        packed = jnp.where(line < column, first, jnp.where(line > column, second, 0.0))
+        out_ref[block, 0:LANES] = packed.astype(jnp.bfloat16)
+        out_ref[block, LANES : 2 * LANES] = between.astype(jnp.bfloat16)
         values = [vec[block, 0:1, :LANES], vec[block, 0:1, LANES:]]
-        for piece in (0, 2):
-            values.append(
-                jnp.sum(jnp.where(line == column, take(piece), 0.0), axis=0, keepdims=True)
-            )
+        for square in (first, second):
+            values.append(jnp.sum(jnp.where(line == column, square, 0.0), axis=0, keepdims=True))
         for at, value in enumerate(values):
             for which, part in enumerate(pieces_of(value)):
                 side[which * 4 + at : which * 4 + at + 1, :] = part
-        out_ref[4 * LANES :] = side[...].astype(jnp.bfloat16)
-
-
-def sum_kernel(meta, params_ref, *refs):
+        out_ref[block, 2 * LANES :] = side[...].astype(jnp.bfloat16)
+
+
+def cross_kernel(flips, blocks, counts, own_ref, other_ref, half_ref, *refs):
+    outs, acc = refs[:-1], refs[-1]
+    core, position = lax.axis_index("state"), lax.axis_index("tm")
+    acc[...] = jnp.zeros_like(acc)
+
+    def tile(index, carry):
+        for slot, flip in enumerate(flips):
+
+            @pl.when(blocks[index, 0] == position ^ flip)
+            def _():
+                rows = valid_rows(index, counts, own_ref)
+                for piece in range(2):
+                    at = pl.multiple_of((piece ^ core) * LANES, LANES)
+                    acc[slot, piece * LANES : (piece + 1) * LANES] += lax.dot_general(
+                        rows[:, piece * LANES : (piece + 1) * LANES],
+                        other_ref[index, :, pl.ds(at, LANES)],
+                        OVER_ROWS,
+                        preferred_element_type=jnp.float32,
+                    )
+
+        return carry
+
+    lax.fori_loop(0, own_ref.shape[0], tile, 0)
+    for slot, flip in enumerate(flips):
+        block = position ^ flip
+        outs[slot][: 2 * LANES] = half_ref[block, : 2 * LANES]
+        outs[slot][2 * LANES : 4 * LANES] = acc[slot].astype(jnp.bfloat16)
+        outs[slot][4 * LANES :] = half_ref[block, 2 * LANES :]
+
+
+def sum_kernel(kappa_ref, rate_ref, gain_ref, *refs):
     parts, out_ref, side = refs[:-2], refs[-2], refs[-1]
-    core = meta[meta.shape[0] - 2]
+    core = lax.axis_index("state")
     total = parts[0][...].astype(jnp.float32)
     for part in parts[1:]:
         total = total + part[...].astype(jnp.float32)
     out_ref[: 4 * LANES] = total[: 4 * LANES].astype(jnp.bfloat16)
     below = total[4 * LANES :]
     values = [below[at : at + 1] + below[at + 4 : at + 5] + below[at + 8 : at + 9] for at in range(4)]
-    for which in range(3):
+    for coefficient in (kappa_ref, rate_ref, gain_ref):
         for piece in range(2):
             at = pl.multiple_of((2 * core + piece) * LANES, LANES)
-            values.append(params_ref[which : which + 1, pl.ds(at, LANES)])
+            values.append(coefficient[:, pl.ds(at, LANES)])
     side[...] = jnp.zeros_like(side)
     for at, value in enumerate(values):
         for which, part in enumerate(pieces_of(value)):
@@ -196,10 +217,10 @@
         innovations_ref[block : block + 1, :] = innovation
 
 
-def assemble_kernel(number, meta, *refs):
+def assemble_kernel(number, *refs):
     own, other, rest = refs[:number], refs[number : 2 * number], refs[2 * number :]
     state_ref, grams, vectors, states_ref, innovations_ref = rest
-    core, position = meta[meta.shape[0] - 2], meta[meta.shape[0] - 1]
+    core, position = lax.axis_index("state"), lax.axis_index("tm")
     half = 2 * LANES
     line = lax.broadcasted_iota(jnp.int32, (LANES, LANES), 0)
     column = lax.broadcasted_iota(jnp.int32, (LANES, LANES), 1)
@@ -245,44 +266,58 @@
     width = kappa.shape[2]
     own = rows_h[0]
     other = lax.ppermute(own, "state", [(i, (i + 1) % state_size) for i in range(state_size)])
-    readings = rows_y[0].astype(jnp.float32)
     state = start_state.reshape(1, width)
-    meta = jnp.concatenate(
-        [tile_block[0, :, 0], tile_count[0], jnp.stack([core, tm_index]).astype(jnp.int32)]
-    )
-    params = jnp.concatenate([kappa[0], rate[0], smooth_gain[0]], axis=0)
     direct = tm_size <= DIRECT_TM and tm_size & (tm_size - 1) == 0
     states_shape = jax.ShapeDtypeStruct((tm_size, width), jnp.float32)
 
     def flip_over(array, flip):
         return lax.ppermute(array, "tm", [(i, i ^ flip) for i in range(tm_size)])
 
+    def ring(array, step):
+        return lax.ppermute(array, "grp", [(i, (i + step) % grp_size) for i in range(grp_size)])
+
     def across(array):
         return lax.ppermute(array, "state", [(i, (i + 1) % state_size) for i in range(state_size)])
 
     if direct:
-        sent = jax.ShapeDtypeStruct((4 * LANES + 16, LANES), jnp.bfloat16)
-        pieces = pl.pallas_call(
-            gram_kernel,
-            out_shape=[sent] * tm_size,
-            in_specs=[SMEM] + [VMEM] * 3,
-            out_specs=[VMEM] * tm_size,
+        blocks = tile_block[0]
+        part_of = pl.pallas_call(
+            half_kernel,
+            out_shape=jax.ShapeDtypeStruct((tm_size, 2 * LANES + 16, LANES), jnp.bfloat16),
+            in_specs=[SMEM, SMEM, VMEM, VMEM],
+            out_specs=VMEM,
             scratch_shapes=[
-                pltpu.VMEM((tm_size, 5 * LANES, LANES), jnp.float32),
+                pltpu.VMEM((tm_size, 3 * LANES, LANES), jnp.float32),
                 pltpu.VMEM((tm_size, 8, half), jnp.float32),
                 pltpu.VMEM((16, LANES), jnp.float32),
+                pltpu.VMEM(rows_y.shape[1:], jnp.float32),
             ],
             compiler_params=KERNEL,
-        )(meta, readings, own, other)
-        parts = [pieces[0]] + [flip_over(pieces[flip], flip) for flip in range(1, tm_size)]
+        )(blocks, tile_count, rows_y[0], own)
+
+        def cross(flips):
+            return pl.pallas_call(
+                functools.partial(cross_kernel, flips),
+                out_shape=[jax.ShapeDtypeStruct((4 * LANES + 16, LANES), jnp.bfloat16)] * len(flips),
+                in_specs=[SMEM, SMEM] + [VMEM] * 3,
+                out_specs=[VMEM] * len(flips),
+                scratch_shapes=[pltpu.VMEM((len(flips), 2 * LANES, LANES), jnp.float32)],
+                compiler_params=KERNEL,
+            )(blocks, tile_count, own, other, part_of)
+
+        order = list(reversed(range(tm_size)))
+        parts = []
+        for flips in (order[: tm_size // 2], order[tm_size // 2 :]):
+            for flip, piece in zip(flips, cross(flips)):
+                parts.append(piece if flip == 0 else flip_over(piece, flip))
         own_sum = pl.pallas_call(
             sum_kernel,
             out_shape=jax.ShapeDtypeStruct((4 * LANES + 32, LANES), jnp.bfloat16),
-            in_specs=[SMEM] + [VMEM] * (tm_size + 1),
+            in_specs=[VMEM] * (tm_size + 3),
             out_specs=VMEM,
             scratch_shapes=[pltpu.VMEM((32, LANES), jnp.float32)],
             compiler_params=KERNEL,
-        )(meta, params, *parts)
+        )(kappa[0], rate[0], smooth_gain[0], *parts)
         own_sums = [own_sum] + [flip_over(own_sum, flip) for flip in range(1, tm_size)]
         other_sums = [across(values) for values in own_sums]
         grams, vectors, new_states, new_innovations = pl.pallas_call(
@@ -293,10 +328,10 @@
                 states_shape,
                 states_shape,
             ),
-            in_specs=[SMEM] + [VMEM] * (2 * tm_size + 1),
+            in_specs=[VMEM] * (2 * tm_size + 1),
             out_specs=[VMEM] * 4,
             compiler_params=KERNEL,
-        )(meta, *own_sums, *other_sums, state)
+        )(*own_sums, *other_sums, state)
         gains = vectors[:, 4]
 
         def run_group(state, group):
@@ -310,6 +345,11 @@
                 compiler_params=KERNEL,
             )(grams, vectors, state)
     else:
+        readings = rows_y[0].astype(jnp.float32)
+        meta = jnp.concatenate(
+            [tile_block[0, :, 0], tile_count[0], jnp.stack([core, tm_index]).astype(jnp.int32)]
+        )
+        params = jnp.concatenate([kappa[0], rate[0], smooth_gain[0]], axis=0)
         gathered = lax.all_gather(params, "tm")
         gains = gathered[:, 2]
         vector = jax.ShapeDtypeStruct((1, width), jnp.float32)
@@ -352,7 +392,7 @@
         states = jnp.where(mine, new_states, states)
         innovations = jnp.where(mine, new_innovations, innovations)
         if group < grp_size - 1:
-            state = lax.ppermute(new_states[-1:], "grp", [(group, group + 1)])
+            state = ring(new_states[-1:], 1)
 
     residual = jnp.zeros((1, width), jnp.float32)
     residuals = [None] * tm_size
@@ -362,7 +402,7 @@
             residuals[block] = running
             running = gains[block][None] * (running + innovations[block][None])
         if group > 0:
-            arrived = lax.ppermute(running, "grp", [(group, group - 1)])
+            arrived = ring(running, -1)
             residual = jnp.where(grp_index == group - 1, arrived, residual)
     smoothed = states + jnp.concatenate(residuals, 0)
 

time: 57.6 us -> 60 us (1.042)
  waiting for transfers between devices: 28.4 us -> 24.3 us
  Pallas kernels: 9.58 us -> 13.3 us
  local copies, waits for them, and re-layouts: 1.25 us -> 4.54 us
  other arithmetic: 2.17 us -> 0.72 us
    pallas_call x1 -> x3, Pallas kernels: 3.33 us -> 8.14 us  [the longest x2 5.04 us: cross(): pl.pallas_call(functools.partial(cross_kernel, flips), out_shape=[jax.Sha...]
    unnamed x10 -> x16, local copies, waits for them, and re-layouts: 1.24 us -> 3.8 us
    ppermute x2, waiting for transfers between devices: 5.45 us -> 3.13 us  [ring(): lax.ppermute(array, 'grp', [(i, (i + step) % grp_size) for i in range(grp...]
    ppermute x1, waiting for transfers between devices: 1.06 us -> 0.01 us  [shards(): lax.ppermute(own, 'state', [(i, (i + 1) % state_size) for i in range(stat...]
    concatenate x2 -> x0, other arithmetic: 0.76 us -> none  [the longest x1 0.75 us: shards(): jnp.concatenate([tile_block[0, :, 0], tile_count[0], jnp.stack([core, tm_...]
    squeeze x0 -> x1, local copies, waits for them, and re-layouts: none -> 0.73 us  [shards(): blocks = tile_block[0]]
    convert_element_type x1 -> x0, other arithmetic: 0.69 us -> none  [shards(): readings = rows_y[0].astype(jnp.float32)]
    ppermute x6, starting transfers between devices: 10.1 us -> 10.7 us  [flip_over(): return lax.ppermute(array, 'tm', [(i, i ^ flip) for i in range(tm_size)])]
  transfers between devices with their start and end apart: 13 -> 13, of which waited for: 9 -> 9; matrix products, arithmetic and copies ran while one was open for 3% -> 1% of each run, Pallas kernels for 0% -> 12%
where the time goes in v5:
time: 60 us; the launch traced here: 59.3 us
  waiting for transfers between devices  24.3 us (40%)
  starting transfers between devices  15.6 us (26%)
  Pallas kernels  13.3 us (22%)
  local copies, waits for them, and re-layouts  4.54 us (8%)
  between operations  0.73 us (1%)
  other arithmetic  0.72 us (1%)
    ppermute x6, waiting for transfers between devices, flip_over(): return lax.ppermute(array, 'tm', [(i, i ^ flip) for i in range(tm_size)])  20 us
    ppermute x6, starting transfers between devices, flip_over(): return lax.ppermute(array, 'tm', [(i, i ^ flip) for i in range(tm_size)])  10.7 us
    pallas_call x2, Pallas kernels, cross(): pl.pallas_call(functools.partial(cross_kernel, flips), out_shape=[jax.Sha...  5.04 us
    ppermute x2, starting transfers between devices, ring(): lax.ppermute(array, 'grp', [(i, (i + step) % grp_size) for i in range(grp...  4.16 us
    unnamed x16, local copies, waits for them, and re-layouts  3.8 us
    ppermute x2, waiting for transfers between devices, ring(): lax.ppermute(array, 'grp', [(i, (i + step) % grp_size) for i in range(grp...  3.13 us
    pallas_call x1, Pallas kernels, shards(): pl.pallas_call(half_kernel, out_shape=jax.ShapeDtypeStruct((tm_size, 2 *...  3.1 us
    pallas_call x1, Pallas kernels, shards(): pl.pallas_call(functools.partial(assemble_kernel, tm_size), out_shape=(ja...  2.78 us
  transfers between devices with their start and end apart: 13, of which 9 were waited for; matrix products, arithmetic and copies ran while one was open for 1% of the time, Pallas kernels for 12%

profile of v5, /device:TPU:0, one launch (start us, length us, event | category | flops | bytes accessed | tf_op | source)
XLA Modules:
  0.0 59.3 jit_solution(2680801514950887894)
XLA Ops:
  1.1 0.7 %copy.11.blocks = s32[16,1]{1,0:T(8,128)S(1)} copy(s32[16,1]{0,1:T(1,128)} %bitcast.45) | data formatting | bytes 128 | tf_op jit(solution)/shard_map/squeeze | solution.py:283
  1.9 1.2 %copy-done = bf16[1,16,128,256]{3,2,1,0:T(8,128)(2,1)S(1)} copy-done((bf16[1,16,128,256]{3,2,1,0:T(8,128)(2,1)S(1)}, bf16[1,16,128,256]{3,2,1,0:T(8,128)(2,1)}, u32[]{:S(2)}) %copy-start) | copy-done | bytes 1048600
  3.1 0.7 %copy-done.2 = s32[1,16]{1,0:T(1,128)S(1)} copy-done((s32[1,16]{1,0:T(1,128)S(1)}, s32[1,16]{1,0:T(1,128)}, u32[]{:S(2)}) %copy-start.2) | copy-done | bytes 88
  3.8 0.7 %copy-done.3 = bf16[1,16,128]{2,1,0:T(8,128)(2,1)S(1)} copy-done((bf16[1,16,128]{2,1,0:T(8,128)(2,1)S(1)}, bf16[1,16,128]{2,1,0:T(8,128)(2,1)}, u32[]{:S(2)}) %copy-start.3) | copy-done | bytes 4120
  4.4 3.1 %shard_map.95.half_ref = bf16[4,272,128]{2,1,0:T(8,128)(2,1)S(1)} custom-call(s32[16,1]{1,0:T(8,128)S(1)} %copy.11.blocks, s32[1,16]{1,0:T(1,128)S(1)} %copy-done.2, bf16[16,128]{1,0:T(8,128)(2,1)S(1)} %bitcast.40, bf16[16,128,256]{2,1,0:T(8,128)(2,1)S(1)} %bitcast.37), custom_call_target="tpu_custom_call" | custom-call | tf_op jit(solution)/shard_map/pallas_call | solution.py:284
  7.6 1.2 %copy-done.1 = bf16[1,16,128,256]{3,2,1,0:T(8,128)(2,1)S(1)} copy-done((bf16[1,16,128,256]{3,2,1,0:T(8,128)(2,1)S(1)}, bf16[1,16,128,256]{3,2,1,0:T(8,128)(2,1)}, u32[]{:S(2)}) %copy-start.1) | copy-done | bytes 1048600
  8.8 1.1 %shard_map.97 = (bf16[528,128]{1,0:T(8,128)(2,1)S(1)}, bf16[528,128]{1,0:T(8,128)(2,1)S(1)}) custom-call(s32[16,1]{1,0:T(8,128)S(1)} %copy.11.blocks, s32[1,16]{1,0:T(1,128)S(1)} %copy-done.2, bf16[16,128,256]{2,1,0:T(8,128)(2,1)S(1)} %bitcast.38, bf16[16,128,256]{2,1,0:T(8,128)(2,1)S(1)} %collective-permute-done.other_ref, ...), custom_call_target="tpu_custom_call" | custom-call | tf_op jit(solution)/shard_map/pallas_call | solution.py:299
  9.9 3.7 %collective-permute-start.3 = (bf16[528,128]{1,0:T(8,128)(2,1)S(1)}, bf16[528,128]{1,0:T(8,128)(2,1)S(1)}, u32[]{:S(2)}, u32[]{:S(2)}) collective-permute-start(bf16[528,128]{1,0:T(8,128)(2,1)S(1)} %get-tuple-element.14), channel_id=1, source_target_pairs={{0,4},{4,0},{8,12},{12,8},{1,5},{5,1},{9,13},{13,9},{2,6},{6,2},{1... | collective-permute-start | bytes 405512 | tf_op jit(solution)/shard_map/ppermute | solution.py:274
  13.6 4.0 %shard_map.96 = (bf16[528,128]{1,0:T(8,128)(2,1)S(1)}, bf16[528,128]{1,0:T(8,128)(2,1)S(1)}) custom-call(s32[16,1]{1,0:T(8,128)S(1)} %copy.11.blocks, s32[1,16]{1,0:T(1,128)S(1)} %copy-done.2, bf16[16,128,256]{2,1,0:T(8,128)(2,1)S(1)} %bitcast.39, bf16[16,128,256]{2,1,0:T(8,128)(2,1)S(1)} %collective-permute-done.other_ref, ...), custom_call_target="tpu_custom_call" | custom-call | tf_op jit(solution)/shard_map/pallas_call | solution.py:299
  17.6 2.5 %collective-permute-start.1 = (bf16[528,128]{1,0:T(8,128)(2,1)S(1)}, bf16[528,128]{1,0:T(8,128)(2,1)S(1)}, u32[]{:S(2)}, u32[]{:S(2)}) collective-permute-start(bf16[528,128]{1,0:T(8,128)(2,1)S(1)} %get-tuple-element.12), channel_id=1, source_target_pairs={{0,12},{4,8},{8,4},{12,0},{1,13},{5,9},{9,5},{13,1},{2,14},{6,10},... | collective-permute-start | bytes 405512 | tf_op jit(solution)/shard_map/ppermute | solution.py:274
  20.1 5.8 %collective-permute-done.1.refs_0_ = bf16[528,128]{1,0:T(8,128)(2,1)S(1)} collective-permute-done((bf16[528,128]{1,0:T(8,128)(2,1)S(1)}, bf16[528,128]{1,0:T(8,128)(2,1)S(1)}, u32[]{:S(2)}, u32[]{:S(2)}) %collective-permute-start.1) | collective-permute-done | bytes 135200 | tf_op jit(solution)/shard_map/ppermute | solution.py:274
  26.0 5.0 %collective-permute-done.2.refs_1_ = bf16[528,128]{1,0:T(8,128)(2,1)S(1)} collective-permute-done((bf16[528,128]{1,0:T(8,128)(2,1)S(1)}, bf16[528,128]{1,0:T(8,128)(2,1)S(1)}, u32[]{:S(2)}, u32[]{:S(2)}) %collective-permute-start.2) | collective-permute-done | bytes 135200 | tf_op jit(solution)/shard_map/ppermute | solution.py:274
  31.1 2.5 %collective-permute-start.6 = (bf16[544,128]{1,0:T(8,128)(2,1)S(1)}, bf16[544,128]{1,0:T(8,128)(2,1)S(1)}, u32[]{:S(2)}, u32[]{:S(2)}) collective-permute-start(bf16[544,128]{1,0:T(8,128)(2,1)S(1)} %shard_map.98.refs_0_), channel_id=1, source_target_pairs={{0,12},{4,8},{8,4},{12,0},{1,13},{5,9},{9,5},{13,1},{2,14},{6,10},... | collective-permute-start | bytes 417800 | tf_op jit(solution)/shard_map/ppermute | solution.py:274
  33.6 1.9 %collective-permute-start.5 = (bf16[544,128]{1,0:T(8,128)(2,1)S(1)}, bf16[544,128]{1,0:T(8,128)(2,1)S(1)}, u32[]{:S(2)}, u32[]{:S(2)}) collective-permute-start(bf16[544,128]{1,0:T(8,128)(2,1)S(1)} %shard_map.98.refs_0_), channel_id=1, source_target_pairs={{0,8},{4,12},{8,0},{12,4},{1,9},{5,13},{9,1},{13,5},{2,10},{6,14},... | collective-permute-start | bytes 417800 | tf_op jit(solution)/shard_map/ppermute | solution.py:274
  35.5 4.0 %collective-permute-done.6.refs_3_ = bf16[544,128]{1,0:T(8,128)(2,1)S(1)} collective-permute-done((bf16[544,128]{1,0:T(8,128)(2,1)S(1)}, bf16[544,128]{1,0:T(8,128)(2,1)S(1)}, u32[]{:S(2)}, u32[]{:S(2)}) %collective-permute-start.6) | collective-permute-done | bytes 139296 | tf_op jit(solution)/shard_map/ppermute | solution.py:274
  39.6 4.9 %collective-permute-done.4.refs_1_ = bf16[544,128]{1,0:T(8,128)(2,1)S(1)} collective-permute-done((bf16[544,128]{1,0:T(8,128)(2,1)S(1)}, bf16[544,128]{1,0:T(8,128)(2,1)S(1)}, u32[]{:S(2)}, u32[]{:S(2)}) %collective-permute-start.4) | collective-permute-done | bytes 139296 | tf_op jit(solution)/shard_map/ppermute | solution.py:274
  45.0 0.8 %collective-permute-done.8.refs_5_ = bf16[544,128]{1,0:T(8,128)(2,1)S(1)} collective-permute-done((bf16[544,128]{1,0:T(8,128)(2,1)S(1)}, bf16[544,128]{1,0:T(8,128)(2,1)S(1)}, u32[]{:S(2)}, u32[]{:S(2)}) %collective-permute-start.8) | collective-permute-done | bytes 139296 | tf_op jit(solution)/shard_map/ppermute | solution.py:280
  46.2 2.8 %shard_map.99 = (bf16[4,512,512]{2,1,0:T(8,128)(2,1)S(1)}, f32[4,5,512]{2,1,0:T(8,128)S(1)}, f32[4,512]{1,0:T(4,128)S(1)}, f32[4,512]{1,0:T(4,128)S(1)}) custom-call(bf16[544,128]{1,0:T(8,128)(2,1)S(1)} %shard_map.98.refs_0_, bf16[544,128]{1,0:T(8,128)(2,1)S(1)} %collective-permute-done.4.refs_1_, bf16[544,128]{1,0:T(8,128)(2,1)S(1)} %collective-permute-done.5.refs_2_, ...), custom_call_target="tpu_custom_call" | custom-call | tf_op jit(solution)/shard_map/pallas_call | solution.py:323
  48.9 2.1 %collective-permute-start.11 = (f32[1,512]{1,0:T(1,128)S(1)}, f32[1,512]{1,0:T(1,128)S(1)}, u32[]{:S(2)}, u32[]{:S(2)}) collective-permute-start(f32[1,512]{1,0:T(1,128)S(1)} %slice.50), channel_id=1, source_target_pairs={{0,2},{2,0},{1,3},{3,1},{4,6},{6,4},{5,7},{7,5},{8,10},{10,8},{9,1... | collective-permute-start | bytes 6152 | tf_op jit(solution)/shard_map/ppermute | solution.py:277
  51.0 1.6 %collective-permute-done.11.state_ref = f32[1,512]{1,0:T(1,128)S(1)} collective-permute-done((f32[1,512]{1,0:T(1,128)S(1)}, f32[1,512]{1,0:T(1,128)S(1)}, u32[]{:S(2)}, u32[]{:S(2)}) %collective-permute-start.11) | collective-permute-done | bytes 2080 | tf_op jit(solution)/shard_map/ppermute | solution.py:277
  52.6 2.3 %shard_map.100 = (f32[4,512]{1,0:T(4,128)S(1)}, f32[4,512]{1,0:T(4,128)S(1)}) custom-call(bf16[4,512,512]{2,1,0:T(8,128)(2,1)S(1)} %get-tuple-element.16.grams, f32[4,5,512]{2,1,0:T(8,128)S(1)} %get-tuple-element.17.vectors, f32[1,512]{1,0:T(1,128)S(1)} %collective-permute-done.11.state_ref), custom_call_target="tpu_custom_call" | custom-call | tf_op jit(solution)/shard_map/pallas_call | solution.py:340
  54.9 2.1 %collective-permute-start.12 = (f32[1,512]{1,0:T(1,128)S(1)}, f32[1,512]{1,0:T(1,128)S(1)}, u32[]{:S(2)}, u32[]{:S(2)}) collective-permute-start(f32[1,512]{1,0:T(1,128)S(1)} %fusion), channel_id=1, source_target_pairs={{0,2},{2,0},{1,3},{3,1},{4,6},{6,4},{5,7},{7,5},{8,10},{10,8},{9,1... | collective-permute-start | bytes 6152 | tf_op jit(solution)/shard_map/ppermute | solution.py:277
  57.0 1.6 %collective-permute-done.12 = f32[1,512]{1,0:T(1,128)S(1)} collective-permute-done((f32[1,512]{1,0:T(1,128)S(1)}, f32[1,512]{1,0:T(1,128)S(1)}, u32[]{:S(2)}, u32[]{:S(2)}) %collective-permute-start.12) | collective-permute-done | bytes 2080 | tf_op jit(solution)/shard_map/ppermute | solution.py:277
  58.6 0.7 %add_bitcast_fusion = (f32[1,1,256]{2,1,0:T(1,128)}, f32[1,1,256]{2,1,0:T(1,128)}) fusion(s32[]{:T(128)S(6)} %select_n.42, s32[]{:T(128)S(6)} %select_n.43, f32[1,512]{1,0:T(1,128)S(1)} %get-tuple-element.25, f32[1,512]{1,0:T(1,128)S(1)} %get-tuple-element.24, f32[1,512]{1,0:T(1,128)S(1)} %get-tuple-element.23, f32[1,512]{1,0:T(1,128)S(1)} %get-tuple-element.22, ...), kind=kLoop, calls=%fused_computation.20 | loop fusion | flops 1024 | bytes 11272 | tf_op jit(solution)/shard_map/reshape | solution.py:411
  (31 shorter events, 1.6 us)
Async XLA Ops:
  0.6 6.9 %collective-permute-start = (bf16[16,128,256]{2,1,0:T(8,128)(2,1)}, bf16[16,128,256]{2,1,0:T(8,128)(2,1)S(1)}, u32[]{:S(2)}, u32[]{:S(2)}) collective-permute-start(bf16[16,128,256]{2,1,0:T(8,128)(2,1)} %bitcast.36), channel_id=1, source_target_pairs={{0,1},{1,0},{2,3},{3,2},{4,5},{5,4},{6,7},{7,6},{8,9},{9,8},{10,11... | collective-permute-start | bytes 3145736 | tf_op jit(solution)/shard_map/ppermute | solution.py:268
  1.9 1.2 %copy-start = (bf16[1,16,128,256]{3,2,1,0:T(8,128)(2,1)S(1)}, bf16[1,16,128,256]{3,2,1,0:T(8,128)(2,1)}, u32[]{:S(2)}) copy-start(bf16[1,16,128,256]{3,2,1,0:T(8,128)(2,1)} %param.8) | copy-start | bytes 3145732
  3.1 0.7 %copy-start.2 = (s32[1,16]{1,0:T(1,128)S(1)}, s32[1,16]{1,0:T(1,128)}, u32[]{:S(2)}) copy-start(s32[1,16]{1,0:T(1,128)} %counts.5) | copy-start | bytes 196
  3.8 0.7 %copy-start.3 = (bf16[1,16,128]{2,1,0:T(8,128)(2,1)S(1)}, bf16[1,16,128]{2,1,0:T(8,128)(2,1)}, u32[]{:S(2)}) copy-start(bf16[1,16,128]{2,1,0:T(8,128)(2,1)} %param.9) | copy-start | bytes 12292
  7.6 1.2 %copy-start.1 = (bf16[1,16,128,256]{3,2,1,0:T(8,128)(2,1)S(1)}, bf16[1,16,128,256]{3,2,1,0:T(8,128)(2,1)}, u32[]{:S(2)}) copy-start(bf16[1,16,128,256]{3,2,1,0:T(8,128)(2,1)} %param.8) | copy-start | bytes 3145732
  8.8 22.2 %copy-start.4 = (f32[1,1,512]{2,1,0:T(1,128)S(1)}, f32[1,1,512]{2,1,0:T(1,128)}, u32[]{:S(2)}) copy-start(f32[1,1,512]{2,1,0:T(1,128)} %param.12) | copy-start | bytes 6148
  8.8 22.2 %copy-start.5 = (f32[1,1,512]{2,1,0:T(1,128)S(1)}, f32[1,1,512]{2,1,0:T(1,128)}, u32[]{:S(2)}) copy-start(f32[1,1,512]{2,1,0:T(1,128)} %param.13) | copy-start | bytes 6148
  8.8 22.2 %copy-start.6 = (f32[1,1,512]{2,1,0:T(1,128)S(1)}, f32[1,1,512]{2,1,0:T(1,128)}, u32[]{:S(2)}) copy-start(f32[1,1,512]{2,1,0:T(1,128)} %param.14) | copy-start | bytes 6148
  9.9 36.3 %copy-start.7 = (f32[512]{0:T(512)S(1)}, f32[512]{0:T(512)}, u32[]{:S(2)}) copy-start(f32[512]{0:T(512)} %param.15) | copy-start | bytes 6148
  9.9 10.3 %collective-permute-start.3 = (bf16[528,128]{1,0:T(8,128)(2,1)S(1)}, bf16[528,128]{1,0:T(8,128)(2,1)S(1)}, u32[]{:S(2)}, u32[]{:S(2)}) collective-permute-start(bf16[528,128]{1,0:T(8,128)(2,1)S(1)} %get-tuple-element.14), channel_id=1, source_target_pairs={{0,4},{4,0},{8,12},{12,8},{1,5},{5,1},{9,13},{13,9},{2,6},{6,2},{1... | collective-permute-start | bytes 405512 | tf_op jit(solution)/shard_map/ppermute | solution.py:274
  17.6 8.4 %collective-permute-start.1 = (bf16[528,128]{1,0:T(8,128)(2,1)S(1)}, bf16[528,128]{1,0:T(8,128)(2,1)S(1)}, u32[]{:S(2)}, u32[]{:S(2)}) collective-permute-start(bf16[528,128]{1,0:T(8,128)(2,1)S(1)} %get-tuple-element.12), channel_id=1, source_target_pairs={{0,12},{4,8},{8,4},{12,0},{1,13},{5,9},{9,5},{13,1},{2,14},{6,10},... | collective-permute-start | bytes 405512 | tf_op jit(solution)/shard_map/ppermute | solution.py:274
  20.1 10.8 %collective-permute-start.2 = (bf16[528,128]{1,0:T(8,128)(2,1)S(1)}, bf16[528,128]{1,0:T(8,128)(2,1)S(1)}, u32[]{:S(2)}, u32[]{:S(2)}) collective-permute-start(bf16[528,128]{1,0:T(8,128)(2,1)S(1)} %get-tuple-element.13), channel_id=1, source_target_pairs={{0,8},{4,12},{8,0},{12,4},{1,9},{5,13},{9,1},{13,5},{2,10},{6,14},... | collective-permute-start | bytes 405512 | tf_op jit(solution)/shard_map/ppermute | solution.py:274
  31.1 8.5 %collective-permute-start.6 = (bf16[544,128]{1,0:T(8,128)(2,1)S(1)}, bf16[544,128]{1,0:T(8,128)(2,1)S(1)}, u32[]{:S(2)}, u32[]{:S(2)}) collective-permute-start(bf16[544,128]{1,0:T(8,128)(2,1)S(1)} %shard_map.98.refs_0_), channel_id=1, source_target_pairs={{0,12},{4,8},{8,4},{12,0},{1,13},{5,9},{9,5},{13,1},{2,14},{6,10},... | collective-permute-start | bytes 417800 | tf_op jit(solution)/shard_map/ppermute | solution.py:274
  33.6 10.8 %collective-permute-start.4 = (bf16[544,128]{1,0:T(8,128)(2,1)S(1)}, bf16[544,128]{1,0:T(8,128)(2,1)S(1)}, u32[]{:S(2)}, u32[]{:S(2)}) collective-permute-start(bf16[544,128]{1,0:T(8,128)(2,1)S(1)} %shard_map.98.refs_0_), channel_id=1, source_target_pairs={{0,4},{4,0},{8,12},{12,8},{1,5},{5,1},{9,13},{13,9},{2,6},{6,2},{1... | collective-permute-start | bytes 417800 | tf_op jit(solution)/shard_map/ppermute | solution.py:274
  33.6 11.2 %collective-permute-start.5 = (bf16[544,128]{1,0:T(8,128)(2,1)S(1)}, bf16[544,128]{1,0:T(8,128)(2,1)S(1)}, u32[]{:S(2)}, u32[]{:S(2)}) collective-permute-start(bf16[544,128]{1,0:T(8,128)(2,1)S(1)} %shard_map.98.refs_0_), channel_id=1, source_target_pairs={{0,8},{4,12},{8,0},{12,4},{1,9},{5,13},{9,1},{13,5},{2,10},{6,14},... | collective-permute-start | bytes 417800 | tf_op jit(solution)/shard_map/ppermute | solution.py:274
  35.5 9.5 %collective-permute-start.7 = (bf16[544,128]{1,0:T(8,128)(2,1)S(1)}, bf16[544,128]{1,0:T(8,128)(2,1)S(1)}, u32[]{:S(2)}, u32[]{:S(2)}) collective-permute-start(bf16[544,128]{1,0:T(8,128)(2,1)S(1)} %shard_map.98.refs_0_), channel_id=1, source_target_pairs={{0,1},{1,0},{2,3},{3,2},{4,5},{5,4},{6,7},{7,6},{8,9},{9,8},{10,11... | collective-permute-start | bytes 417800 | tf_op jit(solution)/shard_map/ppermute | solution.py:280
  39.6 5.4 %collective-permute-start.10 = (bf16[544,128]{1,0:T(8,128)(2,1)S(1)}, bf16[544,128]{1,0:T(8,128)(2,1)S(1)}, u32[]{:S(2)}, u32[]{:S(2)}) collective-permute-start(bf16[544,128]{1,0:T(8,128)(2,1)S(1)} %collective-permute-done.6.refs_3_), channel_id=1, source_target_pairs={{0,1},{1,0},{2,3},{3,2},{4,5},{5,4},{6,7},{7,6},{8,9},{9,8},{10,11... | collective-permute-start | bytes 417800 | tf_op jit(solution)/shard_map/ppermute | solution.py:280
  44.5 1.4 %collective-permute-start.8 = (bf16[544,128]{1,0:T(8,128)(2,1)S(1)}, bf16[544,128]{1,0:T(8,128)(2,1)S(1)}, u32[]{:S(2)}, u32[]{:S(2)}) collective-permute-start(bf16[544,128]{1,0:T(8,128)(2,1)S(1)} %collective-permute-done.4.refs_1_), channel_id=1, source_target_pairs={{0,1},{1,0},{2,3},{3,2},{4,5},{5,4},{6,7},{7,6},{8,9},{9,8},{10,11... | collective-permute-start | bytes 417800 | tf_op jit(solution)/shard_map/ppermute | solution.py:280
  44.8 1.4 %collective-permute-start.9 = (bf16[544,128]{1,0:T(8,128)(2,1)S(1)}, bf16[544,128]{1,0:T(8,128)(2,1)S(1)}, u32[]{:S(2)}, u32[]{:S(2)}) collective-permute-start(bf16[544,128]{1,0:T(8,128)(2,1)S(1)} %collective-permute-done.5.refs_2_), channel_id=1, source_target_pairs={{0,1},{1,0},{2,3},{3,2},{4,5},{5,4},{6,7},{7,6},{8,9},{9,8},{10,11... | collective-permute-start | bytes 417800 | tf_op jit(solution)/shard_map/ppermute | solution.py:280
  48.9 3.7 %collective-permute-start.11 = (f32[1,512]{1,0:T(1,128)S(1)}, f32[1,512]{1,0:T(1,128)S(1)}, u32[]{:S(2)}, u32[]{:S(2)}) collective-permute-start(f32[1,512]{1,0:T(1,128)S(1)} %slice.50), channel_id=1, source_target_pairs={{0,2},{2,0},{1,3},{3,1},{4,6},{6,4},{5,7},{7,5},{8,10},{10,8},{9,1... | collective-permute-start | bytes 6152 | tf_op jit(solution)/shard_map/ppermute | solution.py:277
  54.9 3.7 %collective-permute-start.12 = (f32[1,512]{1,0:T(1,128)S(1)}, f32[1,512]{1,0:T(1,128)S(1)}, u32[]{:S(2)}, u32[]{:S(2)}) collective-permute-start(f32[1,512]{1,0:T(1,128)S(1)} %fusion), channel_id=1, source_target_pairs={{0,2},{2,0},{1,3},{3,1},{4,6},{6,4},{5,7},{7,5},{8,10},{10,8},{9,1... | collective-permute-start | bytes 6152 | tf_op jit(solution)/shard_map/ppermute | solution.py:277

commit v6 on v5

--- a/solution.py
+++ b/solution.py
@@ -15,6 +15,7 @@
 
 VMEM = pl.BlockSpec(memory_space=pltpu.VMEM)
 KERNEL = pltpu.CompilerParams(vmem_limit_bytes=16 * 2**20)
+HBM = pl.BlockSpec(memory_space=pltpu.HBM)
 SMEM = pl.BlockSpec(memory_space=pltpu.SMEM)
 
 
@@ -105,33 +106,57 @@
 OVER_ROWS = (((0,), (0,)), ((), ()))
 
 
-def valid_rows(index, counts, own_ref):
-    rows = own_ref[index].astype(jnp.float32)
-    row = lax.broadcasted_iota(jnp.int32, rows.shape, 0)
-    return jnp.where(row < counts[0, index], rows, 0.0).astype(jnp.bfloat16)
-
-
-def half_kernel(blocks, counts, y_ref, own_ref, out_ref, acc, vec, side, readings):
-    tile_num = own_ref.shape[0]
-    readings[...] = y_ref[...].astype(jnp.float32)
+def flip_of(turn, number, core):
+    flips = list(reversed(range(1, number)))
+    return flips[(turn + core) % len(flips)]
+
+
+def flip_here(turn, number, beside=0):
+    if turn == number - 1:
+        return 0
+    on_core = [flip_of(turn, number, core) for core in range(2)]
+    return jnp.where(lax.axis_index("state") == beside, on_core[0], on_core[1])
+
+
+def half_kernel(
+    blocks_hbm, counts_hbm, y_hbm, own_hbm, out_ref, turned_ref,
+    blocks, counts, y_ref, own_ref, acc, vec, side, readings, small_sems, tile_sems,
+):
+    tile_num, row_num, half = own_ref.shape
+    small = [
+        pltpu.make_async_copy(source, target, small_sems.at[at])
+        for at, (source, target) in enumerate(
+            ((blocks_hbm, blocks), (counts_hbm, counts), (y_hbm, y_ref))
+        )
+    ]
+    tiles = [
+        pltpu.make_async_copy(own_hbm.at[index], own_ref.at[index], tile_sems.at[index])
+        for index in range(tile_num)
+    ]
+    for copy in small + tiles:
+        copy.start()
     acc[...] = jnp.zeros_like(acc)
     vec[...] = jnp.zeros_like(vec)
     side[...] = jnp.zeros_like(side)
-
-    def tile(index, carry):
-        block = blocks[index, 0]
-        rows = valid_rows(index, counts, own_ref)
-        values = jnp.broadcast_to(readings[pl.ds(index, 1), :], (8, rows.shape[0]))
-        square = lax.dot_general(rows, rows, OVER_ROWS, preferred_element_type=jnp.float32)
+    for copy in small:
+        copy.wait()
+    readings[...] = y_ref[...].astype(jnp.float32)
+    row = lax.broadcasted_iota(jnp.int32, (row_num, half), 0)
+    for index in range(tile_num):
+        tiles[index].wait()
+        block = blocks[0, index]
+        rows = jnp.where(row < counts[0, index], own_ref[index].astype(jnp.float32), 0.0)
+        rows = rows.astype(jnp.bfloat16)
+        turned = rows.T
+        turned_ref[index] = turned
+        square = jnp.dot(turned, rows, preferred_element_type=jnp.float32)
         acc[block, 0:LANES] += square[:LANES, :LANES]
         acc[block, LANES : 2 * LANES] += square[:LANES, LANES:]
         acc[block, 2 * LANES : 3 * LANES] += square[LANES:, LANES:]
+        values = jnp.broadcast_to(readings[index : index + 1, :], (8, row_num))
         vec[block] += jnp.dot(
             values.astype(jnp.bfloat16), rows, preferred_element_type=jnp.float32
         )
-        return carry
-
-    lax.fori_loop(0, tile_num, tile, 0, unroll=2)
     line = lax.broadcasted_iota(jnp.int32, (LANES, LANES), 0)
     column = lax.broadcasted_iota(jnp.int32, (LANES, LANES), 1)
     for block in range(out_ref.shape[0]):
@@ -148,34 +173,35 @@
         out_ref[block, 2 * LANES :] = side[...].astype(jnp.bfloat16)
 
 
-def cross_kernel(flips, blocks, counts, own_ref, other_ref, half_ref, *refs):
-    outs, acc = refs[:-1], refs[-1]
+def cross_kernel(blocks_hbm, other_hbm, turned_ref, half_ref, *refs):
+    outs, (blocks, other_ref, acc, small_sem, tile_sems) = refs[:-5], refs[-5:]
+    tile_num = other_ref.shape[0]
+    number = len(outs)
     core, position = lax.axis_index("state"), lax.axis_index("tm")
+    small = pltpu.make_async_copy(blocks_hbm, blocks, small_sem)
+    tiles = [
+        pltpu.make_async_copy(other_hbm.at[index], other_ref.at[index], tile_sems.at[index])
+        for index in range(tile_num)
+    ]
+    for copy in [small] + tiles:
+        copy.start()
     acc[...] = jnp.zeros_like(acc)
-
-    def tile(index, carry):
-        for slot, flip in enumerate(flips):
-
-            @pl.when(blocks[index, 0] == position ^ flip)
-            def _():
-                rows = valid_rows(index, counts, own_ref)
-                for piece in range(2):
-                    at = pl.multiple_of((piece ^ core) * LANES, LANES)
-                    acc[slot, piece * LANES : (piece + 1) * LANES] += lax.dot_general(
-                        rows[:, piece * LANES : (piece + 1) * LANES],
-                        other_ref[index, :, pl.ds(at, LANES)],
-                        OVER_ROWS,
-                        preferred_element_type=jnp.float32,
-                    )
-
-        return carry
-
-    lax.fori_loop(0, own_ref.shape[0], tile, 0)
-    for slot, flip in enumerate(flips):
-        block = position ^ flip
-        outs[slot][: 2 * LANES] = half_ref[block, : 2 * LANES]
-        outs[slot][2 * LANES : 4 * LANES] = acc[slot].astype(jnp.bfloat16)
-        outs[slot][4 * LANES :] = half_ref[block, 2 * LANES :]
+    small.wait()
+    for index in range(tile_num):
+        tiles[index].wait()
+        block = blocks[0, index]
+        for piece in range(2):
+            at = pl.multiple_of((piece ^ core) * LANES, LANES)
+            acc[block, piece * LANES : (piece + 1) * LANES] += jnp.dot(
+                turned_ref[index, piece * LANES : (piece + 1) * LANES, :],
+                other_ref[index, :, pl.ds(at, LANES)],
+                preferred_element_type=jnp.float32,
+            )
+    for turn, out_ref in enumerate(outs):
+        block = position ^ flip_here(turn, number)
+        out_ref[: 2 * LANES] = half_ref[block, : 2 * LANES]
+        out_ref[2 * LANES : 4 * LANES] = acc[block].astype(jnp.bfloat16)
+        out_ref[4 * LANES :] = half_ref[block, 2 * LANES :]
 
 
 def sum_kernel(kappa_ref, rate_ref, gain_ref, *refs):
@@ -224,9 +250,12 @@
     half = 2 * LANES
     line = lax.broadcasted_iota(jnp.int32, (LANES, LANES), 0)
     column = lax.broadcasted_iota(jnp.int32, (LANES, LANES), 1)
-    for flip in range(number):
-        block = position ^ flip
-        for pieces, side in ((own[flip], core), (other[flip], 1 - core)):
+    for turn in range(number):
+        flip, flip_other = flip_here(turn, number), flip_here(turn, number, 1)
+        for pieces, side, block in (
+            (own[turn], core, position ^ flip),
+            (other[turn], 1 - core, position ^ flip_other),
+        ):
 
             def piece(index):
                 return pieces[index * LANES : (index + 1) * LANES, :]
@@ -262,7 +291,7 @@
     tm_size, grp_size = lax.axis_size("tm"), lax.axis_size("grp")
     state_size = lax.axis_size("state")
     tm_index, grp_index, core = (lax.axis_index(name) for name in ("tm", "grp", "state"))
-    tile_num, half = rows_h.shape[1], rows_h.shape[3]
+    tile_num, row_num, half = rows_h.shape[1:]
     width = kappa.shape[2]
     own = rows_h[0]
     other = lax.ppermute(own, "state", [(i, (i + 1) % state_size) for i in range(state_size)])
@@ -270,8 +299,13 @@
     direct = tm_size <= DIRECT_TM and tm_size & (tm_size - 1) == 0
     states_shape = jax.ShapeDtypeStruct((tm_size, width), jnp.float32)
 
-    def flip_over(array, flip):
-        return lax.ppermute(array, "tm", [(i, i ^ flip) for i in range(tm_size)])
+    def flip_over(array, turn):
+        pairs = [
+            (i * state_size + j, (i ^ flip_of(turn, tm_size, j)) * state_size + j)
+            for i in range(tm_size)
+            for j in range(state_size)
+        ]
+        return lax.ppermute(array, ("tm", "state"), pairs)
 
     def ring(array, step):
         return lax.ppermute(array, "grp", [(i, (i + step) % grp_size) for i in range(grp_size)])
@@ -280,36 +314,45 @@
         return lax.ppermute(array, "state", [(i, (i + 1) % state_size) for i in range(state_size)])
 
     if direct:
-        blocks = tile_block[0]
-        part_of = pl.pallas_call(
+        blocks = tile_block[0, :, 0][None]
+        part_of, turned = pl.pallas_call(
             half_kernel,
-            out_shape=jax.ShapeDtypeStruct((tm_size, 2 * LANES + 16, LANES), jnp.bfloat16),
-            in_specs=[SMEM, SMEM, VMEM, VMEM],
-            out_specs=VMEM,
+            out_shape=(
+                jax.ShapeDtypeStruct((tm_size, 2 * LANES + 16, LANES), jnp.bfloat16),
+                jax.ShapeDtypeStruct((tile_num, half, row_num), jnp.bfloat16),
+            ),
+            in_specs=[HBM] * 4,
+            out_specs=(VMEM, VMEM),
             scratch_shapes=[
+                pltpu.SMEM((1, tile_num), jnp.int32),
+                pltpu.SMEM((1, tile_num), jnp.int32),
+                pltpu.VMEM((tile_num, row_num), jnp.bfloat16),
+                pltpu.VMEM((tile_num, row_num, half), jnp.bfloat16),
                 pltpu.VMEM((tm_size, 3 * LANES, LANES), jnp.float32),
                 pltpu.VMEM((tm_size, 8, half), jnp.float32),
                 pltpu.VMEM((16, LANES), jnp.float32),
-                pltpu.VMEM(rows_y.shape[1:], jnp.float32),
+                pltpu.VMEM((tile_num, row_num), jnp.float32),
+                pltpu.SemaphoreType.DMA((3,)),
+                pltpu.SemaphoreType.DMA((tile_num,)),
             ],
             compiler_params=KERNEL,
         )(blocks, tile_count, rows_y[0], own)
-
-        def cross(flips):
-            return pl.pallas_call(
-                functools.partial(cross_kernel, flips),
-                out_shape=[jax.ShapeDtypeStruct((4 * LANES + 16, LANES), jnp.bfloat16)] * len(flips),
-                in_specs=[SMEM, SMEM] + [VMEM] * 3,
-                out_specs=[VMEM] * len(flips),
-                scratch_shapes=[pltpu.VMEM((len(flips), 2 * LANES, LANES), jnp.float32)],
-                compiler_params=KERNEL,
-            )(blocks, tile_count, own, other, part_of)
-
-        order = list(reversed(range(tm_size)))
-        parts = []
-        for flips in (order[: tm_size // 2], order[tm_size // 2 :]):
-            for flip, piece in zip(flips, cross(flips)):
-                parts.append(piece if flip == 0 else flip_over(piece, flip))
+        pieces = pl.pallas_call(
+            cross_kernel,
+            out_shape=[jax.ShapeDtypeStruct((4 * LANES + 16, LANES), jnp.bfloat16)] * tm_size,
+            in_specs=[HBM, HBM, VMEM, VMEM],
+            out_specs=[VMEM] * tm_size,
+            scratch_shapes=[
+                pltpu.SMEM((1, tile_num), jnp.int32),
+                pltpu.VMEM((tile_num, row_num, half), jnp.bfloat16),
+                pltpu.VMEM((tm_size, 2 * LANES, LANES), jnp.float32),
+                pltpu.SemaphoreType.DMA(()),
+                pltpu.SemaphoreType.DMA((tile_num,)),
+            ],
+            compiler_params=KERNEL,
+        )(blocks, other, turned, part_of)
+        turns = range(tm_size - 1)
+        parts = [flip_over(pieces[turn], turn) for turn in turns] + [pieces[-1]]
         own_sum = pl.pallas_call(
             sum_kernel,
             out_shape=jax.ShapeDtypeStruct((4 * LANES + 32, LANES), jnp.bfloat16),
@@ -318,7 +361,7 @@
             scratch_shapes=[pltpu.VMEM((32, LANES), jnp.float32)],
             compiler_params=KERNEL,
         )(kappa[0], rate[0], smooth_gain[0], *parts)
-        own_sums = [own_sum] + [flip_over(own_sum, flip) for flip in range(1, tm_size)]
+        own_sums = [flip_over(own_sum, turn) for turn in turns] + [own_sum]
         other_sums = [across(values) for values in own_sums]
         grams, vectors, new_states, new_innovations = pl.pallas_call(
             functools.partial(assemble_kernel, tm_size),

time: 60 us -> 60.6 us (1.010)
  Pallas kernels: 13.3 us -> 14.9 us
  starting transfers between devices: 15.6 us -> 17.2 us
  local copies, waits for them, and re-layouts: 4.54 us -> 3.24 us
  waiting for transfers between devices: 24.3 us -> 23.5 us
    ppermute x4, starting transfers between devices: 0.22 us -> 3.9 us  [across(): lax.ppermute(array, 'state', [(i, (i + 1) % state_size) for i in range(st...]
    ppermute x6, waiting for transfers between devices: 20 us -> 18.2 us  [flip_over(): return lax.ppermute(array, ('tm', 'state'), pairs)]
    pallas_call x3 -> x2, Pallas kernels: 8.14 us -> 9.79 us  [the longest x1 5.62 us: shards(): pl.pallas_call(half_kernel, out_shape=(jax.ShapeDtypeStruct((tm_size, 2 *...]
    ppermute x2, starting transfers between devices: 4.16 us -> 3.06 us  [ring(): lax.ppermute(array, 'grp', [(i, (i + step) % grp_size) for i in range(grp...]
    ppermute x2, waiting for transfers between devices: 3.13 us -> 4.23 us  [ring(): lax.ppermute(array, 'grp', [(i, (i + step) % grp_size) for i in range(grp...]
    ppermute x6, starting transfers between devices: 10.7 us -> 9.76 us  [flip_over(): return lax.ppermute(array, ('tm', 'state'), pairs)]
    squeeze x1 -> x0, local copies, waits for them, and re-layouts: 0.73 us -> none  [shards(): blocks = tile_block[0]]
  transfers between devices with their start and end apart: 13 -> 13, of which waited for: 9 -> 8; matrix products, arithmetic and copies ran while one was open for 1% -> 0% of each run, Pallas kernels for 12% -> 9%
where the time goes in v6:
time: 60.6 us; the launch traced here: 60.4 us
  waiting for transfers between devices  23.5 us (39%)
  starting transfers between devices  17.2 us (28%)
  Pallas kernels  14.9 us (25%)
  local copies, waits for them, and re-layouts  3.24 us (5%)
  between operations  0.74 us (1%)
  other arithmetic  0.72 us (1%)
    ppermute x6, waiting for transfers between devices, flip_over(): return lax.ppermute(array, ('tm', 'state'), pairs)  18.2 us
    ppermute x6, starting transfers between devices, flip_over(): return lax.ppermute(array, ('tm', 'state'), pairs)  9.76 us
    pallas_call x1, Pallas kernels, shards(): pl.pallas_call(half_kernel, out_shape=(jax.ShapeDtypeStruct((tm_size, 2 *...  5.62 us
    ppermute x2, waiting for transfers between devices, ring(): lax.ppermute(array, 'grp', [(i, (i + step) % grp_size) for i in range(grp...  4.23 us
    pallas_call x1, Pallas kernels, shards(): pl.pallas_call(cross_kernel, out_shape=[jax.ShapeDtypeStruct((4 * LANES +...  4.17 us
    ppermute x4, starting transfers between devices, across(): lax.ppermute(array, 'state', [(i, (i + 1) % state_size) for i in range(st...  3.9 us
    unnamed x16, local copies, waits for them, and re-layouts  3.24 us
    ppermute x2, starting transfers between devices, ring(): lax.ppermute(array, 'grp', [(i, (i + step) % grp_size) for i in range(grp...  3.06 us
  transfers between devices with their start and end apart: 13, of which 8 were waited for; matrix products, arithmetic and copies ran while one was open for 0% of the time, Pallas kernels for 9%

profile of v6, /device:TPU:0, one launch (start us, length us, event | category | flops | bytes accessed | tf_op | source)
XLA Modules:
  0.0 60.4 jit_solution(6897600228620041767)
XLA Ops:
  0.7 0.5 collective-permute-start
  1.2 1.2 %copy-done = bf16[1,16,128,256]{3,2,1,0:T(8,128)(2,1)S(1)} copy-done((bf16[1,16,128,256]{3,2,1,0:T(8,128)(2,1)S(1)}, bf16[1,16,128,256]{3,2,1,0:T(8,128)(2,1)}, u32[]{:S(2)}) %copy-start) | copy-done | bytes 1048600
  2.4 0.7 %copy-done.1 = bf16[1,16,128]{2,1,0:T(8,128)(2,1)S(1)} copy-done((bf16[1,16,128]{2,1,0:T(8,128)(2,1)S(1)}, bf16[1,16,128]{2,1,0:T(8,128)(2,1)}, u32[]{:S(2)}) %copy-start.1) | copy-done | bytes 4120
  3.1 0.7 %copy-done.6 = s32[1,16,1]{1,2,0:T(1,128)S(1)} copy-done((s32[1,16,1]{1,2,0:T(1,128)S(1)}, s32[1,16,1]{1,2,0:T(1,128)}, u32[]{:S(2)}) %copy-start.6) | copy-done | bytes 88
  3.7 0.7 %copy-done.7 = s32[1,16]{1,0:T(1,128)S(1)} copy-done((s32[1,16]{1,0:T(1,128)S(1)}, s32[1,16]{1,0:T(1,128)}, u32[]{:S(2)}) %copy-start.7) | copy-done | bytes 88
  4.4 5.6 %shard_map.95 = (bf16[4,272,128]{2,1,0:T(8,128)(2,1)S(1)}, bf16[16,256,128]{2,1,0:T(8,128)(2,1)S(1)}) custom-call(s32[1,16]{1,0:T(1,128)S(1)} %bitcast.43, s32[1,16]{1,0:T(1,128)S(1)} %copy-done.7, bf16[16,128]{1,0:T(8,128)(2,1)S(1)} %bitcast.38, bf16[16,128,256]{2,1,0:T(8,128)(2,1)S(1)} %bitcast.37), custom_call_target="tpu_custom_call" | custom-call | tf_op jit(solution)/shard_map/pallas_call | solution.py:318
  10.0 4.2 %shard_map.96 = (bf16[528,128]{1,0:T(8,128)(2,1)S(1)}, bf16[528,128]{1,0:T(8,128)(2,1)S(1)}, bf16[528,128]{1,0:T(8,128)(2,1)S(1)}, bf16[528,128]{1,0:T(8,128)(2,1)S(1)}) custom-call(s32[1,16]{1,0:T(1,128)S(1)} %bitcast.44, bf16[16,128,256]{2,1,0:T(8,128)(2,1)S(1)} %collective-permute-done.other_hbm, bf16[16,256,128]{2,1,0:T(8,128)(2,1)S(1)} %get-tuple-element.14.turned_ref, ...), custom_call_target="tpu_custom_call" | custom-call | tf_op jit(solution)/shard_map/pallas_call | solution.py:340
  14.2 4.7 %collective-permute-start.1 = (bf16[528,128]{1,0:T(8,128)(2,1)S(1)}, bf16[528,128]{1,0:T(8,128)(2,1)S(1)}, u32[]{:S(2)}, u32[]{:S(2)}) collective-permute-start(bf16[528,128]{1,0:T(8,128)(2,1)S(1)} %get-tuple-element.16), channel_id=1, source_target_pairs={{0,12},{1,9},{4,8},{5,13},{8,4},{9,1},{12,0},{13,5},{2,14},{3,11},... | collective-permute-start | bytes 405512 | tf_op jit(solution)/shard_map/ppermute | solution.py:308
  18.9 0.6 %collective-permute-start.3 = (bf16[528,128]{1,0:T(8,128)(2,1)S(1)}, bf16[528,128]{1,0:T(8,128)(2,1)S(1)}, u32[]{:S(2)}, u32[]{:S(2)}) collective-permute-start(bf16[528,128]{1,0:T(8,128)(2,1)S(1)} %get-tuple-element.18), channel_id=1, source_target_pairs={{0,4},{1,13},{4,0},{5,9},{8,12},{9,5},{12,8},{13,1},{2,6},{3,15},{... | collective-permute-start | bytes 405512 | tf_op jit(solution)/shard_map/ppermute | solution.py:308
  19.5 3.9 %collective-permute-done.1.refs_0_ = bf16[528,128]{1,0:T(8,128)(2,1)S(1)} collective-permute-done((bf16[528,128]{1,0:T(8,128)(2,1)S(1)}, bf16[528,128]{1,0:T(8,128)(2,1)S(1)}, u32[]{:S(2)}, u32[]{:S(2)}) %collective-permute-start.1) | collective-permute-done | bytes 135200 | tf_op jit(solution)/shard_map/ppermute | solution.py:308
  23.4 7.4 %collective-permute-done.2.refs_1_ = bf16[528,128]{1,0:T(8,128)(2,1)S(1)} collective-permute-done((bf16[528,128]{1,0:T(8,128)(2,1)S(1)}, bf16[528,128]{1,0:T(8,128)(2,1)S(1)}, u32[]{:S(2)}, u32[]{:S(2)}) %collective-permute-start.2) | collective-permute-done | bytes 135200 | tf_op jit(solution)/shard_map/ppermute | solution.py:308
  30.9 2.7 %collective-permute-start.4 = (bf16[544,128]{1,0:T(8,128)(2,1)S(1)}, bf16[544,128]{1,0:T(8,128)(2,1)S(1)}, u32[]{:S(2)}, u32[]{:S(2)}) collective-permute-start(bf16[544,128]{1,0:T(8,128)(2,1)S(1)} %shard_map.97.refs_3_), channel_id=1, source_target_pairs={{0,12},{1,9},{4,8},{5,13},{8,4},{9,1},{12,0},{13,5},{2,14},{3,11},... | collective-permute-start | bytes 417800 | tf_op jit(solution)/shard_map/ppermute | solution.py:308
  33.7 1.7 %collective-permute-start.6 = (bf16[544,128]{1,0:T(8,128)(2,1)S(1)}, bf16[544,128]{1,0:T(8,128)(2,1)S(1)}, u32[]{:S(2)}, u32[]{:S(2)}) collective-permute-start(bf16[544,128]{1,0:T(8,128)(2,1)S(1)} %shard_map.97.refs_3_), channel_id=1, source_target_pairs={{0,4},{1,13},{4,0},{5,9},{8,12},{9,5},{12,8},{13,1},{2,6},{3,15},{... | collective-permute-start | bytes 417800 | tf_op jit(solution)/shard_map/ppermute | solution.py:308
  35.4 4.2 %collective-permute-done.4.refs_0_ = bf16[544,128]{1,0:T(8,128)(2,1)S(1)} collective-permute-done((bf16[544,128]{1,0:T(8,128)(2,1)S(1)}, bf16[544,128]{1,0:T(8,128)(2,1)S(1)}, u32[]{:S(2)}, u32[]{:S(2)}) %collective-permute-start.4) | collective-permute-done | bytes 139296 | tf_op jit(solution)/shard_map/ppermute | solution.py:308
  39.6 3.4 %collective-permute-start.7 = (bf16[544,128]{1,0:T(8,128)(2,1)S(1)}, bf16[544,128]{1,0:T(8,128)(2,1)S(1)}, u32[]{:S(2)}, u32[]{:S(2)}) collective-permute-start(bf16[544,128]{1,0:T(8,128)(2,1)S(1)} %collective-permute-done.4.refs_0_), channel_id=1, source_target_pairs={{0,1},{1,0},{2,3},{3,2},{4,5},{5,4},{6,7},{7,6},{8,9},{9,8},{10,11... | collective-permute-start | bytes 417800 | tf_op jit(solution)/shard_map/ppermute | solution.py:314
  43.0 2.8 %collective-permute-done.5.refs_1_ = bf16[544,128]{1,0:T(8,128)(2,1)S(1)} collective-permute-done((bf16[544,128]{1,0:T(8,128)(2,1)S(1)}, bf16[544,128]{1,0:T(8,128)(2,1)S(1)}, u32[]{:S(2)}, u32[]{:S(2)}) %collective-permute-start.5) | collective-permute-done | bytes 139296 | tf_op jit(solution)/shard_map/ppermute | solution.py:308
  46.3 0.8 %collective-permute-done.8.refs_5_ = bf16[544,128]{1,0:T(8,128)(2,1)S(1)} collective-permute-done((bf16[544,128]{1,0:T(8,128)(2,1)S(1)}, bf16[544,128]{1,0:T(8,128)(2,1)S(1)}, u32[]{:S(2)}, u32[]{:S(2)}) %collective-permute-start.8) | collective-permute-done | bytes 139296 | tf_op jit(solution)/shard_map/ppermute | solution.py:314
  47.3 2.8 %shard_map.98 = (bf16[4,512,512]{2,1,0:T(8,128)(2,1)S(1)}, f32[4,5,512]{2,1,0:T(8,128)S(1)}, f32[4,512]{1,0:T(4,128)S(1)}, f32[4,512]{1,0:T(4,128)S(1)}) custom-call(bf16[544,128]{1,0:T(8,128)(2,1)S(1)} %collective-permute-done.4.refs_0_, bf16[544,128]{1,0:T(8,128)(2,1)S(1)} %collective-permute-done.5.refs_1_, ...), custom_call_target="tpu_custom_call" | custom-call | tf_op jit(solution)/shard_map/pallas_call | solution.py:366
  50.1 1.5 %collective-permute-start.11 = (f32[1,512]{1,0:T(1,128)S(1)}, f32[1,512]{1,0:T(1,128)S(1)}, u32[]{:S(2)}, u32[]{:S(2)}) collective-permute-start(f32[1,512]{1,0:T(1,128)S(1)} %slice.50), channel_id=1, source_target_pairs={{0,2},{2,0},{1,3},{3,1},{4,6},{6,4},{5,7},{7,5},{8,10},{10,8},{9,1... | collective-permute-start | bytes 6152 | tf_op jit(solution)/shard_map/ppermute | solution.py:311
  51.6 2.1 %collective-permute-done.11.state_ref = f32[1,512]{1,0:T(1,128)S(1)} collective-permute-done((f32[1,512]{1,0:T(1,128)S(1)}, f32[1,512]{1,0:T(1,128)S(1)}, u32[]{:S(2)}, u32[]{:S(2)}) %collective-permute-start.11) | collective-permute-done | bytes 2080 | tf_op jit(solution)/shard_map/ppermute | solution.py:311
  53.7 2.3 %shard_map.99 = (f32[4,512]{1,0:T(4,128)S(1)}, f32[4,512]{1,0:T(4,128)S(1)}) custom-call(bf16[4,512,512]{2,1,0:T(8,128)(2,1)S(1)} %get-tuple-element.20.grams, f32[4,5,512]{2,1,0:T(8,128)S(1)} %get-tuple-element.21.vectors, f32[1,512]{1,0:T(1,128)S(1)} %collective-permute-done.11.state_ref), custom_call_target="tpu_custom_call" | custom-call | tf_op jit(solution)/shard_map/pallas_call | solution.py:383
  56.1 1.5 %collective-permute-start.12 = (f32[1,512]{1,0:T(1,128)S(1)}, f32[1,512]{1,0:T(1,128)S(1)}, u32[]{:S(2)}, u32[]{:S(2)}) collective-permute-start(f32[1,512]{1,0:T(1,128)S(1)} %fusion), channel_id=1, source_target_pairs={{0,2},{2,0},{1,3},{3,1},{4,6},{6,4},{5,7},{7,5},{8,10},{10,8},{9,1... | collective-permute-start | bytes 6152 | tf_op jit(solution)/shard_map/ppermute | solution.py:311
  57.6 2.1 %collective-permute-done.12 = f32[1,512]{1,0:T(1,128)S(1)} collective-permute-done((f32[1,512]{1,0:T(1,128)S(1)}, f32[1,512]{1,0:T(1,128)S(1)}, u32[]{:S(2)}, u32[]{:S(2)}) %collective-permute-start.12) | collective-permute-done | bytes 2080 | tf_op jit(solution)/shard_map/ppermute | solution.py:311
  59.7 0.7 %add_bitcast_fusion = (f32[1,1,256]{2,1,0:T(1,128)}, f32[1,1,256]{2,1,0:T(1,128)}) fusion(s32[]{:T(128)S(6)} %select_n.42, s32[]{:T(128)S(6)} %select_n.43, f32[1,512]{1,0:T(1,128)S(1)} %get-tuple-element.29, f32[1,512]{1,0:T(1,128)S(1)} %get-tuple-element.28, f32[1,512]{1,0:T(1,128)S(1)} %get-tuple-element.27, f32[1,512]{1,0:T(1,128)S(1)} %get-tuple-element.26, ...), kind=kLoop, calls=%fused_computation.20 | loop fusion | flops 1024 | bytes 11272 | tf_op jit(solution)/shard_map/reshape | solution.py:454
  (29 shorter events, 0.9 us)
Async XLA Ops:
  0.6 30.2 %copy-start.2 = (f32[1,1,512]{2,1,0:T(1,128)S(1)}, f32[1,1,512]{2,1,0:T(1,128)}, u32[]{:S(2)}) copy-start(f32[1,1,512]{2,1,0:T(1,128)} %param.12) | copy-start | bytes 6148
  0.6 30.2 %copy-start.3 = (f32[1,1,512]{2,1,0:T(1,128)S(1)}, f32[1,1,512]{2,1,0:T(1,128)}, u32[]{:S(2)}) copy-start(f32[1,1,512]{2,1,0:T(1,128)} %param.13) | copy-start | bytes 6148
  0.7 9.4 %collective-permute-start = (bf16[16,128,256]{2,1,0:T(8,128)(2,1)}, bf16[16,128,256]{2,1,0:T(8,128)(2,1)S(1)}, u32[]{:S(2)}, u32[]{:S(2)}) collective-permute-start(bf16[16,128,256]{2,1,0:T(8,128)(2,1)} %bitcast.36), channel_id=1, source_target_pairs={{0,1},{1,0},{2,3},{3,2},{4,5},{5,4},{6,7},{7,6},{8,9},{9,8},{10,11... | collective-permute-start | bytes 3145736 | tf_op jit(solution)/shard_map/ppermute | solution.py:297
  1.2 1.2 %copy-start = (bf16[1,16,128,256]{3,2,1,0:T(8,128)(2,1)S(1)}, bf16[1,16,128,256]{3,2,1,0:T(8,128)(2,1)}, u32[]{:S(2)}) copy-start(bf16[1,16,128,256]{3,2,1,0:T(8,128)(2,1)} %param.8) | copy-start | bytes 3145732
  2.4 0.7 %copy-start.1 = (bf16[1,16,128]{2,1,0:T(8,128)(2,1)S(1)}, bf16[1,16,128]{2,1,0:T(8,128)(2,1)}, u32[]{:S(2)}) copy-start(bf16[1,16,128]{2,1,0:T(8,128)(2,1)} %param.9) | copy-start | bytes 12292
  3.1 0.7 %copy-start.6 = (s32[1,16,1]{1,2,0:T(1,128)S(1)}, s32[1,16,1]{1,2,0:T(1,128)}, u32[]{:S(2)}) copy-start(s32[1,16,1]{1,2,0:T(1,128)} %param.10) | copy-start | bytes 196
  3.7 0.7 %copy-start.7 = (s32[1,16]{1,0:T(1,128)S(1)}, s32[1,16]{1,0:T(1,128)}, u32[]{:S(2)}) copy-start(s32[1,16]{1,0:T(1,128)} %counts_hbm.1) | copy-start | bytes 196
  4.4 26.4 %copy-start.4 = (f32[1,1,512]{2,1,0:T(1,128)S(1)}, f32[1,1,512]{2,1,0:T(1,128)}, u32[]{:S(2)}) copy-start(f32[1,1,512]{2,1,0:T(1,128)} %param.14) | copy-start | bytes 6148
  4.4 42.9 %copy-start.5 = (f32[512]{0:T(512)S(1)}, f32[512]{0:T(512)}, u32[]{:S(2)}) copy-start(f32[512]{0:T(512)} %param.15) | copy-start | bytes 6148
  14.2 9.2 %collective-permute-start.1 = (bf16[528,128]{1,0:T(8,128)(2,1)S(1)}, bf16[528,128]{1,0:T(8,128)(2,1)S(1)}, u32[]{:S(2)}, u32[]{:S(2)}) collective-permute-start(bf16[528,128]{1,0:T(8,128)(2,1)S(1)} %get-tuple-element.16), channel_id=1, source_target_pairs={{0,12},{1,9},{4,8},{5,13},{8,4},{9,1},{12,0},{13,5},{2,14},{3,11},... | collective-permute-start | bytes 405512 | tf_op jit(solution)/shard_map/ppermute | solution.py:308
  18.9 11.9 %collective-permute-start.2 = (bf16[528,128]{1,0:T(8,128)(2,1)S(1)}, bf16[528,128]{1,0:T(8,128)(2,1)S(1)}, u32[]{:S(2)}, u32[]{:S(2)}) collective-permute-start(bf16[528,128]{1,0:T(8,128)(2,1)S(1)} %get-tuple-element.17), channel_id=1, source_target_pairs={{0,8},{1,5},{4,12},{5,1},{8,0},{9,13},{12,4},{13,9},{2,10},{3,7},{... | collective-permute-start | bytes 405512 | tf_op jit(solution)/shard_map/ppermute | solution.py:308
  18.9 11.9 %collective-permute-start.3 = (bf16[528,128]{1,0:T(8,128)(2,1)S(1)}, bf16[528,128]{1,0:T(8,128)(2,1)S(1)}, u32[]{:S(2)}, u32[]{:S(2)}) collective-permute-start(bf16[528,128]{1,0:T(8,128)(2,1)S(1)} %get-tuple-element.18), channel_id=1, source_target_pairs={{0,4},{1,13},{4,0},{5,9},{8,12},{9,5},{12,8},{13,1},{2,6},{3,15},{... | collective-permute-start | bytes 405512 | tf_op jit(solution)/shard_map/ppermute | solution.py:308
  30.9 8.6 %collective-permute-start.4 = (bf16[544,128]{1,0:T(8,128)(2,1)S(1)}, bf16[544,128]{1,0:T(8,128)(2,1)S(1)}, u32[]{:S(2)}, u32[]{:S(2)}) collective-permute-start(bf16[544,128]{1,0:T(8,128)(2,1)S(1)} %shard_map.97.refs_3_), channel_id=1, source_target_pairs={{0,12},{1,9},{4,8},{5,13},{8,4},{9,1},{12,0},{13,5},{2,14},{3,11},... | collective-permute-start | bytes 417800 | tf_op jit(solution)/shard_map/ppermute | solution.py:308
  33.7 12.1 %collective-permute-start.5 = (bf16[544,128]{1,0:T(8,128)(2,1)S(1)}, bf16[544,128]{1,0:T(8,128)(2,1)S(1)}, u32[]{:S(2)}, u32[]{:S(2)}) collective-permute-start(bf16[544,128]{1,0:T(8,128)(2,1)S(1)} %shard_map.97.refs_3_), channel_id=1, source_target_pairs={{0,8},{1,5},{4,12},{5,1},{8,0},{9,13},{12,4},{13,9},{2,10},{3,7},{... | collective-permute-start | bytes 417800 | tf_op jit(solution)/shard_map/ppermute | solution.py:308
  33.7 12.1 %collective-permute-start.6 = (bf16[544,128]{1,0:T(8,128)(2,1)S(1)}, bf16[544,128]{1,0:T(8,128)(2,1)S(1)}, u32[]{:S(2)}, u32[]{:S(2)}) collective-permute-start(bf16[544,128]{1,0:T(8,128)(2,1)S(1)} %shard_map.97.refs_3_), channel_id=1, source_target_pairs={{0,4},{1,13},{4,0},{5,9},{8,12},{9,5},{12,8},{13,1},{2,6},{3,15},{... | collective-permute-start | bytes 417800 | tf_op jit(solution)/shard_map/ppermute | solution.py:308
  35.4 10.9 %collective-permute-start.10 = (bf16[544,128]{1,0:T(8,128)(2,1)S(1)}, bf16[544,128]{1,0:T(8,128)(2,1)S(1)}, u32[]{:S(2)}, u32[]{:S(2)}) collective-permute-start(bf16[544,128]{1,0:T(8,128)(2,1)S(1)} %shard_map.97.refs_3_), channel_id=1, source_target_pairs={{0,1},{1,0},{2,3},{3,2},{4,5},{5,4},{6,7},{7,6},{8,9},{9,8},{10,11... | collective-permute-start | bytes 417800 | tf_op jit(solution)/shard_map/ppermute | solution.py:314
  39.6 6.7 %collective-permute-start.7 = (bf16[544,128]{1,0:T(8,128)(2,1)S(1)}, bf16[544,128]{1,0:T(8,128)(2,1)S(1)}, u32[]{:S(2)}, u32[]{:S(2)}) collective-permute-start(bf16[544,128]{1,0:T(8,128)(2,1)S(1)} %collective-permute-done.4.refs_0_), channel_id=1, source_target_pairs={{0,1},{1,0},{2,3},{3,2},{4,5},{5,4},{6,7},{7,6},{8,9},{9,8},{10,11... | collective-permute-start | bytes 417800 | tf_op jit(solution)/shard_map/ppermute | solution.py:314
  45.7 1.4 %collective-permute-start.8 = (bf16[544,128]{1,0:T(8,128)(2,1)S(1)}, bf16[544,128]{1,0:T(8,128)(2,1)S(1)}, u32[]{:S(2)}, u32[]{:S(2)}) collective-permute-start(bf16[544,128]{1,0:T(8,128)(2,1)S(1)} %collective-permute-done.5.refs_1_), channel_id=1, source_target_pairs={{0,1},{1,0},{2,3},{3,2},{4,5},{5,4},{6,7},{7,6},{8,9},{9,8},{10,11... | collective-permute-start | bytes 417800 | tf_op jit(solution)/shard_map/ppermute | solution.py:314
  45.7 1.6 %collective-permute-start.9 = (bf16[544,128]{1,0:T(8,128)(2,1)S(1)}, bf16[544,128]{1,0:T(8,128)(2,1)S(1)}, u32[]{:S(2)}, u32[]{:S(2)}) collective-permute-start(bf16[544,128]{1,0:T(8,128)(2,1)S(1)} %collective-permute-done.6.refs_2_), channel_id=1, source_target_pairs={{0,1},{1,0},{2,3},{3,2},{4,5},{5,4},{6,7},{7,6},{8,9},{9,8},{10,11... | collective-permute-start | bytes 417800 | tf_op jit(solution)/shard_map/ppermute | solution.py:314
  50.1 3.7 %collective-permute-start.11 = (f32[1,512]{1,0:T(1,128)S(1)}, f32[1,512]{1,0:T(1,128)S(1)}, u32[]{:S(2)}, u32[]{:S(2)}) collective-permute-start(f32[1,512]{1,0:T(1,128)S(1)} %slice.50), channel_id=1, source_target_pairs={{0,2},{2,0},{1,3},{3,1},{4,6},{6,4},{5,7},{7,5},{8,10},{10,8},{9,1... | collective-permute-start | bytes 6152 | tf_op jit(solution)/shard_map/ppermute | solution.py:311
  56.1 3.7 %collective-permute-start.12 = (f32[1,512]{1,0:T(1,128)S(1)}, f32[1,512]{1,0:T(1,128)S(1)}, u32[]{:S(2)}, u32[]{:S(2)}) collective-permute-start(f32[1,512]{1,0:T(1,128)S(1)} %fusion), channel_id=1, source_target_pairs={{0,2},{2,0},{1,3},{3,1},{4,6},{6,4},{5,7},{7,5},{8,10},{10,8},{9,1... | collective-permute-start | bytes 6152 | tf_op jit(solution)/shard_map/ppermute | solution.py:311

commit v7 on v4

--- a/solution.py
+++ b/solution.py
@@ -102,42 +102,50 @@
     return high, middle, values - high - middle
 
 
-def gram_kernel(meta, y_ref, own_ref, other_ref, *refs):
-    outs, acc, vec, side = refs[:-3], refs[-3], refs[-2], refs[-1]
-    tile_num, row_num, half = own_ref.shape
-    core, position = meta[2 * tile_num], meta[2 * tile_num + 1]
+def flip_of(turn, number, core):
+    flips = list(reversed(range(1, number)))
+    return flips[(turn + core) % len(flips)]
+
+
+def flip_here(turn, number, beside=0):
+    if turn == number - 1:
+        return 0
+    on_core = [flip_of(turn, number, core) for core in range(2)]
+    return jnp.where(lax.axis_index("state") == beside, on_core[0], on_core[1])
+
+
+def gram_kernel(blocks, y_ref, own_ref, other_ref, *refs):
+    outs, (acc, vec, side, readings) = refs[:-4], refs[-4:]
+    tile_num, row_num, _ = own_ref.shape
+    number = len(outs)
+    core, position = lax.axis_index("state"), lax.axis_index("tm")
     acc[...] = jnp.zeros_like(acc)
     vec[...] = jnp.zeros_like(vec)
     side[...] = jnp.zeros_like(side)
-    row = lax.broadcasted_iota(jnp.int32, (row_num, half), 0)
-    over_rows = (((0,), (0,)), ((), ()))
-
-    def tile(index, carry):
-        block = meta[index]
-        live = meta[tile_num + index]
-        rows = own_ref[index].astype(jnp.float32)
-        rows = jnp.where(row < live, rows, 0.0).astype(jnp.bfloat16)
-        readings = jnp.broadcast_to(y_ref[pl.ds(index, 1), :], (8, row_num)).astype(jnp.bfloat16)
-        square = lax.dot_general(rows, rows, over_rows, preferred_element_type=jnp.float32)
+    readings[...] = y_ref[...].astype(jnp.float32)
+    for index in range(tile_num):
+        block = blocks[index]
+        rows = own_ref[index]
+        turned = rows.T
+        square = jnp.dot(turned, rows, preferred_element_type=jnp.float32)
         acc[block, 0:LANES] += square[:LANES, :LANES]
         acc[block, LANES : 2 * LANES] += square[:LANES, LANES:]
         acc[block, 2 * LANES : 3 * LANES] += square[LANES:, LANES:]
         for piece in range(2):
             at = pl.multiple_of((piece ^ core) * LANES, LANES)
-            acc[block, (3 + piece) * LANES : (4 + piece) * LANES] += lax.dot_general(
-                rows[:, piece * LANES : (piece + 1) * LANES],
+            acc[block, (3 + piece) * LANES : (4 + piece) * LANES] += jnp.dot(
+                turned[piece * LANES : (piece + 1) * LANES, :],
                 other_ref[index, :, pl.ds(at, LANES)],
-                over_rows,
                 preferred_element_type=jnp.float32,
             )
-        vec[block] += jnp.dot(readings, rows, preferred_element_type=jnp.float32)
-        return carry
-
-    lax.fori_loop(0, tile_num, tile, 0, unroll=2)
+        values = jnp.broadcast_to(readings[index : index + 1, :], (8, row_num))
+        vec[block] += jnp.dot(
+            values.astype(jnp.bfloat16), rows, preferred_element_type=jnp.float32
+        )
     line = lax.broadcasted_iota(jnp.int32, (LANES, LANES), 0)
     column = lax.broadcasted_iota(jnp.int32, (LANES, LANES), 1)
-    for flip, out_ref in enumerate(outs):
-        block = position ^ flip
+    for turn, out_ref in enumerate(outs):
+        block = position ^ flip_here(turn, number)
 
         def take(piece):
             return acc[block, piece * LANES : (piece + 1) * LANES]
@@ -157,19 +165,19 @@
         out_ref[4 * LANES :] = side[...].astype(jnp.bfloat16)
 
 
-def sum_kernel(meta, params_ref, *refs):
+def sum_kernel(kappa_ref, rate_ref, gain_ref, *refs):
     parts, out_ref, side = refs[:-2], refs[-2], refs[-1]
-    core = meta[meta.shape[0] - 2]
+    core = lax.axis_index("state")
     total = parts[0][...].astype(jnp.float32)
     for part in parts[1:]:
         total = total + part[...].astype(jnp.float32)
     out_ref[: 4 * LANES] = total[: 4 * LANES].astype(jnp.bfloat16)
     below = total[4 * LANES :]
     values = [below[at : at + 1] + below[at + 4 : at + 5] + below[at + 8 : at + 9] for at in range(4)]
-    for which in range(3):
+    for coefficient in (kappa_ref, rate_ref, gain_ref):
         for piece in range(2):
             at = pl.multiple_of((2 * core + piece) * LANES, LANES)
-            values.append(params_ref[which : which + 1, pl.ds(at, LANES)])
+            values.append(coefficient[:, pl.ds(at, LANES)])
     side[...] = jnp.zeros_like(side)
     for at, value in enumerate(values):
         for which, part in enumerate(pieces_of(value)):
@@ -196,16 +204,19 @@
         innovations_ref[block : block + 1, :] = innovation
 
 
-def assemble_kernel(number, meta, *refs):
+def assemble_kernel(number, *refs):
     own, other, rest = refs[:number], refs[number : 2 * number], refs[2 * number :]
     state_ref, grams, vectors, states_ref, innovations_ref = rest
-    core, position = meta[meta.shape[0] - 2], meta[meta.shape[0] - 1]
+    core, position = lax.axis_index("state"), lax.axis_index("tm")
     half = 2 * LANES
     line = lax.broadcasted_iota(jnp.int32, (LANES, LANES), 0)
     column = lax.broadcasted_iota(jnp.int32, (LANES, LANES), 1)
-    for flip in range(number):
-        block = position ^ flip
-        for pieces, side in ((own[flip], core), (other[flip], 1 - core)):
+    for turn in range(number):
+        flip, flip_other = flip_here(turn, number), flip_here(turn, number, 1)
+        for pieces, side, block in (
+            (own[turn], core, position ^ flip),
+            (other[turn], 1 - core, position ^ flip_other),
+        ):
 
             def piece(index):
                 return pieces[index * LANES : (index + 1) * LANES, :]
@@ -241,49 +252,55 @@
     tm_size, grp_size = lax.axis_size("tm"), lax.axis_size("grp")
     state_size = lax.axis_size("state")
     tm_index, grp_index, core = (lax.axis_index(name) for name in ("tm", "grp", "state"))
-    tile_num, half = rows_h.shape[1], rows_h.shape[3]
+    tile_num, row_num, half = rows_h.shape[1:]
     width = kappa.shape[2]
     own = rows_h[0]
     other = lax.ppermute(own, "state", [(i, (i + 1) % state_size) for i in range(state_size)])
-    readings = rows_y[0].astype(jnp.float32)
     state = start_state.reshape(1, width)
-    meta = jnp.concatenate(
-        [tile_block[0, :, 0], tile_count[0], jnp.stack([core, tm_index]).astype(jnp.int32)]
-    )
-    params = jnp.concatenate([kappa[0], rate[0], smooth_gain[0]], axis=0)
     direct = tm_size <= DIRECT_TM and tm_size & (tm_size - 1) == 0
     states_shape = jax.ShapeDtypeStruct((tm_size, width), jnp.float32)
 
-    def flip_over(array, flip):
-        return lax.ppermute(array, "tm", [(i, i ^ flip) for i in range(tm_size)])
+    def flip_over(array, turn):
+        pairs = [
+            (i * state_size + j, (i ^ flip_of(turn, tm_size, j)) * state_size + j)
+            for i in range(tm_size)
+            for j in range(state_size)
+        ]
+        return lax.ppermute(array, ("tm", "state"), pairs)
+
+    def ring(array, step):
+        return lax.ppermute(array, "grp", [(i, (i + step) % grp_size) for i in range(grp_size)])
 
     def across(array):
         return lax.ppermute(array, "state", [(i, (i + 1) % state_size) for i in range(state_size)])
 
     if direct:
-        sent = jax.ShapeDtypeStruct((4 * LANES + 16, LANES), jnp.bfloat16)
+        live = jnp.arange(row_num, dtype=jnp.int32)[None, :] < tile_count[0][:, None]
+        valid = jnp.where(live[:, :, None], own, jnp.zeros((), own.dtype))
         pieces = pl.pallas_call(
             gram_kernel,
-            out_shape=[sent] * tm_size,
+            out_shape=[jax.ShapeDtypeStruct((4 * LANES + 16, LANES), jnp.bfloat16)] * tm_size,
             in_specs=[SMEM] + [VMEM] * 3,
             out_specs=[VMEM] * tm_size,
             scratch_shapes=[
                 pltpu.VMEM((tm_size, 5 * LANES, LANES), jnp.float32),
                 pltpu.VMEM((tm_size, 8, half), jnp.float32),
                 pltpu.VMEM((16, LANES), jnp.float32),
+                pltpu.VMEM((tile_num, row_num), jnp.float32),
             ],
             compiler_params=KERNEL,
-        )(meta, readings, own, other)
-        parts = [pieces[0]] + [flip_over(pieces[flip], flip) for flip in range(1, tm_size)]
+        )(tile_block[0, :, 0], rows_y[0], valid, other)
+        turns = range(tm_size - 1)
+        parts = [flip_over(pieces[turn], turn) for turn in turns] + [pieces[-1]]
         own_sum = pl.pallas_call(
             sum_kernel,
             out_shape=jax.ShapeDtypeStruct((4 * LANES + 32, LANES), jnp.bfloat16),
-            in_specs=[SMEM] + [VMEM] * (tm_size + 1),
+            in_specs=[VMEM] * (tm_size + 3),
             out_specs=VMEM,
             scratch_shapes=[pltpu.VMEM((32, LANES), jnp.float32)],
             compiler_params=KERNEL,
-        )(meta, params, *parts)
-        own_sums = [own_sum] + [flip_over(own_sum, flip) for flip in range(1, tm_size)]
+        )(kappa[0], rate[0], smooth_gain[0], *parts)
+        own_sums = [flip_over(own_sum, turn) for turn in turns] + [own_sum]
         other_sums = [across(values) for values in own_sums]
         grams, vectors, new_states, new_innovations = pl.pallas_call(
             functools.partial(assemble_kernel, tm_size),
@@ -293,10 +310,10 @@
                 states_shape,
                 states_shape,
             ),
-            in_specs=[SMEM] + [VMEM] * (2 * tm_size + 1),
+            in_specs=[VMEM] * (2 * tm_size + 1),
             out_specs=[VMEM] * 4,
             compiler_params=KERNEL,
-        )(meta, *own_sums, *other_sums, state)
+        )(*own_sums, *other_sums, state)
         gains = vectors[:, 4]
 
         def run_group(state, group):
@@ -310,6 +327,11 @@
                 compiler_params=KERNEL,
             )(grams, vectors, state)
     else:
+        readings = rows_y[0].astype(jnp.float32)
+        meta = jnp.concatenate(
+            [tile_block[0, :, 0], tile_count[0], jnp.stack([core, tm_index]).astype(jnp.int32)]
+        )
+        params = jnp.concatenate([kappa[0], rate[0], smooth_gain[0]], axis=0)
         gathered = lax.all_gather(params, "tm")
         gains = gathered[:, 2]
         vector = jax.ShapeDtypeStruct((1, width), jnp.float32)
@@ -352,7 +374,7 @@
         states = jnp.where(mine, new_states, states)
         innovations = jnp.where(mine, new_innovations, innovations)
         if group < grp_size - 1:
-            state = lax.ppermute(new_states[-1:], "grp", [(group, group + 1)])
+            state = ring(new_states[-1:], 1)
 
     residual = jnp.zeros((1, width), jnp.float32)
     residuals = [None] * tm_size
@@ -362,7 +384,7 @@
             residuals[block] = running
             running = gains[block][None] * (running + innovations[block][None])
         if group > 0:
-            arrived = lax.ppermute(running, "grp", [(group, group - 1)])
+            arrived = ring(running, -1)
             residual = jnp.where(grp_index == group - 1, arrived, residual)
     smoothed = states + jnp.concatenate(residuals, 0)
 

time: 57.6 us -> 52.4 us (0.910)
  waiting for transfers between devices: 28.4 us -> 23.8 us
  Pallas kernels: 9.58 us -> 7.11 us
  starting transfers between devices: 15.3 us -> 17.6 us
  local copies, waits for them, and re-layouts: 1.25 us -> 0.03 us
  other arithmetic: 2.17 us -> 2.96 us
    ppermute x4, starting transfers between devices: 0.01 us -> 3.83 us  [across(): lax.ppermute(array, 'state', [(i, (i + 1) % state_size) for i in range(st...]
    ppermute x8, waiting for transfers between devices: 26 us -> 22.6 us  [the longest x6 18.4 us: flip_over(): return lax.ppermute(array, ('tm', 'state'), pairs)]
    select_n x0 -> x1, other arithmetic: none -> 1.52 us  [shards(): valid = jnp.where(live[:, :, None], own, jnp.zeros((), own.dtype))]
    ppermute x8, starting transfers between devices: 14.7 us -> 13.2 us  [the longest x6 10.1 us: flip_over(): return lax.ppermute(array, ('tm', 'state'), pairs)]
    pallas_call x1, Pallas kernels: 3.33 us -> 1.95 us  [shards(): pl.pallas_call(gram_kernel, out_shape=[jax.ShapeDtypeStruct((4 * LANES +...]
    unnamed x10 -> x12, local copies, waits for them, and re-layouts: 1.24 us -> 0.03 us
    ppermute x1, waiting for transfers between devices: 1.06 us -> 0.22 us  [shards(): lax.ppermute(own, 'state', [(i, (i + 1) % state_size) for i in range(stat...]
    concatenate x2 -> x0, other arithmetic: 0.76 us -> none  [the longest x1 0.75 us: shards(): jnp.concatenate([tile_block[0, :, 0], tile_count[0], jnp.stack([core, tm_...]
  transfers between devices with their start and end apart: 13 -> 13, of which waited for: 9 -> 9; matrix products, arithmetic and copies ran while one was open for 3% -> 4% of each run, Pallas kernels for 0% -> 0%
where the time goes in v7:
time: 52.4 us; the launch traced here: 52.3 us
  waiting for transfers between devices  23.8 us (45%)
  starting transfers between devices  17.6 us (34%)
  Pallas kernels  7.11 us (14%)
  other arithmetic  2.96 us (6%)
  between operations  0.74 us (1%)
    ppermute x6, waiting for transfers between devices, flip_over(): return lax.ppermute(array, ('tm', 'state'), pairs)  18.4 us
    ppermute x6, starting transfers between devices, flip_over(): return lax.ppermute(array, ('tm', 'state'), pairs)  10.1 us
    ppermute x2, waiting for transfers between devices, ring(): lax.ppermute(array, 'grp', [(i, (i + step) % grp_size) for i in range(grp...  4.19 us
    ppermute x4, starting transfers between devices, across(): lax.ppermute(array, 'state', [(i, (i + 1) % state_size) for i in range(st...  3.83 us
    ppermute x2, starting transfers between devices, ring(): lax.ppermute(array, 'grp', [(i, (i + step) % grp_size) for i in range(grp...  3.11 us
    pallas_call x1, Pallas kernels, shards(): pl.pallas_call(functools.partial(assemble_kernel, tm_size), out_shape=(ja...  2.78 us
    pallas_call x1, Pallas kernels, run_group(): pl.pallas_call(chain_kernel, out_shape=(states_shape, states_shape), in_s...  2.27 us
    pallas_call x1, Pallas kernels, shards(): pl.pallas_call(gram_kernel, out_shape=[jax.ShapeDtypeStruct((4 * LANES +...  1.95 us
  transfers between devices with their start and end apart: 13, of which 9 were waited for; matrix products, arithmetic and copies ran while one was open for 4% of the time, Pallas kernels for 0%

profile of v7, /device:TPU:0, one launch (start us, length us, event | category | flops | bytes accessed | tf_op | source)
XLA Modules:
  0.0 52.3 jit_solution(17592796918333869393)
XLA Ops:
  0.7 0.5 collective-permute-start
  1.2 0.7 %iota_compare_fusion = pred[16,128]{1,0:T(8,128)(4,1)S(1)} fusion(s32[16]{0:T(128)} %bitcast.45), kind=kLoop, calls=%fused_computation.7 | loop fusion | flops 2048 | bytes 2112 | tf_op jit(solution)/shard_map/lt | solution.py:278
  1.9 1.5 %broadcast_select_fusion.own_ref = bf16[16,128,256]{2,1,0:T(8,128)(2,1)S(1)} fusion(pred[16,128]{1,0:T(8,128)(4,1)S(1)} %iota_compare_fusion, bf16[1,16,128,256]{3,2,1,0:T(8,128)(2,1)} %param.8), kind=kLoop, calls=%fused_computation | loop fusion | flops 524288 | bytes 2099200 | tf_op jit(solution)/shard_map/jit(_where)/select_n | solution.py:279
  3.5 0.2 collective-permute-done.other_ref
  3.7 2.0 %shard_map.95 = (bf16[528,128]{1,0:T(8,128)(2,1)S(1)}, bf16[528,128]{1,0:T(8,128)(2,1)S(1)}, bf16[528,128]{1,0:T(8,128)(2,1)S(1)}, bf16[528,128]{1,0:T(8,128)(2,1)S(1)}) custom-call(s32[16]{0:T(128)S(1)} %bitcast.43, bf16[16,128]{1,0:T(8,128)(2,1)S(1)} %bitcast.38, bf16[16,128,256]{2,1,0:T(8,128)(2,1)S(1)} %broadcast_select_fusion.own_ref, ...), custom_call_target="tpu_custom_call" | custom-call | tf_op jit(solution)/shard_map/pallas_call | solution.py:280
  5.6 5.1 %collective-permute-start.1 = (bf16[528,128]{1,0:T(8,128)(2,1)S(1)}, bf16[528,128]{1,0:T(8,128)(2,1)S(1)}, u32[]{:S(2)}, u32[]{:S(2)}) collective-permute-start(bf16[528,128]{1,0:T(8,128)(2,1)S(1)} %get-tuple-element.12), channel_id=1, source_target_pairs={{0,12},{1,9},{4,8},{5,13},{8,4},{9,1},{12,0},{13,5},{2,14},{3,11},... | collective-permute-start | bytes 405512 | tf_op jit(solution)/shard_map/ppermute | solution.py:269
  10.7 0.6 %collective-permute-start.3 = (bf16[528,128]{1,0:T(8,128)(2,1)S(1)}, bf16[528,128]{1,0:T(8,128)(2,1)S(1)}, u32[]{:S(2)}, u32[]{:S(2)}) collective-permute-start(bf16[528,128]{1,0:T(8,128)(2,1)S(1)} %get-tuple-element.14), channel_id=1, source_target_pairs={{0,4},{1,13},{4,0},{5,9},{8,12},{9,5},{12,8},{13,1},{2,6},{3,15},{... | collective-permute-start | bytes 405512 | tf_op jit(solution)/shard_map/ppermute | solution.py:269
  11.3 3.8 %collective-permute-done.1.refs_0_ = bf16[528,128]{1,0:T(8,128)(2,1)S(1)} collective-permute-done((bf16[528,128]{1,0:T(8,128)(2,1)S(1)}, bf16[528,128]{1,0:T(8,128)(2,1)S(1)}, u32[]{:S(2)}, u32[]{:S(2)}) %collective-permute-start.1) | collective-permute-done | bytes 135200 | tf_op jit(solution)/shard_map/ppermute | solution.py:269
  15.1 7.2 %collective-permute-done.2.refs_1_ = bf16[528,128]{1,0:T(8,128)(2,1)S(1)} collective-permute-done((bf16[528,128]{1,0:T(8,128)(2,1)S(1)}, bf16[528,128]{1,0:T(8,128)(2,1)S(1)}, u32[]{:S(2)}, u32[]{:S(2)}) %collective-permute-start.2) | collective-permute-done | bytes 135200 | tf_op jit(solution)/shard_map/ppermute | solution.py:269
  22.4 3.4 %collective-permute-start.4 = (bf16[544,128]{1,0:T(8,128)(2,1)S(1)}, bf16[544,128]{1,0:T(8,128)(2,1)S(1)}, u32[]{:S(2)}, u32[]{:S(2)}) collective-permute-start(bf16[544,128]{1,0:T(8,128)(2,1)S(1)} %shard_map.96.refs_3_), channel_id=1, source_target_pairs={{0,12},{1,9},{4,8},{5,13},{8,4},{9,1},{12,0},{13,5},{2,14},{3,11},... | collective-permute-start | bytes 417800 | tf_op jit(solution)/shard_map/ppermute | solution.py:269
  25.7 1.1 %collective-permute-start.6 = (bf16[544,128]{1,0:T(8,128)(2,1)S(1)}, bf16[544,128]{1,0:T(8,128)(2,1)S(1)}, u32[]{:S(2)}, u32[]{:S(2)}) collective-permute-start(bf16[544,128]{1,0:T(8,128)(2,1)S(1)} %shard_map.96.refs_3_), channel_id=1, source_target_pairs={{0,4},{1,13},{4,0},{5,9},{8,12},{9,5},{12,8},{13,1},{2,6},{3,15},{... | collective-permute-start | bytes 417800 | tf_op jit(solution)/shard_map/ppermute | solution.py:269
  26.8 4.1 %collective-permute-done.4.refs_0_ = bf16[544,128]{1,0:T(8,128)(2,1)S(1)} collective-permute-done((bf16[544,128]{1,0:T(8,128)(2,1)S(1)}, bf16[544,128]{1,0:T(8,128)(2,1)S(1)}, u32[]{:S(2)}, u32[]{:S(2)}) %collective-permute-start.4) | collective-permute-done | bytes 139296 | tf_op jit(solution)/shard_map/ppermute | solution.py:269
  30.9 3.3 %collective-permute-start.7 = (bf16[544,128]{1,0:T(8,128)(2,1)S(1)}, bf16[544,128]{1,0:T(8,128)(2,1)S(1)}, u32[]{:S(2)}, u32[]{:S(2)}) collective-permute-start(bf16[544,128]{1,0:T(8,128)(2,1)S(1)} %collective-permute-done.4.refs_0_), channel_id=1, source_target_pairs={{0,1},{1,0},{2,3},{3,2},{4,5},{5,4},{6,7},{7,6},{8,9},{9,8},{10,11... | collective-permute-start | bytes 417800 | tf_op jit(solution)/shard_map/ppermute | solution.py:275
  34.2 3.4 %collective-permute-done.5.refs_1_ = bf16[544,128]{1,0:T(8,128)(2,1)S(1)} collective-permute-done((bf16[544,128]{1,0:T(8,128)(2,1)S(1)}, bf16[544,128]{1,0:T(8,128)(2,1)S(1)}, u32[]{:S(2)}, u32[]{:S(2)}) %collective-permute-start.5) | collective-permute-done | bytes 139296 | tf_op jit(solution)/shard_map/ppermute | solution.py:269
  37.6 0.5 collective-permute-start.9
  38.1 0.8 %collective-permute-done.8.refs_5_ = bf16[544,128]{1,0:T(8,128)(2,1)S(1)} collective-permute-done((bf16[544,128]{1,0:T(8,128)(2,1)S(1)}, bf16[544,128]{1,0:T(8,128)(2,1)S(1)}, u32[]{:S(2)}, u32[]{:S(2)}) %collective-permute-start.8) | collective-permute-done | bytes 139296 | tf_op jit(solution)/shard_map/ppermute | solution.py:275
  39.0 0.2 collective-permute-done.9.refs_6_
  39.2 2.8 %shard_map.97 = (bf16[4,512,512]{2,1,0:T(8,128)(2,1)S(1)}, f32[4,5,512]{2,1,0:T(8,128)S(1)}, f32[4,512]{1,0:T(4,128)S(1)}, f32[4,512]{1,0:T(4,128)S(1)}) custom-call(bf16[544,128]{1,0:T(8,128)(2,1)S(1)} %collective-permute-done.4.refs_0_, bf16[544,128]{1,0:T(8,128)(2,1)S(1)} %collective-permute-done.5.refs_1_, ...), custom_call_target="tpu_custom_call" | custom-call | tf_op jit(solution)/shard_map/pallas_call | solution.py:305
  42.0 1.6 %collective-permute-start.11 = (f32[1,512]{1,0:T(1,128)S(1)}, f32[1,512]{1,0:T(1,128)S(1)}, u32[]{:S(2)}, u32[]{:S(2)}) collective-permute-start(f32[1,512]{1,0:T(1,128)S(1)} %slice.50), channel_id=1, source_target_pairs={{0,2},{2,0},{1,3},{3,1},{4,6},{6,4},{5,7},{7,5},{8,10},{10,8},{9,1... | collective-permute-start | bytes 6152 | tf_op jit(solution)/shard_map/ppermute | solution.py:272
  43.5 2.1 %collective-permute-done.11.state_ref = f32[1,512]{1,0:T(1,128)S(1)} collective-permute-done((f32[1,512]{1,0:T(1,128)S(1)}, f32[1,512]{1,0:T(1,128)S(1)}, u32[]{:S(2)}, u32[]{:S(2)}) %collective-permute-start.11) | collective-permute-done | bytes 2080 | tf_op jit(solution)/shard_map/ppermute | solution.py:272
  45.6 2.3 %shard_map.98 = (f32[4,512]{1,0:T(4,128)S(1)}, f32[4,512]{1,0:T(4,128)S(1)}) custom-call(bf16[4,512,512]{2,1,0:T(8,128)(2,1)S(1)} %get-tuple-element.16.grams, f32[4,5,512]{2,1,0:T(8,128)S(1)} %get-tuple-element.17.vectors, f32[1,512]{1,0:T(1,128)S(1)} %collective-permute-done.11.state_ref), custom_call_target="tpu_custom_call" | custom-call | tf_op jit(solution)/shard_map/pallas_call | solution.py:322
  47.9 1.6 %collective-permute-start.12 = (f32[1,512]{1,0:T(1,128)S(1)}, f32[1,512]{1,0:T(1,128)S(1)}, u32[]{:S(2)}, u32[]{:S(2)}) collective-permute-start(f32[1,512]{1,0:T(1,128)S(1)} %fusion), channel_id=1, source_target_pairs={{0,2},{2,0},{1,3},{3,1},{4,6},{6,4},{5,7},{7,5},{8,10},{10,8},{9,1... | collective-permute-start | bytes 6152 | tf_op jit(solution)/shard_map/ppermute | solution.py:272
  49.5 2.1 %collective-permute-done.12 = f32[1,512]{1,0:T(1,128)S(1)} collective-permute-done((f32[1,512]{1,0:T(1,128)S(1)}, f32[1,512]{1,0:T(1,128)S(1)}, u32[]{:S(2)}, u32[]{:S(2)}) %collective-permute-start.12) | collective-permute-done | bytes 2080 | tf_op jit(solution)/shard_map/ppermute | solution.py:272
  51.6 0.7 %add_bitcast_fusion = (f32[1,1,256]{2,1,0:T(1,128)}, f32[1,1,256]{2,1,0:T(1,128)}) fusion(s32[]{:T(128)S(6)} %select_n.47, s32[]{:T(128)S(6)} %select_n.48, f32[1,512]{1,0:T(1,128)S(1)} %get-tuple-element.25, f32[1,512]{1,0:T(1,128)S(1)} %get-tuple-element.24, f32[1,512]{1,0:T(1,128)S(1)} %get-tuple-element.23, f32[1,512]{1,0:T(1,128)S(1)} %get-tuple-element.22, ...), kind=kLoop, calls=%fused_computation.22 | loop fusion | flops 1024 | bytes 11272 | tf_op jit(solution)/shard_map/reshape | solution.py:393
  (26 shorter events, 0.2 us)
Async XLA Ops:
  0.6 3.0 %copy-start.5 = (s32[1,16,1]{1,2,0:T(1,128)S(1)}, s32[1,16,1]{1,2,0:T(1,128)}, u32[]{:S(2)}) copy-start(s32[1,16,1]{1,2,0:T(1,128)} %param.10) | copy-start | bytes 196
  0.6 3.0 %copy-start = (bf16[1,16,128]{2,1,0:T(8,128)(2,1)S(1)}, bf16[1,16,128]{2,1,0:T(8,128)(2,1)}, u32[]{:S(2)}) copy-start(bf16[1,16,128]{2,1,0:T(8,128)(2,1)} %param.9) | copy-start | bytes 12292
  0.7 3.0 %collective-permute-start = (bf16[16,128,256]{2,1,0:T(8,128)(2,1)}, bf16[16,128,256]{2,1,0:T(8,128)(2,1)S(1)}, u32[]{:S(2)}, u32[]{:S(2)}) collective-permute-start(bf16[16,128,256]{2,1,0:T(8,128)(2,1)} %bitcast.44), channel_id=1, source_target_pairs={{0,1},{1,0},{2,3},{3,2},{4,5},{5,4},{6,7},{7,6},{8,9},{9,8},{10,11... | collective-permute-start | bytes 3145736 | tf_op jit(solution)/shard_map/ppermute | solution.py:258
  1.9 20.3 %copy-start.1 = (f32[1,1,512]{2,1,0:T(1,128)S(1)}, f32[1,1,512]{2,1,0:T(1,128)}, u32[]{:S(2)}) copy-start(f32[1,1,512]{2,1,0:T(1,128)} %param.12) | copy-start | bytes 6148
  1.9 20.3 %copy-start.2 = (f32[1,1,512]{2,1,0:T(1,128)S(1)}, f32[1,1,512]{2,1,0:T(1,128)}, u32[]{:S(2)}) copy-start(f32[1,1,512]{2,1,0:T(1,128)} %param.13) | copy-start | bytes 6148
  1.9 20.3 %copy-start.3 = (f32[1,1,512]{2,1,0:T(1,128)S(1)}, f32[1,1,512]{2,1,0:T(1,128)}, u32[]{:S(2)}) copy-start(f32[1,1,512]{2,1,0:T(1,128)} %param.14) | copy-start | bytes 6148
  1.9 37.2 %copy-start.4 = (f32[512]{0:T(512)S(1)}, f32[512]{0:T(512)}, u32[]{:S(2)}) copy-start(f32[512]{0:T(512)} %param.15) | copy-start | bytes 6148
  5.6 9.4 %collective-permute-start.1 = (bf16[528,128]{1,0:T(8,128)(2,1)S(1)}, bf16[528,128]{1,0:T(8,128)(2,1)S(1)}, u32[]{:S(2)}, u32[]{:S(2)}) collective-permute-start(bf16[528,128]{1,0:T(8,128)(2,1)S(1)} %get-tuple-element.12), channel_id=1, source_target_pairs={{0,12},{1,9},{4,8},{5,13},{8,4},{9,1},{12,0},{13,5},{2,14},{3,11},... | collective-permute-start | bytes 405512 | tf_op jit(solution)/shard_map/ppermute | solution.py:269
  10.7 11.5 %collective-permute-start.2 = (bf16[528,128]{1,0:T(8,128)(2,1)S(1)}, bf16[528,128]{1,0:T(8,128)(2,1)S(1)}, u32[]{:S(2)}, u32[]{:S(2)}) collective-permute-start(bf16[528,128]{1,0:T(8,128)(2,1)S(1)} %get-tuple-element.13), channel_id=1, source_target_pairs={{0,8},{1,5},{4,12},{5,1},{8,0},{9,13},{12,4},{13,9},{2,10},{3,7},{... | collective-permute-start | bytes 405512 | tf_op jit(solution)/shard_map/ppermute | solution.py:269
  10.7 11.5 %collective-permute-start.3 = (bf16[528,128]{1,0:T(8,128)(2,1)S(1)}, bf16[528,128]{1,0:T(8,128)(2,1)S(1)}, u32[]{:S(2)}, u32[]{:S(2)}) collective-permute-start(bf16[528,128]{1,0:T(8,128)(2,1)S(1)} %get-tuple-element.14), channel_id=1, source_target_pairs={{0,4},{1,13},{4,0},{5,9},{8,12},{9,5},{12,8},{13,1},{2,6},{3,15},{... | collective-permute-start | bytes 405512 | tf_op jit(solution)/shard_map/ppermute | solution.py:269
  22.4 8.5 %collective-permute-start.4 = (bf16[544,128]{1,0:T(8,128)(2,1)S(1)}, bf16[544,128]{1,0:T(8,128)(2,1)S(1)}, u32[]{:S(2)}, u32[]{:S(2)}) collective-permute-start(bf16[544,128]{1,0:T(8,128)(2,1)S(1)} %shard_map.96.refs_3_), channel_id=1, source_target_pairs={{0,12},{1,9},{4,8},{5,13},{8,4},{9,1},{12,0},{13,5},{2,14},{3,11},... | collective-permute-start | bytes 417800 | tf_op jit(solution)/shard_map/ppermute | solution.py:269
  25.7 11.9 %collective-permute-start.5 = (bf16[544,128]{1,0:T(8,128)(2,1)S(1)}, bf16[544,128]{1,0:T(8,128)(2,1)S(1)}, u32[]{:S(2)}, u32[]{:S(2)}) collective-permute-start(bf16[544,128]{1,0:T(8,128)(2,1)S(1)} %shard_map.96.refs_3_), channel_id=1, source_target_pairs={{0,8},{1,5},{4,12},{5,1},{8,0},{9,13},{12,4},{13,9},{2,10},{3,7},{... | collective-permute-start | bytes 417800 | tf_op jit(solution)/shard_map/ppermute | solution.py:269
  25.7 11.9 %collective-permute-start.6 = (bf16[544,128]{1,0:T(8,128)(2,1)S(1)}, bf16[544,128]{1,0:T(8,128)(2,1)S(1)}, u32[]{:S(2)}, u32[]{:S(2)}) collective-permute-start(bf16[544,128]{1,0:T(8,128)(2,1)S(1)} %shard_map.96.refs_3_), channel_id=1, source_target_pairs={{0,4},{1,13},{4,0},{5,9},{8,12},{9,5},{12,8},{13,1},{2,6},{3,15},{... | collective-permute-start | bytes 417800 | tf_op jit(solution)/shard_map/ppermute | solution.py:269
  26.8 11.3 %collective-permute-start.10 = (bf16[544,128]{1,0:T(8,128)(2,1)S(1)}, bf16[544,128]{1,0:T(8,128)(2,1)S(1)}, u32[]{:S(2)}, u32[]{:S(2)}) collective-permute-start(bf16[544,128]{1,0:T(8,128)(2,1)S(1)} %shard_map.96.refs_3_), channel_id=1, source_target_pairs={{0,1},{1,0},{2,3},{3,2},{4,5},{5,4},{6,7},{7,6},{8,9},{9,8},{10,11... | collective-permute-start | bytes 417800 | tf_op jit(solution)/shard_map/ppermute | solution.py:275
  30.9 7.3 %collective-permute-start.7 = (bf16[544,128]{1,0:T(8,128)(2,1)S(1)}, bf16[544,128]{1,0:T(8,128)(2,1)S(1)}, u32[]{:S(2)}, u32[]{:S(2)}) collective-permute-start(bf16[544,128]{1,0:T(8,128)(2,1)S(1)} %collective-permute-done.4.refs_0_), channel_id=1, source_target_pairs={{0,1},{1,0},{2,3},{3,2},{4,5},{5,4},{6,7},{7,6},{8,9},{9,8},{10,11... | collective-permute-start | bytes 417800 | tf_op jit(solution)/shard_map/ppermute | solution.py:275
  37.6 1.4 %collective-permute-start.8 = (bf16[544,128]{1,0:T(8,128)(2,1)S(1)}, bf16[544,128]{1,0:T(8,128)(2,1)S(1)}, u32[]{:S(2)}, u32[]{:S(2)}) collective-permute-start(bf16[544,128]{1,0:T(8,128)(2,1)S(1)} %collective-permute-done.5.refs_1_), channel_id=1, source_target_pairs={{0,1},{1,0},{2,3},{3,2},{4,5},{5,4},{6,7},{7,6},{8,9},{9,8},{10,11... | collective-permute-start | bytes 417800 | tf_op jit(solution)/shard_map/ppermute | solution.py:275
  37.6 1.6 %collective-permute-start.9 = (bf16[544,128]{1,0:T(8,128)(2,1)S(1)}, bf16[544,128]{1,0:T(8,128)(2,1)S(1)}, u32[]{:S(2)}, u32[]{:S(2)}) collective-permute-start(bf16[544,128]{1,0:T(8,128)(2,1)S(1)} %collective-permute-done.6.refs_2_), channel_id=1, source_target_pairs={{0,1},{1,0},{2,3},{3,2},{4,5},{5,4},{6,7},{7,6},{8,9},{9,8},{10,11... | collective-permute-start | bytes 417800 | tf_op jit(solution)/shard_map/ppermute | solution.py:275
  42.0 3.7 %collective-permute-start.11 = (f32[1,512]{1,0:T(1,128)S(1)}, f32[1,512]{1,0:T(1,128)S(1)}, u32[]{:S(2)}, u32[]{:S(2)}) collective-permute-start(f32[1,512]{1,0:T(1,128)S(1)} %slice.50), channel_id=1, source_target_pairs={{0,2},{2,0},{1,3},{3,1},{4,6},{6,4},{5,7},{7,5},{8,10},{10,8},{9,1... | collective-permute-start | bytes 6152 | tf_op jit(solution)/shard_map/ppermute | solution.py:272
  47.9 3.7 %collective-permute-start.12 = (f32[1,512]{1,0:T(1,128)S(1)}, f32[1,512]{1,0:T(1,128)S(1)}, u32[]{:S(2)}, u32[]{:S(2)}) collective-permute-start(f32[1,512]{1,0:T(1,128)S(1)} %fusion), channel_id=1, source_target_pairs={{0,2},{2,0},{1,3},{3,1},{4,6},{6,4},{5,7},{7,5},{8,10},{10,8},{9,1... | collective-permute-start | bytes 6152 | tf_op jit(solution)/shard_map/ppermute | solution.py:272

commit v8 on v7

--- a/solution.py
+++ b/solution.py
@@ -26,6 +26,38 @@
         lower_cell = jnp.where(cell == width - 1, 0.0, pltpu.roll(field, width - 1, 1))
         field = field + coeff * (upper_cell + lower_cell - 2.0 * field) - decay * field
     return field
+
+
+def band_of(coeff, decay):
+    width = coeff.shape[1]
+    cell = lax.broadcasted_iota(jnp.int32, coeff.shape, 1)
+    from_upper = jnp.where(cell == 0, 0.0, coeff)
+    from_lower = jnp.where(cell == width - 1, 0.0, coeff)
+    stay = 1.0 - 2.0 * coeff - decay
+    band = {-1: from_upper, 0: stay, 1: from_lower}
+    for _ in range(STEPS - 1):
+        longer = {}
+        for offset, values in band.items():
+            for step, weight, turned in (
+                (-1, from_upper, lambda: pltpu.roll(values, 1, 1)),
+                (0, stay, lambda: values),
+                (1, from_lower, lambda: pltpu.roll(values, width - 1, 1)),
+            ):
+                term = weight * turned()
+                longer[offset + step] = longer[offset + step] + term if offset + step in longer else term
+        band = longer
+    return [band[offset] for offset in range(-STEPS, STEPS + 1)]
+
+
+def apply_band(field, band):
+    width = field.shape[1]
+    total = band[STEPS : STEPS + 1] * field
+    for offset in range(1, STEPS + 1):
+        total = total + (
+            band[STEPS - offset : STEPS - offset + 1] * pltpu.roll(field, offset, 1)
+            + band[STEPS + offset : STEPS + offset + 1] * pltpu.roll(field, width - offset, 1)
+        )
+    return total
 
 
 def row_pass(block, state, meta, y_ref, own_ref, other_ref, acc, part_ref):
@@ -114,7 +146,7 @@
     return jnp.where(lax.axis_index("state") == beside, on_core[0], on_core[1])
 
 
-def gram_kernel(blocks, y_ref, own_ref, other_ref, *refs):
+def gram_kernel(blocks, y_ref, own_ref, other_ref, kappa_ref, rate_ref, gain_ref, *refs):
     outs, (acc, vec, side, readings) = refs[:-4], refs[-4:]
     tile_num, row_num, _ = own_ref.shape
     number = len(outs)
@@ -159,37 +191,56 @@
             values.append(
                 jnp.sum(jnp.where(line == column, take(piece), 0.0), axis=0, keepdims=True)
             )
+        for coefficient in (kappa_ref, rate_ref, gain_ref):
+            for piece in range(2):
+                at = pl.multiple_of((2 * core + piece) * LANES, LANES)
+                values.append(coefficient[:, pl.ds(at, LANES)])
         for at, value in enumerate(values):
             for which, part in enumerate(pieces_of(value)):
-                side[which * 4 + at : which * 4 + at + 1, :] = part
+                side[which * VECTORS + at : which * VECTORS + at + 1, :] = part
         out_ref[4 * LANES :] = side[...].astype(jnp.bfloat16)
 
 
-def sum_kernel(kappa_ref, rate_ref, gain_ref, *refs):
-    parts, out_ref, side = refs[:-2], refs[-2], refs[-1]
+def sum_kernel(*refs):
+    parts, (out_ref, coefficients, side) = refs[:-3], refs[-3:]
+    number = len(parts)
+    position = lax.axis_index("tm")
+    total = parts[0][: 4 * LANES].astype(jnp.float32)
+    for part in parts[1:]:
+        total = total + part[: 4 * LANES].astype(jnp.float32)
+    out_ref[: 4 * LANES] = total.astype(jnp.bfloat16)
+    values = None
+    for turn, part in enumerate(parts):
+        below = part[4 * LANES :].astype(jnp.float32)
+        below = below[:VECTORS] + below[VECTORS : 2 * VECTORS] + below[2 * VECTORS : 3 * VECTORS]
+        coefficients[position ^ flip_here(turn, number), 0 : VECTORS - 4] = below[4:]
+        values = below[:4] if values is None else values + below[:4]
+    side[...] = jnp.zeros_like(side)
+    for which, part in enumerate(pieces_of(values)):
+        side[which * 4 : which * 4 + 4, :] = part
+    out_ref[4 * LANES :] = side[...].astype(jnp.bfloat16)
+
+
+def band_kernel(here_ref, there_ref, band_ref, whole):
     core = lax.axis_index("state")
-    total = parts[0][...].astype(jnp.float32)
-    for part in parts[1:]:
-        total = total + part[...].astype(jnp.float32)
-    out_ref[: 4 * LANES] = total[: 4 * LANES].astype(jnp.bfloat16)
-    below = total[4 * LANES :]
-    values = [below[at : at + 1] + below[at + 4 : at + 5] + below[at + 8 : at + 9] for at in range(4)]
-    for coefficient in (kappa_ref, rate_ref, gain_ref):
-        for piece in range(2):
-            at = pl.multiple_of((2 * core + piece) * LANES, LANES)
-            values.append(coefficient[:, pl.ds(at, LANES)])
-    side[...] = jnp.zeros_like(side)
-    for at, value in enumerate(values):
-        for which, part in enumerate(pieces_of(value)):
-            side[which * VECTORS + at : which * VECTORS + at + 1, :] = part
-    out_ref[4 * LANES :] = side[...].astype(jnp.bfloat16)
-
-
-def chain(grams, vectors, state, states_ref, innovations_ref):
+    block_num = here_ref.shape[0]
+    for source, side in ((here_ref, core), (there_ref, 1 - core)):
+        for block in range(block_num):
+            for at in range(VECTORS - 4):
+                lanes = pl.ds(pl.multiple_of((2 * side + at % 2) * LANES, LANES), LANES)
+                whole[at // 2, block : block + 1, lanes] = source[block, at : at + 1]
+    band = band_of(whole[0], whole[1]) + [whole[2]]
+    for at, values in enumerate(band):
+        for block in range(block_num):
+            band_ref[block, at : at + 1, :] = values[block : block + 1]
+
+
+def chain(grams, vectors, bands, state, states_ref, innovations_ref):
     width = state.shape[1]
     line = lax.broadcasted_iota(jnp.int32, (16, width), 0)
     for block in range(grams.shape[0]):
-        info, diagonal, coeff, decay = (vectors[block, which : which + 1, :] for which in range(4))
+        info, diagonal = vectors[block, 0:1, :], vectors[block, 1:2, :]
+        band = bands[block, : 2 * STEPS + 1, :]
         high, middle, low = pieces_of(state)
         split = jnp.where(line == 0, high, jnp.where(line == 1, middle, jnp.where(line == 2, low, 0.0)))
         product = jnp.dot(
@@ -198,15 +249,15 @@
         product = jnp.sum(product, axis=0, keepdims=True) + diagonal * state
         trace_val = jnp.sum(diagonal, axis=1, keepdims=True)
         lam_val = width / (2.0 * (width + trace_val))
-        innovation = -lam_val * stencil(product - info, coeff, decay)
-        state = stencil(state, coeff, decay) + innovation
+        innovation = -lam_val * apply_band(product - info, band)
+        state = apply_band(state, band) + innovation
         states_ref[block : block + 1, :] = state
         innovations_ref[block : block + 1, :] = innovation
 
 
 def assemble_kernel(number, *refs):
     own, other, rest = refs[:number], refs[number : 2 * number], refs[2 * number :]
-    state_ref, grams, vectors, states_ref, innovations_ref = rest
+    bands, state_ref, grams, vectors, states_ref, innovations_ref = rest
     core, position = lax.axis_index("state"), lax.axis_index("tm")
     half = 2 * LANES
     line = lax.broadcasted_iota(jnp.int32, (LANES, LANES), 0)
@@ -237,15 +288,15 @@
                 put(here + index * LANES, beyond, piece(2 + index))
                 put(beyond, here + index * LANES, piece(2 + index).T)
             below = pieces[4 * LANES :, :].astype(jnp.float32)
-            below = below[:VECTORS] + below[VECTORS : 2 * VECTORS] + below[2 * VECTORS : 3 * VECTORS]
-            for at in range(VECTORS):
+            below = below[:4] + below[4:8] + below[8:12]
+            for at in range(4):
                 lanes = pl.ds(pl.multiple_of(here + (at % 2) * LANES, LANES), LANES)
                 vectors[block, at // 2 : at // 2 + 1, lanes] = below[at : at + 1]
-    chain(grams, vectors, state_ref[...], states_ref, innovations_ref)
-
-
-def chain_kernel(grams, vectors, state_ref, states_ref, innovations_ref):
-    chain(grams, vectors, state_ref[...], states_ref, innovations_ref)
+    chain(grams, vectors, bands, state_ref[...], states_ref, innovations_ref)
+
+
+def chain_kernel(grams, vectors, bands, state_ref, states_ref, innovations_ref):
+    chain(grams, vectors, bands, state_ref[...], states_ref, innovations_ref)
 
 
 def shards(rows_h, rows_y, tile_block, tile_count, kappa, rate, smooth_gain, start_state):
@@ -279,42 +330,52 @@
         valid = jnp.where(live[:, :, None], own, jnp.zeros((), own.dtype))
         pieces = pl.pallas_call(
             gram_kernel,
-            out_shape=[jax.ShapeDtypeStruct((4 * LANES + 16, LANES), jnp.bfloat16)] * tm_size,
-            in_specs=[SMEM] + [VMEM] * 3,
+            out_shape=[jax.ShapeDtypeStruct((4 * LANES + 32, LANES), jnp.bfloat16)] * tm_size,
+            in_specs=[SMEM] + [VMEM] * 6,
             out_specs=[VMEM] * tm_size,
             scratch_shapes=[
                 pltpu.VMEM((tm_size, 5 * LANES, LANES), jnp.float32),
                 pltpu.VMEM((tm_size, 8, half), jnp.float32),
-                pltpu.VMEM((16, LANES), jnp.float32),
+                pltpu.VMEM((32, LANES), jnp.float32),
                 pltpu.VMEM((tile_num, row_num), jnp.float32),
             ],
             compiler_params=KERNEL,
-        )(tile_block[0, :, 0], rows_y[0], valid, other)
+        )(tile_block[0, :, 0], rows_y[0], valid, other, kappa[0], rate[0], smooth_gain[0])
         turns = range(tm_size - 1)
         parts = [flip_over(pieces[turn], turn) for turn in turns] + [pieces[-1]]
-        own_sum = pl.pallas_call(
+        half_coefficients = jax.ShapeDtypeStruct((tm_size, 8, LANES), jnp.float32)
+        own_sum, here = pl.pallas_call(
             sum_kernel,
-            out_shape=jax.ShapeDtypeStruct((4 * LANES + 32, LANES), jnp.bfloat16),
-            in_specs=[VMEM] * (tm_size + 3),
+            out_shape=(jax.ShapeDtypeStruct((4 * LANES + 16, LANES), jnp.bfloat16), half_coefficients),
+            in_specs=[VMEM] * tm_size,
+            out_specs=(VMEM, VMEM),
+            scratch_shapes=[pltpu.VMEM((16, LANES), jnp.float32)],
+            compiler_params=KERNEL,
+        )(*parts)
+        own_sums = [flip_over(own_sum, turn) for turn in turns] + [own_sum]
+        here, own_sums[0] = lax.optimization_barrier((here, own_sums[0]))
+        bands = pl.pallas_call(
+            band_kernel,
+            out_shape=jax.ShapeDtypeStruct((tm_size, 16, width), jnp.float32),
+            in_specs=[VMEM, VMEM],
             out_specs=VMEM,
-            scratch_shapes=[pltpu.VMEM((32, LANES), jnp.float32)],
+            scratch_shapes=[pltpu.VMEM((3, tm_size, width), jnp.float32)],
             compiler_params=KERNEL,
-        )(kappa[0], rate[0], smooth_gain[0], *parts)
-        own_sums = [flip_over(own_sum, turn) for turn in turns] + [own_sum]
+        )(here, across(here))
         other_sums = [across(values) for values in own_sums]
         grams, vectors, new_states, new_innovations = pl.pallas_call(
             functools.partial(assemble_kernel, tm_size),
             out_shape=(
                 jax.ShapeDtypeStruct((tm_size, width, width), jnp.bfloat16),
-                jax.ShapeDtypeStruct((tm_size, VECTORS // 2, width), jnp.float32),
+                jax.ShapeDtypeStruct((tm_size, 8, width), jnp.float32),
                 states_shape,
                 states_shape,
             ),
-            in_specs=[VMEM] * (2 * tm_size + 1),
+            in_specs=[VMEM] * (2 * tm_size + 2),
             out_specs=[VMEM] * 4,
             compiler_params=KERNEL,
-        )(*own_sums, *other_sums, state)
-        gains = vectors[:, 4]
+        )(*own_sums, *other_sums, bands, state)
+        gains = bands[:, 2 * STEPS + 1]
 
         def run_group(state, group):
             if group == 0:
@@ -322,10 +383,10 @@
             return pl.pallas_call(
                 chain_kernel,
                 out_shape=(states_shape, states_shape),
-                in_specs=[VMEM] * 3,
+                in_specs=[VMEM] * 4,
                 out_specs=(VMEM, VMEM),
                 compiler_params=KERNEL,
-            )(grams, vectors, state)
+            )(grams, vectors, bands, state)
     else:
         readings = rows_y[0].astype(jnp.float32)
         meta = jnp.concatenate(

time: 52.4 us -> 50.8 us (0.969)
  Pallas kernels: 7.11 us -> 5.28 us
    pallas_call x1, Pallas kernels: 2.27 us -> 1.17 us  [run_group(): pl.pallas_call(chain_kernel, out_shape=(states_shape, states_shape), in_s...]
    pallas_call x1, Pallas kernels: 2.78 us -> 1.71 us  [shards(): pl.pallas_call(functools.partial(assemble_kernel, tm_size), out_shape=(ja...]
    ppermute x4 -> x5, starting transfers between devices: 3.83 us -> 3.66 us  [across(): lax.ppermute(array, 'state', [(i, (i + 1) % state_size) for i in range(st...]
    ppermute x4 -> x5, waiting for transfers between devices: 1.04 us -> 1.19 us  [across(): lax.ppermute(array, 'state', [(i, (i + 1) % state_size) for i in range(st...]
  transfers between devices with their start and end apart: 13 -> 14, of which waited for: 9 -> 8; matrix products, arithmetic and copies ran while one was open for 4% -> 4% of each run, Pallas kernels for 0% -> 1%
where the time goes in v8:
time: 50.8 us; the launch traced here: 50.7 us
  waiting for transfers between devices  24.2 us (48%)
  starting transfers between devices  17.4 us (34%)
  Pallas kernels  5.28 us (10%)
  other arithmetic  2.94 us (6%)
  between operations  0.79 us (2%)
    ppermute x6, waiting for transfers between devices, flip_over(): return lax.ppermute(array, ('tm', 'state'), pairs)  18.6 us
    ppermute x6, starting transfers between devices, flip_over(): return lax.ppermute(array, ('tm', 'state'), pairs)  10.1 us
    ppermute x2, waiting for transfers between devices, ring(): lax.ppermute(array, 'grp', [(i, (i + step) % grp_size) for i in range(grp...  4.19 us
    ppermute x5, starting transfers between devices, across(): lax.ppermute(array, 'state', [(i, (i + 1) % state_size) for i in range(st...  3.66 us
    ppermute x2, starting transfers between devices, ring(): lax.ppermute(array, 'grp', [(i, (i + step) % grp_size) for i in range(grp...  3.11 us
    pallas_call x1, Pallas kernels, shards(): pl.pallas_call(gram_kernel, out_shape=[jax.ShapeDtypeStruct((4 * LANES +...  1.96 us
    pallas_call x1, Pallas kernels, shards(): pl.pallas_call(functools.partial(assemble_kernel, tm_size), out_shape=(ja...  1.71 us
    select_n x1, other arithmetic, shards(): valid = jnp.where(live[:, :, None], own, jnp.zeros((), own.dtype))  1.5 us
  transfers between devices with their start and end apart: 14, of which 8 were waited for; matrix products, arithmetic and copies ran while one was open for 4% of the time, Pallas kernels for 1%

profile of v8, /device:TPU:0, one launch (start us, length us, event | category | flops | bytes accessed | tf_op | source)
XLA Modules:
  0.0 50.7 jit_solution(16110913193489484929)
XLA Ops:
  0.7 0.5 %collective-permute-start = (bf16[16,128,256]{2,1,0:T(8,128)(2,1)}, bf16[16,128,256]{2,1,0:T(8,128)(2,1)S(1)}, u32[]{:S(2)}, u32[]{:S(2)}) collective-permute-start(bf16[16,128,256]{2,1,0:T(8,128)(2,1)} %bitcast.43), channel_id=1, source_target_pairs={{0,1},{1,0},{2,3},{3,2},{4,5},{5,4},{6,7},{7,6},{8,9},{9,8},{10,11... | collective-permute-start | bytes 3145736 | tf_op jit(solution)/shard_map/ppermute | solution.py:309
  1.2 0.7 %iota_compare_fusion = pred[16,128]{1,0:T(8,128)(4,1)S(1)} fusion(s32[16]{0:T(128)} %bitcast.44), kind=kLoop, calls=%fused_computation.7 | loop fusion | flops 2048 | bytes 2112 | tf_op jit(solution)/shard_map/lt | solution.py:329
  1.9 1.5 %broadcast_select_fusion.own_ref = bf16[16,128,256]{2,1,0:T(8,128)(2,1)S(1)} fusion(pred[16,128]{1,0:T(8,128)(4,1)S(1)} %iota_compare_fusion, bf16[1,16,128,256]{3,2,1,0:T(8,128)(2,1)} %param.8), kind=kLoop, calls=%fused_computation | loop fusion | flops 524288 | bytes 2099200 | tf_op jit(solution)/shard_map/jit(_where)/select_n | solution.py:330
  3.4 0.3 collective-permute-done.other_ref
  3.7 2.0 %shard_map.95 = (bf16[544,128]{1,0:T(8,128)(2,1)S(1)}, bf16[544,128]{1,0:T(8,128)(2,1)S(1)}, bf16[544,128]{1,0:T(8,128)(2,1)S(1)}, bf16[544,128]{1,0:T(8,128)(2,1)S(1)}) custom-call(s32[16]{0:T(128)S(1)} %bitcast.42, bf16[16,128]{1,0:T(8,128)(2,1)S(1)} %bitcast.37, bf16[16,128,256]{2,1,0:T(8,128)(2,1)S(1)} %broadcast_select_fusion.own_ref, ...), custom_call_target="tpu_custom_call" | custom-call | tf_op jit(solution)/shard_map/pallas_call | solution.py:331
  5.7 5.1 %collective-permute-start.1 = (bf16[544,128]{1,0:T(8,128)(2,1)S(1)}, bf16[544,128]{1,0:T(8,128)(2,1)S(1)}, u32[]{:S(2)}, u32[]{:S(2)}) collective-permute-start(bf16[544,128]{1,0:T(8,128)(2,1)S(1)} %get-tuple-element.16), channel_id=1, source_target_pairs={{0,12},{1,9},{4,8},{5,13},{8,4},{9,1},{12,0},{13,5},{2,14},{3,11},... | collective-permute-start | bytes 417800 | tf_op jit(solution)/shard_map/ppermute | solution.py:320
  10.7 0.6 %collective-permute-start.3 = (bf16[544,128]{1,0:T(8,128)(2,1)S(1)}, bf16[544,128]{1,0:T(8,128)(2,1)S(1)}, u32[]{:S(2)}, u32[]{:S(2)}) collective-permute-start(bf16[544,128]{1,0:T(8,128)(2,1)S(1)} %get-tuple-element.18), channel_id=1, source_target_pairs={{0,4},{1,13},{4,0},{5,9},{8,12},{9,5},{12,8},{13,1},{2,6},{3,15},{... | collective-permute-start | bytes 417800 | tf_op jit(solution)/shard_map/ppermute | solution.py:320
  11.4 3.9 %collective-permute-done.1.refs_0_ = bf16[544,128]{1,0:T(8,128)(2,1)S(1)} collective-permute-done((bf16[544,128]{1,0:T(8,128)(2,1)S(1)}, bf16[544,128]{1,0:T(8,128)(2,1)S(1)}, u32[]{:S(2)}, u32[]{:S(2)}) %collective-permute-start.1) | collective-permute-done | bytes 139296 | tf_op jit(solution)/shard_map/ppermute | solution.py:320
  15.2 7.4 %collective-permute-done.2.refs_1_ = bf16[544,128]{1,0:T(8,128)(2,1)S(1)} collective-permute-done((bf16[544,128]{1,0:T(8,128)(2,1)S(1)}, bf16[544,128]{1,0:T(8,128)(2,1)S(1)}, u32[]{:S(2)}, u32[]{:S(2)}) %collective-permute-start.2) | collective-permute-done | bytes 139296 | tf_op jit(solution)/shard_map/ppermute | solution.py:320
  22.8 3.4 %collective-permute-start.4 = (bf16[528,128]{1,0:T(8,128)(2,1)S(1)}, bf16[528,128]{1,0:T(8,128)(2,1)S(1)}, u32[]{:S(2)}, u32[]{:S(2)}) collective-permute-start(bf16[528,128]{1,0:T(8,128)(2,1)S(1)} %get-tuple-element.21.refs_3_), channel_id=1, source_target_pairs={{0,12},{1,9},{4,8},{5,13},{8,4},{9,1},{12,0},{13,5},{2,14},{3,11},... | collective-permute-start | bytes 405512 | tf_op jit(solution)/shard_map/ppermute | solution.py:320
  26.1 1.1 %collective-permute-start.6 = (bf16[528,128]{1,0:T(8,128)(2,1)S(1)}, bf16[528,128]{1,0:T(8,128)(2,1)S(1)}, u32[]{:S(2)}, u32[]{:S(2)}) collective-permute-start(bf16[528,128]{1,0:T(8,128)(2,1)S(1)} %get-tuple-element.21.refs_3_), channel_id=1, source_target_pairs={{0,4},{1,13},{4,0},{5,9},{8,12},{9,5},{12,8},{13,1},{2,6},{3,15},{... | collective-permute-start | bytes 405512 | tf_op jit(solution)/shard_map/ppermute | solution.py:320
  27.2 4.0 %collective-permute-done.4.refs_0_ = bf16[528,128]{1,0:T(8,128)(2,1)S(1)} collective-permute-done((bf16[528,128]{1,0:T(8,128)(2,1)S(1)}, bf16[528,128]{1,0:T(8,128)(2,1)S(1)}, u32[]{:S(2)}, u32[]{:S(2)}) %collective-permute-start.4) | collective-permute-done | bytes 135200 | tf_op jit(solution)/shard_map/ppermute | solution.py:320
  31.2 3.1 %collective-permute-start.7 = (bf16[528,128]{1,0:T(8,128)(2,1)S(1)}, bf16[528,128]{1,0:T(8,128)(2,1)S(1)}, u32[]{:S(2)}, u32[]{:S(2)}) collective-permute-start(bf16[528,128]{1,0:T(8,128)(2,1)S(1)} %collective-permute-done.4.refs_0_), channel_id=1, source_target_pairs={{0,1},{1,0},{2,3},{3,2},{4,5},{5,4},{6,7},{7,6},{8,9},{9,8},{10,11... | collective-permute-start | bytes 405512 | tf_op jit(solution)/shard_map/ppermute | solution.py:326
  34.3 3.3 %collective-permute-done.5.refs_1_ = bf16[528,128]{1,0:T(8,128)(2,1)S(1)} collective-permute-done((bf16[528,128]{1,0:T(8,128)(2,1)S(1)}, bf16[528,128]{1,0:T(8,128)(2,1)S(1)}, u32[]{:S(2)}, u32[]{:S(2)}) %collective-permute-start.5) | collective-permute-done | bytes 135200 | tf_op jit(solution)/shard_map/ppermute | solution.py:320
  37.7 0.5 %collective-permute-start.9 = (bf16[528,128]{1,0:T(8,128)(2,1)S(1)}, bf16[528,128]{1,0:T(8,128)(2,1)S(1)}, u32[]{:S(2)}, u32[]{:S(2)}) collective-permute-start(bf16[528,128]{1,0:T(8,128)(2,1)S(1)} %collective-permute-done.6.refs_2_), channel_id=1, source_target_pairs={{0,1},{1,0},{2,3},{3,2},{4,5},{5,4},{6,7},{7,6},{8,9},{9,8},{10,11... | collective-permute-start | bytes 405512 | tf_op jit(solution)/shard_map/ppermute | solution.py:326
  38.2 1.2 %collective-permute-done.11.there_ref = f32[4,8,128]{2,1,0:T(8,128)S(1)} collective-permute-done((f32[4,8,128]{2,1,0:T(8,128)S(1)}, f32[4,8,128]{2,1,0:T(8,128)S(1)}, u32[]{:S(2)}, u32[]{:S(2)}) %collective-permute-start.11) | collective-permute-done | bytes 16416 | tf_op jit(solution)/shard_map/ppermute | solution.py:326
  39.3 0.3 shard_map.97.refs_8_.bands
  39.7 1.7 %shard_map.98 = (bf16[4,512,512]{2,1,0:T(8,128)(2,1)S(1)}, f32[4,8,512]{2,1,0:T(8,128)S(1)}, f32[4,512]{1,0:T(4,128)S(1)}, f32[4,512]{1,0:T(4,128)S(1)}) custom-call(bf16[528,128]{1,0:T(8,128)(2,1)S(1)} %collective-permute-done.4.refs_0_, bf16[528,128]{1,0:T(8,128)(2,1)S(1)} %collective-permute-done.5.refs_1_, ...), custom_call_target="tpu_custom_call" | custom-call | tf_op jit(solution)/shard_map/pallas_call | solution.py:366
  41.5 1.6 %collective-permute-start.12 = (f32[1,512]{1,0:T(1,128)S(1)}, f32[1,512]{1,0:T(1,128)S(1)}, u32[]{:S(2)}, u32[]{:S(2)}) collective-permute-start(f32[1,512]{1,0:T(1,128)S(1)} %slice.50), channel_id=1, source_target_pairs={{0,2},{2,0},{1,3},{3,1},{4,6},{6,4},{5,7},{7,5},{8,10},{10,8},{9,1... | collective-permute-start | bytes 6152 | tf_op jit(solution)/shard_map/ppermute | solution.py:323
  43.0 2.1 %collective-permute-done.12.state_ref = f32[1,512]{1,0:T(1,128)S(1)} collective-permute-done((f32[1,512]{1,0:T(1,128)S(1)}, f32[1,512]{1,0:T(1,128)S(1)}, u32[]{:S(2)}, u32[]{:S(2)}) %collective-permute-start.12) | collective-permute-done | bytes 2080 | tf_op jit(solution)/shard_map/ppermute | solution.py:323
  45.1 1.2 %shard_map.99 = (f32[4,512]{1,0:T(4,128)S(1)}, f32[4,512]{1,0:T(4,128)S(1)}) custom-call(bf16[4,512,512]{2,1,0:T(8,128)(2,1)S(1)} %get-tuple-element.24.grams, f32[4,8,512]{2,1,0:T(8,128)S(1)} %get-tuple-element.25.vectors, f32[4,16,512]{2,1,0:T(8,128)S(1)} %shard_map.97.refs_8_.bands, f32[1,512]{1,0:T(1,128)S(1)} %collective-permute-done.12.state_ref), custom_call_target="tpu_custom_call" | custom-call | tf_op jit(solution)/shard_map/pallas_call | solution.py:383
  46.3 1.6 %collective-permute-start.13 = (f32[1,512]{1,0:T(1,128)S(1)}, f32[1,512]{1,0:T(1,128)S(1)}, u32[]{:S(2)}, u32[]{:S(2)}) collective-permute-start(f32[1,512]{1,0:T(1,128)S(1)} %fusion), channel_id=1, source_target_pairs={{0,2},{2,0},{1,3},{3,1},{4,6},{6,4},{5,7},{7,5},{8,10},{10,8},{9,1... | collective-permute-start | bytes 6152 | tf_op jit(solution)/shard_map/ppermute | solution.py:323
  47.9 2.1 %collective-permute-done.13 = f32[1,512]{1,0:T(1,128)S(1)} collective-permute-done((f32[1,512]{1,0:T(1,128)S(1)}, f32[1,512]{1,0:T(1,128)S(1)}, u32[]{:S(2)}, u32[]{:S(2)}) %collective-permute-start.13) | collective-permute-done | bytes 2080 | tf_op jit(solution)/shard_map/ppermute | solution.py:323
  50.0 0.7 %add_bitcast_fusion = (f32[1,1,256]{2,1,0:T(1,128)}, f32[1,1,256]{2,1,0:T(1,128)}) fusion(s32[]{:T(128)S(6)} %select_n.47, s32[]{:T(128)S(6)} %select_n.48, f32[1,512]{1,0:T(1,128)S(1)} %get-tuple-element.33, f32[1,512]{1,0:T(1,128)S(1)} %get-tuple-element.32, f32[1,512]{1,0:T(1,128)S(1)} %get-tuple-element.31, f32[1,512]{1,0:T(1,128)S(1)} %get-tuple-element.30, ...), kind=kLoop, calls=%fused_computation.21 | loop fusion | flops 1024 | bytes 11272 | tf_op jit(solution)/shard_map/reshape | solution.py:454
  (29 shorter events, 0.2 us)
Async XLA Ops:
  0.6 3.1 %copy-start.5 = (s32[1,16,1]{1,2,0:T(1,128)S(1)}, s32[1,16,1]{1,2,0:T(1,128)}, u32[]{:S(2)}) copy-start(s32[1,16,1]{1,2,0:T(1,128)} %param.10) | copy-start | bytes 196
  0.6 3.1 %copy-start = (bf16[1,16,128]{2,1,0:T(8,128)(2,1)S(1)}, bf16[1,16,128]{2,1,0:T(8,128)(2,1)}, u32[]{:S(2)}) copy-start(bf16[1,16,128]{2,1,0:T(8,128)(2,1)} %param.9) | copy-start | bytes 12292
  0.7 3.1 %copy-start.2 = (f32[1,1,512]{2,1,0:T(1,128)S(1)}, f32[1,1,512]{2,1,0:T(1,128)}, u32[]{:S(2)}) copy-start(f32[1,1,512]{2,1,0:T(1,128)} %param.12) | copy-start | bytes 6148
  0.7 3.0 %copy-start.3 = (f32[1,1,512]{2,1,0:T(1,128)S(1)}, f32[1,1,512]{2,1,0:T(1,128)}, u32[]{:S(2)}) copy-start(f32[1,1,512]{2,1,0:T(1,128)} %param.13) | copy-start | bytes 6148
  0.7 3.0 %copy-start.4 = (f32[1,1,512]{2,1,0:T(1,128)S(1)}, f32[1,1,512]{2,1,0:T(1,128)}, u32[]{:S(2)}) copy-start(f32[1,1,512]{2,1,0:T(1,128)} %param.14) | copy-start | bytes 6148
  0.7 3.0 %collective-permute-start = (bf16[16,128,256]{2,1,0:T(8,128)(2,1)}, bf16[16,128,256]{2,1,0:T(8,128)(2,1)S(1)}, u32[]{:S(2)}, u32[]{:S(2)}) collective-permute-start(bf16[16,128,256]{2,1,0:T(8,128)(2,1)} %bitcast.43), channel_id=1, source_target_pairs={{0,1},{1,0},{2,3},{3,2},{4,5},{5,4},{6,7},{7,6},{8,9},{9,8},{10,11... | collective-permute-start | bytes 3145736 | tf_op jit(solution)/shard_map/ppermute | solution.py:309
  1.9 37.8 %copy-start.1 = (f32[512]{0:T(512)S(1)}, f32[512]{0:T(512)}, u32[]{:S(2)}) copy-start(f32[512]{0:T(512)} %param.15) | copy-start | bytes 6148
  5.7 9.5 %collective-permute-start.1 = (bf16[544,128]{1,0:T(8,128)(2,1)S(1)}, bf16[544,128]{1,0:T(8,128)(2,1)S(1)}, u32[]{:S(2)}, u32[]{:S(2)}) collective-permute-start(bf16[544,128]{1,0:T(8,128)(2,1)S(1)} %get-tuple-element.16), channel_id=1, source_target_pairs={{0,12},{1,9},{4,8},{5,13},{8,4},{9,1},{12,0},{13,5},{2,14},{3,11},... | collective-permute-start | bytes 417800 | tf_op jit(solution)/shard_map/ppermute | solution.py:320
  10.7 11.9 %collective-permute-start.2 = (bf16[544,128]{1,0:T(8,128)(2,1)S(1)}, bf16[544,128]{1,0:T(8,128)(2,1)S(1)}, u32[]{:S(2)}, u32[]{:S(2)}) collective-permute-start(bf16[544,128]{1,0:T(8,128)(2,1)S(1)} %get-tuple-element.17), channel_id=1, source_target_pairs={{0,8},{1,5},{4,12},{5,1},{8,0},{9,13},{12,4},{13,9},{2,10},{3,7},{... | collective-permute-start | bytes 417800 | tf_op jit(solution)/shard_map/ppermute | solution.py:320
  10.7 11.9 %collective-permute-start.3 = (bf16[544,128]{1,0:T(8,128)(2,1)S(1)}, bf16[544,128]{1,0:T(8,128)(2,1)S(1)}, u32[]{:S(2)}, u32[]{:S(2)}) collective-permute-start(bf16[544,128]{1,0:T(8,128)(2,1)S(1)} %get-tuple-element.18), channel_id=1, source_target_pairs={{0,4},{1,13},{4,0},{5,9},{8,12},{9,5},{12,8},{13,1},{2,6},{3,15},{... | collective-permute-start | bytes 417800 | tf_op jit(solution)/shard_map/ppermute | solution.py:320
  22.8 8.4 %collective-permute-start.4 = (bf16[528,128]{1,0:T(8,128)(2,1)S(1)}, bf16[528,128]{1,0:T(8,128)(2,1)S(1)}, u32[]{:S(2)}, u32[]{:S(2)}) collective-permute-start(bf16[528,128]{1,0:T(8,128)(2,1)S(1)} %get-tuple-element.21.refs_3_), channel_id=1, source_target_pairs={{0,12},{1,9},{4,8},{5,13},{8,4},{9,1},{12,0},{13,5},{2,14},{3,11},... | collective-permute-start | bytes 405512 | tf_op jit(solution)/shard_map/ppermute | solution.py:320
  26.1 11.5 %collective-permute-start.5 = (bf16[528,128]{1,0:T(8,128)(2,1)S(1)}, bf16[528,128]{1,0:T(8,128)(2,1)S(1)}, u32[]{:S(2)}, u32[]{:S(2)}) collective-permute-start(bf16[528,128]{1,0:T(8,128)(2,1)S(1)} %get-tuple-element.21.refs_3_), channel_id=1, source_target_pairs={{0,8},{1,5},{4,12},{5,1},{8,0},{9,13},{12,4},{13,9},{2,10},{3,7},{... | collective-permute-start | bytes 405512 | tf_op jit(solution)/shard_map/ppermute | solution.py:320
  26.1 11.5 %collective-permute-start.6 = (bf16[528,128]{1,0:T(8,128)(2,1)S(1)}, bf16[528,128]{1,0:T(8,128)(2,1)S(1)}, u32[]{:S(2)}, u32[]{:S(2)}) collective-permute-start(bf16[528,128]{1,0:T(8,128)(2,1)S(1)} %get-tuple-element.21.refs_3_), channel_id=1, source_target_pairs={{0,4},{1,13},{4,0},{5,9},{8,12},{9,5},{12,8},{13,1},{2,6},{3,15},{... | collective-permute-start | bytes 405512 | tf_op jit(solution)/shard_map/ppermute | solution.py:320
  27.2 12.5 %collective-permute-start.10 = (bf16[528,128]{1,0:T(8,128)(2,1)S(1)}, bf16[528,128]{1,0:T(8,128)(2,1)S(1)}, u32[]{:S(2)}, u32[]{:S(2)}) collective-permute-start(bf16[528,128]{1,0:T(8,128)(2,1)S(1)} %get-tuple-element.21.refs_3_), channel_id=1, source_target_pairs={{0,1},{1,0},{2,3},{3,2},{4,5},{5,4},{6,7},{7,6},{8,9},{9,8},{10,11... | collective-permute-start | bytes 405512 | tf_op jit(solution)/shard_map/ppermute | solution.py:326
  31.2 8.5 %collective-permute-start.7 = (bf16[528,128]{1,0:T(8,128)(2,1)S(1)}, bf16[528,128]{1,0:T(8,128)(2,1)S(1)}, u32[]{:S(2)}, u32[]{:S(2)}) collective-permute-start(bf16[528,128]{1,0:T(8,128)(2,1)S(1)} %collective-permute-done.4.refs_0_), channel_id=1, source_target_pairs={{0,1},{1,0},{2,3},{3,2},{4,5},{5,4},{6,7},{7,6},{8,9},{9,8},{10,11... | collective-permute-start | bytes 405512 | tf_op jit(solution)/shard_map/ppermute | solution.py:326
  37.6 2.1 %collective-permute-start.8 = (bf16[528,128]{1,0:T(8,128)(2,1)S(1)}, bf16[528,128]{1,0:T(8,128)(2,1)S(1)}, u32[]{:S(2)}, u32[]{:S(2)}) collective-permute-start(bf16[528,128]{1,0:T(8,128)(2,1)S(1)} %collective-permute-done.5.refs_1_), channel_id=1, source_target_pairs={{0,1},{1,0},{2,3},{3,2},{4,5},{5,4},{6,7},{7,6},{8,9},{9,8},{10,11... | collective-permute-start | bytes 405512 | tf_op jit(solution)/shard_map/ppermute | solution.py:326
  37.7 2.1 %collective-permute-start.9 = (bf16[528,128]{1,0:T(8,128)(2,1)S(1)}, bf16[528,128]{1,0:T(8,128)(2,1)S(1)}, u32[]{:S(2)}, u32[]{:S(2)}) collective-permute-start(bf16[528,128]{1,0:T(8,128)(2,1)S(1)} %collective-permute-done.6.refs_2_), channel_id=1, source_target_pairs={{0,1},{1,0},{2,3},{3,2},{4,5},{5,4},{6,7},{7,6},{8,9},{9,8},{10,11... | collective-permute-start | bytes 405512 | tf_op jit(solution)/shard_map/ppermute | solution.py:326
  38.2 1.2 %collective-permute-start.11 = (f32[4,8,128]{2,1,0:T(8,128)S(1)}, f32[4,8,128]{2,1,0:T(8,128)S(1)}, u32[]{:S(2)}, u32[]{:S(2)}) collective-permute-start(f32[4,8,128]{2,1,0:T(8,128)S(1)} %get-tuple-element.23.here_ref), channel_id=1, source_target_pairs={{0,1},{1,0},{2,3},{3,2},{4,5},{5,4},{6,7},{7,6},{8,9},{9,8},{10,11... | collective-permute-start | bytes 49160 | tf_op jit(solution)/shard_map/ppermute | solution.py:326
  41.5 3.7 %collective-permute-start.12 = (f32[1,512]{1,0:T(1,128)S(1)}, f32[1,512]{1,0:T(1,128)S(1)}, u32[]{:S(2)}, u32[]{:S(2)}) collective-permute-start(f32[1,512]{1,0:T(1,128)S(1)} %slice.50), channel_id=1, source_target_pairs={{0,2},{2,0},{1,3},{3,1},{4,6},{6,4},{5,7},{7,5},{8,10},{10,8},{9,1... | collective-permute-start | bytes 6152 | tf_op jit(solution)/shard_map/ppermute | solution.py:323
  46.3 3.7 %collective-permute-start.13 = (f32[1,512]{1,0:T(1,128)S(1)}, f32[1,512]{1,0:T(1,128)S(1)}, u32[]{:S(2)}, u32[]{:S(2)}) collective-permute-start(f32[1,512]{1,0:T(1,128)S(1)} %fusion), channel_id=1, source_target_pairs={{0,2},{2,0},{1,3},{3,1},{4,6},{6,4},{5,7},{7,5},{8,10},{10,8},{9,1... | collective-permute-start | bytes 6152 | tf_op jit(solution)/shard_map/ppermute | solution.py:323

commit v9 on v8

--- a/solution.py
+++ b/solution.py
@@ -146,8 +146,8 @@
     return jnp.where(lax.axis_index("state") == beside, on_core[0], on_core[1])
 
 
-def gram_kernel(blocks, y_ref, own_ref, other_ref, kappa_ref, rate_ref, gain_ref, *refs):
-    outs, (acc, vec, side, readings) = refs[:-4], refs[-4:]
+def half_kernel(blocks, y_ref, own_ref, kappa_ref, rate_ref, gain_ref, *refs):
+    outs, (turned_ref, acc, vec, side, readings) = refs[:-5], refs[-5:]
     tile_num, row_num, _ = own_ref.shape
     number = len(outs)
     core, position = lax.axis_index("state"), lax.axis_index("tm")
@@ -159,17 +159,11 @@
         block = blocks[index]
         rows = own_ref[index]
         turned = rows.T
+        turned_ref[index] = turned
         square = jnp.dot(turned, rows, preferred_element_type=jnp.float32)
         acc[block, 0:LANES] += square[:LANES, :LANES]
         acc[block, LANES : 2 * LANES] += square[:LANES, LANES:]
         acc[block, 2 * LANES : 3 * LANES] += square[LANES:, LANES:]
-        for piece in range(2):
-            at = pl.multiple_of((piece ^ core) * LANES, LANES)
-            acc[block, (3 + piece) * LANES : (4 + piece) * LANES] += jnp.dot(
-                turned[piece * LANES : (piece + 1) * LANES, :],
-                other_ref[index, :, pl.ds(at, LANES)],
-                preferred_element_type=jnp.float32,
-            )
         values = jnp.broadcast_to(readings[index : index + 1, :], (8, row_num))
         vec[block] += jnp.dot(
             values.astype(jnp.bfloat16), rows, preferred_element_type=jnp.float32
@@ -178,19 +172,13 @@
     column = lax.broadcasted_iota(jnp.int32, (LANES, LANES), 1)
     for turn, out_ref in enumerate(outs):
         block = position ^ flip_here(turn, number)
-
-        def take(piece):
-            return acc[block, piece * LANES : (piece + 1) * LANES]
-
-        packed = jnp.where(line < column, take(0), jnp.where(line > column, take(2), 0.0))
+        first, between, second = (acc[block, at * LANES : (at + 1) * LANES] for at in range(3))
+        packed = jnp.where(line < column, first, jnp.where(line > column, second, 0.0))
         out_ref[0:LANES] = packed.astype(jnp.bfloat16)
-        for at, piece in ((1, 1), (2, 3), (3, 4)):
-            out_ref[at * LANES : (at + 1) * LANES] = take(piece).astype(jnp.bfloat16)
+        out_ref[LANES : 2 * LANES] = between.astype(jnp.bfloat16)
         values = [vec[block, 0:1, :LANES], vec[block, 0:1, LANES:]]
-        for piece in (0, 2):
-            values.append(
-                jnp.sum(jnp.where(line == column, take(piece), 0.0), axis=0, keepdims=True)
-            )
+        for square in (first, second):
+            values.append(jnp.sum(jnp.where(line == column, square, 0.0), axis=0, keepdims=True))
         for coefficient in (kappa_ref, rate_ref, gain_ref):
             for piece in range(2):
                 at = pl.multiple_of((2 * core + piece) * LANES, LANES)
@@ -198,20 +186,39 @@
         for at, value in enumerate(values):
             for which, part in enumerate(pieces_of(value)):
                 side[which * VECTORS + at : which * VECTORS + at + 1, :] = part
-        out_ref[4 * LANES :] = side[...].astype(jnp.bfloat16)
+        out_ref[2 * LANES :] = side[...].astype(jnp.bfloat16)
+
+
+def cross_kernel(blocks, turned_ref, other_ref, *refs):
+    outs, acc = refs[:-1], refs[-1]
+    number = len(outs)
+    core, position = lax.axis_index("state"), lax.axis_index("tm")
+    acc[...] = jnp.zeros_like(acc)
+    for index in range(other_ref.shape[0]):
+        block = blocks[index]
+        for piece in range(2):
+            at = pl.multiple_of((piece ^ core) * LANES, LANES)
+            acc[block, piece * LANES : (piece + 1) * LANES] += jnp.dot(
+                turned_ref[index, piece * LANES : (piece + 1) * LANES, :],
+                other_ref[index, :, pl.ds(at, LANES)],
+                preferred_element_type=jnp.float32,
+            )
+    for turn, out_ref in enumerate(outs):
+        out_ref[...] = acc[position ^ flip_here(turn, number)].astype(jnp.bfloat16)
 
 
 def sum_kernel(*refs):
     parts, (out_ref, coefficients, side) = refs[:-3], refs[-3:]
-    number = len(parts)
+    number = len(parts) // 2
     position = lax.axis_index("tm")
-    total = parts[0][: 4 * LANES].astype(jnp.float32)
-    for part in parts[1:]:
-        total = total + part[: 4 * LANES].astype(jnp.float32)
-    out_ref[: 4 * LANES] = total.astype(jnp.bfloat16)
+    for at, some in enumerate((parts[:number], parts[number:])):
+        total = some[0][: 2 * LANES].astype(jnp.float32)
+        for part in some[1:]:
+            total = total + part[: 2 * LANES].astype(jnp.float32)
+        out_ref[2 * at * LANES : 2 * (at + 1) * LANES] = total.astype(jnp.bfloat16)
     values = None
-    for turn, part in enumerate(parts):
-        below = part[4 * LANES :].astype(jnp.float32)
+    for turn, part in enumerate(parts[:number]):
+        below = part[2 * LANES :].astype(jnp.float32)
         below = below[:VECTORS] + below[VECTORS : 2 * VECTORS] + below[2 * VECTORS : 3 * VECTORS]
         coefficients[position ^ flip_here(turn, number), 0 : VECTORS - 4] = below[4:]
         values = below[:4] if values is None else values + below[:4]
@@ -328,30 +335,42 @@
     if direct:
         live = jnp.arange(row_num, dtype=jnp.int32)[None, :] < tile_count[0][:, None]
         valid = jnp.where(live[:, :, None], own, jnp.zeros((), own.dtype))
-        pieces = pl.pallas_call(
-            gram_kernel,
-            out_shape=[jax.ShapeDtypeStruct((4 * LANES + 32, LANES), jnp.bfloat16)] * tm_size,
-            in_specs=[SMEM] + [VMEM] * 6,
-            out_specs=[VMEM] * tm_size,
+        second_half = jax.ShapeDtypeStruct((2 * LANES, LANES), jnp.bfloat16)
+        blocks = tile_block[0, :, 0]
+        *pieces, turned = pl.pallas_call(
+            half_kernel,
+            out_shape=[jax.ShapeDtypeStruct((2 * LANES + 32, LANES), jnp.bfloat16)] * tm_size
+            + [jax.ShapeDtypeStruct((tile_num, half, row_num), jnp.bfloat16)],
+            in_specs=[SMEM] + [VMEM] * 5,
+            out_specs=[VMEM] * (tm_size + 1),
             scratch_shapes=[
-                pltpu.VMEM((tm_size, 5 * LANES, LANES), jnp.float32),
+                pltpu.VMEM((tm_size, 3 * LANES, LANES), jnp.float32),
                 pltpu.VMEM((tm_size, 8, half), jnp.float32),
                 pltpu.VMEM((32, LANES), jnp.float32),
                 pltpu.VMEM((tile_num, row_num), jnp.float32),
             ],
             compiler_params=KERNEL,
-        )(tile_block[0, :, 0], rows_y[0], valid, other, kappa[0], rate[0], smooth_gain[0])
+        )(blocks, rows_y[0], valid, kappa[0], rate[0], smooth_gain[0])
         turns = range(tm_size - 1)
         parts = [flip_over(pieces[turn], turn) for turn in turns] + [pieces[-1]]
+        pieces2 = pl.pallas_call(
+            cross_kernel,
+            out_shape=[second_half] * tm_size,
+            in_specs=[SMEM] + [VMEM] * 2,
+            out_specs=[VMEM] * tm_size,
+            scratch_shapes=[pltpu.VMEM((tm_size, 2 * LANES, LANES), jnp.float32)],
+            compiler_params=KERNEL,
+        )(blocks, turned, other)
+        parts2 = [flip_over(pieces2[turn], turn) for turn in turns] + [pieces2[-1]]
         half_coefficients = jax.ShapeDtypeStruct((tm_size, 8, LANES), jnp.float32)
         own_sum, here = pl.pallas_call(
             sum_kernel,
             out_shape=(jax.ShapeDtypeStruct((4 * LANES + 16, LANES), jnp.bfloat16), half_coefficients),
-            in_specs=[VMEM] * tm_size,
+            in_specs=[VMEM] * (2 * tm_size),
             out_specs=(VMEM, VMEM),
             scratch_shapes=[pltpu.VMEM((16, LANES), jnp.float32)],
             compiler_params=KERNEL,
-        )(*parts)
+        )(*parts, *parts2)
         own_sums = [flip_over(own_sum, turn) for turn in turns] + [own_sum]
         here, own_sums[0] = lax.optimization_barrier((here, own_sums[0]))
         bands = pl.pallas_call(

time: 50.8 us -> 49.7 us (0.978)
  waiting for transfers between devices: 24.2 us -> 18 us
  starting transfers between devices: 17.4 us -> 21.6 us
  Pallas kernels: 5.28 us -> 6.16 us
    ppermute x6 -> x9, waiting for transfers between devices: 18.6 us -> 12.6 us  [flip_over(): return lax.ppermute(array, ('tm', 'state'), pairs)]
    ppermute x6 -> x9, starting transfers between devices: 10.1 us -> 14.2 us  [flip_over(): return lax.ppermute(array, ('tm', 'state'), pairs)]
    pallas_call x1 -> x2, Pallas kernels: 1.96 us -> 2.86 us  [the longest x1 1.8 us: shards(): pl.pallas_call(half_kernel, out_shape=[jax.ShapeDtypeStruct((2 * LANES +...]
  transfers between devices with their start and end apart: 14 -> 17, of which waited for: 8 -> 8; matrix products, arithmetic and copies ran while one was open for 4% -> 4% of each run, Pallas kernels for 1% -> 6%
where the time goes in v9:
time: 49.7 us; the launch traced here: 49.5 us
  starting transfers between devices  21.6 us (43%)
  waiting for transfers between devices  18 us (36%)
  Pallas kernels  6.16 us (12%)
  other arithmetic  2.93 us (6%)
  between operations  0.84 us (2%)
    ppermute x9, starting transfers between devices, flip_over(): return lax.ppermute(array, ('tm', 'state'), pairs)  14.2 us
    ppermute x9, waiting for transfers between devices, flip_over(): return lax.ppermute(array, ('tm', 'state'), pairs)  12.6 us
    ppermute x2, waiting for transfers between devices, ring(): lax.ppermute(array, 'grp', [(i, (i + step) % grp_size) for i in range(grp...  4.17 us
    ppermute x5, starting transfers between devices, across(): lax.ppermute(array, 'state', [(i, (i + 1) % state_size) for i in range(st...  3.73 us
    ppermute x2, starting transfers between devices, ring(): lax.ppermute(array, 'grp', [(i, (i + step) % grp_size) for i in range(grp...  3.13 us
    pallas_call x1, Pallas kernels, shards(): pl.pallas_call(half_kernel, out_shape=[jax.ShapeDtypeStruct((2 * LANES +...  1.8 us
    pallas_call x1, Pallas kernels, shards(): pl.pallas_call(functools.partial(assemble_kernel, tm_size), out_shape=(ja...  1.71 us
    select_n x1, other arithmetic, shards(): valid = jnp.where(live[:, :, None], own, jnp.zeros((), own.dtype))  1.48 us
  transfers between devices with their start and end apart: 17, of which 8 were waited for; matrix products, arithmetic and copies ran while one was open for 4% of the time, Pallas kernels for 6%

profile of v9, /device:TPU:0, one launch (start us, length us, event | category | flops | bytes accessed | tf_op | source)
XLA Modules:
  0.0 49.5 jit_solution(4987646968175109461)
XLA Ops:
  1.2 0.7 %iota_compare_fusion = pred[16,128]{1,0:T(8,128)(4,1)S(1)} fusion(s32[16]{0:T(128)} %bitcast.45), kind=kLoop, calls=%fused_computation.7 | loop fusion | flops 2048 | bytes 2112 | tf_op jit(solution)/shard_map/lt | solution.py:336
  1.9 1.5 %broadcast_select_fusion.own_ref = bf16[16,128,256]{2,1,0:T(8,128)(2,1)S(1)} fusion(pred[16,128]{1,0:T(8,128)(4,1)S(1)} %iota_compare_fusion, bf16[1,16,128,256]{3,2,1,0:T(8,128)(2,1)} %param.8), kind=kLoop, calls=%fused_computation | loop fusion | flops 524288 | bytes 2099200 | tf_op jit(solution)/shard_map/jit(_where)/select_n | solution.py:337
  3.5 1.8 %shard_map.95 = (bf16[288,128]{1,0:T(8,128)(2,1)S(1)}, bf16[288,128]{1,0:T(8,128)(2,1)S(1)}, bf16[288,128]{1,0:T(8,128)(2,1)S(1)}, bf16[288,128]{1,0:T(8,128)(2,1)S(1)}, bf16[16,256,128]{2,1,0:T(8,128)(2,1)S(1)}) custom-call(s32[16]{0:T(128)S(1)} %bitcast.42, bf16[16,128]{1,0:T(8,128)(2,1)S(1)} %bitcast.37, ...), custom_call_target="tpu_custom_call" | custom-call | tf_op jit(solution)/shard_map/pallas_call | solution.py:340
  5.3 4.7 %collective-permute-start = (bf16[288,128]{1,0:T(8,128)(2,1)S(1)}, bf16[288,128]{1,0:T(8,128)(2,1)S(1)}, u32[]{:S(2)}, u32[]{:S(2)}) collective-permute-start(bf16[288,128]{1,0:T(8,128)(2,1)S(1)} %get-tuple-element.21), channel_id=1, source_target_pairs={{0,12},{1,9},{4,8},{5,13},{8,4},{9,1},{12,0},{13,5},{2,14},{3,11},... | collective-permute-start | bytes 221192 | tf_op jit(solution)/shard_map/ppermute | solution.py:327
  10.0 0.6 %collective-permute-start.2 = (bf16[288,128]{1,0:T(8,128)(2,1)S(1)}, bf16[288,128]{1,0:T(8,128)(2,1)S(1)}, u32[]{:S(2)}, u32[]{:S(2)}) collective-permute-start(bf16[288,128]{1,0:T(8,128)(2,1)S(1)} %get-tuple-element.23), channel_id=1, source_target_pairs={{0,4},{1,13},{4,0},{5,9},{8,12},{9,5},{12,8},{13,1},{2,6},{3,15},{... | collective-permute-start | bytes 221192 | tf_op jit(solution)/shard_map/ppermute | solution.py:327
  10.6 1.1 %shard_map.96 = (bf16[256,128]{1,0:T(8,128)(2,1)S(1)}, bf16[256,128]{1,0:T(8,128)(2,1)S(1)}, bf16[256,128]{1,0:T(8,128)(2,1)S(1)}, bf16[256,128]{1,0:T(8,128)(2,1)S(1)}) custom-call(s32[16]{0:T(128)S(1)} %bitcast.43, bf16[16,256,128]{2,1,0:T(8,128)(2,1)S(1)} %get-tuple-element.25.turned_ref, bf16[16,128,256]{2,1,0:T(8,128)(2,1)S(1)} %collective-permute-done.3.other_ref), custom_call_target="tpu_custom_call" | custom-call | tf_op jit(solution)/shard_map/pallas_call | solution.py:356
  11.7 3.8 %collective-permute-start.4 = (bf16[256,128]{1,0:T(8,128)(2,1)S(1)}, bf16[256,128]{1,0:T(8,128)(2,1)S(1)}, u32[]{:S(2)}, u32[]{:S(2)}) collective-permute-start(bf16[256,128]{1,0:T(8,128)(2,1)S(1)} %get-tuple-element.26), channel_id=1, source_target_pairs={{0,12},{1,9},{4,8},{5,13},{8,4},{9,1},{12,0},{13,5},{2,14},{3,11},... | collective-permute-start | bytes 196616 | tf_op jit(solution)/shard_map/ppermute | solution.py:327
  15.5 0.6 %collective-permute-start.6 = (bf16[256,128]{1,0:T(8,128)(2,1)S(1)}, bf16[256,128]{1,0:T(8,128)(2,1)S(1)}, u32[]{:S(2)}, u32[]{:S(2)}) collective-permute-start(bf16[256,128]{1,0:T(8,128)(2,1)S(1)} %get-tuple-element.28), channel_id=1, source_target_pairs={{0,4},{1,13},{4,0},{5,9},{8,12},{9,5},{12,8},{13,1},{2,6},{3,15},{... | collective-permute-start | bytes 196616 | tf_op jit(solution)/shard_map/ppermute | solution.py:327
  16.1 2.1 %collective-permute-done.1.refs_1_ = bf16[288,128]{1,0:T(8,128)(2,1)S(1)} collective-permute-done((bf16[288,128]{1,0:T(8,128)(2,1)S(1)}, bf16[288,128]{1,0:T(8,128)(2,1)S(1)}, u32[]{:S(2)}, u32[]{:S(2)}) %collective-permute-start.1) | collective-permute-done | bytes 73760 | tf_op jit(solution)/shard_map/ppermute | solution.py:327
  18.2 0.6 %collective-permute-done.4.refs_4_ = bf16[256,128]{1,0:T(8,128)(2,1)S(1)} collective-permute-done((bf16[256,128]{1,0:T(8,128)(2,1)S(1)}, bf16[256,128]{1,0:T(8,128)(2,1)S(1)}, u32[]{:S(2)}, u32[]{:S(2)}) %collective-permute-start.4) | collective-permute-done | bytes 65568 | tf_op jit(solution)/shard_map/ppermute | solution.py:327
  18.8 3.5 %collective-permute-done.5.refs_5_ = bf16[256,128]{1,0:T(8,128)(2,1)S(1)} collective-permute-done((bf16[256,128]{1,0:T(8,128)(2,1)S(1)}, bf16[256,128]{1,0:T(8,128)(2,1)S(1)}, u32[]{:S(2)}, u32[]{:S(2)}) %collective-permute-start.5) | collective-permute-done | bytes 65568 | tf_op jit(solution)/shard_map/ppermute | solution.py:327
  22.3 2.7 %collective-permute-start.7 = (bf16[528,128]{1,0:T(8,128)(2,1)S(1)}, bf16[528,128]{1,0:T(8,128)(2,1)S(1)}, u32[]{:S(2)}, u32[]{:S(2)}) collective-permute-start(bf16[528,128]{1,0:T(8,128)(2,1)S(1)} %get-tuple-element.31.refs_3_), channel_id=1, source_target_pairs={{0,12},{1,9},{4,8},{5,13},{8,4},{9,1},{12,0},{13,5},{2,14},{3,11},... | collective-permute-start | bytes 405512 | tf_op jit(solution)/shard_map/ppermute | solution.py:327
  25.1 1.7 %collective-permute-start.9 = (bf16[528,128]{1,0:T(8,128)(2,1)S(1)}, bf16[528,128]{1,0:T(8,128)(2,1)S(1)}, u32[]{:S(2)}, u32[]{:S(2)}) collective-permute-start(bf16[528,128]{1,0:T(8,128)(2,1)S(1)} %get-tuple-element.31.refs_3_), channel_id=1, source_target_pairs={{0,4},{1,13},{4,0},{5,9},{8,12},{9,5},{12,8},{13,1},{2,6},{3,15},{... | collective-permute-start | bytes 405512 | tf_op jit(solution)/shard_map/ppermute | solution.py:327
  26.8 4.1 %collective-permute-done.7.refs_0_ = bf16[528,128]{1,0:T(8,128)(2,1)S(1)} collective-permute-done((bf16[528,128]{1,0:T(8,128)(2,1)S(1)}, bf16[528,128]{1,0:T(8,128)(2,1)S(1)}, u32[]{:S(2)}, u32[]{:S(2)}) %collective-permute-start.7) | collective-permute-done | bytes 135200 | tf_op jit(solution)/shard_map/ppermute | solution.py:327
  30.9 3.2 %collective-permute-start.10 = (bf16[528,128]{1,0:T(8,128)(2,1)S(1)}, bf16[528,128]{1,0:T(8,128)(2,1)S(1)}, u32[]{:S(2)}, u32[]{:S(2)}) collective-permute-start(bf16[528,128]{1,0:T(8,128)(2,1)S(1)} %collective-permute-done.7.refs_0_), channel_id=1, source_target_pairs={{0,1},{1,0},{2,3},{3,2},{4,5},{5,4},{6,7},{7,6},{8,9},{9,8},{10,11... | collective-permute-start | bytes 405512 | tf_op jit(solution)/shard_map/ppermute | solution.py:333
  34.1 2.4 %collective-permute-done.8.refs_1_ = bf16[528,128]{1,0:T(8,128)(2,1)S(1)} collective-permute-done((bf16[528,128]{1,0:T(8,128)(2,1)S(1)}, bf16[528,128]{1,0:T(8,128)(2,1)S(1)}, u32[]{:S(2)}, u32[]{:S(2)}) %collective-permute-start.8) | collective-permute-done | bytes 135200 | tf_op jit(solution)/shard_map/ppermute | solution.py:327
  37.0 1.2 %collective-permute-done.14.there_ref = f32[4,8,128]{2,1,0:T(8,128)S(1)} collective-permute-done((f32[4,8,128]{2,1,0:T(8,128)S(1)}, f32[4,8,128]{2,1,0:T(8,128)S(1)}, u32[]{:S(2)}, u32[]{:S(2)}) %collective-permute-start.14) | collective-permute-done | bytes 16416 | tf_op jit(solution)/shard_map/ppermute | solution.py:333
  38.6 1.7 %shard_map.99 = (bf16[4,512,512]{2,1,0:T(8,128)(2,1)S(1)}, f32[4,8,512]{2,1,0:T(8,128)S(1)}, f32[4,512]{1,0:T(4,128)S(1)}, f32[4,512]{1,0:T(4,128)S(1)}) custom-call(bf16[528,128]{1,0:T(8,128)(2,1)S(1)} %collective-permute-done.7.refs_0_, bf16[528,128]{1,0:T(8,128)(2,1)S(1)} %collective-permute-done.8.refs_1_, ...), custom_call_target="tpu_custom_call" | custom-call | tf_op jit(solution)/shard_map/pallas_call | solution.py:385
  40.3 1.6 %collective-permute-start.15 = (f32[1,512]{1,0:T(1,128)S(1)}, f32[1,512]{1,0:T(1,128)S(1)}, u32[]{:S(2)}, u32[]{:S(2)}) collective-permute-start(f32[1,512]{1,0:T(1,128)S(1)} %slice.50), channel_id=1, source_target_pairs={{0,2},{2,0},{1,3},{3,1},{4,6},{6,4},{5,7},{7,5},{8,10},{10,8},{9,1... | collective-permute-start | bytes 6152 | tf_op jit(solution)/shard_map/ppermute | solution.py:330
  41.9 2.1 %collective-permute-done.15.state_ref = f32[1,512]{1,0:T(1,128)S(1)} collective-permute-done((f32[1,512]{1,0:T(1,128)S(1)}, f32[1,512]{1,0:T(1,128)S(1)}, u32[]{:S(2)}, u32[]{:S(2)}) %collective-permute-start.15) | collective-permute-done | bytes 2080 | tf_op jit(solution)/shard_map/ppermute | solution.py:330
  44.0 1.2 %shard_map.100 = (f32[4,512]{1,0:T(4,128)S(1)}, f32[4,512]{1,0:T(4,128)S(1)}) custom-call(bf16[4,512,512]{2,1,0:T(8,128)(2,1)S(1)} %get-tuple-element.34.grams, f32[4,8,512]{2,1,0:T(8,128)S(1)} %get-tuple-element.35.vectors, f32[4,16,512]{2,1,0:T(8,128)S(1)} %shard_map.98.refs_8_.bands, f32[1,512]{1,0:T(1,128)S(1)} %collective-permute-done.15.state_ref), custom_call_target="tpu_custom_call" | custom-call | tf_op jit(solution)/shard_map/pallas_call | solution.py:402
  45.2 1.6 %collective-permute-start.16 = (f32[1,512]{1,0:T(1,128)S(1)}, f32[1,512]{1,0:T(1,128)S(1)}, u32[]{:S(2)}, u32[]{:S(2)}) collective-permute-start(f32[1,512]{1,0:T(1,128)S(1)} %fusion), channel_id=1, source_target_pairs={{0,2},{2,0},{1,3},{3,1},{4,6},{6,4},{5,7},{7,5},{8,10},{10,8},{9,1... | collective-permute-start | bytes 6152 | tf_op jit(solution)/shard_map/ppermute | solution.py:330
  46.8 2.1 %collective-permute-done.16 = f32[1,512]{1,0:T(1,128)S(1)} collective-permute-done((f32[1,512]{1,0:T(1,128)S(1)}, f32[1,512]{1,0:T(1,128)S(1)}, u32[]{:S(2)}, u32[]{:S(2)}) %collective-permute-start.16) | collective-permute-done | bytes 2080 | tf_op jit(solution)/shard_map/ppermute | solution.py:330
  48.9 0.7 %add_bitcast_fusion = (f32[1,1,256]{2,1,0:T(1,128)}, f32[1,1,256]{2,1,0:T(1,128)}) fusion(s32[]{:T(128)S(6)} %select_n.47, s32[]{:T(128)S(6)} %select_n.48, f32[1,512]{1,0:T(1,128)S(1)} %get-tuple-element.43, f32[1,512]{1,0:T(1,128)S(1)} %get-tuple-element.42, f32[1,512]{1,0:T(1,128)S(1)} %get-tuple-element.41, f32[1,512]{1,0:T(1,128)S(1)} %get-tuple-element.40, ...), kind=kLoop, calls=%fused_computation.21 | loop fusion | flops 1024 | bytes 11272 | tf_op jit(solution)/shard_map/reshape | solution.py:473
  (36 shorter events, 1.6 us)
Async XLA Ops:
  0.6 2.8 %copy-start.5 = (s32[1,16,1]{1,2,0:T(1,128)S(1)}, s32[1,16,1]{1,2,0:T(1,128)}, u32[]{:S(2)}) copy-start(s32[1,16,1]{1,2,0:T(1,128)} %param.10) | copy-start | bytes 196
  0.6 2.8 %copy-start = (bf16[1,16,128]{2,1,0:T(8,128)(2,1)S(1)}, bf16[1,16,128]{2,1,0:T(8,128)(2,1)}, u32[]{:S(2)}) copy-start(bf16[1,16,128]{2,1,0:T(8,128)(2,1)} %param.9) | copy-start | bytes 12292
  0.7 2.8 %copy-start.1 = (f32[1,1,512]{2,1,0:T(1,128)S(1)}, f32[1,1,512]{2,1,0:T(1,128)}, u32[]{:S(2)}) copy-start(f32[1,1,512]{2,1,0:T(1,128)} %param.12) | copy-start | bytes 6148
  0.7 2.8 %copy-start.2 = (f32[1,1,512]{2,1,0:T(1,128)S(1)}, f32[1,1,512]{2,1,0:T(1,128)}, u32[]{:S(2)}) copy-start(f32[1,1,512]{2,1,0:T(1,128)} %param.13) | copy-start | bytes 6148
  0.7 2.8 %copy-start.3 = (f32[1,1,512]{2,1,0:T(1,128)S(1)}, f32[1,1,512]{2,1,0:T(1,128)}, u32[]{:S(2)}) copy-start(f32[1,1,512]{2,1,0:T(1,128)} %param.14) | copy-start | bytes 6148
  0.7 9.9 %collective-permute-start.3 = (bf16[16,128,256]{2,1,0:T(8,128)(2,1)}, bf16[16,128,256]{2,1,0:T(8,128)(2,1)S(1)}, u32[]{:S(2)}, u32[]{:S(2)}) collective-permute-start(bf16[16,128,256]{2,1,0:T(8,128)(2,1)} %bitcast.44), channel_id=1, source_target_pairs={{0,1},{1,0},{2,3},{3,2},{4,5},{5,4},{6,7},{7,6},{8,9},{9,8},{10,11... | collective-permute-start | bytes 3145736 | tf_op jit(solution)/shard_map/ppermute | solution.py:316
  3.4 35.2 %copy-start.4 = (f32[512]{0:T(512)S(1)}, f32[512]{0:T(512)}, u32[]{:S(2)}) copy-start(f32[512]{0:T(512)} %param.15) | copy-start | bytes 6148
  5.3 10.2 %collective-permute-start = (bf16[288,128]{1,0:T(8,128)(2,1)S(1)}, bf16[288,128]{1,0:T(8,128)(2,1)S(1)}, u32[]{:S(2)}, u32[]{:S(2)}) collective-permute-start(bf16[288,128]{1,0:T(8,128)(2,1)S(1)} %get-tuple-element.21), channel_id=1, source_target_pairs={{0,12},{1,9},{4,8},{5,13},{8,4},{9,1},{12,0},{13,5},{2,14},{3,11},... | collective-permute-start | bytes 221192 | tf_op jit(solution)/shard_map/ppermute | solution.py:327
  10.0 8.2 %collective-permute-start.1 = (bf16[288,128]{1,0:T(8,128)(2,1)S(1)}, bf16[288,128]{1,0:T(8,128)(2,1)S(1)}, u32[]{:S(2)}, u32[]{:S(2)}) collective-permute-start(bf16[288,128]{1,0:T(8,128)(2,1)S(1)} %get-tuple-element.22), channel_id=1, source_target_pairs={{0,8},{1,5},{4,12},{5,1},{8,0},{9,13},{12,4},{13,9},{2,10},{3,7},{... | collective-permute-start | bytes 221192 | tf_op jit(solution)/shard_map/ppermute | solution.py:327
  10.0 8.2 %collective-permute-start.2 = (bf16[288,128]{1,0:T(8,128)(2,1)S(1)}, bf16[288,128]{1,0:T(8,128)(2,1)S(1)}, u32[]{:S(2)}, u32[]{:S(2)}) collective-permute-start(bf16[288,128]{1,0:T(8,128)(2,1)S(1)} %get-tuple-element.23), channel_id=1, source_target_pairs={{0,4},{1,13},{4,0},{5,9},{8,12},{9,5},{12,8},{13,1},{2,6},{3,15},{... | collective-permute-start | bytes 221192 | tf_op jit(solution)/shard_map/ppermute | solution.py:327
  11.7 7.1 %collective-permute-start.4 = (bf16[256,128]{1,0:T(8,128)(2,1)S(1)}, bf16[256,128]{1,0:T(8,128)(2,1)S(1)}, u32[]{:S(2)}, u32[]{:S(2)}) collective-permute-start(bf16[256,128]{1,0:T(8,128)(2,1)S(1)} %get-tuple-element.26), channel_id=1, source_target_pairs={{0,12},{1,9},{4,8},{5,13},{8,4},{9,1},{12,0},{13,5},{2,14},{3,11},... | collective-permute-start | bytes 196616 | tf_op jit(solution)/shard_map/ppermute | solution.py:327
  15.5 6.8 %collective-permute-start.5 = (bf16[256,128]{1,0:T(8,128)(2,1)S(1)}, bf16[256,128]{1,0:T(8,128)(2,1)S(1)}, u32[]{:S(2)}, u32[]{:S(2)}) collective-permute-start(bf16[256,128]{1,0:T(8,128)(2,1)S(1)} %get-tuple-element.27), channel_id=1, source_target_pairs={{0,8},{1,5},{4,12},{5,1},{8,0},{9,13},{12,4},{13,9},{2,10},{3,7},{... | collective-permute-start | bytes 196616 | tf_op jit(solution)/shard_map/ppermute | solution.py:327
  15.5 6.7 %collective-permute-start.6 = (bf16[256,128]{1,0:T(8,128)(2,1)S(1)}, bf16[256,128]{1,0:T(8,128)(2,1)S(1)}, u32[]{:S(2)}, u32[]{:S(2)}) collective-permute-start(bf16[256,128]{1,0:T(8,128)(2,1)S(1)} %get-tuple-element.28), channel_id=1, source_target_pairs={{0,4},{1,13},{4,0},{5,9},{8,12},{9,5},{12,8},{13,1},{2,6},{3,15},{... | collective-permute-start | bytes 196616 | tf_op jit(solution)/shard_map/ppermute | solution.py:327
  22.3 8.5 %collective-permute-start.7 = (bf16[528,128]{1,0:T(8,128)(2,1)S(1)}, bf16[528,128]{1,0:T(8,128)(2,1)S(1)}, u32[]{:S(2)}, u32[]{:S(2)}) collective-permute-start(bf16[528,128]{1,0:T(8,128)(2,1)S(1)} %get-tuple-element.31.refs_3_), channel_id=1, source_target_pairs={{0,12},{1,9},{4,8},{5,13},{8,4},{9,1},{12,0},{13,5},{2,14},{3,11},... | collective-permute-start | bytes 405512 | tf_op jit(solution)/shard_map/ppermute | solution.py:327
  25.1 11.4 %collective-permute-start.8 = (bf16[528,128]{1,0:T(8,128)(2,1)S(1)}, bf16[528,128]{1,0:T(8,128)(2,1)S(1)}, u32[]{:S(2)}, u32[]{:S(2)}) collective-permute-start(bf16[528,128]{1,0:T(8,128)(2,1)S(1)} %get-tuple-element.31.refs_3_), channel_id=1, source_target_pairs={{0,8},{1,5},{4,12},{5,1},{8,0},{9,13},{12,4},{13,9},{2,10},{3,7},{... | collective-permute-start | bytes 405512 | tf_op jit(solution)/shard_map/ppermute | solution.py:327
  25.1 11.4 %collective-permute-start.9 = (bf16[528,128]{1,0:T(8,128)(2,1)S(1)}, bf16[528,128]{1,0:T(8,128)(2,1)S(1)}, u32[]{:S(2)}, u32[]{:S(2)}) collective-permute-start(bf16[528,128]{1,0:T(8,128)(2,1)S(1)} %get-tuple-element.31.refs_3_), channel_id=1, source_target_pairs={{0,4},{1,13},{4,0},{5,9},{8,12},{9,5},{12,8},{13,1},{2,6},{3,15},{... | collective-permute-start | bytes 405512 | tf_op jit(solution)/shard_map/ppermute | solution.py:327
  26.8 11.7 %collective-permute-start.13 = (bf16[528,128]{1,0:T(8,128)(2,1)S(1)}, bf16[528,128]{1,0:T(8,128)(2,1)S(1)}, u32[]{:S(2)}, u32[]{:S(2)}) collective-permute-start(bf16[528,128]{1,0:T(8,128)(2,1)S(1)} %get-tuple-element.31.refs_3_), channel_id=1, source_target_pairs={{0,1},{1,0},{2,3},{3,2},{4,5},{5,4},{6,7},{7,6},{8,9},{9,8},{10,11... | collective-permute-start | bytes 405512 | tf_op jit(solution)/shard_map/ppermute | solution.py:333
  30.9 7.7 %collective-permute-start.10 = (bf16[528,128]{1,0:T(8,128)(2,1)S(1)}, bf16[528,128]{1,0:T(8,128)(2,1)S(1)}, u32[]{:S(2)}, u32[]{:S(2)}) collective-permute-start(bf16[528,128]{1,0:T(8,128)(2,1)S(1)} %collective-permute-done.7.refs_0_), channel_id=1, source_target_pairs={{0,1},{1,0},{2,3},{3,2},{4,5},{5,4},{6,7},{7,6},{8,9},{9,8},{10,11... | collective-permute-start | bytes 405512 | tf_op jit(solution)/shard_map/ppermute | solution.py:333
  36.5 2.1 %collective-permute-start.11 = (bf16[528,128]{1,0:T(8,128)(2,1)S(1)}, bf16[528,128]{1,0:T(8,128)(2,1)S(1)}, u32[]{:S(2)}, u32[]{:S(2)}) collective-permute-start(bf16[528,128]{1,0:T(8,128)(2,1)S(1)} %collective-permute-done.8.refs_1_), channel_id=1, source_target_pairs={{0,1},{1,0},{2,3},{3,2},{4,5},{5,4},{6,7},{7,6},{8,9},{9,8},{10,11... | collective-permute-start | bytes 405512 | tf_op jit(solution)/shard_map/ppermute | solution.py:333
  36.5 2.1 %collective-permute-start.12 = (bf16[528,128]{1,0:T(8,128)(2,1)S(1)}, bf16[528,128]{1,0:T(8,128)(2,1)S(1)}, u32[]{:S(2)}, u32[]{:S(2)}) collective-permute-start(bf16[528,128]{1,0:T(8,128)(2,1)S(1)} %collective-permute-done.9.refs_2_), channel_id=1, source_target_pairs={{0,1},{1,0},{2,3},{3,2},{4,5},{5,4},{6,7},{7,6},{8,9},{9,8},{10,11... | collective-permute-start | bytes 405512 | tf_op jit(solution)/shard_map/ppermute | solution.py:333
  37.0 1.2 %collective-permute-start.14 = (f32[4,8,128]{2,1,0:T(8,128)S(1)}, f32[4,8,128]{2,1,0:T(8,128)S(1)}, u32[]{:S(2)}, u32[]{:S(2)}) collective-permute-start(f32[4,8,128]{2,1,0:T(8,128)S(1)} %get-tuple-element.33.here_ref), channel_id=1, source_target_pairs={{0,1},{1,0},{2,3},{3,2},{4,5},{5,4},{6,7},{7,6},{8,9},{9,8},{10,11... | collective-permute-start | bytes 49160 | tf_op jit(solution)/shard_map/ppermute | solution.py:333
  40.3 3.7 %collective-permute-start.15 = (f32[1,512]{1,0:T(1,128)S(1)}, f32[1,512]{1,0:T(1,128)S(1)}, u32[]{:S(2)}, u32[]{:S(2)}) collective-permute-start(f32[1,512]{1,0:T(1,128)S(1)} %slice.50), channel_id=1, source_target_pairs={{0,2},{2,0},{1,3},{3,1},{4,6},{6,4},{5,7},{7,5},{8,10},{10,8},{9,1... | collective-permute-start | bytes 6152 | tf_op jit(solution)/shard_map/ppermute | solution.py:330
  45.2 3.7 %collective-permute-start.16 = (f32[1,512]{1,0:T(1,128)S(1)}, f32[1,512]{1,0:T(1,128)S(1)}, u32[]{:S(2)}, u32[]{:S(2)}) collective-permute-start(f32[1,512]{1,0:T(1,128)S(1)} %fusion), channel_id=1, source_target_pairs={{0,2},{2,0},{1,3},{3,1},{4,6},{6,4},{5,7},{7,5},{8,10},{10,8},{9,1... | collective-permute-start | bytes 6152 | tf_op jit(solution)/shard_map/ppermute | solution.py:330

commit v10 on v9

--- a/solution.py
+++ b/solution.py
@@ -11,7 +11,7 @@
 LANES = 128
 GROUP_ROWS = 16
 VECTORS = 10
-DIRECT_TM = 4
+FLIPS = {1: (), 2: (1,), 4: (2, 1, 3)}
 
 VMEM = pl.BlockSpec(memory_space=pltpu.VMEM)
 KERNEL = pltpu.CompilerParams(vmem_limit_bytes=16 * 2**20)
@@ -135,8 +135,7 @@
 
 
 def flip_of(turn, number, core):
-    flips = list(reversed(range(1, number)))
-    return flips[(turn + core) % len(flips)]
+    return FLIPS[number][:: 1 - 2 * core][turn]
 
 
 def flip_here(turn, number, beside=0):
@@ -315,7 +314,7 @@
     own = rows_h[0]
     other = lax.ppermute(own, "state", [(i, (i + 1) % state_size) for i in range(state_size)])
     state = start_state.reshape(1, width)
-    direct = tm_size <= DIRECT_TM and tm_size & (tm_size - 1) == 0
+    direct = tm_size in FLIPS
     states_shape = jax.ShapeDtypeStruct((tm_size, width), jnp.float32)
 
     def flip_over(array, turn):
@@ -333,8 +332,8 @@
         return lax.ppermute(array, "state", [(i, (i + 1) % state_size) for i in range(state_size)])
 
     if direct:
-        live = jnp.arange(row_num, dtype=jnp.int32)[None, :] < tile_count[0][:, None]
-        valid = jnp.where(live[:, :, None], own, jnp.zeros((), own.dtype))
+        row = lax.broadcasted_iota(jnp.int32, own.shape, 1)
+        valid = jnp.where(row < tile_count[0][:, None, None], own, jnp.zeros((), own.dtype))
         second_half = jax.ShapeDtypeStruct((2 * LANES, LANES), jnp.bfloat16)
         blocks = tile_block[0, :, 0]
         *pieces, turned = pl.pallas_call(
@@ -372,7 +371,6 @@
             compiler_params=KERNEL,
         )(*parts, *parts2)
         own_sums = [flip_over(own_sum, turn) for turn in turns] + [own_sum]
-        here, own_sums[0] = lax.optimization_barrier((here, own_sums[0]))
         bands = pl.pallas_call(
             band_kernel,
             out_shape=jax.ShapeDtypeStruct((tm_size, 16, width), jnp.float32),
@@ -381,6 +379,7 @@
             scratch_shapes=[pltpu.VMEM((3, tm_size, width), jnp.float32)],
             compiler_params=KERNEL,
         )(here, across(here))
+        bands, own_sums[0] = lax.optimization_barrier((bands, own_sums[0]))
         other_sums = [across(values) for values in own_sums]
         grams, vectors, new_states, new_innovations = pl.pallas_call(
             functools.partial(assemble_kernel, tm_size),

time: 49.7 us -> 46.8 us (0.942)
  starting transfers between devices: 21.6 us -> 19.6 us
  other arithmetic: 2.93 us -> 2.37 us
    ppermute x5, starting transfers between devices: 3.73 us -> 0.52 us  [across(): lax.ppermute(array, 'state', [(i, (i + 1) % state_size) for i in range(st...]
    ppermute x9, starting transfers between devices: 14.2 us -> 15.5 us  [flip_over(): return lax.ppermute(array, ('tm', 'state'), pairs)]
    ppermute x9, waiting for transfers between devices: 12.6 us -> 11.5 us  [flip_over(): return lax.ppermute(array, ('tm', 'state'), pairs)]
    ppermute x5, waiting for transfers between devices: 1.19 us -> 2.02 us  [across(): lax.ppermute(array, 'state', [(i, (i + 1) % state_size) for i in range(st...]
    lt x1 -> x0, other arithmetic: 0.73 us -> none  [shards(): jnp.arange(row_num, dtype=jnp.int32)[None, :] < tile_count[0][:, None]]
  transfers between devices with their start and end apart: 17 -> 17, of which waited for: 8 -> 10; matrix products, arithmetic and copies ran while one was open for 4% -> 4% of each run, Pallas kernels for 6% -> 7%
where the time goes in v10:
time: 46.8 us; the launch traced here: 46.7 us
  starting transfers between devices  19.6 us (42%)
  waiting for transfers between devices  17.7 us (38%)
  Pallas kernels  6.16 us (13%)
  other arithmetic  2.37 us (5%)
  between operations  0.8 us (2%)
    ppermute x9, starting transfers between devices, flip_over(): return lax.ppermute(array, ('tm', 'state'), pairs)  15.5 us
    ppermute x9, waiting for transfers between devices, flip_over(): return lax.ppermute(array, ('tm', 'state'), pairs)  11.5 us
    ppermute x2, waiting for transfers between devices, ring(): lax.ppermute(array, 'grp', [(i, (i + step) % grp_size) for i in range(grp...  4.19 us
    ppermute x2, starting transfers between devices, ring(): lax.ppermute(array, 'grp', [(i, (i + step) % grp_size) for i in range(grp...  3.11 us
    ppermute x5, waiting for transfers between devices, across(): lax.ppermute(array, 'state', [(i, (i + 1) % state_size) for i in range(st...  2.02 us
    pallas_call x1, Pallas kernels, shards(): pl.pallas_call(half_kernel, out_shape=[jax.ShapeDtypeStruct((2 * LANES +...  1.8 us
    pallas_call x1, Pallas kernels, shards(): pl.pallas_call(functools.partial(assemble_kernel, tm_size), out_shape=(ja...  1.71 us
    select_n x1, other arithmetic, shards(): jnp.where(row < tile_count[0][:, None, None], own, jnp.zeros((), own.dtype))  1.65 us
  transfers between devices with their start and end apart: 17, of which 10 were waited for; matrix products, arithmetic and copies ran while one was open for 4% of the time, Pallas kernels for 7%

profile of v10, /device:TPU:0, one launch (start us, length us, event | category | flops | bytes accessed | tf_op | source)
XLA Modules:
  0.0 46.7 jit_solution(1563468964312678282)
XLA Ops:
  1.2 1.7 %fusion.own_ref = bf16[16,128,256]{2,1,0:T(8,128)(2,1)S(1)} fusion(s32[16]{0:T(128)} %bitcast.46, bf16[1,16,128,256]{3,2,1,0:T(8,128)(2,1)} %param.8), kind=kLoop, calls=%fused_computation.1 | loop fusion | flops 1048576 | bytes 2097216 | tf_op jit(solution)/shard_map/jit(_where)/select_n | solution.py:336
  2.9 1.8 %shard_map.95 = (bf16[288,128]{1,0:T(8,128)(2,1)S(1)}, bf16[288,128]{1,0:T(8,128)(2,1)S(1)}, bf16[288,128]{1,0:T(8,128)(2,1)S(1)}, bf16[288,128]{1,0:T(8,128)(2,1)S(1)}, bf16[16,256,128]{2,1,0:T(8,128)(2,1)S(1)}) custom-call(s32[16]{0:T(128)S(1)} %bitcast.43, bf16[16,128]{1,0:T(8,128)(2,1)S(1)} %bitcast.38, bf16[16,128,256]{2,1,0:T(8,128)(2,1)S(1)} %fusion.own_ref, ...), custom_call_target="tpu_custom_call" | custom-call | tf_op jit(solution)/shard_map/pallas_call | solution.py:339
  4.7 3.7 %collective-permute-start = (bf16[288,128]{1,0:T(8,128)(2,1)S(1)}, bf16[288,128]{1,0:T(8,128)(2,1)S(1)}, u32[]{:S(2)}, u32[]{:S(2)}) collective-permute-start(bf16[288,128]{1,0:T(8,128)(2,1)S(1)} %get-tuple-element.21), channel_id=1, source_target_pairs={{0,8},{1,13},{4,12},{5,9},{8,0},{9,5},{12,4},{13,1},{2,10},{3,15},... | collective-permute-start | bytes 221192 | tf_op jit(solution)/shard_map/ppermute | solution.py:326
  8.4 1.6 %collective-permute-start.1 = (bf16[288,128]{1,0:T(8,128)(2,1)S(1)}, bf16[288,128]{1,0:T(8,128)(2,1)S(1)}, u32[]{:S(2)}, u32[]{:S(2)}) collective-permute-start(bf16[288,128]{1,0:T(8,128)(2,1)S(1)} %get-tuple-element.22), channel_id=1, source_target_pairs={{0,4},{1,5},{4,0},{5,1},{8,12},{9,13},{12,8},{13,9},{2,6},{3,7},{6... | collective-permute-start | bytes 221192 | tf_op jit(solution)/shard_map/ppermute | solution.py:326
  10.0 1.1 %shard_map.96 = (bf16[256,128]{1,0:T(8,128)(2,1)S(1)}, bf16[256,128]{1,0:T(8,128)(2,1)S(1)}, bf16[256,128]{1,0:T(8,128)(2,1)S(1)}, bf16[256,128]{1,0:T(8,128)(2,1)S(1)}) custom-call(s32[16]{0:T(128)S(1)} %bitcast.44, bf16[16,256,128]{2,1,0:T(8,128)(2,1)S(1)} %get-tuple-element.25.turned_ref, bf16[16,128,256]{2,1,0:T(8,128)(2,1)S(1)} %collective-permute-done.3.other_ref), custom_call_target="tpu_custom_call" | custom-call | tf_op jit(solution)/shard_map/pallas_call | solution.py:355
  11.0 2.0 %collective-permute-start.4 = (bf16[256,128]{1,0:T(8,128)(2,1)S(1)}, bf16[256,128]{1,0:T(8,128)(2,1)S(1)}, u32[]{:S(2)}, u32[]{:S(2)}) collective-permute-start(bf16[256,128]{1,0:T(8,128)(2,1)S(1)} %get-tuple-element.26), channel_id=1, source_target_pairs={{0,8},{1,13},{4,12},{5,9},{8,0},{9,5},{12,4},{13,1},{2,10},{3,15},... | collective-permute-start | bytes 196616 | tf_op jit(solution)/shard_map/ppermute | solution.py:326
  13.0 2.5 %collective-permute-start.5 = (bf16[256,128]{1,0:T(8,128)(2,1)S(1)}, bf16[256,128]{1,0:T(8,128)(2,1)S(1)}, u32[]{:S(2)}, u32[]{:S(2)}) collective-permute-start(bf16[256,128]{1,0:T(8,128)(2,1)S(1)} %get-tuple-element.27), channel_id=1, source_target_pairs={{0,4},{1,5},{4,0},{5,1},{8,12},{9,13},{12,8},{13,9},{2,6},{3,7},{6... | collective-permute-start | bytes 196616 | tf_op jit(solution)/shard_map/ppermute | solution.py:326
  15.5 1.4 %collective-permute-start.6 = (bf16[256,128]{1,0:T(8,128)(2,1)S(1)}, bf16[256,128]{1,0:T(8,128)(2,1)S(1)}, u32[]{:S(2)}, u32[]{:S(2)}) collective-permute-start(bf16[256,128]{1,0:T(8,128)(2,1)S(1)} %get-tuple-element.28), channel_id=1, source_target_pairs={{0,12},{1,9},{4,8},{5,13},{8,4},{9,1},{12,0},{13,5},{2,14},{3,11},... | collective-permute-start | bytes 196616 | tf_op jit(solution)/shard_map/ppermute | solution.py:326
  16.8 3.2 %collective-permute-done.4.refs_4_ = bf16[256,128]{1,0:T(8,128)(2,1)S(1)} collective-permute-done((bf16[256,128]{1,0:T(8,128)(2,1)S(1)}, bf16[256,128]{1,0:T(8,128)(2,1)S(1)}, u32[]{:S(2)}, u32[]{:S(2)}) %collective-permute-start.4) | collective-permute-done | bytes 65568 | tf_op jit(solution)/shard_map/ppermute | solution.py:326
  20.1 1.6 %collective-permute-done.6.refs_6_ = bf16[256,128]{1,0:T(8,128)(2,1)S(1)} collective-permute-done((bf16[256,128]{1,0:T(8,128)(2,1)S(1)}, bf16[256,128]{1,0:T(8,128)(2,1)S(1)}, u32[]{:S(2)}, u32[]{:S(2)}) %collective-permute-start.6) | collective-permute-done | bytes 65568 | tf_op jit(solution)/shard_map/ppermute | solution.py:326
  21.8 2.4 %collective-permute-start.8 = (bf16[528,128]{1,0:T(8,128)(2,1)S(1)}, bf16[528,128]{1,0:T(8,128)(2,1)S(1)}, u32[]{:S(2)}, u32[]{:S(2)}) collective-permute-start(bf16[528,128]{1,0:T(8,128)(2,1)S(1)} %get-tuple-element.31.refs_3_), channel_id=1, source_target_pairs={{0,8},{1,13},{4,12},{5,9},{8,0},{9,5},{12,4},{13,1},{2,10},{3,15},... | collective-permute-start | bytes 405512 | tf_op jit(solution)/shard_map/ppermute | solution.py:326
  24.2 0.8 %collective-permute-start.9 = (bf16[528,128]{1,0:T(8,128)(2,1)S(1)}, bf16[528,128]{1,0:T(8,128)(2,1)S(1)}, u32[]{:S(2)}, u32[]{:S(2)}) collective-permute-start(bf16[528,128]{1,0:T(8,128)(2,1)S(1)} %get-tuple-element.31.refs_3_), channel_id=1, source_target_pairs={{0,4},{1,5},{4,0},{5,1},{8,12},{9,13},{12,8},{13,9},{2,6},{3,7},{6... | collective-permute-start | bytes 405512 | tf_op jit(solution)/shard_map/ppermute | solution.py:326
  24.9 1.3 %collective-permute-start.10 = (bf16[528,128]{1,0:T(8,128)(2,1)S(1)}, bf16[528,128]{1,0:T(8,128)(2,1)S(1)}, u32[]{:S(2)}, u32[]{:S(2)}) collective-permute-start(bf16[528,128]{1,0:T(8,128)(2,1)S(1)} %get-tuple-element.31.refs_3_), channel_id=1, source_target_pairs={{0,12},{1,9},{4,8},{5,13},{8,4},{9,1},{12,0},{13,5},{2,14},{3,11},... | collective-permute-start | bytes 405512 | tf_op jit(solution)/shard_map/ppermute | solution.py:326
  26.7 0.7 %collective-permute-done.7.there_ref = f32[4,8,128]{2,1,0:T(8,128)S(1)} collective-permute-done((f32[4,8,128]{2,1,0:T(8,128)S(1)}, f32[4,8,128]{2,1,0:T(8,128)S(1)}, u32[]{:S(2)}, u32[]{:S(2)}) %collective-permute-start.7) | collective-permute-done | bytes 16416 | tf_op jit(solution)/shard_map/ppermute | solution.py:332
  27.7 4.4 %collective-permute-done.8.refs_0_ = bf16[528,128]{1,0:T(8,128)(2,1)S(1)} collective-permute-done((bf16[528,128]{1,0:T(8,128)(2,1)S(1)}, bf16[528,128]{1,0:T(8,128)(2,1)S(1)}, u32[]{:S(2)}, u32[]{:S(2)}) %collective-permute-start.8) | collective-permute-done | bytes 135200 | tf_op jit(solution)/shard_map/ppermute | solution.py:326
  32.1 1.4 %collective-permute-done.9.refs_1_ = bf16[528,128]{1,0:T(8,128)(2,1)S(1)} collective-permute-done((bf16[528,128]{1,0:T(8,128)(2,1)S(1)}, bf16[528,128]{1,0:T(8,128)(2,1)S(1)}, u32[]{:S(2)}, u32[]{:S(2)}) %collective-permute-start.9) | collective-permute-done | bytes 135200 | tf_op jit(solution)/shard_map/ppermute | solution.py:326
  33.5 0.8 %collective-permute-done.10.refs_2_ = bf16[528,128]{1,0:T(8,128)(2,1)S(1)} collective-permute-done((bf16[528,128]{1,0:T(8,128)(2,1)S(1)}, bf16[528,128]{1,0:T(8,128)(2,1)S(1)}, u32[]{:S(2)}, u32[]{:S(2)}) %collective-permute-start.10) | collective-permute-done | bytes 135200 | tf_op jit(solution)/shard_map/ppermute | solution.py:326
  34.9 0.8 %collective-permute-done.13.refs_6_ = bf16[528,128]{1,0:T(8,128)(2,1)S(1)} collective-permute-done((bf16[528,128]{1,0:T(8,128)(2,1)S(1)}, bf16[528,128]{1,0:T(8,128)(2,1)S(1)}, u32[]{:S(2)}, u32[]{:S(2)}) %collective-permute-start.13) | collective-permute-done | bytes 135200 | tf_op jit(solution)/shard_map/ppermute | solution.py:332
  35.7 1.7 %shard_map.99 = (bf16[4,512,512]{2,1,0:T(8,128)(2,1)S(1)}, f32[4,8,512]{2,1,0:T(8,128)S(1)}, f32[4,512]{1,0:T(4,128)S(1)}, f32[4,512]{1,0:T(4,128)S(1)}) custom-call(bf16[528,128]{1,0:T(8,128)(2,1)S(1)} %collective-permute-done.8.refs_0_, bf16[528,128]{1,0:T(8,128)(2,1)S(1)} %collective-permute-done.9.refs_1_, ...), custom_call_target="tpu_custom_call" | custom-call | tf_op jit(solution)/shard_map/pallas_call | solution.py:384
  37.5 1.6 %collective-permute-start.15 = (f32[1,512]{1,0:T(1,128)S(1)}, f32[1,512]{1,0:T(1,128)S(1)}, u32[]{:S(2)}, u32[]{:S(2)}) collective-permute-start(f32[1,512]{1,0:T(1,128)S(1)} %slice.50), channel_id=1, source_target_pairs={{0,2},{2,0},{1,3},{3,1},{4,6},{6,4},{5,7},{7,5},{8,10},{10,8},{9,1... | collective-permute-start | bytes 6152 | tf_op jit(solution)/shard_map/ppermute | solution.py:329
  39.0 2.1 %collective-permute-done.15.state_ref = f32[1,512]{1,0:T(1,128)S(1)} collective-permute-done((f32[1,512]{1,0:T(1,128)S(1)}, f32[1,512]{1,0:T(1,128)S(1)}, u32[]{:S(2)}, u32[]{:S(2)}) %collective-permute-start.15) | collective-permute-done | bytes 2080 | tf_op jit(solution)/shard_map/ppermute | solution.py:329
  41.1 1.2 %shard_map.100 = (f32[4,512]{1,0:T(4,128)S(1)}, f32[4,512]{1,0:T(4,128)S(1)}) custom-call(bf16[4,512,512]{2,1,0:T(8,128)(2,1)S(1)} %get-tuple-element.34.grams, f32[4,8,512]{2,1,0:T(8,128)S(1)} %get-tuple-element.35.vectors, f32[4,16,512]{2,1,0:T(8,128)S(1)} %shard_map.98.refs_8_.bands, f32[1,512]{1,0:T(1,128)S(1)} %collective-permute-done.15.state_ref), custom_call_target="tpu_custom_call" | custom-call | tf_op jit(solution)/shard_map/pallas_call | solution.py:401
  42.3 1.6 %collective-permute-start.16 = (f32[1,512]{1,0:T(1,128)S(1)}, f32[1,512]{1,0:T(1,128)S(1)}, u32[]{:S(2)}, u32[]{:S(2)}) collective-permute-start(f32[1,512]{1,0:T(1,128)S(1)} %fusion.1), channel_id=1, source_target_pairs={{0,2},{2,0},{1,3},{3,1},{4,6},{6,4},{5,7},{7,5},{8,10},{10,8},{9,1... | collective-permute-start | bytes 6152 | tf_op jit(solution)/shard_map/ppermute | solution.py:329
  43.9 2.1 %collective-permute-done.16 = f32[1,512]{1,0:T(1,128)S(1)} collective-permute-done((f32[1,512]{1,0:T(1,128)S(1)}, f32[1,512]{1,0:T(1,128)S(1)}, u32[]{:S(2)}, u32[]{:S(2)}) %collective-permute-start.16) | collective-permute-done | bytes 2080 | tf_op jit(solution)/shard_map/ppermute | solution.py:329
  (35 shorter events, 2.7 us)
Async XLA Ops:
  0.6 2.2 %copy-start.5 = (s32[1,16,1]{1,2,0:T(1,128)S(1)}, s32[1,16,1]{1,2,0:T(1,128)}, u32[]{:S(2)}) copy-start(s32[1,16,1]{1,2,0:T(1,128)} %param.10) | copy-start | bytes 196
  0.6 2.2 %copy-start = (bf16[1,16,128]{2,1,0:T(8,128)(2,1)S(1)}, bf16[1,16,128]{2,1,0:T(8,128)(2,1)}, u32[]{:S(2)}) copy-start(bf16[1,16,128]{2,1,0:T(8,128)(2,1)} %param.9) | copy-start | bytes 12292
  0.7 2.2 %copy-start.1 = (f32[1,1,512]{2,1,0:T(1,128)S(1)}, f32[1,1,512]{2,1,0:T(1,128)}, u32[]{:S(2)}) copy-start(f32[1,1,512]{2,1,0:T(1,128)} %param.12) | copy-start | bytes 6148
  0.7 2.2 %copy-start.2 = (f32[1,1,512]{2,1,0:T(1,128)S(1)}, f32[1,1,512]{2,1,0:T(1,128)}, u32[]{:S(2)}) copy-start(f32[1,1,512]{2,1,0:T(1,128)} %param.13) | copy-start | bytes 6148
  0.7 2.2 %copy-start.3 = (f32[1,1,512]{2,1,0:T(1,128)S(1)}, f32[1,1,512]{2,1,0:T(1,128)}, u32[]{:S(2)}) copy-start(f32[1,1,512]{2,1,0:T(1,128)} %param.14) | copy-start | bytes 6148
  0.7 9.3 %collective-permute-start.3 = (bf16[16,128,256]{2,1,0:T(8,128)(2,1)}, bf16[16,128,256]{2,1,0:T(8,128)(2,1)S(1)}, u32[]{:S(2)}, u32[]{:S(2)}) collective-permute-start(bf16[16,128,256]{2,1,0:T(8,128)(2,1)} %bitcast.45), channel_id=1, source_target_pairs={{0,1},{1,0},{2,3},{3,2},{4,5},{5,4},{6,7},{7,6},{8,9},{9,8},{10,11... | collective-permute-start | bytes 3145736 | tf_op jit(solution)/shard_map/ppermute | solution.py:315
  2.9 32.9 %copy-start.4 = (f32[512]{0:T(512)S(1)}, f32[512]{0:T(512)}, u32[]{:S(2)}) copy-start(f32[512]{0:T(512)} %param.15) | copy-start | bytes 6148
  4.7 10.8 %collective-permute-start = (bf16[288,128]{1,0:T(8,128)(2,1)S(1)}, bf16[288,128]{1,0:T(8,128)(2,1)S(1)}, u32[]{:S(2)}, u32[]{:S(2)}) collective-permute-start(bf16[288,128]{1,0:T(8,128)(2,1)S(1)} %get-tuple-element.21), channel_id=1, source_target_pairs={{0,8},{1,13},{4,12},{5,9},{8,0},{9,5},{12,4},{13,1},{2,10},{3,15},... | collective-permute-start | bytes 221192 | tf_op jit(solution)/shard_map/ppermute | solution.py:326
  8.4 8.5 %collective-permute-start.1 = (bf16[288,128]{1,0:T(8,128)(2,1)S(1)}, bf16[288,128]{1,0:T(8,128)(2,1)S(1)}, u32[]{:S(2)}, u32[]{:S(2)}) collective-permute-start(bf16[288,128]{1,0:T(8,128)(2,1)S(1)} %get-tuple-element.22), channel_id=1, source_target_pairs={{0,4},{1,5},{4,0},{5,1},{8,12},{9,13},{12,8},{13,9},{2,6},{3,7},{6... | collective-permute-start | bytes 221192 | tf_op jit(solution)/shard_map/ppermute | solution.py:326
  10.0 6.9 %collective-permute-start.2 = (bf16[288,128]{1,0:T(8,128)(2,1)S(1)}, bf16[288,128]{1,0:T(8,128)(2,1)S(1)}, u32[]{:S(2)}, u32[]{:S(2)}) collective-permute-start(bf16[288,128]{1,0:T(8,128)(2,1)S(1)} %get-tuple-element.23), channel_id=1, source_target_pairs={{0,12},{1,9},{4,8},{5,13},{8,4},{9,1},{12,0},{13,5},{2,14},{3,11},... | collective-permute-start | bytes 221192 | tf_op jit(solution)/shard_map/ppermute | solution.py:326
  11.0 9.0 %collective-permute-start.4 = (bf16[256,128]{1,0:T(8,128)(2,1)S(1)}, bf16[256,128]{1,0:T(8,128)(2,1)S(1)}, u32[]{:S(2)}, u32[]{:S(2)}) collective-permute-start(bf16[256,128]{1,0:T(8,128)(2,1)S(1)} %get-tuple-element.26), channel_id=1, source_target_pairs={{0,8},{1,13},{4,12},{5,9},{8,0},{9,5},{12,4},{13,1},{2,10},{3,15},... | collective-permute-start | bytes 196616 | tf_op jit(solution)/shard_map/ppermute | solution.py:326
  13.0 7.1 %collective-permute-start.5 = (bf16[256,128]{1,0:T(8,128)(2,1)S(1)}, bf16[256,128]{1,0:T(8,128)(2,1)S(1)}, u32[]{:S(2)}, u32[]{:S(2)}) collective-permute-start(bf16[256,128]{1,0:T(8,128)(2,1)S(1)} %get-tuple-element.27), channel_id=1, source_target_pairs={{0,4},{1,5},{4,0},{5,1},{8,12},{9,13},{12,8},{13,9},{2,6},{3,7},{6... | collective-permute-start | bytes 196616 | tf_op jit(solution)/shard_map/ppermute | solution.py:326
  15.5 6.2 %collective-permute-start.6 = (bf16[256,128]{1,0:T(8,128)(2,1)S(1)}, bf16[256,128]{1,0:T(8,128)(2,1)S(1)}, u32[]{:S(2)}, u32[]{:S(2)}) collective-permute-start(bf16[256,128]{1,0:T(8,128)(2,1)S(1)} %get-tuple-element.28), channel_id=1, source_target_pairs={{0,12},{1,9},{4,8},{5,13},{8,4},{9,1},{12,0},{13,5},{2,14},{3,11},... | collective-permute-start | bytes 196616 | tf_op jit(solution)/shard_map/ppermute | solution.py:326
  21.8 10.3 %collective-permute-start.8 = (bf16[528,128]{1,0:T(8,128)(2,1)S(1)}, bf16[528,128]{1,0:T(8,128)(2,1)S(1)}, u32[]{:S(2)}, u32[]{:S(2)}) collective-permute-start(bf16[528,128]{1,0:T(8,128)(2,1)S(1)} %get-tuple-element.31.refs_3_), channel_id=1, source_target_pairs={{0,8},{1,13},{4,12},{5,9},{8,0},{9,5},{12,4},{13,1},{2,10},{3,15},... | collective-permute-start | bytes 405512 | tf_op jit(solution)/shard_map/ppermute | solution.py:326
  24.2 9.4 %collective-permute-start.9 = (bf16[528,128]{1,0:T(8,128)(2,1)S(1)}, bf16[528,128]{1,0:T(8,128)(2,1)S(1)}, u32[]{:S(2)}, u32[]{:S(2)}) collective-permute-start(bf16[528,128]{1,0:T(8,128)(2,1)S(1)} %get-tuple-element.31.refs_3_), channel_id=1, source_target_pairs={{0,4},{1,5},{4,0},{5,1},{8,12},{9,13},{12,8},{13,9},{2,6},{3,7},{6... | collective-permute-start | bytes 405512 | tf_op jit(solution)/shard_map/ppermute | solution.py:326
  24.9 9.4 %collective-permute-start.10 = (bf16[528,128]{1,0:T(8,128)(2,1)S(1)}, bf16[528,128]{1,0:T(8,128)(2,1)S(1)}, u32[]{:S(2)}, u32[]{:S(2)}) collective-permute-start(bf16[528,128]{1,0:T(8,128)(2,1)S(1)} %get-tuple-element.31.refs_3_), channel_id=1, source_target_pairs={{0,12},{1,9},{4,8},{5,13},{8,4},{9,1},{12,0},{13,5},{2,14},{3,11},... | collective-permute-start | bytes 405512 | tf_op jit(solution)/shard_map/ppermute | solution.py:326
  26.2 1.2 %collective-permute-start.7 = (f32[4,8,128]{2,1,0:T(8,128)S(1)}, f32[4,8,128]{2,1,0:T(8,128)S(1)}, u32[]{:S(2)}, u32[]{:S(2)}) collective-permute-start(f32[4,8,128]{2,1,0:T(8,128)S(1)} %get-tuple-element.30.here_ref), channel_id=1, source_target_pairs={{0,1},{1,0},{2,3},{3,2},{4,5},{5,4},{6,7},{7,6},{8,9},{9,8},{10,11... | collective-permute-start | bytes 49160 | tf_op jit(solution)/shard_map/ppermute | solution.py:332
  26.2 8.2 %collective-permute-start.14 = (bf16[528,128]{1,0:T(8,128)(2,1)S(1)}, bf16[528,128]{1,0:T(8,128)(2,1)S(1)}, u32[]{:S(2)}, u32[]{:S(2)}) collective-permute-start(bf16[528,128]{1,0:T(8,128)(2,1)S(1)} %get-tuple-element.31.refs_3_), channel_id=1, source_target_pairs={{0,1},{1,0},{2,3},{3,2},{4,5},{5,4},{6,7},{7,6},{8,9},{9,8},{10,11... | collective-permute-start | bytes 405512 | tf_op jit(solution)/shard_map/ppermute | solution.py:332
  32.1 2.3 %collective-permute-start.11 = (bf16[528,128]{1,0:T(8,128)(2,1)S(1)}, bf16[528,128]{1,0:T(8,128)(2,1)S(1)}, u32[]{:S(2)}, u32[]{:S(2)}) collective-permute-start(bf16[528,128]{1,0:T(8,128)(2,1)S(1)} %collective-permute-done.8.refs_0_), channel_id=1, source_target_pairs={{0,1},{1,0},{2,3},{3,2},{4,5},{5,4},{6,7},{7,6},{8,9},{9,8},{10,11... | collective-permute-start | bytes 405512 | tf_op jit(solution)/shard_map/ppermute | solution.py:332
  33.5 1.4 %collective-permute-start.12 = (bf16[528,128]{1,0:T(8,128)(2,1)S(1)}, bf16[528,128]{1,0:T(8,128)(2,1)S(1)}, u32[]{:S(2)}, u32[]{:S(2)}) collective-permute-start(bf16[528,128]{1,0:T(8,128)(2,1)S(1)} %collective-permute-done.9.refs_1_), channel_id=1, source_target_pairs={{0,1},{1,0},{2,3},{3,2},{4,5},{5,4},{6,7},{7,6},{8,9},{9,8},{10,11... | collective-permute-start | bytes 405512 | tf_op jit(solution)/shard_map/ppermute | solution.py:332
  34.4 1.4 %collective-permute-start.13 = (bf16[528,128]{1,0:T(8,128)(2,1)S(1)}, bf16[528,128]{1,0:T(8,128)(2,1)S(1)}, u32[]{:S(2)}, u32[]{:S(2)}) collective-permute-start(bf16[528,128]{1,0:T(8,128)(2,1)S(1)} %collective-permute-done.10.refs_2_), channel_id=1, source_target_pairs={{0,1},{1,0},{2,3},{3,2},{4,5},{5,4},{6,7},{7,6},{8,9},{9,8},{10,11... | collective-permute-start | bytes 405512 | tf_op jit(solution)/shard_map/ppermute | solution.py:332
  37.5 3.7 %collective-permute-start.15 = (f32[1,512]{1,0:T(1,128)S(1)}, f32[1,512]{1,0:T(1,128)S(1)}, u32[]{:S(2)}, u32[]{:S(2)}) collective-permute-start(f32[1,512]{1,0:T(1,128)S(1)} %slice.50), channel_id=1, source_target_pairs={{0,2},{2,0},{1,3},{3,1},{4,6},{6,4},{5,7},{7,5},{8,10},{10,8},{9,1... | collective-permute-start | bytes 6152 | tf_op jit(solution)/shard_map/ppermute | solution.py:329
  42.3 3.7 %collective-permute-start.16 = (f32[1,512]{1,0:T(1,128)S(1)}, f32[1,512]{1,0:T(1,128)S(1)}, u32[]{:S(2)}, u32[]{:S(2)}) collective-permute-start(f32[1,512]{1,0:T(1,128)S(1)} %fusion.1), channel_id=1, source_target_pairs={{0,2},{2,0},{1,3},{3,1},{4,6},{6,4},{5,7},{7,5},{8,10},{10,8},{9,1... | collective-permute-start | bytes 6152 | tf_op jit(solution)/shard_map/ppermute | solution.py:329

commit v11 on v10

--- a/solution.py
+++ b/solution.py
@@ -261,18 +261,16 @@
         innovations_ref[block : block + 1, :] = innovation
 
 
-def assemble_kernel(number, *refs):
-    own, other, rest = refs[:number], refs[number : 2 * number], refs[2 * number :]
-    bands, state_ref, grams, vectors, states_ref, innovations_ref = rest
+def put_grams(number, turns, own, other, grams, vectors):
     core, position = lax.axis_index("state"), lax.axis_index("tm")
     half = 2 * LANES
     line = lax.broadcasted_iota(jnp.int32, (LANES, LANES), 0)
     column = lax.broadcasted_iota(jnp.int32, (LANES, LANES), 1)
-    for turn in range(number):
+    for at, turn in enumerate(turns):
         flip, flip_other = flip_here(turn, number), flip_here(turn, number, 1)
         for pieces, side, block in (
-            (own[turn], core, position ^ flip),
-            (other[turn], 1 - core, position ^ flip_other),
+            (own[at], core, position ^ flip),
+            (other[at], 1 - core, position ^ flip_other),
         ):
 
             def piece(index):
@@ -295,9 +293,21 @@
                 put(beyond, here + index * LANES, piece(2 + index).T)
             below = pieces[4 * LANES :, :].astype(jnp.float32)
             below = below[:4] + below[4:8] + below[8:12]
-            for at in range(4):
-                lanes = pl.ds(pl.multiple_of(here + (at % 2) * LANES, LANES), LANES)
-                vectors[block, at // 2 : at // 2 + 1, lanes] = below[at : at + 1]
+            for vector in range(4):
+                lanes = pl.ds(pl.multiple_of(here + (vector % 2) * LANES, LANES), LANES)
+                vectors[block, vector // 2 : vector // 2 + 1, lanes] = below[vector : vector + 1]
+
+
+def early_kernel(number, turns, *refs):
+    count = len(turns)
+    put_grams(number, turns, refs[:count], refs[count : 2 * count], refs[-2], refs[-1])
+
+
+def assemble_kernel(number, turns, *refs):
+    count = len(turns)
+    own, other, rest = refs[:count], refs[count : 2 * count], refs[2 * count :]
+    _, _, bands, state_ref, grams, vectors, states_ref, innovations_ref = rest
+    put_grams(number, turns, own, other, grams, vectors)
     chain(grams, vectors, bands, state_ref[...], states_ref, innovations_ref)
 
 
@@ -326,7 +336,12 @@
         return lax.ppermute(array, ("tm", "state"), pairs)
 
     def ring(array, step):
-        return lax.ppermute(array, "grp", [(i, (i + step) % grp_size) for i in range(grp_size)])
+        pairs = [
+            (i * state_size + j, (i + step) % grp_size * state_size + state_size - 1 - j)
+            for i in range(grp_size)
+            for j in range(state_size)
+        ]
+        return lax.ppermute(array, ("grp", "state"), pairs)
 
     def across(array):
         return lax.ppermute(array, "state", [(i, (i + 1) % state_size) for i in range(state_size)])
@@ -381,18 +396,29 @@
         )(here, across(here))
         bands, own_sums[0] = lax.optimization_barrier((bands, own_sums[0]))
         other_sums = [across(values) for values in own_sums]
+        whole = (
+            jax.ShapeDtypeStruct((tm_size, width, width), jnp.bfloat16),
+            jax.ShapeDtypeStruct((tm_size, 8, width), jnp.float32),
+        )
+        late = [tm_size - 2]
+        early = [turn for turn in range(tm_size) if turn not in late]
+        arrays = [own_sums[turn] for turn in early] + [other_sums[turn] for turn in early]
+        grams, vectors = pl.pallas_call(
+            functools.partial(early_kernel, tm_size, early),
+            out_shape=whole,
+            in_specs=[VMEM] * len(arrays),
+            out_specs=[VMEM] * 2,
+            compiler_params=KERNEL,
+        )(*arrays)
+        arrays = [own_sums[turn] for turn in late] + [other_sums[turn] for turn in late]
         grams, vectors, new_states, new_innovations = pl.pallas_call(
-            functools.partial(assemble_kernel, tm_size),
-            out_shape=(
-                jax.ShapeDtypeStruct((tm_size, width, width), jnp.bfloat16),
-                jax.ShapeDtypeStruct((tm_size, 8, width), jnp.float32),
-                states_shape,
-                states_shape,
-            ),
-            in_specs=[VMEM] * (2 * tm_size + 2),
+            functools.partial(assemble_kernel, tm_size, late),
+            out_shape=whole + (states_shape, states_shape),
+            in_specs=[VMEM] * (len(arrays) + 4),
             out_specs=[VMEM] * 4,
+            input_output_aliases={len(arrays): 0, len(arrays) + 1: 1},
             compiler_params=KERNEL,
-        )(*own_sums, *other_sums, bands, state)
+        )(*arrays, grams, vectors, bands, state)
         gains = bands[:, 2 * STEPS + 1]
 
         def run_group(state, group):

time: 46.8 us -> 45.3 us (0.968)
  waiting for transfers between devices: 17.7 us -> 16.6 us
  starting transfers between devices: 19.6 us -> 19.1 us
    ppermute x2, waiting for transfers between devices: 4.19 us -> 3.53 us  [ring(): return lax.ppermute(array, ('grp', 'state'), pairs)]
    ppermute x2, starting transfers between devices: 3.11 us -> 2.61 us  [ring(): return lax.ppermute(array, ('grp', 'state'), pairs)]
    pallas_call x1 -> x2, Pallas kernels: 1.71 us -> 1.79 us  [the longest x1 1.37 us: shards(): pl.pallas_call(functools.partial(assemble_kernel, tm_size, late), out_sha...]
  transfers between devices with their start and end apart: 17 -> 17, of which waited for: 10 -> 10; matrix products, arithmetic and copies ran while one was open for 4% -> 4% of each run, Pallas kernels for 7% -> 8%
where the time goes in v11:
time: 45.3 us; the launch traced here: 45.2 us
  starting transfers between devices  19.1 us (42%)
  waiting for transfers between devices  16.6 us (37%)
  Pallas kernels  6.24 us (14%)
  other arithmetic  2.37 us (5%)
  between operations  0.81 us (2%)
    ppermute x9, starting transfers between devices, flip_over(): return lax.ppermute(array, ('tm', 'state'), pairs)  15.5 us
    ppermute x9, waiting for transfers between devices, flip_over(): return lax.ppermute(array, ('tm', 'state'), pairs)  11.5 us
    ppermute x2, waiting for transfers between devices, ring(): return lax.ppermute(array, ('grp', 'state'), pairs)  3.53 us
    ppermute x2, starting transfers between devices, ring(): return lax.ppermute(array, ('grp', 'state'), pairs)  2.61 us
    pallas_call x1, Pallas kernels, shards(): pl.pallas_call(half_kernel, out_shape=[jax.ShapeDtypeStruct((2 * LANES +...  1.8 us
    select_n x1, other arithmetic, shards(): jnp.where(row < tile_count[0][:, None, None], own, jnp.zeros((), own.dtype))  1.65 us
    ppermute x5, waiting for transfers between devices, across(): lax.ppermute(array, 'state', [(i, (i + 1) % state_size) for i in range(st...  1.59 us
    pallas_call x1, Pallas kernels, shards(): pl.pallas_call(functools.partial(assemble_kernel, tm_size, late), out_sha...  1.37 us
  transfers between devices with their start and end apart: 17, of which 10 were waited for; matrix products, arithmetic and copies ran while one was open for 4% of the time, Pallas kernels for 8%

profile of v11, /device:TPU:0, one launch (start us, length us, event | category | flops | bytes accessed | tf_op | source)
XLA Modules:
  0.0 45.2 jit_solution(17090846834621264213)
XLA Ops:
  1.2 1.7 %fusion.own_ref = bf16[16,128,256]{2,1,0:T(8,128)(2,1)S(1)} fusion(s32[16]{0:T(128)} %bitcast.46, bf16[1,16,128,256]{3,2,1,0:T(8,128)(2,1)} %param.8), kind=kLoop, calls=%fused_computation.1 | loop fusion | flops 1048576 | bytes 2097216 | tf_op jit(solution)/shard_map/jit(_where)/select_n | solution.py:351
  2.9 1.8 %shard_map.95 = (bf16[288,128]{1,0:T(8,128)(2,1)S(1)}, bf16[288,128]{1,0:T(8,128)(2,1)S(1)}, bf16[288,128]{1,0:T(8,128)(2,1)S(1)}, bf16[288,128]{1,0:T(8,128)(2,1)S(1)}, bf16[16,256,128]{2,1,0:T(8,128)(2,1)S(1)}) custom-call(s32[16]{0:T(128)S(1)} %bitcast.42, bf16[16,128]{1,0:T(8,128)(2,1)S(1)} %bitcast.38, bf16[16,128,256]{2,1,0:T(8,128)(2,1)S(1)} %fusion.own_ref, ...), custom_call_target="tpu_custom_call" | custom-call | tf_op jit(solution)/shard_map/pallas_call | solution.py:354
  4.7 3.6 %collective-permute-start = (bf16[288,128]{1,0:T(8,128)(2,1)S(1)}, bf16[288,128]{1,0:T(8,128)(2,1)S(1)}, u32[]{:S(2)}, u32[]{:S(2)}) collective-permute-start(bf16[288,128]{1,0:T(8,128)(2,1)S(1)} %get-tuple-element.23), channel_id=1, source_target_pairs={{0,8},{1,13},{4,12},{5,9},{8,0},{9,5},{12,4},{13,1},{2,10},{3,15},... | collective-permute-start | bytes 221192 | tf_op jit(solution)/shard_map/ppermute | solution.py:336
  8.4 1.6 %collective-permute-start.1 = (bf16[288,128]{1,0:T(8,128)(2,1)S(1)}, bf16[288,128]{1,0:T(8,128)(2,1)S(1)}, u32[]{:S(2)}, u32[]{:S(2)}) collective-permute-start(bf16[288,128]{1,0:T(8,128)(2,1)S(1)} %get-tuple-element.24), channel_id=1, source_target_pairs={{0,4},{1,5},{4,0},{5,1},{8,12},{9,13},{12,8},{13,9},{2,6},{3,7},{6... | collective-permute-start | bytes 221192 | tf_op jit(solution)/shard_map/ppermute | solution.py:336
  10.0 1.1 %shard_map.96 = (bf16[256,128]{1,0:T(8,128)(2,1)S(1)}, bf16[256,128]{1,0:T(8,128)(2,1)S(1)}, bf16[256,128]{1,0:T(8,128)(2,1)S(1)}, bf16[256,128]{1,0:T(8,128)(2,1)S(1)}) custom-call(s32[16]{0:T(128)S(1)} %bitcast.43, bf16[16,256,128]{2,1,0:T(8,128)(2,1)S(1)} %get-tuple-element.27.turned_ref, bf16[16,128,256]{2,1,0:T(8,128)(2,1)S(1)} %collective-permute-done.3.other_ref), custom_call_target="tpu_custom_call" | custom-call | tf_op jit(solution)/shard_map/pallas_call | solution.py:370
  11.0 2.0 %collective-permute-start.4 = (bf16[256,128]{1,0:T(8,128)(2,1)S(1)}, bf16[256,128]{1,0:T(8,128)(2,1)S(1)}, u32[]{:S(2)}, u32[]{:S(2)}) collective-permute-start(bf16[256,128]{1,0:T(8,128)(2,1)S(1)} %get-tuple-element.28), channel_id=1, source_target_pairs={{0,8},{1,13},{4,12},{5,9},{8,0},{9,5},{12,4},{13,1},{2,10},{3,15},... | collective-permute-start | bytes 196616 | tf_op jit(solution)/shard_map/ppermute | solution.py:336
  13.0 2.5 %collective-permute-start.5 = (bf16[256,128]{1,0:T(8,128)(2,1)S(1)}, bf16[256,128]{1,0:T(8,128)(2,1)S(1)}, u32[]{:S(2)}, u32[]{:S(2)}) collective-permute-start(bf16[256,128]{1,0:T(8,128)(2,1)S(1)} %get-tuple-element.29), channel_id=1, source_target_pairs={{0,4},{1,5},{4,0},{5,1},{8,12},{9,13},{12,8},{13,9},{2,6},{3,7},{6... | collective-permute-start | bytes 196616 | tf_op jit(solution)/shard_map/ppermute | solution.py:336
  15.5 1.3 %collective-permute-start.6 = (bf16[256,128]{1,0:T(8,128)(2,1)S(1)}, bf16[256,128]{1,0:T(8,128)(2,1)S(1)}, u32[]{:S(2)}, u32[]{:S(2)}) collective-permute-start(bf16[256,128]{1,0:T(8,128)(2,1)S(1)} %get-tuple-element.30), channel_id=1, source_target_pairs={{0,12},{1,9},{4,8},{5,13},{8,4},{9,1},{12,0},{13,5},{2,14},{3,11},... | collective-permute-start | bytes 196616 | tf_op jit(solution)/shard_map/ppermute | solution.py:336
  16.8 3.2 %collective-permute-done.4.refs_4_ = bf16[256,128]{1,0:T(8,128)(2,1)S(1)} collective-permute-done((bf16[256,128]{1,0:T(8,128)(2,1)S(1)}, bf16[256,128]{1,0:T(8,128)(2,1)S(1)}, u32[]{:S(2)}, u32[]{:S(2)}) %collective-permute-start.4) | collective-permute-done | bytes 65568 | tf_op jit(solution)/shard_map/ppermute | solution.py:336
  20.1 1.6 %collective-permute-done.6.refs_6_ = bf16[256,128]{1,0:T(8,128)(2,1)S(1)} collective-permute-done((bf16[256,128]{1,0:T(8,128)(2,1)S(1)}, bf16[256,128]{1,0:T(8,128)(2,1)S(1)}, u32[]{:S(2)}, u32[]{:S(2)}) %collective-permute-start.6) | collective-permute-done | bytes 65568 | tf_op jit(solution)/shard_map/ppermute | solution.py:336
  21.8 2.4 %collective-permute-start.10 = (bf16[528,128]{1,0:T(8,128)(2,1)S(1)}, bf16[528,128]{1,0:T(8,128)(2,1)S(1)}, u32[]{:S(2)}, u32[]{:S(2)}) collective-permute-start(bf16[528,128]{1,0:T(8,128)(2,1)S(1)} %get-tuple-element.32.refs_2_), channel_id=1, source_target_pairs={{0,8},{1,13},{4,12},{5,9},{8,0},{9,5},{12,4},{13,1},{2,10},{3,15},... | collective-permute-start | bytes 405512 | tf_op jit(solution)/shard_map/ppermute | solution.py:336
  24.1 0.8 %collective-permute-start.11 = (bf16[528,128]{1,0:T(8,128)(2,1)S(1)}, bf16[528,128]{1,0:T(8,128)(2,1)S(1)}, u32[]{:S(2)}, u32[]{:S(2)}) collective-permute-start(bf16[528,128]{1,0:T(8,128)(2,1)S(1)} %get-tuple-element.32.refs_2_), channel_id=1, source_target_pairs={{0,4},{1,5},{4,0},{5,1},{8,12},{9,13},{12,8},{13,9},{2,6},{3,7},{6... | collective-permute-start | bytes 405512 | tf_op jit(solution)/shard_map/ppermute | solution.py:336
  24.9 1.3 %collective-permute-start.7 = (bf16[528,128]{1,0:T(8,128)(2,1)S(1)}, bf16[528,128]{1,0:T(8,128)(2,1)S(1)}, u32[]{:S(2)}, u32[]{:S(2)}) collective-permute-start(bf16[528,128]{1,0:T(8,128)(2,1)S(1)} %get-tuple-element.32.refs_2_), channel_id=1, source_target_pairs={{0,12},{1,9},{4,8},{5,13},{8,4},{9,1},{12,0},{13,5},{2,14},{3,11},... | collective-permute-start | bytes 405512 | tf_op jit(solution)/shard_map/ppermute | solution.py:336
  26.7 0.7 %collective-permute-done.9.there_ref = f32[4,8,128]{2,1,0:T(8,128)S(1)} collective-permute-done((f32[4,8,128]{2,1,0:T(8,128)S(1)}, f32[4,8,128]{2,1,0:T(8,128)S(1)}, u32[]{:S(2)}, u32[]{:S(2)}) %collective-permute-start.9) | collective-permute-done | bytes 16416 | tf_op jit(solution)/shard_map/ppermute | solution.py:347
  27.7 4.4 %collective-permute-done.10.refs_0_ = bf16[528,128]{1,0:T(8,128)(2,1)S(1)} collective-permute-done((bf16[528,128]{1,0:T(8,128)(2,1)S(1)}, bf16[528,128]{1,0:T(8,128)(2,1)S(1)}, u32[]{:S(2)}, u32[]{:S(2)}) %collective-permute-start.10) | collective-permute-done | bytes 135200 | tf_op jit(solution)/shard_map/ppermute | solution.py:336
  32.1 1.3 %collective-permute-done.11.refs_1_ = bf16[528,128]{1,0:T(8,128)(2,1)S(1)} collective-permute-done((bf16[528,128]{1,0:T(8,128)(2,1)S(1)}, bf16[528,128]{1,0:T(8,128)(2,1)S(1)}, u32[]{:S(2)}, u32[]{:S(2)}) %collective-permute-start.11) | collective-permute-done | bytes 135200 | tf_op jit(solution)/shard_map/ppermute | solution.py:336
  33.4 0.9 %collective-permute-done.7.refs_0_ = bf16[528,128]{1,0:T(8,128)(2,1)S(1)} collective-permute-done((bf16[528,128]{1,0:T(8,128)(2,1)S(1)}, bf16[528,128]{1,0:T(8,128)(2,1)S(1)}, u32[]{:S(2)}, u32[]{:S(2)}) %collective-permute-start.7) | collective-permute-done | bytes 135200 | tf_op jit(solution)/shard_map/ppermute | solution.py:336
  35.7 1.4 %shard_map.100 = (bf16[4,512,512]{2,1,0:T(8,128)(2,1)S(1)}, f32[4,8,512]{2,1,0:T(8,128)S(1)}, f32[4,512]{1,0:T(4,128)S(1)}, f32[4,512]{1,0:T(4,128)S(1)}) custom-call(bf16[528,128]{1,0:T(8,128)(2,1)S(1)} %collective-permute-done.7.refs_0_, bf16[528,128]{1,0:T(8,128)(2,1)S(1)} %collective-permute-done.8.refs_1_, ...), custom_call_target="tpu_custom_call", output_to_operand_aliasing={{0}: (2, {}), {1}: (3, {})} | custom-call | tf_op jit(solution)/shard_map/pallas_call | solution.py:414
  37.1 1.3 %collective-permute-start.15 = (f32[1,512]{1,0:T(1,128)S(1)}, f32[1,512]{1,0:T(1,128)S(1)}, u32[]{:S(2)}, u32[]{:S(2)}) collective-permute-start(f32[1,512]{1,0:T(1,128)S(1)} %slice.50), channel_id=1, source_target_pairs={{0,3},{1,2},{2,1},{3,0},{4,7},{5,6},{6,5},{7,4},{8,11},{9,10},{10,... | collective-permute-start | bytes 6152 | tf_op jit(solution)/shard_map/ppermute | solution.py:344
  38.4 1.8 %collective-permute-done.15.state_ref = f32[1,512]{1,0:T(1,128)S(1)} collective-permute-done((f32[1,512]{1,0:T(1,128)S(1)}, f32[1,512]{1,0:T(1,128)S(1)}, u32[]{:S(2)}, u32[]{:S(2)}) %collective-permute-start.15) | collective-permute-done | bytes 2080 | tf_op jit(solution)/shard_map/ppermute | solution.py:344
  40.2 1.2 %shard_map.101 = (f32[4,512]{1,0:T(4,128)S(1)}, f32[4,512]{1,0:T(4,128)S(1)}) custom-call(bf16[4,512,512]{2,1,0:T(8,128)(2,1)S(1)} %get-tuple-element.38.grams, f32[4,8,512]{2,1,0:T(8,128)S(1)} %get-tuple-element.39.vectors, f32[4,16,512]{2,1,0:T(8,128)S(1)} %shard_map.98.refs_4_.bands, f32[1,512]{1,0:T(1,128)S(1)} %collective-permute-done.15.state_ref), custom_call_target="tpu_custom_call" | custom-call | tf_op jit(solution)/shard_map/pallas_call | solution.py:427
  41.4 1.3 %collective-permute-start.16 = (f32[1,512]{1,0:T(1,128)S(1)}, f32[1,512]{1,0:T(1,128)S(1)}, u32[]{:S(2)}, u32[]{:S(2)}) collective-permute-start(f32[1,512]{1,0:T(1,128)S(1)} %fusion.1), channel_id=1, source_target_pairs={{0,3},{1,2},{2,1},{3,0},{4,7},{5,6},{6,5},{7,4},{8,11},{9,10},{10,... | collective-permute-start | bytes 6152 | tf_op jit(solution)/shard_map/ppermute | solution.py:344
  42.7 1.8 %collective-permute-done.16 = f32[1,512]{1,0:T(1,128)S(1)} collective-permute-done((f32[1,512]{1,0:T(1,128)S(1)}, f32[1,512]{1,0:T(1,128)S(1)}, u32[]{:S(2)}, u32[]{:S(2)}) %collective-permute-start.16) | collective-permute-done | bytes 2080 | tf_op jit(solution)/shard_map/ppermute | solution.py:344
  44.5 0.7 %add_bitcast_fusion = (f32[1,1,256]{2,1,0:T(1,128)}, f32[1,1,256]{2,1,0:T(1,128)}) fusion(s32[]{:T(128)S(6)} %select_n.47, s32[]{:T(128)S(6)} %select_n.48, f32[1,512]{1,0:T(1,128)S(1)} %get-tuple-element.47, f32[1,512]{1,0:T(1,128)S(1)} %get-tuple-element.46, f32[1,512]{1,0:T(1,128)S(1)} %get-tuple-element.45, f32[1,512]{1,0:T(1,128)S(1)} %get-tuple-element.44, ...), kind=kLoop, calls=%fused_computation.22 | loop fusion | flops 1024 | bytes 11272 | tf_op jit(solution)/shard_map/reshape | solution.py:498
  (36 shorter events, 2.9 us)
Async XLA Ops:
  0.6 2.2 %copy-start.4 = (s32[1,16,1]{1,2,0:T(1,128)S(1)}, s32[1,16,1]{1,2,0:T(1,128)}, u32[]{:S(2)}) copy-start(s32[1,16,1]{1,2,0:T(1,128)} %param.10) | copy-start | bytes 196
  0.6 2.2 %copy-start = (bf16[1,16,128]{2,1,0:T(8,128)(2,1)S(1)}, bf16[1,16,128]{2,1,0:T(8,128)(2,1)}, u32[]{:S(2)}) copy-start(bf16[1,16,128]{2,1,0:T(8,128)(2,1)} %param.9) | copy-start | bytes 12292
  0.7 2.2 %copy-start.1 = (f32[1,1,512]{2,1,0:T(1,128)S(1)}, f32[1,1,512]{2,1,0:T(1,128)}, u32[]{:S(2)}) copy-start(f32[1,1,512]{2,1,0:T(1,128)} %param.12) | copy-start | bytes 6148
  0.7 2.2 %copy-start.2 = (f32[1,1,512]{2,1,0:T(1,128)S(1)}, f32[1,1,512]{2,1,0:T(1,128)}, u32[]{:S(2)}) copy-start(f32[1,1,512]{2,1,0:T(1,128)} %param.13) | copy-start | bytes 6148
  0.7 2.2 %copy-start.3 = (f32[1,1,512]{2,1,0:T(1,128)S(1)}, f32[1,1,512]{2,1,0:T(1,128)}, u32[]{:S(2)}) copy-start(f32[1,1,512]{2,1,0:T(1,128)} %param.14) | copy-start | bytes 6148
  0.7 9.3 %collective-permute-start.3 = (bf16[16,128,256]{2,1,0:T(8,128)(2,1)}, bf16[16,128,256]{2,1,0:T(8,128)(2,1)S(1)}, u32[]{:S(2)}, u32[]{:S(2)}) collective-permute-start(bf16[16,128,256]{2,1,0:T(8,128)(2,1)} %bitcast.45), channel_id=1, source_target_pairs={{0,1},{1,0},{2,3},{3,2},{4,5},{5,4},{6,7},{7,6},{8,9},{9,8},{10,11... | collective-permute-start | bytes 3145736 | tf_op jit(solution)/shard_map/ppermute | solution.py:325
  2.9 32.8 %copy-start.5 = (f32[512]{0:T(512)S(1)}, f32[512]{0:T(512)}, u32[]{:S(2)}) copy-start(f32[512]{0:T(512)} %param.15) | copy-start | bytes 6148
  4.7 10.8 %collective-permute-start = (bf16[288,128]{1,0:T(8,128)(2,1)S(1)}, bf16[288,128]{1,0:T(8,128)(2,1)S(1)}, u32[]{:S(2)}, u32[]{:S(2)}) collective-permute-start(bf16[288,128]{1,0:T(8,128)(2,1)S(1)} %get-tuple-element.23), channel_id=1, source_target_pairs={{0,8},{1,13},{4,12},{5,9},{8,0},{9,5},{12,4},{13,1},{2,10},{3,15},... | collective-permute-start | bytes 221192 | tf_op jit(solution)/shard_map/ppermute | solution.py:336
  8.4 8.5 %collective-permute-start.1 = (bf16[288,128]{1,0:T(8,128)(2,1)S(1)}, bf16[288,128]{1,0:T(8,128)(2,1)S(1)}, u32[]{:S(2)}, u32[]{:S(2)}) collective-permute-start(bf16[288,128]{1,0:T(8,128)(2,1)S(1)} %get-tuple-element.24), channel_id=1, source_target_pairs={{0,4},{1,5},{4,0},{5,1},{8,12},{9,13},{12,8},{13,9},{2,6},{3,7},{6... | collective-permute-start | bytes 221192 | tf_op jit(solution)/shard_map/ppermute | solution.py:336
  10.0 6.9 %collective-permute-start.2 = (bf16[288,128]{1,0:T(8,128)(2,1)S(1)}, bf16[288,128]{1,0:T(8,128)(2,1)S(1)}, u32[]{:S(2)}, u32[]{:S(2)}) collective-permute-start(bf16[288,128]{1,0:T(8,128)(2,1)S(1)} %get-tuple-element.25), channel_id=1, source_target_pairs={{0,12},{1,9},{4,8},{5,13},{8,4},{9,1},{12,0},{13,5},{2,14},{3,11},... | collective-permute-start | bytes 221192 | tf_op jit(solution)/shard_map/ppermute | solution.py:336
  11.0 9.0 %collective-permute-start.4 = (bf16[256,128]{1,0:T(8,128)(2,1)S(1)}, bf16[256,128]{1,0:T(8,128)(2,1)S(1)}, u32[]{:S(2)}, u32[]{:S(2)}) collective-permute-start(bf16[256,128]{1,0:T(8,128)(2,1)S(1)} %get-tuple-element.28), channel_id=1, source_target_pairs={{0,8},{1,13},{4,12},{5,9},{8,0},{9,5},{12,4},{13,1},{2,10},{3,15},... | collective-permute-start | bytes 196616 | tf_op jit(solution)/shard_map/ppermute | solution.py:336
  13.0 7.1 %collective-permute-start.5 = (bf16[256,128]{1,0:T(8,128)(2,1)S(1)}, bf16[256,128]{1,0:T(8,128)(2,1)S(1)}, u32[]{:S(2)}, u32[]{:S(2)}) collective-permute-start(bf16[256,128]{1,0:T(8,128)(2,1)S(1)} %get-tuple-element.29), channel_id=1, source_target_pairs={{0,4},{1,5},{4,0},{5,1},{8,12},{9,13},{12,8},{13,9},{2,6},{3,7},{6... | collective-permute-start | bytes 196616 | tf_op jit(solution)/shard_map/ppermute | solution.py:336
  15.5 6.2 %collective-permute-start.6 = (bf16[256,128]{1,0:T(8,128)(2,1)S(1)}, bf16[256,128]{1,0:T(8,128)(2,1)S(1)}, u32[]{:S(2)}, u32[]{:S(2)}) collective-permute-start(bf16[256,128]{1,0:T(8,128)(2,1)S(1)} %get-tuple-element.30), channel_id=1, source_target_pairs={{0,12},{1,9},{4,8},{5,13},{8,4},{9,1},{12,0},{13,5},{2,14},{3,11},... | collective-permute-start | bytes 196616 | tf_op jit(solution)/shard_map/ppermute | solution.py:336
  21.8 10.3 %collective-permute-start.10 = (bf16[528,128]{1,0:T(8,128)(2,1)S(1)}, bf16[528,128]{1,0:T(8,128)(2,1)S(1)}, u32[]{:S(2)}, u32[]{:S(2)}) collective-permute-start(bf16[528,128]{1,0:T(8,128)(2,1)S(1)} %get-tuple-element.32.refs_2_), channel_id=1, source_target_pairs={{0,8},{1,13},{4,12},{5,9},{8,0},{9,5},{12,4},{13,1},{2,10},{3,15},... | collective-permute-start | bytes 405512 | tf_op jit(solution)/shard_map/ppermute | solution.py:336
  24.1 9.3 %collective-permute-start.11 = (bf16[528,128]{1,0:T(8,128)(2,1)S(1)}, bf16[528,128]{1,0:T(8,128)(2,1)S(1)}, u32[]{:S(2)}, u32[]{:S(2)}) collective-permute-start(bf16[528,128]{1,0:T(8,128)(2,1)S(1)} %get-tuple-element.32.refs_2_), channel_id=1, source_target_pairs={{0,4},{1,5},{4,0},{5,1},{8,12},{9,13},{12,8},{13,9},{2,6},{3,7},{6... | collective-permute-start | bytes 405512 | tf_op jit(solution)/shard_map/ppermute | solution.py:336
  24.9 9.4 %collective-permute-start.7 = (bf16[528,128]{1,0:T(8,128)(2,1)S(1)}, bf16[528,128]{1,0:T(8,128)(2,1)S(1)}, u32[]{:S(2)}, u32[]{:S(2)}) collective-permute-start(bf16[528,128]{1,0:T(8,128)(2,1)S(1)} %get-tuple-element.32.refs_2_), channel_id=1, source_target_pairs={{0,12},{1,9},{4,8},{5,13},{8,4},{9,1},{12,0},{13,5},{2,14},{3,11},... | collective-permute-start | bytes 405512 | tf_op jit(solution)/shard_map/ppermute | solution.py:336
  26.2 1.2 %collective-permute-start.9 = (f32[4,8,128]{2,1,0:T(8,128)S(1)}, f32[4,8,128]{2,1,0:T(8,128)S(1)}, u32[]{:S(2)}, u32[]{:S(2)}) collective-permute-start(f32[4,8,128]{2,1,0:T(8,128)S(1)} %get-tuple-element.33.here_ref), channel_id=1, source_target_pairs={{0,1},{1,0},{2,3},{3,2},{4,5},{5,4},{6,7},{7,6},{8,9},{9,8},{10,11... | collective-permute-start | bytes 49160 | tf_op jit(solution)/shard_map/ppermute | solution.py:347
  26.2 8.2 %collective-permute-start.14 = (bf16[528,128]{1,0:T(8,128)(2,1)S(1)}, bf16[528,128]{1,0:T(8,128)(2,1)S(1)}, u32[]{:S(2)}, u32[]{:S(2)}) collective-permute-start(bf16[528,128]{1,0:T(8,128)(2,1)S(1)} %get-tuple-element.32.refs_2_), channel_id=1, source_target_pairs={{0,1},{1,0},{2,3},{3,2},{4,5},{5,4},{6,7},{7,6},{8,9},{9,8},{10,11... | collective-permute-start | bytes 405512 | tf_op jit(solution)/shard_map/ppermute | solution.py:347
  32.1 2.3 %collective-permute-start.12 = (bf16[528,128]{1,0:T(8,128)(2,1)S(1)}, bf16[528,128]{1,0:T(8,128)(2,1)S(1)}, u32[]{:S(2)}, u32[]{:S(2)}) collective-permute-start(bf16[528,128]{1,0:T(8,128)(2,1)S(1)} %collective-permute-done.10.refs_0_), channel_id=1, source_target_pairs={{0,1},{1,0},{2,3},{3,2},{4,5},{5,4},{6,7},{7,6},{8,9},{9,8},{10,11... | collective-permute-start | bytes 405512 | tf_op jit(solution)/shard_map/ppermute | solution.py:347
  33.4 1.4 %collective-permute-start.13 = (bf16[528,128]{1,0:T(8,128)(2,1)S(1)}, bf16[528,128]{1,0:T(8,128)(2,1)S(1)}, u32[]{:S(2)}, u32[]{:S(2)}) collective-permute-start(bf16[528,128]{1,0:T(8,128)(2,1)S(1)} %collective-permute-done.11.refs_1_), channel_id=1, source_target_pairs={{0,1},{1,0},{2,3},{3,2},{4,5},{5,4},{6,7},{7,6},{8,9},{9,8},{10,11... | collective-permute-start | bytes 405512 | tf_op jit(solution)/shard_map/ppermute | solution.py:347
  34.4 1.4 %collective-permute-start.8 = (bf16[528,128]{1,0:T(8,128)(2,1)S(1)}, bf16[528,128]{1,0:T(8,128)(2,1)S(1)}, u32[]{:S(2)}, u32[]{:S(2)}) collective-permute-start(bf16[528,128]{1,0:T(8,128)(2,1)S(1)} %collective-permute-done.7.refs_0_), channel_id=1, source_target_pairs={{0,1},{1,0},{2,3},{3,2},{4,5},{5,4},{6,7},{7,6},{8,9},{9,8},{10,11... | collective-permute-start | bytes 405512 | tf_op jit(solution)/shard_map/ppermute | solution.py:347
  37.1 3.1 %collective-permute-start.15 = (f32[1,512]{1,0:T(1,128)S(1)}, f32[1,512]{1,0:T(1,128)S(1)}, u32[]{:S(2)}, u32[]{:S(2)}) collective-permute-start(f32[1,512]{1,0:T(1,128)S(1)} %slice.50), channel_id=1, source_target_pairs={{0,3},{1,2},{2,1},{3,0},{4,7},{5,6},{6,5},{7,4},{8,11},{9,10},{10,... | collective-permute-start | bytes 6152 | tf_op jit(solution)/shard_map/ppermute | solution.py:344
  41.4 3.1 %collective-permute-start.16 = (f32[1,512]{1,0:T(1,128)S(1)}, f32[1,512]{1,0:T(1,128)S(1)}, u32[]{:S(2)}, u32[]{:S(2)}) collective-permute-start(f32[1,512]{1,0:T(1,128)S(1)} %fusion.1), channel_id=1, source_target_pairs={{0,3},{1,2},{2,1},{3,0},{4,7},{5,6},{6,5},{7,4},{8,11},{9,10},{10,... | collective-permute-start | bytes 6152 | tf_op jit(solution)/shard_map/ppermute | solution.py:344

commit v12 on v11

--- a/solution.py
+++ b/solution.py
@@ -308,11 +308,13 @@
     own, other, rest = refs[:count], refs[count : 2 * count], refs[2 * count :]
     _, _, bands, state_ref, grams, vectors, states_ref, innovations_ref = rest
     put_grams(number, turns, own, other, grams, vectors)
-    chain(grams, vectors, bands, state_ref[...], states_ref, innovations_ref)
-
-
-def chain_kernel(grams, vectors, bands, state_ref, states_ref, innovations_ref):
-    chain(grams, vectors, bands, state_ref[...], states_ref, innovations_ref)
+    chain_kernel(0, grams, vectors, bands, state_ref, states_ref, innovations_ref)
+
+
+def chain_kernel(group, grams, vectors, bands, state_ref, states_ref, innovations_ref):
+    @pl.when(lax.axis_index("grp") == group)
+    def _():
+        chain(grams, vectors, bands, state_ref[...], states_ref, innovations_ref)
 
 
 def shards(rows_h, rows_y, tile_block, tile_count, kappa, rate, smooth_gain, start_state):
@@ -425,7 +427,7 @@
             if group == 0:
                 return new_states, new_innovations
             return pl.pallas_call(
-                chain_kernel,
+                functools.partial(chain_kernel, group),
                 out_shape=(states_shape, states_shape),
                 in_specs=[VMEM] * 4,
                 out_specs=(VMEM, VMEM),

time: 45.3 us -> 44.1 us (0.974)
  waiting for transfers between devices: 16.6 us -> 17.8 us
  Pallas kernels: 6.24 us -> 5.06 us
  starting transfers between devices: 19.1 us -> 18 us
    pallas_call x1, Pallas kernels: 1.17 us -> 0.01 us  [run_group(): pl.pallas_call(functools.partial(chain_kernel, group), out_shape=(states_...]
    ppermute x2, waiting for transfers between devices: 3.53 us -> 4.7 us  [ring(): return lax.ppermute(array, ('grp', 'state'), pairs)]
    ppermute x2, starting transfers between devices: 2.61 us -> 1.45 us  [ring(): return lax.ppermute(array, ('grp', 'state'), pairs)]
where the time goes in v12:
time: 44.1 us; the launch traced here: 44 us
  starting transfers between devices  18 us (41%)
  waiting for transfers between devices  17.8 us (40%)
  Pallas kernels  5.06 us (11%)
  other arithmetic  2.37 us (5%)
  between operations  0.79 us (2%)
    ppermute x9, starting transfers between devices, flip_over(): return lax.ppermute(array, ('tm', 'state'), pairs)  15.5 us
    ppermute x9, waiting for transfers between devices, flip_over(): return lax.ppermute(array, ('tm', 'state'), pairs)  11.5 us
    ppermute x2, waiting for transfers between devices, ring(): return lax.ppermute(array, ('grp', 'state'), pairs)  4.7 us
    pallas_call x1, Pallas kernels, shards(): pl.pallas_call(half_kernel, out_shape=[jax.ShapeDtypeStruct((2 * LANES +...  1.8 us
    select_n x1, other arithmetic, shards(): jnp.where(row < tile_count[0][:, None, None], own, jnp.zeros((), own.dtype))  1.65 us
    ppermute x5, waiting for transfers between devices, across(): lax.ppermute(array, 'state', [(i, (i + 1) % state_size) for i in range(st...  1.59 us
    ppermute x2, starting transfers between devices, ring(): return lax.ppermute(array, ('grp', 'state'), pairs)  1.45 us
    pallas_call x1, Pallas kernels, shards(): pl.pallas_call(functools.partial(assemble_kernel, tm_size, late), out_sha...  1.36 us
  transfers between devices with their start and end apart: 17, of which 10 were waited for; matrix products, arithmetic and copies ran while one was open for 4% of the time, Pallas kernels for 8%

profile of v12, /device:TPU:0, one launch (start us, length us, event | category | flops | bytes accessed | tf_op | source)
XLA Modules:
  0.0 44.0 jit_solution(9441615643946992079)
XLA Ops:
  0.7 0.5 %collective-permute-start.3 = (bf16[16,128,256]{2,1,0:T(8,128)(2,1)}, bf16[16,128,256]{2,1,0:T(8,128)(2,1)S(1)}, u32[]{:S(2)}, u32[]{:S(2)}) collective-permute-start(bf16[16,128,256]{2,1,0:T(8,128)(2,1)} %bitcast.45), channel_id=1, source_target_pairs={{0,1},{1,0},{2,3},{3,2},{4,5},{5,4},{6,7},{7,6},{8,9},{9,8},{10,11... | collective-permute-start | bytes 3145736 | tf_op jit(solution)/shard_map/ppermute | solution.py:327
  1.2 1.7 %fusion.own_ref = bf16[16,128,256]{2,1,0:T(8,128)(2,1)S(1)} fusion(s32[16]{0:T(128)} %bitcast.46, bf16[1,16,128,256]{3,2,1,0:T(8,128)(2,1)} %param.8), kind=kLoop, calls=%fused_computation.1 | loop fusion | flops 1048576 | bytes 2097216 | tf_op jit(solution)/shard_map/jit(_where)/select_n | solution.py:353
  2.9 1.8 %shard_map.95 = (bf16[288,128]{1,0:T(8,128)(2,1)S(1)}, bf16[288,128]{1,0:T(8,128)(2,1)S(1)}, bf16[288,128]{1,0:T(8,128)(2,1)S(1)}, bf16[288,128]{1,0:T(8,128)(2,1)S(1)}, bf16[16,256,128]{2,1,0:T(8,128)(2,1)S(1)}) custom-call(s32[16]{0:T(128)S(1)} %bitcast.42, bf16[16,128]{1,0:T(8,128)(2,1)S(1)} %bitcast.38, bf16[16,128,256]{2,1,0:T(8,128)(2,1)S(1)} %fusion.own_ref, ...), custom_call_target="tpu_custom_call" | custom-call | tf_op jit(solution)/shard_map/pallas_call | solution.py:356
  4.7 3.7 %collective-permute-start = (bf16[288,128]{1,0:T(8,128)(2,1)S(1)}, bf16[288,128]{1,0:T(8,128)(2,1)S(1)}, u32[]{:S(2)}, u32[]{:S(2)}) collective-permute-start(bf16[288,128]{1,0:T(8,128)(2,1)S(1)} %get-tuple-element.23), channel_id=1, source_target_pairs={{0,8},{1,13},{4,12},{5,9},{8,0},{9,5},{12,4},{13,1},{2,10},{3,15},... | collective-permute-start | bytes 221192 | tf_op jit(solution)/shard_map/ppermute | solution.py:338
  8.4 1.6 %collective-permute-start.1 = (bf16[288,128]{1,0:T(8,128)(2,1)S(1)}, bf16[288,128]{1,0:T(8,128)(2,1)S(1)}, u32[]{:S(2)}, u32[]{:S(2)}) collective-permute-start(bf16[288,128]{1,0:T(8,128)(2,1)S(1)} %get-tuple-element.24), channel_id=1, source_target_pairs={{0,4},{1,5},{4,0},{5,1},{8,12},{9,13},{12,8},{13,9},{2,6},{3,7},{6... | collective-permute-start | bytes 221192 | tf_op jit(solution)/shard_map/ppermute | solution.py:338
  10.0 1.1 %shard_map.96 = (bf16[256,128]{1,0:T(8,128)(2,1)S(1)}, bf16[256,128]{1,0:T(8,128)(2,1)S(1)}, bf16[256,128]{1,0:T(8,128)(2,1)S(1)}, bf16[256,128]{1,0:T(8,128)(2,1)S(1)}) custom-call(s32[16]{0:T(128)S(1)} %bitcast.43, bf16[16,256,128]{2,1,0:T(8,128)(2,1)S(1)} %get-tuple-element.27.turned_ref, bf16[16,128,256]{2,1,0:T(8,128)(2,1)S(1)} %collective-permute-done.3.other_ref), custom_call_target="tpu_custom_call" | custom-call | tf_op jit(solution)/shard_map/pallas_call | solution.py:372
  11.0 2.0 %collective-permute-start.4 = (bf16[256,128]{1,0:T(8,128)(2,1)S(1)}, bf16[256,128]{1,0:T(8,128)(2,1)S(1)}, u32[]{:S(2)}, u32[]{:S(2)}) collective-permute-start(bf16[256,128]{1,0:T(8,128)(2,1)S(1)} %get-tuple-element.28), channel_id=1, source_target_pairs={{0,8},{1,13},{4,12},{5,9},{8,0},{9,5},{12,4},{13,1},{2,10},{3,15},... | collective-permute-start | bytes 196616 | tf_op jit(solution)/shard_map/ppermute | solution.py:338
  13.0 2.5 %collective-permute-start.5 = (bf16[256,128]{1,0:T(8,128)(2,1)S(1)}, bf16[256,128]{1,0:T(8,128)(2,1)S(1)}, u32[]{:S(2)}, u32[]{:S(2)}) collective-permute-start(bf16[256,128]{1,0:T(8,128)(2,1)S(1)} %get-tuple-element.29), channel_id=1, source_target_pairs={{0,4},{1,5},{4,0},{5,1},{8,12},{9,13},{12,8},{13,9},{2,6},{3,7},{6... | collective-permute-start | bytes 196616 | tf_op jit(solution)/shard_map/ppermute | solution.py:338
  15.5 1.4 %collective-permute-start.6 = (bf16[256,128]{1,0:T(8,128)(2,1)S(1)}, bf16[256,128]{1,0:T(8,128)(2,1)S(1)}, u32[]{:S(2)}, u32[]{:S(2)}) collective-permute-start(bf16[256,128]{1,0:T(8,128)(2,1)S(1)} %get-tuple-element.30), channel_id=1, source_target_pairs={{0,12},{1,9},{4,8},{5,13},{8,4},{9,1},{12,0},{13,5},{2,14},{3,11},... | collective-permute-start | bytes 196616 | tf_op jit(solution)/shard_map/ppermute | solution.py:338
  16.8 3.2 %collective-permute-done.4.refs_4_ = bf16[256,128]{1,0:T(8,128)(2,1)S(1)} collective-permute-done((bf16[256,128]{1,0:T(8,128)(2,1)S(1)}, bf16[256,128]{1,0:T(8,128)(2,1)S(1)}, u32[]{:S(2)}, u32[]{:S(2)}) %collective-permute-start.4) | collective-permute-done | bytes 65568 | tf_op jit(solution)/shard_map/ppermute | solution.py:338
  20.1 1.6 %collective-permute-done.6.refs_6_ = bf16[256,128]{1,0:T(8,128)(2,1)S(1)} collective-permute-done((bf16[256,128]{1,0:T(8,128)(2,1)S(1)}, bf16[256,128]{1,0:T(8,128)(2,1)S(1)}, u32[]{:S(2)}, u32[]{:S(2)}) %collective-permute-start.6) | collective-permute-done | bytes 65568 | tf_op jit(solution)/shard_map/ppermute | solution.py:338
  21.8 2.4 %collective-permute-start.10 = (bf16[528,128]{1,0:T(8,128)(2,1)S(1)}, bf16[528,128]{1,0:T(8,128)(2,1)S(1)}, u32[]{:S(2)}, u32[]{:S(2)}) collective-permute-start(bf16[528,128]{1,0:T(8,128)(2,1)S(1)} %get-tuple-element.32.refs_2_), channel_id=1, source_target_pairs={{0,8},{1,13},{4,12},{5,9},{8,0},{9,5},{12,4},{13,1},{2,10},{3,15},... | collective-permute-start | bytes 405512 | tf_op jit(solution)/shard_map/ppermute | solution.py:338
  24.2 0.8 %collective-permute-start.11 = (bf16[528,128]{1,0:T(8,128)(2,1)S(1)}, bf16[528,128]{1,0:T(8,128)(2,1)S(1)}, u32[]{:S(2)}, u32[]{:S(2)}) collective-permute-start(bf16[528,128]{1,0:T(8,128)(2,1)S(1)} %get-tuple-element.32.refs_2_), channel_id=1, source_target_pairs={{0,4},{1,5},{4,0},{5,1},{8,12},{9,13},{12,8},{13,9},{2,6},{3,7},{6... | collective-permute-start | bytes 405512 | tf_op jit(solution)/shard_map/ppermute | solution.py:338
  24.9 1.3 %collective-permute-start.7 = (bf16[528,128]{1,0:T(8,128)(2,1)S(1)}, bf16[528,128]{1,0:T(8,128)(2,1)S(1)}, u32[]{:S(2)}, u32[]{:S(2)}) collective-permute-start(bf16[528,128]{1,0:T(8,128)(2,1)S(1)} %get-tuple-element.32.refs_2_), channel_id=1, source_target_pairs={{0,12},{1,9},{4,8},{5,13},{8,4},{9,1},{12,0},{13,5},{2,14},{3,11},... | collective-permute-start | bytes 405512 | tf_op jit(solution)/shard_map/ppermute | solution.py:338
  26.7 0.7 %collective-permute-done.9.there_ref = f32[4,8,128]{2,1,0:T(8,128)S(1)} collective-permute-done((f32[4,8,128]{2,1,0:T(8,128)S(1)}, f32[4,8,128]{2,1,0:T(8,128)S(1)}, u32[]{:S(2)}, u32[]{:S(2)}) %collective-permute-start.9) | collective-permute-done | bytes 16416 | tf_op jit(solution)/shard_map/ppermute | solution.py:349
  27.7 4.4 %collective-permute-done.10.refs_0_ = bf16[528,128]{1,0:T(8,128)(2,1)S(1)} collective-permute-done((bf16[528,128]{1,0:T(8,128)(2,1)S(1)}, bf16[528,128]{1,0:T(8,128)(2,1)S(1)}, u32[]{:S(2)}, u32[]{:S(2)}) %collective-permute-start.10) | collective-permute-done | bytes 135200 | tf_op jit(solution)/shard_map/ppermute | solution.py:338
  32.1 1.4 %collective-permute-done.11.refs_1_ = bf16[528,128]{1,0:T(8,128)(2,1)S(1)} collective-permute-done((bf16[528,128]{1,0:T(8,128)(2,1)S(1)}, bf16[528,128]{1,0:T(8,128)(2,1)S(1)}, u32[]{:S(2)}, u32[]{:S(2)}) %collective-permute-start.11) | collective-permute-done | bytes 135200 | tf_op jit(solution)/shard_map/ppermute | solution.py:338
  33.5 0.8 %collective-permute-done.7.refs_0_ = bf16[528,128]{1,0:T(8,128)(2,1)S(1)} collective-permute-done((bf16[528,128]{1,0:T(8,128)(2,1)S(1)}, bf16[528,128]{1,0:T(8,128)(2,1)S(1)}, u32[]{:S(2)}, u32[]{:S(2)}) %collective-permute-start.7) | collective-permute-done | bytes 135200 | tf_op jit(solution)/shard_map/ppermute | solution.py:338
  34.4 0.5 %collective-permute-done.13.refs_4_ = bf16[528,128]{1,0:T(8,128)(2,1)S(1)} collective-permute-done((bf16[528,128]{1,0:T(8,128)(2,1)S(1)}, bf16[528,128]{1,0:T(8,128)(2,1)S(1)}, u32[]{:S(2)}, u32[]{:S(2)}) %collective-permute-start.13) | collective-permute-done | bytes 135200 | tf_op jit(solution)/shard_map/ppermute | solution.py:349
  35.7 1.4 %shard_map.100 = (bf16[4,512,512]{2,1,0:T(8,128)(2,1)S(1)}, f32[4,8,512]{2,1,0:T(8,128)S(1)}, f32[4,512]{1,0:T(4,128)S(1)}, f32[4,512]{1,0:T(4,128)S(1)}) custom-call(bf16[528,128]{1,0:T(8,128)(2,1)S(1)} %collective-permute-done.7.refs_0_, bf16[528,128]{1,0:T(8,128)(2,1)S(1)} %collective-permute-done.8.refs_1_, ...), custom_call_target="tpu_custom_call", output_to_operand_aliasing={{0}: (2, {}), {1}: (3, {})} | custom-call | tf_op jit(solution)/shard_map/pallas_call | solution.py:416
  37.2 2.9 %collective-permute-done.15.state_ref = f32[1,512]{1,0:T(1,128)S(1)} collective-permute-done((f32[1,512]{1,0:T(1,128)S(1)}, f32[1,512]{1,0:T(1,128)S(1)}, u32[]{:S(2)}, u32[]{:S(2)}) %collective-permute-start.15) | collective-permute-done | bytes 2080 | tf_op jit(solution)/shard_map/ppermute | solution.py:346
  40.2 1.3 %collective-permute-start.16 = (f32[1,512]{1,0:T(1,128)S(1)}, f32[1,512]{1,0:T(1,128)S(1)}, u32[]{:S(2)}, u32[]{:S(2)}) collective-permute-start(f32[1,512]{1,0:T(1,128)S(1)} %fusion.1), channel_id=1, source_target_pairs={{0,3},{1,2},{2,1},{3,0},{4,7},{5,6},{6,5},{7,4},{8,11},{9,10},{10,... | collective-permute-start | bytes 6152 | tf_op jit(solution)/shard_map/ppermute | solution.py:346
  41.5 1.7 %collective-permute-done.16 = f32[1,512]{1,0:T(1,128)S(1)} collective-permute-done((f32[1,512]{1,0:T(1,128)S(1)}, f32[1,512]{1,0:T(1,128)S(1)}, u32[]{:S(2)}, u32[]{:S(2)}) %collective-permute-start.16) | collective-permute-done | bytes 2080 | tf_op jit(solution)/shard_map/ppermute | solution.py:346
  43.3 0.7 %add_bitcast_fusion = (f32[1,1,256]{2,1,0:T(1,128)}, f32[1,1,256]{2,1,0:T(1,128)}) fusion(s32[]{:T(128)S(6)} %select_n.47, s32[]{:T(128)S(6)} %select_n.48, f32[1,512]{1,0:T(1,128)S(1)} %get-tuple-element.47, f32[1,512]{1,0:T(1,128)S(1)} %get-tuple-element.46, f32[1,512]{1,0:T(1,128)S(1)} %get-tuple-element.45, f32[1,512]{1,0:T(1,128)S(1)} %get-tuple-element.44, ...), kind=kLoop, calls=%fused_computation.22 | loop fusion | flops 1024 | bytes 11272 | tf_op jit(solution)/shard_map/reshape | solution.py:500
  (36 shorter events, 2.0 us)
Async XLA Ops:
  0.6 2.2 %copy-start.4 = (s32[1,16,1]{1,2,0:T(1,128)S(1)}, s32[1,16,1]{1,2,0:T(1,128)}, u32[]{:S(2)}) copy-start(s32[1,16,1]{1,2,0:T(1,128)} %param.10) | copy-start | bytes 196
  0.6 2.2 %copy-start = (bf16[1,16,128]{2,1,0:T(8,128)(2,1)S(1)}, bf16[1,16,128]{2,1,0:T(8,128)(2,1)}, u32[]{:S(2)}) copy-start(bf16[1,16,128]{2,1,0:T(8,128)(2,1)} %param.9) | copy-start | bytes 12292
  0.7 2.2 %copy-start.1 = (f32[1,1,512]{2,1,0:T(1,128)S(1)}, f32[1,1,512]{2,1,0:T(1,128)}, u32[]{:S(2)}) copy-start(f32[1,1,512]{2,1,0:T(1,128)} %param.12) | copy-start | bytes 6148
  0.7 2.2 %copy-start.2 = (f32[1,1,512]{2,1,0:T(1,128)S(1)}, f32[1,1,512]{2,1,0:T(1,128)}, u32[]{:S(2)}) copy-start(f32[1,1,512]{2,1,0:T(1,128)} %param.13) | copy-start | bytes 6148
  0.7 2.2 %copy-start.3 = (f32[1,1,512]{2,1,0:T(1,128)S(1)}, f32[1,1,512]{2,1,0:T(1,128)}, u32[]{:S(2)}) copy-start(f32[1,1,512]{2,1,0:T(1,128)} %param.14) | copy-start | bytes 6148
  0.7 9.3 %collective-permute-start.3 = (bf16[16,128,256]{2,1,0:T(8,128)(2,1)}, bf16[16,128,256]{2,1,0:T(8,128)(2,1)S(1)}, u32[]{:S(2)}, u32[]{:S(2)}) collective-permute-start(bf16[16,128,256]{2,1,0:T(8,128)(2,1)} %bitcast.45), channel_id=1, source_target_pairs={{0,1},{1,0},{2,3},{3,2},{4,5},{5,4},{6,7},{7,6},{8,9},{9,8},{10,11... | collective-permute-start | bytes 3145736 | tf_op jit(solution)/shard_map/ppermute | solution.py:327
  2.9 32.8 %copy-start.5 = (f32[512]{0:T(512)S(1)}, f32[512]{0:T(512)}, u32[]{:S(2)}) copy-start(f32[512]{0:T(512)} %param.15) | copy-start | bytes 6148
  4.7 10.8 %collective-permute-start = (bf16[288,128]{1,0:T(8,128)(2,1)S(1)}, bf16[288,128]{1,0:T(8,128)(2,1)S(1)}, u32[]{:S(2)}, u32[]{:S(2)}) collective-permute-start(bf16[288,128]{1,0:T(8,128)(2,1)S(1)} %get-tuple-element.23), channel_id=1, source_target_pairs={{0,8},{1,13},{4,12},{5,9},{8,0},{9,5},{12,4},{13,1},{2,10},{3,15},... | collective-permute-start | bytes 221192 | tf_op jit(solution)/shard_map/ppermute | solution.py:338
  8.4 8.5 %collective-permute-start.1 = (bf16[288,128]{1,0:T(8,128)(2,1)S(1)}, bf16[288,128]{1,0:T(8,128)(2,1)S(1)}, u32[]{:S(2)}, u32[]{:S(2)}) collective-permute-start(bf16[288,128]{1,0:T(8,128)(2,1)S(1)} %get-tuple-element.24), channel_id=1, source_target_pairs={{0,4},{1,5},{4,0},{5,1},{8,12},{9,13},{12,8},{13,9},{2,6},{3,7},{6... | collective-permute-start | bytes 221192 | tf_op jit(solution)/shard_map/ppermute | solution.py:338
  10.0 6.9 %collective-permute-start.2 = (bf16[288,128]{1,0:T(8,128)(2,1)S(1)}, bf16[288,128]{1,0:T(8,128)(2,1)S(1)}, u32[]{:S(2)}, u32[]{:S(2)}) collective-permute-start(bf16[288,128]{1,0:T(8,128)(2,1)S(1)} %get-tuple-element.25), channel_id=1, source_target_pairs={{0,12},{1,9},{4,8},{5,13},{8,4},{9,1},{12,0},{13,5},{2,14},{3,11},... | collective-permute-start | bytes 221192 | tf_op jit(solution)/shard_map/ppermute | solution.py:338
  11.0 9.0 %collective-permute-start.4 = (bf16[256,128]{1,0:T(8,128)(2,1)S(1)}, bf16[256,128]{1,0:T(8,128)(2,1)S(1)}, u32[]{:S(2)}, u32[]{:S(2)}) collective-permute-start(bf16[256,128]{1,0:T(8,128)(2,1)S(1)} %get-tuple-element.28), channel_id=1, source_target_pairs={{0,8},{1,13},{4,12},{5,9},{8,0},{9,5},{12,4},{13,1},{2,10},{3,15},... | collective-permute-start | bytes 196616 | tf_op jit(solution)/shard_map/ppermute | solution.py:338
  13.0 7.1 %collective-permute-start.5 = (bf16[256,128]{1,0:T(8,128)(2,1)S(1)}, bf16[256,128]{1,0:T(8,128)(2,1)S(1)}, u32[]{:S(2)}, u32[]{:S(2)}) collective-permute-start(bf16[256,128]{1,0:T(8,128)(2,1)S(1)} %get-tuple-element.29), channel_id=1, source_target_pairs={{0,4},{1,5},{4,0},{5,1},{8,12},{9,13},{12,8},{13,9},{2,6},{3,7},{6... | collective-permute-start | bytes 196616 | tf_op jit(solution)/shard_map/ppermute | solution.py:338
  15.5 6.2 %collective-permute-start.6 = (bf16[256,128]{1,0:T(8,128)(2,1)S(1)}, bf16[256,128]{1,0:T(8,128)(2,1)S(1)}, u32[]{:S(2)}, u32[]{:S(2)}) collective-permute-start(bf16[256,128]{1,0:T(8,128)(2,1)S(1)} %get-tuple-element.30), channel_id=1, source_target_pairs={{0,12},{1,9},{4,8},{5,13},{8,4},{9,1},{12,0},{13,5},{2,14},{3,11},... | collective-permute-start | bytes 196616 | tf_op jit(solution)/shard_map/ppermute | solution.py:338
  21.8 10.3 %collective-permute-start.10 = (bf16[528,128]{1,0:T(8,128)(2,1)S(1)}, bf16[528,128]{1,0:T(8,128)(2,1)S(1)}, u32[]{:S(2)}, u32[]{:S(2)}) collective-permute-start(bf16[528,128]{1,0:T(8,128)(2,1)S(1)} %get-tuple-element.32.refs_2_), channel_id=1, source_target_pairs={{0,8},{1,13},{4,12},{5,9},{8,0},{9,5},{12,4},{13,1},{2,10},{3,15},... | collective-permute-start | bytes 405512 | tf_op jit(solution)/shard_map/ppermute | solution.py:338
  24.2 9.4 %collective-permute-start.11 = (bf16[528,128]{1,0:T(8,128)(2,1)S(1)}, bf16[528,128]{1,0:T(8,128)(2,1)S(1)}, u32[]{:S(2)}, u32[]{:S(2)}) collective-permute-start(bf16[528,128]{1,0:T(8,128)(2,1)S(1)} %get-tuple-element.32.refs_2_), channel_id=1, source_target_pairs={{0,4},{1,5},{4,0},{5,1},{8,12},{9,13},{12,8},{13,9},{2,6},{3,7},{6... | collective-permute-start | bytes 405512 | tf_op jit(solution)/shard_map/ppermute | solution.py:338
  24.9 9.4 %collective-permute-start.7 = (bf16[528,128]{1,0:T(8,128)(2,1)S(1)}, bf16[528,128]{1,0:T(8,128)(2,1)S(1)}, u32[]{:S(2)}, u32[]{:S(2)}) collective-permute-start(bf16[528,128]{1,0:T(8,128)(2,1)S(1)} %get-tuple-element.32.refs_2_), channel_id=1, source_target_pairs={{0,12},{1,9},{4,8},{5,13},{8,4},{9,1},{12,0},{13,5},{2,14},{3,11},... | collective-permute-start | bytes 405512 | tf_op jit(solution)/shard_map/ppermute | solution.py:338
  26.2 1.2 %collective-permute-start.9 = (f32[4,8,128]{2,1,0:T(8,128)S(1)}, f32[4,8,128]{2,1,0:T(8,128)S(1)}, u32[]{:S(2)}, u32[]{:S(2)}) collective-permute-start(f32[4,8,128]{2,1,0:T(8,128)S(1)} %get-tuple-element.33.here_ref), channel_id=1, source_target_pairs={{0,1},{1,0},{2,3},{3,2},{4,5},{5,4},{6,7},{7,6},{8,9},{9,8},{10,11... | collective-permute-start | bytes 49160 | tf_op jit(solution)/shard_map/ppermute | solution.py:349
  26.2 8.2 %collective-permute-start.14 = (bf16[528,128]{1,0:T(8,128)(2,1)S(1)}, bf16[528,128]{1,0:T(8,128)(2,1)S(1)}, u32[]{:S(2)}, u32[]{:S(2)}) collective-permute-start(bf16[528,128]{1,0:T(8,128)(2,1)S(1)} %get-tuple-element.32.refs_2_), channel_id=1, source_target_pairs={{0,1},{1,0},{2,3},{3,2},{4,5},{5,4},{6,7},{7,6},{8,9},{9,8},{10,11... | collective-permute-start | bytes 405512 | tf_op jit(solution)/shard_map/ppermute | solution.py:349
  32.1 2.3 %collective-permute-start.12 = (bf16[528,128]{1,0:T(8,128)(2,1)S(1)}, bf16[528,128]{1,0:T(8,128)(2,1)S(1)}, u32[]{:S(2)}, u32[]{:S(2)}) collective-permute-start(bf16[528,128]{1,0:T(8,128)(2,1)S(1)} %collective-permute-done.10.refs_0_), channel_id=1, source_target_pairs={{0,1},{1,0},{2,3},{3,2},{4,5},{5,4},{6,7},{7,6},{8,9},{9,8},{10,11... | collective-permute-start | bytes 405512 | tf_op jit(solution)/shard_map/ppermute | solution.py:349
  33.5 1.4 %collective-permute-start.13 = (bf16[528,128]{1,0:T(8,128)(2,1)S(1)}, bf16[528,128]{1,0:T(8,128)(2,1)S(1)}, u32[]{:S(2)}, u32[]{:S(2)}) collective-permute-start(bf16[528,128]{1,0:T(8,128)(2,1)S(1)} %collective-permute-done.11.refs_1_), channel_id=1, source_target_pairs={{0,1},{1,0},{2,3},{3,2},{4,5},{5,4},{6,7},{7,6},{8,9},{9,8},{10,11... | collective-permute-start | bytes 405512 | tf_op jit(solution)/shard_map/ppermute | solution.py:349
  34.4 1.4 %collective-permute-start.8 = (bf16[528,128]{1,0:T(8,128)(2,1)S(1)}, bf16[528,128]{1,0:T(8,128)(2,1)S(1)}, u32[]{:S(2)}, u32[]{:S(2)}) collective-permute-start(bf16[528,128]{1,0:T(8,128)(2,1)S(1)} %collective-permute-done.7.refs_0_), channel_id=1, source_target_pairs={{0,1},{1,0},{2,3},{3,2},{4,5},{5,4},{6,7},{7,6},{8,9},{9,8},{10,11... | collective-permute-start | bytes 405512 | tf_op jit(solution)/shard_map/ppermute | solution.py:349
  37.1 3.1 %collective-permute-start.15 = (f32[1,512]{1,0:T(1,128)S(1)}, f32[1,512]{1,0:T(1,128)S(1)}, u32[]{:S(2)}, u32[]{:S(2)}) collective-permute-start(f32[1,512]{1,0:T(1,128)S(1)} %slice.50), channel_id=1, source_target_pairs={{0,3},{1,2},{2,1},{3,0},{4,7},{5,6},{6,5},{7,4},{8,11},{9,10},{10,... | collective-permute-start | bytes 6152 | tf_op jit(solution)/shard_map/ppermute | solution.py:346
  40.2 3.1 %collective-permute-start.16 = (f32[1,512]{1,0:T(1,128)S(1)}, f32[1,512]{1,0:T(1,128)S(1)}, u32[]{:S(2)}, u32[]{:S(2)}) collective-permute-start(f32[1,512]{1,0:T(1,128)S(1)} %fusion.1), channel_id=1, source_target_pairs={{0,3},{1,2},{2,1},{3,0},{4,7},{5,6},{6,5},{7,4},{8,11},{9,10},{10,... | collective-permute-start | bytes 6152 | tf_op jit(solution)/shard_map/ppermute | solution.py:346

commit v13 on v12

--- a/solution.py
+++ b/solution.py
@@ -146,7 +146,7 @@
 
 
 def half_kernel(blocks, y_ref, own_ref, kappa_ref, rate_ref, gain_ref, *refs):
-    outs, (turned_ref, acc, vec, side, readings) = refs[:-5], refs[-5:]
+    outs, (turned_ref, acc, vec, side, readings, values) = refs[:-6], refs[-6:]
     tile_num, row_num, _ = own_ref.shape
     number = len(outs)
     core, position = lax.axis_index("state"), lax.axis_index("tm")
@@ -154,19 +154,22 @@
     vec[...] = jnp.zeros_like(vec)
     side[...] = jnp.zeros_like(side)
     readings[...] = y_ref[...].astype(jnp.float32)
+    for at, coefficient in enumerate((kappa_ref, rate_ref, gain_ref)):
+        for piece in range(2):
+            lanes = pl.ds(pl.multiple_of((2 * core + piece) * LANES, LANES), LANES)
+            values[4 + 2 * at + piece : 5 + 2 * at + piece, :] = coefficient[:, lanes]
     for index in range(tile_num):
         block = blocks[index]
         rows = own_ref[index]
         turned = rows.T
         turned_ref[index] = turned
-        square = jnp.dot(turned, rows, preferred_element_type=jnp.float32)
+        observed = jnp.broadcast_to(readings[index : index + 1, :], (16, row_num))
+        both = jnp.concatenate([turned, observed.astype(jnp.bfloat16)], axis=0)
+        square = jnp.dot(both, rows, preferred_element_type=jnp.float32)
         acc[block, 0:LANES] += square[:LANES, :LANES]
         acc[block, LANES : 2 * LANES] += square[:LANES, LANES:]
-        acc[block, 2 * LANES : 3 * LANES] += square[LANES:, LANES:]
-        values = jnp.broadcast_to(readings[index : index + 1, :], (8, row_num))
-        vec[block] += jnp.dot(
-            values.astype(jnp.bfloat16), rows, preferred_element_type=jnp.float32
-        )
+        acc[block, 2 * LANES : 3 * LANES] += square[LANES : 2 * LANES, LANES:]
+        vec[block] += square[2 * LANES : 2 * LANES + 8, :]
     line = lax.broadcasted_iota(jnp.int32, (LANES, LANES), 0)
     column = lax.broadcasted_iota(jnp.int32, (LANES, LANES), 1)
     for turn, out_ref in enumerate(outs):
@@ -175,16 +178,14 @@
         packed = jnp.where(line < column, first, jnp.where(line > column, second, 0.0))
         out_ref[0:LANES] = packed.astype(jnp.bfloat16)
         out_ref[LANES : 2 * LANES] = between.astype(jnp.bfloat16)
-        values = [vec[block, 0:1, :LANES], vec[block, 0:1, LANES:]]
-        for square in (first, second):
-            values.append(jnp.sum(jnp.where(line == column, square, 0.0), axis=0, keepdims=True))
-        for coefficient in (kappa_ref, rate_ref, gain_ref):
-            for piece in range(2):
-                at = pl.multiple_of((2 * core + piece) * LANES, LANES)
-                values.append(coefficient[:, pl.ds(at, LANES)])
-        for at, value in enumerate(values):
-            for which, part in enumerate(pieces_of(value)):
-                side[which * VECTORS + at : which * VECTORS + at + 1, :] = part
+        values[0:1, :] = vec[block, 0:1, :LANES]
+        values[1:2, :] = vec[block, 0:1, LANES:]
+        for at, square in ((2, first), (3, second)):
+            values[at : at + 1, :] = jnp.sum(
+                jnp.where(line == column, square, 0.0), axis=0, keepdims=True
+            )
+        for which, part in enumerate(pieces_of(values[...])):
+            side[which * VECTORS : (which + 1) * VECTORS, :] = part
         out_ref[2 * LANES :] = side[...].astype(jnp.bfloat16)
 
 
@@ -364,6 +365,7 @@
                 pltpu.VMEM((tm_size, 8, half), jnp.float32),
                 pltpu.VMEM((32, LANES), jnp.float32),
                 pltpu.VMEM((tile_num, row_num), jnp.float32),
+                pltpu.VMEM((VECTORS, LANES), jnp.float32),
             ],
             compiler_params=KERNEL,
         )(blocks, rows_y[0], valid, kappa[0], rate[0], smooth_gain[0])

time: 44.1 us -> 43.9 us (level)
  no operation moved by 1% of the time
where the time goes in v13:
time: 43.9 us; the launch traced here: 43.7 us
  starting transfers between devices  18 us (41%)
  waiting for transfers between devices  17.7 us (40%)
  Pallas kernels  4.83 us (11%)
  other arithmetic  2.37 us (5%)
  between operations  0.79 us (2%)
    ppermute x9, starting transfers between devices, flip_over(): return lax.ppermute(array, ('tm', 'state'), pairs)  15.5 us
    ppermute x9, waiting for transfers between devices, flip_over(): return lax.ppermute(array, ('tm', 'state'), pairs)  11.5 us
    ppermute x2, waiting for transfers between devices, ring(): return lax.ppermute(array, ('grp', 'state'), pairs)  4.69 us
    select_n x1, other arithmetic, shards(): jnp.where(row < tile_count[0][:, None, None], own, jnp.zeros((), own.dtype))  1.65 us
    ppermute x5, waiting for transfers between devices, across(): lax.ppermute(array, 'state', [(i, (i + 1) % state_size) for i in range(st...  1.59 us
    pallas_call x1, Pallas kernels, shards(): pl.pallas_call(half_kernel, out_shape=[jax.ShapeDtypeStruct((2 * LANES +...  1.57 us
    ppermute x2, starting transfers between devices, ring(): return lax.ppermute(array, ('grp', 'state'), pairs)  1.45 us
    pallas_call x1, Pallas kernels, shards(): pl.pallas_call(functools.partial(assemble_kernel, tm_size, late), out_sha...  1.36 us
  transfers between devices with their start and end apart: 17, of which 10 were waited for; matrix products, arithmetic and copies ran while one was open for 4% of the time, Pallas kernels for 8%

profile of v13, /device:TPU:0, one launch (start us, length us, event | category | flops | bytes accessed | tf_op | source)
XLA Modules:
  0.0 43.7 jit_solution(2373464459928456215)
XLA Ops:
  0.7 0.5 %collective-permute-start.3 = (bf16[16,128,256]{2,1,0:T(8,128)(2,1)}, bf16[16,128,256]{2,1,0:T(8,128)(2,1)S(1)}, u32[]{:S(2)}, u32[]{:S(2)}) collective-permute-start(bf16[16,128,256]{2,1,0:T(8,128)(2,1)} %bitcast.45), channel_id=1, source_target_pairs={{0,1},{1,0},{2,3},{3,2},{4,5},{5,4},{6,7},{7,6},{8,9},{9,8},{10,11... | collective-permute-start | bytes 3145736 | tf_op jit(solution)/shard_map/ppermute | solution.py:328
  1.2 1.7 %fusion.own_ref = bf16[16,128,256]{2,1,0:T(8,128)(2,1)S(1)} fusion(s32[16]{0:T(128)} %bitcast.46, bf16[1,16,128,256]{3,2,1,0:T(8,128)(2,1)} %param.8), kind=kLoop, calls=%fused_computation.1 | loop fusion | flops 1048576 | bytes 2097216 | tf_op jit(solution)/shard_map/jit(_where)/select_n | solution.py:354
  2.9 1.6 %shard_map.95 = (bf16[288,128]{1,0:T(8,128)(2,1)S(1)}, bf16[288,128]{1,0:T(8,128)(2,1)S(1)}, bf16[288,128]{1,0:T(8,128)(2,1)S(1)}, bf16[288,128]{1,0:T(8,128)(2,1)S(1)}, bf16[16,256,128]{2,1,0:T(8,128)(2,1)S(1)}) custom-call(s32[16]{0:T(128)S(1)} %bitcast.42, bf16[16,128]{1,0:T(8,128)(2,1)S(1)} %bitcast.38, bf16[16,128,256]{2,1,0:T(8,128)(2,1)S(1)} %fusion.own_ref, ...), custom_call_target="tpu_custom_call" | custom-call | tf_op jit(solution)/shard_map/pallas_call | solution.py:357
  4.5 3.7 %collective-permute-start = (bf16[288,128]{1,0:T(8,128)(2,1)S(1)}, bf16[288,128]{1,0:T(8,128)(2,1)S(1)}, u32[]{:S(2)}, u32[]{:S(2)}) collective-permute-start(bf16[288,128]{1,0:T(8,128)(2,1)S(1)} %get-tuple-element.23), channel_id=1, source_target_pairs={{0,8},{1,13},{4,12},{5,9},{8,0},{9,5},{12,4},{13,1},{2,10},{3,15},... | collective-permute-start | bytes 221192 | tf_op jit(solution)/shard_map/ppermute | solution.py:339
  8.2 1.6 %collective-permute-start.1 = (bf16[288,128]{1,0:T(8,128)(2,1)S(1)}, bf16[288,128]{1,0:T(8,128)(2,1)S(1)}, u32[]{:S(2)}, u32[]{:S(2)}) collective-permute-start(bf16[288,128]{1,0:T(8,128)(2,1)S(1)} %get-tuple-element.24), channel_id=1, source_target_pairs={{0,4},{1,5},{4,0},{5,1},{8,12},{9,13},{12,8},{13,9},{2,6},{3,7},{6... | collective-permute-start | bytes 221192 | tf_op jit(solution)/shard_map/ppermute | solution.py:339
  9.7 1.1 %shard_map.96 = (bf16[256,128]{1,0:T(8,128)(2,1)S(1)}, bf16[256,128]{1,0:T(8,128)(2,1)S(1)}, bf16[256,128]{1,0:T(8,128)(2,1)S(1)}, bf16[256,128]{1,0:T(8,128)(2,1)S(1)}) custom-call(s32[16]{0:T(128)S(1)} %bitcast.43, bf16[16,256,128]{2,1,0:T(8,128)(2,1)S(1)} %get-tuple-element.27.turned_ref, bf16[16,128,256]{2,1,0:T(8,128)(2,1)S(1)} %collective-permute-done.3.other_ref), custom_call_target="tpu_custom_call" | custom-call | tf_op jit(solution)/shard_map/pallas_call | solution.py:374
  10.8 2.0 %collective-permute-start.4 = (bf16[256,128]{1,0:T(8,128)(2,1)S(1)}, bf16[256,128]{1,0:T(8,128)(2,1)S(1)}, u32[]{:S(2)}, u32[]{:S(2)}) collective-permute-start(bf16[256,128]{1,0:T(8,128)(2,1)S(1)} %get-tuple-element.28), channel_id=1, source_target_pairs={{0,8},{1,13},{4,12},{5,9},{8,0},{9,5},{12,4},{13,1},{2,10},{3,15},... | collective-permute-start | bytes 196616 | tf_op jit(solution)/shard_map/ppermute | solution.py:339
  12.8 2.5 %collective-permute-start.5 = (bf16[256,128]{1,0:T(8,128)(2,1)S(1)}, bf16[256,128]{1,0:T(8,128)(2,1)S(1)}, u32[]{:S(2)}, u32[]{:S(2)}) collective-permute-start(bf16[256,128]{1,0:T(8,128)(2,1)S(1)} %get-tuple-element.29), channel_id=1, source_target_pairs={{0,4},{1,5},{4,0},{5,1},{8,12},{9,13},{12,8},{13,9},{2,6},{3,7},{6... | collective-permute-start | bytes 196616 | tf_op jit(solution)/shard_map/ppermute | solution.py:339
  15.3 1.4 %collective-permute-start.6 = (bf16[256,128]{1,0:T(8,128)(2,1)S(1)}, bf16[256,128]{1,0:T(8,128)(2,1)S(1)}, u32[]{:S(2)}, u32[]{:S(2)}) collective-permute-start(bf16[256,128]{1,0:T(8,128)(2,1)S(1)} %get-tuple-element.30), channel_id=1, source_target_pairs={{0,12},{1,9},{4,8},{5,13},{8,4},{9,1},{12,0},{13,5},{2,14},{3,11},... | collective-permute-start | bytes 196616 | tf_op jit(solution)/shard_map/ppermute | solution.py:339
  16.6 3.2 %collective-permute-done.4.refs_4_ = bf16[256,128]{1,0:T(8,128)(2,1)S(1)} collective-permute-done((bf16[256,128]{1,0:T(8,128)(2,1)S(1)}, bf16[256,128]{1,0:T(8,128)(2,1)S(1)}, u32[]{:S(2)}, u32[]{:S(2)}) %collective-permute-start.4) | collective-permute-done | bytes 65568 | tf_op jit(solution)/shard_map/ppermute | solution.py:339
  19.8 1.6 %collective-permute-done.6.refs_6_ = bf16[256,128]{1,0:T(8,128)(2,1)S(1)} collective-permute-done((bf16[256,128]{1,0:T(8,128)(2,1)S(1)}, bf16[256,128]{1,0:T(8,128)(2,1)S(1)}, u32[]{:S(2)}, u32[]{:S(2)}) %collective-permute-start.6) | collective-permute-done | bytes 65568 | tf_op jit(solution)/shard_map/ppermute | solution.py:339
  21.5 2.4 %collective-permute-start.10 = (bf16[528,128]{1,0:T(8,128)(2,1)S(1)}, bf16[528,128]{1,0:T(8,128)(2,1)S(1)}, u32[]{:S(2)}, u32[]{:S(2)}) collective-permute-start(bf16[528,128]{1,0:T(8,128)(2,1)S(1)} %get-tuple-element.32.refs_2_), channel_id=1, source_target_pairs={{0,8},{1,13},{4,12},{5,9},{8,0},{9,5},{12,4},{13,1},{2,10},{3,15},... | collective-permute-start | bytes 405512 | tf_op jit(solution)/shard_map/ppermute | solution.py:339
  23.9 0.8 %collective-permute-start.11 = (bf16[528,128]{1,0:T(8,128)(2,1)S(1)}, bf16[528,128]{1,0:T(8,128)(2,1)S(1)}, u32[]{:S(2)}, u32[]{:S(2)}) collective-permute-start(bf16[528,128]{1,0:T(8,128)(2,1)S(1)} %get-tuple-element.32.refs_2_), channel_id=1, source_target_pairs={{0,4},{1,5},{4,0},{5,1},{8,12},{9,13},{12,8},{13,9},{2,6},{3,7},{6... | collective-permute-start | bytes 405512 | tf_op jit(solution)/shard_map/ppermute | solution.py:339
  24.7 1.3 %collective-permute-start.7 = (bf16[528,128]{1,0:T(8,128)(2,1)S(1)}, bf16[528,128]{1,0:T(8,128)(2,1)S(1)}, u32[]{:S(2)}, u32[]{:S(2)}) collective-permute-start(bf16[528,128]{1,0:T(8,128)(2,1)S(1)} %get-tuple-element.32.refs_2_), channel_id=1, source_target_pairs={{0,12},{1,9},{4,8},{5,13},{8,4},{9,1},{12,0},{13,5},{2,14},{3,11},... | collective-permute-start | bytes 405512 | tf_op jit(solution)/shard_map/ppermute | solution.py:339
  26.0 0.5 %collective-permute-start.14 = (bf16[528,128]{1,0:T(8,128)(2,1)S(1)}, bf16[528,128]{1,0:T(8,128)(2,1)S(1)}, u32[]{:S(2)}, u32[]{:S(2)}) collective-permute-start(bf16[528,128]{1,0:T(8,128)(2,1)S(1)} %get-tuple-element.32.refs_2_), channel_id=1, source_target_pairs={{0,1},{1,0},{2,3},{3,2},{4,5},{5,4},{6,7},{7,6},{8,9},{9,8},{10,11... | collective-permute-start | bytes 405512 | tf_op jit(solution)/shard_map/ppermute | solution.py:350
  26.5 0.7 %collective-permute-done.9.there_ref = f32[4,8,128]{2,1,0:T(8,128)S(1)} collective-permute-done((f32[4,8,128]{2,1,0:T(8,128)S(1)}, f32[4,8,128]{2,1,0:T(8,128)S(1)}, u32[]{:S(2)}, u32[]{:S(2)}) %collective-permute-start.9) | collective-permute-done | bytes 16416 | tf_op jit(solution)/shard_map/ppermute | solution.py:350
  27.5 4.4 %collective-permute-done.10.refs_0_ = bf16[528,128]{1,0:T(8,128)(2,1)S(1)} collective-permute-done((bf16[528,128]{1,0:T(8,128)(2,1)S(1)}, bf16[528,128]{1,0:T(8,128)(2,1)S(1)}, u32[]{:S(2)}, u32[]{:S(2)}) %collective-permute-start.10) | collective-permute-done | bytes 135200 | tf_op jit(solution)/shard_map/ppermute | solution.py:339
  31.9 1.4 %collective-permute-done.11.refs_1_ = bf16[528,128]{1,0:T(8,128)(2,1)S(1)} collective-permute-done((bf16[528,128]{1,0:T(8,128)(2,1)S(1)}, bf16[528,128]{1,0:T(8,128)(2,1)S(1)}, u32[]{:S(2)}, u32[]{:S(2)}) %collective-permute-start.11) | collective-permute-done | bytes 135200 | tf_op jit(solution)/shard_map/ppermute | solution.py:339
  33.3 0.9 %collective-permute-done.7.refs_0_ = bf16[528,128]{1,0:T(8,128)(2,1)S(1)} collective-permute-done((bf16[528,128]{1,0:T(8,128)(2,1)S(1)}, bf16[528,128]{1,0:T(8,128)(2,1)S(1)}, u32[]{:S(2)}, u32[]{:S(2)}) %collective-permute-start.7) | collective-permute-done | bytes 135200 | tf_op jit(solution)/shard_map/ppermute | solution.py:339
  35.5 1.4 %shard_map.100 = (bf16[4,512,512]{2,1,0:T(8,128)(2,1)S(1)}, f32[4,8,512]{2,1,0:T(8,128)S(1)}, f32[4,512]{1,0:T(4,128)S(1)}, f32[4,512]{1,0:T(4,128)S(1)}) custom-call(bf16[528,128]{1,0:T(8,128)(2,1)S(1)} %collective-permute-done.7.refs_0_, bf16[528,128]{1,0:T(8,128)(2,1)S(1)} %collective-permute-done.8.refs_1_, ...), custom_call_target="tpu_custom_call", output_to_operand_aliasing={{0}: (2, {}), {1}: (3, {})} | custom-call | tf_op jit(solution)/shard_map/pallas_call | solution.py:418
  37.0 2.9 %collective-permute-done.15.state_ref = f32[1,512]{1,0:T(1,128)S(1)} collective-permute-done((f32[1,512]{1,0:T(1,128)S(1)}, f32[1,512]{1,0:T(1,128)S(1)}, u32[]{:S(2)}, u32[]{:S(2)}) %collective-permute-start.15) | collective-permute-done | bytes 2080 | tf_op jit(solution)/shard_map/ppermute | solution.py:347
  40.0 1.3 %collective-permute-start.16 = (f32[1,512]{1,0:T(1,128)S(1)}, f32[1,512]{1,0:T(1,128)S(1)}, u32[]{:S(2)}, u32[]{:S(2)}) collective-permute-start(f32[1,512]{1,0:T(1,128)S(1)} %fusion.1), channel_id=1, source_target_pairs={{0,3},{1,2},{2,1},{3,0},{4,7},{5,6},{6,5},{7,4},{8,11},{9,10},{10,... | collective-permute-start | bytes 6152 | tf_op jit(solution)/shard_map/ppermute | solution.py:347
  41.3 1.7 %collective-permute-done.16 = f32[1,512]{1,0:T(1,128)S(1)} collective-permute-done((f32[1,512]{1,0:T(1,128)S(1)}, f32[1,512]{1,0:T(1,128)S(1)}, u32[]{:S(2)}, u32[]{:S(2)}) %collective-permute-start.16) | collective-permute-done | bytes 2080 | tf_op jit(solution)/shard_map/ppermute | solution.py:347
  43.1 0.7 %add_bitcast_fusion = (f32[1,1,256]{2,1,0:T(1,128)}, f32[1,1,256]{2,1,0:T(1,128)}) fusion(s32[]{:T(128)S(6)} %select_n.47, s32[]{:T(128)S(6)} %select_n.48, f32[1,512]{1,0:T(1,128)S(1)} %get-tuple-element.47, f32[1,512]{1,0:T(1,128)S(1)} %get-tuple-element.46, f32[1,512]{1,0:T(1,128)S(1)} %get-tuple-element.45, f32[1,512]{1,0:T(1,128)S(1)} %get-tuple-element.44, ...), kind=kLoop, calls=%fused_computation.22 | loop fusion | flops 1024 | bytes 11272 | tf_op jit(solution)/shard_map/reshape | solution.py:502
  (36 shorter events, 2.0 us)
Async XLA Ops:
  0.6 2.2 %copy-start.4 = (s32[1,16,1]{1,2,0:T(1,128)S(1)}, s32[1,16,1]{1,2,0:T(1,128)}, u32[]{:S(2)}) copy-start(s32[1,16,1]{1,2,0:T(1,128)} %param.10) | copy-start | bytes 196
  0.6 2.2 %copy-start = (bf16[1,16,128]{2,1,0:T(8,128)(2,1)S(1)}, bf16[1,16,128]{2,1,0:T(8,128)(2,1)}, u32[]{:S(2)}) copy-start(bf16[1,16,128]{2,1,0:T(8,128)(2,1)} %param.9) | copy-start | bytes 12292
  0.7 2.2 %copy-start.1 = (f32[1,1,512]{2,1,0:T(1,128)S(1)}, f32[1,1,512]{2,1,0:T(1,128)}, u32[]{:S(2)}) copy-start(f32[1,1,512]{2,1,0:T(1,128)} %param.12) | copy-start | bytes 6148
  0.7 2.2 %copy-start.2 = (f32[1,1,512]{2,1,0:T(1,128)S(1)}, f32[1,1,512]{2,1,0:T(1,128)}, u32[]{:S(2)}) copy-start(f32[1,1,512]{2,1,0:T(1,128)} %param.13) | copy-start | bytes 6148
  0.7 2.2 %copy-start.3 = (f32[1,1,512]{2,1,0:T(1,128)S(1)}, f32[1,1,512]{2,1,0:T(1,128)}, u32[]{:S(2)}) copy-start(f32[1,1,512]{2,1,0:T(1,128)} %param.14) | copy-start | bytes 6148
  0.7 9.1 %collective-permute-start.3 = (bf16[16,128,256]{2,1,0:T(8,128)(2,1)}, bf16[16,128,256]{2,1,0:T(8,128)(2,1)S(1)}, u32[]{:S(2)}, u32[]{:S(2)}) collective-permute-start(bf16[16,128,256]{2,1,0:T(8,128)(2,1)} %bitcast.45), channel_id=1, source_target_pairs={{0,1},{1,0},{2,3},{3,2},{4,5},{5,4},{6,7},{7,6},{8,9},{9,8},{10,11... | collective-permute-start | bytes 3145736 | tf_op jit(solution)/shard_map/ppermute | solution.py:328
  2.9 32.6 %copy-start.5 = (f32[512]{0:T(512)S(1)}, f32[512]{0:T(512)}, u32[]{:S(2)}) copy-start(f32[512]{0:T(512)} %param.15) | copy-start | bytes 6148
  4.5 10.8 %collective-permute-start = (bf16[288,128]{1,0:T(8,128)(2,1)S(1)}, bf16[288,128]{1,0:T(8,128)(2,1)S(1)}, u32[]{:S(2)}, u32[]{:S(2)}) collective-permute-start(bf16[288,128]{1,0:T(8,128)(2,1)S(1)} %get-tuple-element.23), channel_id=1, source_target_pairs={{0,8},{1,13},{4,12},{5,9},{8,0},{9,5},{12,4},{13,1},{2,10},{3,15},... | collective-permute-start | bytes 221192 | tf_op jit(solution)/shard_map/ppermute | solution.py:339
  8.2 8.5 %collective-permute-start.1 = (bf16[288,128]{1,0:T(8,128)(2,1)S(1)}, bf16[288,128]{1,0:T(8,128)(2,1)S(1)}, u32[]{:S(2)}, u32[]{:S(2)}) collective-permute-start(bf16[288,128]{1,0:T(8,128)(2,1)S(1)} %get-tuple-element.24), channel_id=1, source_target_pairs={{0,4},{1,5},{4,0},{5,1},{8,12},{9,13},{12,8},{13,9},{2,6},{3,7},{6... | collective-permute-start | bytes 221192 | tf_op jit(solution)/shard_map/ppermute | solution.py:339
  9.7 6.9 %collective-permute-start.2 = (bf16[288,128]{1,0:T(8,128)(2,1)S(1)}, bf16[288,128]{1,0:T(8,128)(2,1)S(1)}, u32[]{:S(2)}, u32[]{:S(2)}) collective-permute-start(bf16[288,128]{1,0:T(8,128)(2,1)S(1)} %get-tuple-element.25), channel_id=1, source_target_pairs={{0,12},{1,9},{4,8},{5,13},{8,4},{9,1},{12,0},{13,5},{2,14},{3,11},... | collective-permute-start | bytes 221192 | tf_op jit(solution)/shard_map/ppermute | solution.py:339
  10.8 9.0 %collective-permute-start.4 = (bf16[256,128]{1,0:T(8,128)(2,1)S(1)}, bf16[256,128]{1,0:T(8,128)(2,1)S(1)}, u32[]{:S(2)}, u32[]{:S(2)}) collective-permute-start(bf16[256,128]{1,0:T(8,128)(2,1)S(1)} %get-tuple-element.28), channel_id=1, source_target_pairs={{0,8},{1,13},{4,12},{5,9},{8,0},{9,5},{12,4},{13,1},{2,10},{3,15},... | collective-permute-start | bytes 196616 | tf_op jit(solution)/shard_map/ppermute | solution.py:339
  12.8 7.1 %collective-permute-start.5 = (bf16[256,128]{1,0:T(8,128)(2,1)S(1)}, bf16[256,128]{1,0:T(8,128)(2,1)S(1)}, u32[]{:S(2)}, u32[]{:S(2)}) collective-permute-start(bf16[256,128]{1,0:T(8,128)(2,1)S(1)} %get-tuple-element.29), channel_id=1, source_target_pairs={{0,4},{1,5},{4,0},{5,1},{8,12},{9,13},{12,8},{13,9},{2,6},{3,7},{6... | collective-permute-start | bytes 196616 | tf_op jit(solution)/shard_map/ppermute | solution.py:339
  15.3 6.2 %collective-permute-start.6 = (bf16[256,128]{1,0:T(8,128)(2,1)S(1)}, bf16[256,128]{1,0:T(8,128)(2,1)S(1)}, u32[]{:S(2)}, u32[]{:S(2)}) collective-permute-start(bf16[256,128]{1,0:T(8,128)(2,1)S(1)} %get-tuple-element.30), channel_id=1, source_target_pairs={{0,12},{1,9},{4,8},{5,13},{8,4},{9,1},{12,0},{13,5},{2,14},{3,11},... | collective-permute-start | bytes 196616 | tf_op jit(solution)/shard_map/ppermute | solution.py:339
  21.5 10.3 %collective-permute-start.10 = (bf16[528,128]{1,0:T(8,128)(2,1)S(1)}, bf16[528,128]{1,0:T(8,128)(2,1)S(1)}, u32[]{:S(2)}, u32[]{:S(2)}) collective-permute-start(bf16[528,128]{1,0:T(8,128)(2,1)S(1)} %get-tuple-element.32.refs_2_), channel_id=1, source_target_pairs={{0,8},{1,13},{4,12},{5,9},{8,0},{9,5},{12,4},{13,1},{2,10},{3,15},... | collective-permute-start | bytes 405512 | tf_op jit(solution)/shard_map/ppermute | solution.py:339
  23.9 9.3 %collective-permute-start.11 = (bf16[528,128]{1,0:T(8,128)(2,1)S(1)}, bf16[528,128]{1,0:T(8,128)(2,1)S(1)}, u32[]{:S(2)}, u32[]{:S(2)}) collective-permute-start(bf16[528,128]{1,0:T(8,128)(2,1)S(1)} %get-tuple-element.32.refs_2_), channel_id=1, source_target_pairs={{0,4},{1,5},{4,0},{5,1},{8,12},{9,13},{12,8},{13,9},{2,6},{3,7},{6... | collective-permute-start | bytes 405512 | tf_op jit(solution)/shard_map/ppermute | solution.py:339
  24.7 9.4 %collective-permute-start.7 = (bf16[528,128]{1,0:T(8,128)(2,1)S(1)}, bf16[528,128]{1,0:T(8,128)(2,1)S(1)}, u32[]{:S(2)}, u32[]{:S(2)}) collective-permute-start(bf16[528,128]{1,0:T(8,128)(2,1)S(1)} %get-tuple-element.32.refs_2_), channel_id=1, source_target_pairs={{0,12},{1,9},{4,8},{5,13},{8,4},{9,1},{12,0},{13,5},{2,14},{3,11},... | collective-permute-start | bytes 405512 | tf_op jit(solution)/shard_map/ppermute | solution.py:339
  26.0 1.2 %collective-permute-start.9 = (f32[4,8,128]{2,1,0:T(8,128)S(1)}, f32[4,8,128]{2,1,0:T(8,128)S(1)}, u32[]{:S(2)}, u32[]{:S(2)}) collective-permute-start(f32[4,8,128]{2,1,0:T(8,128)S(1)} %get-tuple-element.33.here_ref), channel_id=1, source_target_pairs={{0,1},{1,0},{2,3},{3,2},{4,5},{5,4},{6,7},{7,6},{8,9},{9,8},{10,11... | collective-permute-start | bytes 49160 | tf_op jit(solution)/shard_map/ppermute | solution.py:350
  26.0 8.2 %collective-permute-start.14 = (bf16[528,128]{1,0:T(8,128)(2,1)S(1)}, bf16[528,128]{1,0:T(8,128)(2,1)S(1)}, u32[]{:S(2)}, u32[]{:S(2)}) collective-permute-start(bf16[528,128]{1,0:T(8,128)(2,1)S(1)} %get-tuple-element.32.refs_2_), channel_id=1, source_target_pairs={{0,1},{1,0},{2,3},{3,2},{4,5},{5,4},{6,7},{7,6},{8,9},{9,8},{10,11... | collective-permute-start | bytes 405512 | tf_op jit(solution)/shard_map/ppermute | solution.py:350
  31.9 2.3 %collective-permute-start.12 = (bf16[528,128]{1,0:T(8,128)(2,1)S(1)}, bf16[528,128]{1,0:T(8,128)(2,1)S(1)}, u32[]{:S(2)}, u32[]{:S(2)}) collective-permute-start(bf16[528,128]{1,0:T(8,128)(2,1)S(1)} %collective-permute-done.10.refs_0_), channel_id=1, source_target_pairs={{0,1},{1,0},{2,3},{3,2},{4,5},{5,4},{6,7},{7,6},{8,9},{9,8},{10,11... | collective-permute-start | bytes 405512 | tf_op jit(solution)/shard_map/ppermute | solution.py:350
  33.3 1.4 %collective-permute-start.13 = (bf16[528,128]{1,0:T(8,128)(2,1)S(1)}, bf16[528,128]{1,0:T(8,128)(2,1)S(1)}, u32[]{:S(2)}, u32[]{:S(2)}) collective-permute-start(bf16[528,128]{1,0:T(8,128)(2,1)S(1)} %collective-permute-done.11.refs_1_), channel_id=1, source_target_pairs={{0,1},{1,0},{2,3},{3,2},{4,5},{5,4},{6,7},{7,6},{8,9},{9,8},{10,11... | collective-permute-start | bytes 405512 | tf_op jit(solution)/shard_map/ppermute | solution.py:350
  34.1 1.4 %collective-permute-start.8 = (bf16[528,128]{1,0:T(8,128)(2,1)S(1)}, bf16[528,128]{1,0:T(8,128)(2,1)S(1)}, u32[]{:S(2)}, u32[]{:S(2)}) collective-permute-start(bf16[528,128]{1,0:T(8,128)(2,1)S(1)} %collective-permute-done.7.refs_0_), channel_id=1, source_target_pairs={{0,1},{1,0},{2,3},{3,2},{4,5},{5,4},{6,7},{7,6},{8,9},{9,8},{10,11... | collective-permute-start | bytes 405512 | tf_op jit(solution)/shard_map/ppermute | solution.py:350
  36.9 3.1 %collective-permute-start.15 = (f32[1,512]{1,0:T(1,128)S(1)}, f32[1,512]{1,0:T(1,128)S(1)}, u32[]{:S(2)}, u32[]{:S(2)}) collective-permute-start(f32[1,512]{1,0:T(1,128)S(1)} %slice.50), channel_id=1, source_target_pairs={{0,3},{1,2},{2,1},{3,0},{4,7},{5,6},{6,5},{7,4},{8,11},{9,10},{10,... | collective-permute-start | bytes 6152 | tf_op jit(solution)/shard_map/ppermute | solution.py:347
  40.0 3.1 %collective-permute-start.16 = (f32[1,512]{1,0:T(1,128)S(1)}, f32[1,512]{1,0:T(1,128)S(1)}, u32[]{:S(2)}, u32[]{:S(2)}) collective-permute-start(f32[1,512]{1,0:T(1,128)S(1)} %fusion.1), channel_id=1, source_target_pairs={{0,3},{1,2},{2,1},{3,0},{4,7},{5,6},{6,5},{7,4},{8,11},{9,10},{10,... | collective-permute-start | bytes 6152 | tf_op jit(solution)/shard_map/ppermute | solution.py:347

commit v14 on v13

--- a/solution.py
+++ b/solution.py
@@ -145,7 +145,7 @@
     return jnp.where(lax.axis_index("state") == beside, on_core[0], on_core[1])
 
 
-def half_kernel(blocks, y_ref, own_ref, kappa_ref, rate_ref, gain_ref, *refs):
+def half_kernel(blocks, counts, y_ref, own_ref, kappa_ref, rate_ref, gain_ref, *refs):
     outs, (turned_ref, acc, vec, side, readings, values) = refs[:-6], refs[-6:]
     tile_num, row_num, _ = own_ref.shape
     number = len(outs)
@@ -158,9 +158,11 @@
         for piece in range(2):
             lanes = pl.ds(pl.multiple_of((2 * core + piece) * LANES, LANES), LANES)
             values[4 + 2 * at + piece : 5 + 2 * at + piece, :] = coefficient[:, lanes]
+    row = lax.broadcasted_iota(jnp.int32, own_ref.shape[1:], 0)
     for index in range(tile_num):
         block = blocks[index]
-        rows = own_ref[index]
+        rows = jnp.where(row < counts[index], own_ref[index].astype(jnp.float32), 0.0)
+        rows = rows.astype(jnp.bfloat16)
         turned = rows.T
         turned_ref[index] = turned
         observed = jnp.broadcast_to(readings[index : index + 1, :], (16, row_num))
@@ -350,15 +352,14 @@
         return lax.ppermute(array, "state", [(i, (i + 1) % state_size) for i in range(state_size)])
 
     if direct:
-        row = lax.broadcasted_iota(jnp.int32, own.shape, 1)
-        valid = jnp.where(row < tile_count[0][:, None, None], own, jnp.zeros((), own.dtype))
+        valid = jnp.where(own == own, own, jnp.zeros((), own.dtype))
         second_half = jax.ShapeDtypeStruct((2 * LANES, LANES), jnp.bfloat16)
         blocks = tile_block[0, :, 0]
         *pieces, turned = pl.pallas_call(
             half_kernel,
             out_shape=[jax.ShapeDtypeStruct((2 * LANES + 32, LANES), jnp.bfloat16)] * tm_size
             + [jax.ShapeDtypeStruct((tile_num, half, row_num), jnp.bfloat16)],
-            in_specs=[SMEM] + [VMEM] * 5,
+            in_specs=[SMEM] * 2 + [VMEM] * 5,
             out_specs=[VMEM] * (tm_size + 1),
             scratch_shapes=[
                 pltpu.VMEM((tm_size, 3 * LANES, LANES), jnp.float32),
@@ -368,7 +369,7 @@
                 pltpu.VMEM((VECTORS, LANES), jnp.float32),
             ],
             compiler_params=KERNEL,
-        )(blocks, rows_y[0], valid, kappa[0], rate[0], smooth_gain[0])
+        )(blocks, tile_count[0], rows_y[0], valid, kappa[0], rate[0], smooth_gain[0])
         turns = range(tm_size - 1)
         parts = [flip_over(pieces[turn], turn) for turn in turns] + [pieces[-1]]
         pieces2 = pl.pallas_call(

time: 43.9 us -> 43.7 us (level)
  transfers between devices with their start and end apart: 17 -> 17, of which waited for: 10 -> 10; matrix products, arithmetic and copies ran while one was open for 4% -> 3% of each run, Pallas kernels for 8% -> 8%
where the time goes in v14:
time: 43.7 us; the launch traced here: 43.5 us
  starting transfers between devices  18 us (41%)
  waiting for transfers between devices  17.7 us (41%)
  Pallas kernels  4.95 us (11%)
  other arithmetic  2.01 us (5%)
  between operations  0.8 us (2%)
    ppermute x9, starting transfers between devices, flip_over(): return lax.ppermute(array, ('tm', 'state'), pairs)  15.5 us
    ppermute x9, waiting for transfers between devices, flip_over(): return lax.ppermute(array, ('tm', 'state'), pairs)  11.5 us
    ppermute x2, waiting for transfers between devices, ring(): return lax.ppermute(array, ('grp', 'state'), pairs)  4.7 us
    pallas_call x1, Pallas kernels, shards(): pl.pallas_call(half_kernel, out_shape=[jax.ShapeDtypeStruct((2 * LANES +...  1.7 us
    ppermute x5, waiting for transfers between devices, across(): lax.ppermute(array, 'state', [(i, (i + 1) % state_size) for i in range(st...  1.59 us
    ppermute x2, starting transfers between devices, ring(): return lax.ppermute(array, ('grp', 'state'), pairs)  1.45 us
    pallas_call x1, Pallas kernels, shards(): pl.pallas_call(functools.partial(assemble_kernel, tm_size, late), out_sha...  1.36 us
    select_n x1, other arithmetic, shards(): valid = jnp.where(own == own, own, jnp.zeros((), own.dtype))  1.29 us
  transfers between devices with their start and end apart: 17, of which 10 were waited for; matrix products, arithmetic and copies ran while one was open for 3% of the time, Pallas kernels for 8%

profile of v14, /device:TPU:0, one launch (start us, length us, event | category | flops | bytes accessed | tf_op | source)
XLA Modules:
  0.0 43.5 jit_solution(135167164926099693)
XLA Ops:
  0.7 0.5 %collective-permute-start.3 = (bf16[16,128,256]{2,1,0:T(8,128)(2,1)}, bf16[16,128,256]{2,1,0:T(8,128)(2,1)S(1)}, u32[]{:S(2)}, u32[]{:S(2)}) collective-permute-start(bf16[16,128,256]{2,1,0:T(8,128)(2,1)} %bitcast.46), channel_id=1, source_target_pairs={{0,1},{1,0},{2,3},{3,2},{4,5},{5,4},{6,7},{7,6},{8,9},{9,8},{10,11... | collective-permute-start | bytes 3145736 | tf_op jit(solution)/shard_map/ppermute | solution.py:330
  1.2 1.3 %compare_select_fusion.own_ref = bf16[16,128,256]{2,1,0:T(8,128)(2,1)S(1)} fusion(bf16[1,16,128,256]{3,2,1,0:T(8,128)(2,1)} %param.8), kind=kLoop, calls=%fused_computation | loop fusion | flops 1048576 | bytes 2097152 | tf_op jit(solution)/shard_map/jit(_where)/select_n | solution.py:355
  2.6 1.7 %shard_map.95 = (bf16[288,128]{1,0:T(8,128)(2,1)S(1)}, bf16[288,128]{1,0:T(8,128)(2,1)S(1)}, bf16[288,128]{1,0:T(8,128)(2,1)S(1)}, bf16[288,128]{1,0:T(8,128)(2,1)S(1)}, bf16[16,256,128]{2,1,0:T(8,128)(2,1)S(1)}) custom-call(s32[16]{0:T(128)S(1)} %bitcast.39, s32[16]{0:T(128)S(1)} %bitcast.45, bf16[16,128]{1,0:T(8,128)(2,1)S(1)} %bitcast.38, ...), custom_call_target="tpu_custom_call" | custom-call | tf_op jit(solution)/shard_map/pallas_call | solution.py:358
  4.3 3.7 %collective-permute-start = (bf16[288,128]{1,0:T(8,128)(2,1)S(1)}, bf16[288,128]{1,0:T(8,128)(2,1)S(1)}, u32[]{:S(2)}, u32[]{:S(2)}) collective-permute-start(bf16[288,128]{1,0:T(8,128)(2,1)S(1)} %get-tuple-element.23), channel_id=1, source_target_pairs={{0,8},{1,13},{4,12},{5,9},{8,0},{9,5},{12,4},{13,1},{2,10},{3,15},... | collective-permute-start | bytes 221192 | tf_op jit(solution)/shard_map/ppermute | solution.py:341
  7.9 1.6 %collective-permute-start.1 = (bf16[288,128]{1,0:T(8,128)(2,1)S(1)}, bf16[288,128]{1,0:T(8,128)(2,1)S(1)}, u32[]{:S(2)}, u32[]{:S(2)}) collective-permute-start(bf16[288,128]{1,0:T(8,128)(2,1)S(1)} %get-tuple-element.24), channel_id=1, source_target_pairs={{0,4},{1,5},{4,0},{5,1},{8,12},{9,13},{12,8},{13,9},{2,6},{3,7},{6... | collective-permute-start | bytes 221192 | tf_op jit(solution)/shard_map/ppermute | solution.py:341
  9.5 1.1 %shard_map.96 = (bf16[256,128]{1,0:T(8,128)(2,1)S(1)}, bf16[256,128]{1,0:T(8,128)(2,1)S(1)}, bf16[256,128]{1,0:T(8,128)(2,1)S(1)}, bf16[256,128]{1,0:T(8,128)(2,1)S(1)}) custom-call(s32[16]{0:T(128)S(1)} %bitcast.40, bf16[16,256,128]{2,1,0:T(8,128)(2,1)S(1)} %get-tuple-element.27.turned_ref, bf16[16,128,256]{2,1,0:T(8,128)(2,1)S(1)} %collective-permute-done.3.other_ref), custom_call_target="tpu_custom_call" | custom-call | tf_op jit(solution)/shard_map/pallas_call | solution.py:375
  10.6 2.0 %collective-permute-start.4 = (bf16[256,128]{1,0:T(8,128)(2,1)S(1)}, bf16[256,128]{1,0:T(8,128)(2,1)S(1)}, u32[]{:S(2)}, u32[]{:S(2)}) collective-permute-start(bf16[256,128]{1,0:T(8,128)(2,1)S(1)} %get-tuple-element.28), channel_id=1, source_target_pairs={{0,8},{1,13},{4,12},{5,9},{8,0},{9,5},{12,4},{13,1},{2,10},{3,15},... | collective-permute-start | bytes 196616 | tf_op jit(solution)/shard_map/ppermute | solution.py:341
  12.6 2.5 %collective-permute-start.5 = (bf16[256,128]{1,0:T(8,128)(2,1)S(1)}, bf16[256,128]{1,0:T(8,128)(2,1)S(1)}, u32[]{:S(2)}, u32[]{:S(2)}) collective-permute-start(bf16[256,128]{1,0:T(8,128)(2,1)S(1)} %get-tuple-element.29), channel_id=1, source_target_pairs={{0,4},{1,5},{4,0},{5,1},{8,12},{9,13},{12,8},{13,9},{2,6},{3,7},{6... | collective-permute-start | bytes 196616 | tf_op jit(solution)/shard_map/ppermute | solution.py:341
  15.0 1.4 %collective-permute-start.6 = (bf16[256,128]{1,0:T(8,128)(2,1)S(1)}, bf16[256,128]{1,0:T(8,128)(2,1)S(1)}, u32[]{:S(2)}, u32[]{:S(2)}) collective-permute-start(bf16[256,128]{1,0:T(8,128)(2,1)S(1)} %get-tuple-element.30), channel_id=1, source_target_pairs={{0,12},{1,9},{4,8},{5,13},{8,4},{9,1},{12,0},{13,5},{2,14},{3,11},... | collective-permute-start | bytes 196616 | tf_op jit(solution)/shard_map/ppermute | solution.py:341
  16.4 3.2 %collective-permute-done.4.refs_4_ = bf16[256,128]{1,0:T(8,128)(2,1)S(1)} collective-permute-done((bf16[256,128]{1,0:T(8,128)(2,1)S(1)}, bf16[256,128]{1,0:T(8,128)(2,1)S(1)}, u32[]{:S(2)}, u32[]{:S(2)}) %collective-permute-start.4) | collective-permute-done | bytes 65568 | tf_op jit(solution)/shard_map/ppermute | solution.py:341
  19.6 1.6 %collective-permute-done.6.refs_6_ = bf16[256,128]{1,0:T(8,128)(2,1)S(1)} collective-permute-done((bf16[256,128]{1,0:T(8,128)(2,1)S(1)}, bf16[256,128]{1,0:T(8,128)(2,1)S(1)}, u32[]{:S(2)}, u32[]{:S(2)}) %collective-permute-start.6) | collective-permute-done | bytes 65568 | tf_op jit(solution)/shard_map/ppermute | solution.py:341
  21.3 2.4 %collective-permute-start.10 = (bf16[528,128]{1,0:T(8,128)(2,1)S(1)}, bf16[528,128]{1,0:T(8,128)(2,1)S(1)}, u32[]{:S(2)}, u32[]{:S(2)}) collective-permute-start(bf16[528,128]{1,0:T(8,128)(2,1)S(1)} %get-tuple-element.32.refs_2_), channel_id=1, source_target_pairs={{0,8},{1,13},{4,12},{5,9},{8,0},{9,5},{12,4},{13,1},{2,10},{3,15},... | collective-permute-start | bytes 405512 | tf_op jit(solution)/shard_map/ppermute | solution.py:341
  23.7 0.8 %collective-permute-start.11 = (bf16[528,128]{1,0:T(8,128)(2,1)S(1)}, bf16[528,128]{1,0:T(8,128)(2,1)S(1)}, u32[]{:S(2)}, u32[]{:S(2)}) collective-permute-start(bf16[528,128]{1,0:T(8,128)(2,1)S(1)} %get-tuple-element.32.refs_2_), channel_id=1, source_target_pairs={{0,4},{1,5},{4,0},{5,1},{8,12},{9,13},{12,8},{13,9},{2,6},{3,7},{6... | collective-permute-start | bytes 405512 | tf_op jit(solution)/shard_map/ppermute | solution.py:341
  24.5 1.3 %collective-permute-start.7 = (bf16[528,128]{1,0:T(8,128)(2,1)S(1)}, bf16[528,128]{1,0:T(8,128)(2,1)S(1)}, u32[]{:S(2)}, u32[]{:S(2)}) collective-permute-start(bf16[528,128]{1,0:T(8,128)(2,1)S(1)} %get-tuple-element.32.refs_2_), channel_id=1, source_target_pairs={{0,12},{1,9},{4,8},{5,13},{8,4},{9,1},{12,0},{13,5},{2,14},{3,11},... | collective-permute-start | bytes 405512 | tf_op jit(solution)/shard_map/ppermute | solution.py:341
  25.8 0.5 %collective-permute-start.14 = (bf16[528,128]{1,0:T(8,128)(2,1)S(1)}, bf16[528,128]{1,0:T(8,128)(2,1)S(1)}, u32[]{:S(2)}, u32[]{:S(2)}) collective-permute-start(bf16[528,128]{1,0:T(8,128)(2,1)S(1)} %get-tuple-element.32.refs_2_), channel_id=1, source_target_pairs={{0,1},{1,0},{2,3},{3,2},{4,5},{5,4},{6,7},{7,6},{8,9},{9,8},{10,11... | collective-permute-start | bytes 405512 | tf_op jit(solution)/shard_map/ppermute | solution.py:352
  26.3 0.7 %collective-permute-done.9.there_ref = f32[4,8,128]{2,1,0:T(8,128)S(1)} collective-permute-done((f32[4,8,128]{2,1,0:T(8,128)S(1)}, f32[4,8,128]{2,1,0:T(8,128)S(1)}, u32[]{:S(2)}, u32[]{:S(2)}) %collective-permute-start.9) | collective-permute-done | bytes 16416 | tf_op jit(solution)/shard_map/ppermute | solution.py:352
  27.3 4.4 %collective-permute-done.10.refs_0_ = bf16[528,128]{1,0:T(8,128)(2,1)S(1)} collective-permute-done((bf16[528,128]{1,0:T(8,128)(2,1)S(1)}, bf16[528,128]{1,0:T(8,128)(2,1)S(1)}, u32[]{:S(2)}, u32[]{:S(2)}) %collective-permute-start.10) | collective-permute-done | bytes 135200 | tf_op jit(solution)/shard_map/ppermute | solution.py:341
  31.6 1.4 %collective-permute-done.11.refs_1_ = bf16[528,128]{1,0:T(8,128)(2,1)S(1)} collective-permute-done((bf16[528,128]{1,0:T(8,128)(2,1)S(1)}, bf16[528,128]{1,0:T(8,128)(2,1)S(1)}, u32[]{:S(2)}, u32[]{:S(2)}) %collective-permute-start.11) | collective-permute-done | bytes 135200 | tf_op jit(solution)/shard_map/ppermute | solution.py:341
  33.0 0.9 %collective-permute-done.7.refs_0_ = bf16[528,128]{1,0:T(8,128)(2,1)S(1)} collective-permute-done((bf16[528,128]{1,0:T(8,128)(2,1)S(1)}, bf16[528,128]{1,0:T(8,128)(2,1)S(1)}, u32[]{:S(2)}, u32[]{:S(2)}) %collective-permute-start.7) | collective-permute-done | bytes 135200 | tf_op jit(solution)/shard_map/ppermute | solution.py:341
  35.3 1.4 %shard_map.100 = (bf16[4,512,512]{2,1,0:T(8,128)(2,1)S(1)}, f32[4,8,512]{2,1,0:T(8,128)S(1)}, f32[4,512]{1,0:T(4,128)S(1)}, f32[4,512]{1,0:T(4,128)S(1)}) custom-call(bf16[528,128]{1,0:T(8,128)(2,1)S(1)} %collective-permute-done.7.refs_0_, bf16[528,128]{1,0:T(8,128)(2,1)S(1)} %collective-permute-done.8.refs_1_, ...), custom_call_target="tpu_custom_call", output_to_operand_aliasing={{0}: (2, {}), {1}: (3, {})} | custom-call | tf_op jit(solution)/shard_map/pallas_call | solution.py:419
  36.8 2.9 %collective-permute-done.15.state_ref = f32[1,512]{1,0:T(1,128)S(1)} collective-permute-done((f32[1,512]{1,0:T(1,128)S(1)}, f32[1,512]{1,0:T(1,128)S(1)}, u32[]{:S(2)}, u32[]{:S(2)}) %collective-permute-start.15) | collective-permute-done | bytes 2080 | tf_op jit(solution)/shard_map/ppermute | solution.py:349
  39.8 1.3 %collective-permute-start.16 = (f32[1,512]{1,0:T(1,128)S(1)}, f32[1,512]{1,0:T(1,128)S(1)}, u32[]{:S(2)}, u32[]{:S(2)}) collective-permute-start(f32[1,512]{1,0:T(1,128)S(1)} %fusion), channel_id=1, source_target_pairs={{0,3},{1,2},{2,1},{3,0},{4,7},{5,6},{6,5},{7,4},{8,11},{9,10},{10,... | collective-permute-start | bytes 6152 | tf_op jit(solution)/shard_map/ppermute | solution.py:349
  41.1 1.7 %collective-permute-done.16 = f32[1,512]{1,0:T(1,128)S(1)} collective-permute-done((f32[1,512]{1,0:T(1,128)S(1)}, f32[1,512]{1,0:T(1,128)S(1)}, u32[]{:S(2)}, u32[]{:S(2)}) %collective-permute-start.16) | collective-permute-done | bytes 2080 | tf_op jit(solution)/shard_map/ppermute | solution.py:349
  42.9 0.7 %add_bitcast_fusion = (f32[1,1,256]{2,1,0:T(1,128)}, f32[1,1,256]{2,1,0:T(1,128)}) fusion(s32[]{:T(128)S(6)} %select_n.47, s32[]{:T(128)S(6)} %select_n.48, f32[1,512]{1,0:T(1,128)S(1)} %get-tuple-element.47, f32[1,512]{1,0:T(1,128)S(1)} %get-tuple-element.46, f32[1,512]{1,0:T(1,128)S(1)} %get-tuple-element.45, f32[1,512]{1,0:T(1,128)S(1)} %get-tuple-element.44, ...), kind=kLoop, calls=%fused_computation.21 | loop fusion | flops 1024 | bytes 11272 | tf_op jit(solution)/shard_map/reshape | solution.py:503
  (38 shorter events, 2.0 us)
Async XLA Ops:
  0.6 1.9 %copy-start.1 = (s32[1,16,1]{1,2,0:T(1,128)S(1)}, s32[1,16,1]{1,2,0:T(1,128)}, u32[]{:S(2)}) copy-start(s32[1,16,1]{1,2,0:T(1,128)} %param.10) | copy-start | bytes 196
  0.6 1.9 %copy-start.6 = (s32[1,16]{1,0:T(1,128)S(1)}, s32[1,16]{1,0:T(1,128)}, u32[]{:S(2)}) copy-start(s32[1,16]{1,0:T(1,128)} %param.11) | copy-start | bytes 196
  0.7 1.9 %copy-start = (bf16[1,16,128]{2,1,0:T(8,128)(2,1)S(1)}, bf16[1,16,128]{2,1,0:T(8,128)(2,1)}, u32[]{:S(2)}) copy-start(bf16[1,16,128]{2,1,0:T(8,128)(2,1)} %param.9) | copy-start | bytes 12292
  0.7 1.9 %copy-start.2 = (f32[1,1,512]{2,1,0:T(1,128)S(1)}, f32[1,1,512]{2,1,0:T(1,128)}, u32[]{:S(2)}) copy-start(f32[1,1,512]{2,1,0:T(1,128)} %param.12) | copy-start | bytes 6148
  0.7 1.9 %copy-start.3 = (f32[1,1,512]{2,1,0:T(1,128)S(1)}, f32[1,1,512]{2,1,0:T(1,128)}, u32[]{:S(2)}) copy-start(f32[1,1,512]{2,1,0:T(1,128)} %param.13) | copy-start | bytes 6148
  0.7 1.9 %copy-start.4 = (f32[1,1,512]{2,1,0:T(1,128)S(1)}, f32[1,1,512]{2,1,0:T(1,128)}, u32[]{:S(2)}) copy-start(f32[1,1,512]{2,1,0:T(1,128)} %param.14) | copy-start | bytes 6148
  0.7 8.8 %collective-permute-start.3 = (bf16[16,128,256]{2,1,0:T(8,128)(2,1)}, bf16[16,128,256]{2,1,0:T(8,128)(2,1)S(1)}, u32[]{:S(2)}, u32[]{:S(2)}) collective-permute-start(bf16[16,128,256]{2,1,0:T(8,128)(2,1)} %bitcast.46), channel_id=1, source_target_pairs={{0,1},{1,0},{2,3},{3,2},{4,5},{5,4},{6,7},{7,6},{8,9},{9,8},{10,11... | collective-permute-start | bytes 3145736 | tf_op jit(solution)/shard_map/ppermute | solution.py:330
  2.6 32.7 %copy-start.5 = (f32[512]{0:T(512)S(1)}, f32[512]{0:T(512)}, u32[]{:S(2)}) copy-start(f32[512]{0:T(512)} %param.15) | copy-start | bytes 6148
  4.3 10.8 %collective-permute-start = (bf16[288,128]{1,0:T(8,128)(2,1)S(1)}, bf16[288,128]{1,0:T(8,128)(2,1)S(1)}, u32[]{:S(2)}, u32[]{:S(2)}) collective-permute-start(bf16[288,128]{1,0:T(8,128)(2,1)S(1)} %get-tuple-element.23), channel_id=1, source_target_pairs={{0,8},{1,13},{4,12},{5,9},{8,0},{9,5},{12,4},{13,1},{2,10},{3,15},... | collective-permute-start | bytes 221192 | tf_op jit(solution)/shard_map/ppermute | solution.py:341
  7.9 8.5 %collective-permute-start.1 = (bf16[288,128]{1,0:T(8,128)(2,1)S(1)}, bf16[288,128]{1,0:T(8,128)(2,1)S(1)}, u32[]{:S(2)}, u32[]{:S(2)}) collective-permute-start(bf16[288,128]{1,0:T(8,128)(2,1)S(1)} %get-tuple-element.24), channel_id=1, source_target_pairs={{0,4},{1,5},{4,0},{5,1},{8,12},{9,13},{12,8},{13,9},{2,6},{3,7},{6... | collective-permute-start | bytes 221192 | tf_op jit(solution)/shard_map/ppermute | solution.py:341
  9.5 6.9 %collective-permute-start.2 = (bf16[288,128]{1,0:T(8,128)(2,1)S(1)}, bf16[288,128]{1,0:T(8,128)(2,1)S(1)}, u32[]{:S(2)}, u32[]{:S(2)}) collective-permute-start(bf16[288,128]{1,0:T(8,128)(2,1)S(1)} %get-tuple-element.25), channel_id=1, source_target_pairs={{0,12},{1,9},{4,8},{5,13},{8,4},{9,1},{12,0},{13,5},{2,14},{3,11},... | collective-permute-start | bytes 221192 | tf_op jit(solution)/shard_map/ppermute | solution.py:341
  10.6 9.0 %collective-permute-start.4 = (bf16[256,128]{1,0:T(8,128)(2,1)S(1)}, bf16[256,128]{1,0:T(8,128)(2,1)S(1)}, u32[]{:S(2)}, u32[]{:S(2)}) collective-permute-start(bf16[256,128]{1,0:T(8,128)(2,1)S(1)} %get-tuple-element.28), channel_id=1, source_target_pairs={{0,8},{1,13},{4,12},{5,9},{8,0},{9,5},{12,4},{13,1},{2,10},{3,15},... | collective-permute-start | bytes 196616 | tf_op jit(solution)/shard_map/ppermute | solution.py:341
  12.6 7.1 %collective-permute-start.5 = (bf16[256,128]{1,0:T(8,128)(2,1)S(1)}, bf16[256,128]{1,0:T(8,128)(2,1)S(1)}, u32[]{:S(2)}, u32[]{:S(2)}) collective-permute-start(bf16[256,128]{1,0:T(8,128)(2,1)S(1)} %get-tuple-element.29), channel_id=1, source_target_pairs={{0,4},{1,5},{4,0},{5,1},{8,12},{9,13},{12,8},{13,9},{2,6},{3,7},{6... | collective-permute-start | bytes 196616 | tf_op jit(solution)/shard_map/ppermute | solution.py:341
  15.0 6.2 %collective-permute-start.6 = (bf16[256,128]{1,0:T(8,128)(2,1)S(1)}, bf16[256,128]{1,0:T(8,128)(2,1)S(1)}, u32[]{:S(2)}, u32[]{:S(2)}) collective-permute-start(bf16[256,128]{1,0:T(8,128)(2,1)S(1)} %get-tuple-element.30), channel_id=1, source_target_pairs={{0,12},{1,9},{4,8},{5,13},{8,4},{9,1},{12,0},{13,5},{2,14},{3,11},... | collective-permute-start | bytes 196616 | tf_op jit(solution)/shard_map/ppermute | solution.py:341
  21.3 10.3 %collective-permute-start.10 = (bf16[528,128]{1,0:T(8,128)(2,1)S(1)}, bf16[528,128]{1,0:T(8,128)(2,1)S(1)}, u32[]{:S(2)}, u32[]{:S(2)}) collective-permute-start(bf16[528,128]{1,0:T(8,128)(2,1)S(1)} %get-tuple-element.32.refs_2_), channel_id=1, source_target_pairs={{0,8},{1,13},{4,12},{5,9},{8,0},{9,5},{12,4},{13,1},{2,10},{3,15},... | collective-permute-start | bytes 405512 | tf_op jit(solution)/shard_map/ppermute | solution.py:341
  23.7 9.3 %collective-permute-start.11 = (bf16[528,128]{1,0:T(8,128)(2,1)S(1)}, bf16[528,128]{1,0:T(8,128)(2,1)S(1)}, u32[]{:S(2)}, u32[]{:S(2)}) collective-permute-start(bf16[528,128]{1,0:T(8,128)(2,1)S(1)} %get-tuple-element.32.refs_2_), channel_id=1, source_target_pairs={{0,4},{1,5},{4,0},{5,1},{8,12},{9,13},{12,8},{13,9},{2,6},{3,7},{6... | collective-permute-start | bytes 405512 | tf_op jit(solution)/shard_map/ppermute | solution.py:341
  24.5 9.4 %collective-permute-start.7 = (bf16[528,128]{1,0:T(8,128)(2,1)S(1)}, bf16[528,128]{1,0:T(8,128)(2,1)S(1)}, u32[]{:S(2)}, u32[]{:S(2)}) collective-permute-start(bf16[528,128]{1,0:T(8,128)(2,1)S(1)} %get-tuple-element.32.refs_2_), channel_id=1, source_target_pairs={{0,12},{1,9},{4,8},{5,13},{8,4},{9,1},{12,0},{13,5},{2,14},{3,11},... | collective-permute-start | bytes 405512 | tf_op jit(solution)/shard_map/ppermute | solution.py:341
  25.8 1.2 %collective-permute-start.9 = (f32[4,8,128]{2,1,0:T(8,128)S(1)}, f32[4,8,128]{2,1,0:T(8,128)S(1)}, u32[]{:S(2)}, u32[]{:S(2)}) collective-permute-start(f32[4,8,128]{2,1,0:T(8,128)S(1)} %get-tuple-element.33.here_ref), channel_id=1, source_target_pairs={{0,1},{1,0},{2,3},{3,2},{4,5},{5,4},{6,7},{7,6},{8,9},{9,8},{10,11... | collective-permute-start | bytes 49160 | tf_op jit(solution)/shard_map/ppermute | solution.py:352
  25.8 8.2 %collective-permute-start.14 = (bf16[528,128]{1,0:T(8,128)(2,1)S(1)}, bf16[528,128]{1,0:T(8,128)(2,1)S(1)}, u32[]{:S(2)}, u32[]{:S(2)}) collective-permute-start(bf16[528,128]{1,0:T(8,128)(2,1)S(1)} %get-tuple-element.32.refs_2_), channel_id=1, source_target_pairs={{0,1},{1,0},{2,3},{3,2},{4,5},{5,4},{6,7},{7,6},{8,9},{9,8},{10,11... | collective-permute-start | bytes 405512 | tf_op jit(solution)/shard_map/ppermute | solution.py:352
  31.6 2.3 %collective-permute-start.12 = (bf16[528,128]{1,0:T(8,128)(2,1)S(1)}, bf16[528,128]{1,0:T(8,128)(2,1)S(1)}, u32[]{:S(2)}, u32[]{:S(2)}) collective-permute-start(bf16[528,128]{1,0:T(8,128)(2,1)S(1)} %collective-permute-done.10.refs_0_), channel_id=1, source_target_pairs={{0,1},{1,0},{2,3},{3,2},{4,5},{5,4},{6,7},{7,6},{8,9},{9,8},{10,11... | collective-permute-start | bytes 405512 | tf_op jit(solution)/shard_map/ppermute | solution.py:352
  33.0 1.4 %collective-permute-start.13 = (bf16[528,128]{1,0:T(8,128)(2,1)S(1)}, bf16[528,128]{1,0:T(8,128)(2,1)S(1)}, u32[]{:S(2)}, u32[]{:S(2)}) collective-permute-start(bf16[528,128]{1,0:T(8,128)(2,1)S(1)} %collective-permute-done.11.refs_1_), channel_id=1, source_target_pairs={{0,1},{1,0},{2,3},{3,2},{4,5},{5,4},{6,7},{7,6},{8,9},{9,8},{10,11... | collective-permute-start | bytes 405512 | tf_op jit(solution)/shard_map/ppermute | solution.py:352
  33.9 1.4 %collective-permute-start.8 = (bf16[528,128]{1,0:T(8,128)(2,1)S(1)}, bf16[528,128]{1,0:T(8,128)(2,1)S(1)}, u32[]{:S(2)}, u32[]{:S(2)}) collective-permute-start(bf16[528,128]{1,0:T(8,128)(2,1)S(1)} %collective-permute-done.7.refs_0_), channel_id=1, source_target_pairs={{0,1},{1,0},{2,3},{3,2},{4,5},{5,4},{6,7},{7,6},{8,9},{9,8},{10,11... | collective-permute-start | bytes 405512 | tf_op jit(solution)/shard_map/ppermute | solution.py:352
  36.7 3.1 %collective-permute-start.15 = (f32[1,512]{1,0:T(1,128)S(1)}, f32[1,512]{1,0:T(1,128)S(1)}, u32[]{:S(2)}, u32[]{:S(2)}) collective-permute-start(f32[1,512]{1,0:T(1,128)S(1)} %slice.50), channel_id=1, source_target_pairs={{0,3},{1,2},{2,1},{3,0},{4,7},{5,6},{6,5},{7,4},{8,11},{9,10},{10,... | collective-permute-start | bytes 6152 | tf_op jit(solution)/shard_map/ppermute | solution.py:349
  39.8 3.1 %collective-permute-start.16 = (f32[1,512]{1,0:T(1,128)S(1)}, f32[1,512]{1,0:T(1,128)S(1)}, u32[]{:S(2)}, u32[]{:S(2)}) collective-permute-start(f32[1,512]{1,0:T(1,128)S(1)} %fusion), channel_id=1, source_target_pairs={{0,3},{1,2},{2,1},{3,0},{4,7},{5,6},{6,5},{7,4},{8,11},{9,10},{10,... | collective-permute-start | bytes 6152 | tf_op jit(solution)/shard_map/ppermute | solution.py:349

commit v15 on v14

--- a/solution.py
+++ b/solution.py
@@ -158,15 +158,15 @@
         for piece in range(2):
             lanes = pl.ds(pl.multiple_of((2 * core + piece) * LANES, LANES), LANES)
             values[4 + 2 * at + piece : 5 + 2 * at + piece, :] = coefficient[:, lanes]
-    row = lax.broadcasted_iota(jnp.int32, own_ref.shape[1:], 0)
+    row = lax.broadcasted_iota(jnp.int32, (1, row_num), 1)
     for index in range(tile_num):
         block = blocks[index]
-        rows = jnp.where(row < counts[index], own_ref[index].astype(jnp.float32), 0.0)
-        rows = rows.astype(jnp.bfloat16)
-        turned = rows.T
+        rows = own_ref[index]
+        live = jnp.where(row < counts[index], 1.0, 0.0).astype(jnp.bfloat16)
+        turned = rows.T * live
         turned_ref[index] = turned
         observed = jnp.broadcast_to(readings[index : index + 1, :], (16, row_num))
-        both = jnp.concatenate([turned, observed.astype(jnp.bfloat16)], axis=0)
+        both = jnp.concatenate([turned, observed.astype(jnp.bfloat16) * live], axis=0)
         square = jnp.dot(both, rows, preferred_element_type=jnp.float32)
         acc[block, 0:LANES] += square[:LANES, :LANES]
         acc[block, LANES : 2 * LANES] += square[:LANES, LANES:]

time: 43.7 us -> 43.5 us (level)
  no operation moved by 1% of the time
where the time goes in v15:
time: 43.5 us; the launch traced here: 43.4 us
  starting transfers between devices  18 us (41%)
  waiting for transfers between devices  17.8 us (41%)
  Pallas kernels  4.78 us (11%)
  other arithmetic  2.01 us (5%)
  between operations  0.8 us (2%)
    ppermute x9, starting transfers between devices, flip_over(): return lax.ppermute(array, ('tm', 'state'), pairs)  15.5 us
    ppermute x9, waiting for transfers between devices, flip_over(): return lax.ppermute(array, ('tm', 'state'), pairs)  11.5 us
    ppermute x2, waiting for transfers between devices, ring(): return lax.ppermute(array, ('grp', 'state'), pairs)  4.71 us
    ppermute x5, waiting for transfers between devices, across(): lax.ppermute(array, 'state', [(i, (i + 1) % state_size) for i in range(st...  1.59 us
    pallas_call x1, Pallas kernels, shards(): pl.pallas_call(half_kernel, out_shape=[jax.ShapeDtypeStruct((2 * LANES +...  1.53 us
    ppermute x2, starting transfers between devices, ring(): return lax.ppermute(array, ('grp', 'state'), pairs)  1.43 us
    pallas_call x1, Pallas kernels, shards(): pl.pallas_call(functools.partial(assemble_kernel, tm_size, late), out_sha...  1.36 us
    select_n x1, other arithmetic, shards(): valid = jnp.where(own == own, own, jnp.zeros((), own.dtype))  1.29 us
  transfers between devices with their start and end apart: 17, of which 10 were waited for; matrix products, arithmetic and copies ran while one was open for 3% of the time, Pallas kernels for 8%

profile of v15, /device:TPU:0, one launch (start us, length us, event | category | flops | bytes accessed | tf_op | source)
XLA Modules:
  0.0 43.4 jit_solution(18108223933209595057)
XLA Ops:
  0.7 0.5 %collective-permute-start.3 = (bf16[16,128,256]{2,1,0:T(8,128)(2,1)}, bf16[16,128,256]{2,1,0:T(8,128)(2,1)S(1)}, u32[]{:S(2)}, u32[]{:S(2)}) collective-permute-start(bf16[16,128,256]{2,1,0:T(8,128)(2,1)} %bitcast.46), channel_id=1, source_target_pairs={{0,1},{1,0},{2,3},{3,2},{4,5},{5,4},{6,7},{7,6},{8,9},{9,8},{10,11... | collective-permute-start | bytes 3145736 | tf_op jit(solution)/shard_map/ppermute | solution.py:330
  1.2 1.3 %compare_select_fusion.own_ref = bf16[16,128,256]{2,1,0:T(8,128)(2,1)S(1)} fusion(bf16[1,16,128,256]{3,2,1,0:T(8,128)(2,1)} %param.8), kind=kLoop, calls=%fused_computation | loop fusion | flops 1048576 | bytes 2097152 | tf_op jit(solution)/shard_map/jit(_where)/select_n | solution.py:355
  2.6 1.5 %shard_map.95 = (bf16[288,128]{1,0:T(8,128)(2,1)S(1)}, bf16[288,128]{1,0:T(8,128)(2,1)S(1)}, bf16[288,128]{1,0:T(8,128)(2,1)S(1)}, bf16[288,128]{1,0:T(8,128)(2,1)S(1)}, bf16[16,256,128]{2,1,0:T(8,128)(2,1)S(1)}) custom-call(s32[16]{0:T(128)S(1)} %bitcast.39, s32[16]{0:T(128)S(1)} %bitcast.45, bf16[16,128]{1,0:T(8,128)(2,1)S(1)} %bitcast.38, ...), custom_call_target="tpu_custom_call" | custom-call | tf_op jit(solution)/shard_map/pallas_call | solution.py:358
  4.1 3.7 %collective-permute-start = (bf16[288,128]{1,0:T(8,128)(2,1)S(1)}, bf16[288,128]{1,0:T(8,128)(2,1)S(1)}, u32[]{:S(2)}, u32[]{:S(2)}) collective-permute-start(bf16[288,128]{1,0:T(8,128)(2,1)S(1)} %get-tuple-element.23), channel_id=1, source_target_pairs={{0,8},{1,13},{4,12},{5,9},{8,0},{9,5},{12,4},{13,1},{2,10},{3,15},... | collective-permute-start | bytes 221192 | tf_op jit(solution)/shard_map/ppermute | solution.py:341
  7.8 1.6 %collective-permute-start.1 = (bf16[288,128]{1,0:T(8,128)(2,1)S(1)}, bf16[288,128]{1,0:T(8,128)(2,1)S(1)}, u32[]{:S(2)}, u32[]{:S(2)}) collective-permute-start(bf16[288,128]{1,0:T(8,128)(2,1)S(1)} %get-tuple-element.24), channel_id=1, source_target_pairs={{0,4},{1,5},{4,0},{5,1},{8,12},{9,13},{12,8},{13,9},{2,6},{3,7},{6... | collective-permute-start | bytes 221192 | tf_op jit(solution)/shard_map/ppermute | solution.py:341
  9.3 1.1 %shard_map.96 = (bf16[256,128]{1,0:T(8,128)(2,1)S(1)}, bf16[256,128]{1,0:T(8,128)(2,1)S(1)}, bf16[256,128]{1,0:T(8,128)(2,1)S(1)}, bf16[256,128]{1,0:T(8,128)(2,1)S(1)}) custom-call(s32[16]{0:T(128)S(1)} %bitcast.40, bf16[16,256,128]{2,1,0:T(8,128)(2,1)S(1)} %get-tuple-element.27.turned_ref, bf16[16,128,256]{2,1,0:T(8,128)(2,1)S(1)} %collective-permute-done.3.other_ref), custom_call_target="tpu_custom_call" | custom-call | tf_op jit(solution)/shard_map/pallas_call | solution.py:375
  10.4 2.0 %collective-permute-start.4 = (bf16[256,128]{1,0:T(8,128)(2,1)S(1)}, bf16[256,128]{1,0:T(8,128)(2,1)S(1)}, u32[]{:S(2)}, u32[]{:S(2)}) collective-permute-start(bf16[256,128]{1,0:T(8,128)(2,1)S(1)} %get-tuple-element.28), channel_id=1, source_target_pairs={{0,8},{1,13},{4,12},{5,9},{8,0},{9,5},{12,4},{13,1},{2,10},{3,15},... | collective-permute-start | bytes 196616 | tf_op jit(solution)/shard_map/ppermute | solution.py:341
  12.4 2.5 %collective-permute-start.5 = (bf16[256,128]{1,0:T(8,128)(2,1)S(1)}, bf16[256,128]{1,0:T(8,128)(2,1)S(1)}, u32[]{:S(2)}, u32[]{:S(2)}) collective-permute-start(bf16[256,128]{1,0:T(8,128)(2,1)S(1)} %get-tuple-element.29), channel_id=1, source_target_pairs={{0,4},{1,5},{4,0},{5,1},{8,12},{9,13},{12,8},{13,9},{2,6},{3,7},{6... | collective-permute-start | bytes 196616 | tf_op jit(solution)/shard_map/ppermute | solution.py:341
  14.9 1.3 %collective-permute-start.6 = (bf16[256,128]{1,0:T(8,128)(2,1)S(1)}, bf16[256,128]{1,0:T(8,128)(2,1)S(1)}, u32[]{:S(2)}, u32[]{:S(2)}) collective-permute-start(bf16[256,128]{1,0:T(8,128)(2,1)S(1)} %get-tuple-element.30), channel_id=1, source_target_pairs={{0,12},{1,9},{4,8},{5,13},{8,4},{9,1},{12,0},{13,5},{2,14},{3,11},... | collective-permute-start | bytes 196616 | tf_op jit(solution)/shard_map/ppermute | solution.py:341
  16.2 3.2 %collective-permute-done.4.refs_4_ = bf16[256,128]{1,0:T(8,128)(2,1)S(1)} collective-permute-done((bf16[256,128]{1,0:T(8,128)(2,1)S(1)}, bf16[256,128]{1,0:T(8,128)(2,1)S(1)}, u32[]{:S(2)}, u32[]{:S(2)}) %collective-permute-start.4) | collective-permute-done | bytes 65568 | tf_op jit(solution)/shard_map/ppermute | solution.py:341
  19.5 1.6 %collective-permute-done.6.refs_6_ = bf16[256,128]{1,0:T(8,128)(2,1)S(1)} collective-permute-done((bf16[256,128]{1,0:T(8,128)(2,1)S(1)}, bf16[256,128]{1,0:T(8,128)(2,1)S(1)}, u32[]{:S(2)}, u32[]{:S(2)}) %collective-permute-start.6) | collective-permute-done | bytes 65568 | tf_op jit(solution)/shard_map/ppermute | solution.py:341
  21.1 2.4 %collective-permute-start.10 = (bf16[528,128]{1,0:T(8,128)(2,1)S(1)}, bf16[528,128]{1,0:T(8,128)(2,1)S(1)}, u32[]{:S(2)}, u32[]{:S(2)}) collective-permute-start(bf16[528,128]{1,0:T(8,128)(2,1)S(1)} %get-tuple-element.32.refs_2_), channel_id=1, source_target_pairs={{0,8},{1,13},{4,12},{5,9},{8,0},{9,5},{12,4},{13,1},{2,10},{3,15},... | collective-permute-start | bytes 405512 | tf_op jit(solution)/shard_map/ppermute | solution.py:341
  23.5 0.8 %collective-permute-start.11 = (bf16[528,128]{1,0:T(8,128)(2,1)S(1)}, bf16[528,128]{1,0:T(8,128)(2,1)S(1)}, u32[]{:S(2)}, u32[]{:S(2)}) collective-permute-start(bf16[528,128]{1,0:T(8,128)(2,1)S(1)} %get-tuple-element.32.refs_2_), channel_id=1, source_target_pairs={{0,4},{1,5},{4,0},{5,1},{8,12},{9,13},{12,8},{13,9},{2,6},{3,7},{6... | collective-permute-start | bytes 405512 | tf_op jit(solution)/shard_map/ppermute | solution.py:341
  24.3 1.3 %collective-permute-start.7 = (bf16[528,128]{1,0:T(8,128)(2,1)S(1)}, bf16[528,128]{1,0:T(8,128)(2,1)S(1)}, u32[]{:S(2)}, u32[]{:S(2)}) collective-permute-start(bf16[528,128]{1,0:T(8,128)(2,1)S(1)} %get-tuple-element.32.refs_2_), channel_id=1, source_target_pairs={{0,12},{1,9},{4,8},{5,13},{8,4},{9,1},{12,0},{13,5},{2,14},{3,11},... | collective-permute-start | bytes 405512 | tf_op jit(solution)/shard_map/ppermute | solution.py:341
  25.6 0.5 %collective-permute-start.14 = (bf16[528,128]{1,0:T(8,128)(2,1)S(1)}, bf16[528,128]{1,0:T(8,128)(2,1)S(1)}, u32[]{:S(2)}, u32[]{:S(2)}) collective-permute-start(bf16[528,128]{1,0:T(8,128)(2,1)S(1)} %get-tuple-element.32.refs_2_), channel_id=1, source_target_pairs={{0,1},{1,0},{2,3},{3,2},{4,5},{5,4},{6,7},{7,6},{8,9},{9,8},{10,11... | collective-permute-start | bytes 405512 | tf_op jit(solution)/shard_map/ppermute | solution.py:352
  26.1 0.7 %collective-permute-done.9.there_ref = f32[4,8,128]{2,1,0:T(8,128)S(1)} collective-permute-done((f32[4,8,128]{2,1,0:T(8,128)S(1)}, f32[4,8,128]{2,1,0:T(8,128)S(1)}, u32[]{:S(2)}, u32[]{:S(2)}) %collective-permute-start.9) | collective-permute-done | bytes 16416 | tf_op jit(solution)/shard_map/ppermute | solution.py:352
  27.1 4.4 %collective-permute-done.10.refs_0_ = bf16[528,128]{1,0:T(8,128)(2,1)S(1)} collective-permute-done((bf16[528,128]{1,0:T(8,128)(2,1)S(1)}, bf16[528,128]{1,0:T(8,128)(2,1)S(1)}, u32[]{:S(2)}, u32[]{:S(2)}) %collective-permute-start.10) | collective-permute-done | bytes 135200 | tf_op jit(solution)/shard_map/ppermute | solution.py:341
  31.5 1.4 %collective-permute-done.11.refs_1_ = bf16[528,128]{1,0:T(8,128)(2,1)S(1)} collective-permute-done((bf16[528,128]{1,0:T(8,128)(2,1)S(1)}, bf16[528,128]{1,0:T(8,128)(2,1)S(1)}, u32[]{:S(2)}, u32[]{:S(2)}) %collective-permute-start.11) | collective-permute-done | bytes 135200 | tf_op jit(solution)/shard_map/ppermute | solution.py:341
  32.9 0.9 %collective-permute-done.7.refs_0_ = bf16[528,128]{1,0:T(8,128)(2,1)S(1)} collective-permute-done((bf16[528,128]{1,0:T(8,128)(2,1)S(1)}, bf16[528,128]{1,0:T(8,128)(2,1)S(1)}, u32[]{:S(2)}, u32[]{:S(2)}) %collective-permute-start.7) | collective-permute-done | bytes 135200 | tf_op jit(solution)/shard_map/ppermute | solution.py:341
  35.1 1.4 %shard_map.100 = (bf16[4,512,512]{2,1,0:T(8,128)(2,1)S(1)}, f32[4,8,512]{2,1,0:T(8,128)S(1)}, f32[4,512]{1,0:T(4,128)S(1)}, f32[4,512]{1,0:T(4,128)S(1)}) custom-call(bf16[528,128]{1,0:T(8,128)(2,1)S(1)} %collective-permute-done.7.refs_0_, bf16[528,128]{1,0:T(8,128)(2,1)S(1)} %collective-permute-done.8.refs_1_, ...), custom_call_target="tpu_custom_call", output_to_operand_aliasing={{0}: (2, {}), {1}: (3, {})} | custom-call | tf_op jit(solution)/shard_map/pallas_call | solution.py:419
  36.6 3.0 %collective-permute-done.15.state_ref = f32[1,512]{1,0:T(1,128)S(1)} collective-permute-done((f32[1,512]{1,0:T(1,128)S(1)}, f32[1,512]{1,0:T(1,128)S(1)}, u32[]{:S(2)}, u32[]{:S(2)}) %collective-permute-start.15) | collective-permute-done | bytes 2080 | tf_op jit(solution)/shard_map/ppermute | solution.py:349
  39.6 1.3 %collective-permute-start.16 = (f32[1,512]{1,0:T(1,128)S(1)}, f32[1,512]{1,0:T(1,128)S(1)}, u32[]{:S(2)}, u32[]{:S(2)}) collective-permute-start(f32[1,512]{1,0:T(1,128)S(1)} %fusion), channel_id=1, source_target_pairs={{0,3},{1,2},{2,1},{3,0},{4,7},{5,6},{6,5},{7,4},{8,11},{9,10},{10,... | collective-permute-start | bytes 6152 | tf_op jit(solution)/shard_map/ppermute | solution.py:349
  40.9 1.8 %collective-permute-done.16 = f32[1,512]{1,0:T(1,128)S(1)} collective-permute-done((f32[1,512]{1,0:T(1,128)S(1)}, f32[1,512]{1,0:T(1,128)S(1)}, u32[]{:S(2)}, u32[]{:S(2)}) %collective-permute-start.16) | collective-permute-done | bytes 2080 | tf_op jit(solution)/shard_map/ppermute | solution.py:349
  42.7 0.7 %add_bitcast_fusion = (f32[1,1,256]{2,1,0:T(1,128)}, f32[1,1,256]{2,1,0:T(1,128)}) fusion(s32[]{:T(128)S(6)} %select_n.47, s32[]{:T(128)S(6)} %select_n.48, f32[1,512]{1,0:T(1,128)S(1)} %get-tuple-element.47, f32[1,512]{1,0:T(1,128)S(1)} %get-tuple-element.46, f32[1,512]{1,0:T(1,128)S(1)} %get-tuple-element.45, f32[1,512]{1,0:T(1,128)S(1)} %get-tuple-element.44, ...), kind=kLoop, calls=%fused_computation.21 | loop fusion | flops 1024 | bytes 11272 | tf_op jit(solution)/shard_map/reshape | solution.py:503
  (38 shorter events, 2.0 us)
Async XLA Ops:
  0.6 1.9 %copy-start.1 = (s32[1,16,1]{1,2,0:T(1,128)S(1)}, s32[1,16,1]{1,2,0:T(1,128)}, u32[]{:S(2)}) copy-start(s32[1,16,1]{1,2,0:T(1,128)} %param.10) | copy-start | bytes 196
  0.6 1.9 %copy-start.6 = (s32[1,16]{1,0:T(1,128)S(1)}, s32[1,16]{1,0:T(1,128)}, u32[]{:S(2)}) copy-start(s32[1,16]{1,0:T(1,128)} %param.11) | copy-start | bytes 196
  0.7 1.9 %copy-start = (bf16[1,16,128]{2,1,0:T(8,128)(2,1)S(1)}, bf16[1,16,128]{2,1,0:T(8,128)(2,1)}, u32[]{:S(2)}) copy-start(bf16[1,16,128]{2,1,0:T(8,128)(2,1)} %param.9) | copy-start | bytes 12292
  0.7 1.9 %copy-start.2 = (f32[1,1,512]{2,1,0:T(1,128)S(1)}, f32[1,1,512]{2,1,0:T(1,128)}, u32[]{:S(2)}) copy-start(f32[1,1,512]{2,1,0:T(1,128)} %param.12) | copy-start | bytes 6148
  0.7 1.9 %copy-start.3 = (f32[1,1,512]{2,1,0:T(1,128)S(1)}, f32[1,1,512]{2,1,0:T(1,128)}, u32[]{:S(2)}) copy-start(f32[1,1,512]{2,1,0:T(1,128)} %param.13) | copy-start | bytes 6148
  0.7 1.9 %copy-start.4 = (f32[1,1,512]{2,1,0:T(1,128)S(1)}, f32[1,1,512]{2,1,0:T(1,128)}, u32[]{:S(2)}) copy-start(f32[1,1,512]{2,1,0:T(1,128)} %param.14) | copy-start | bytes 6148
  0.7 8.7 %collective-permute-start.3 = (bf16[16,128,256]{2,1,0:T(8,128)(2,1)}, bf16[16,128,256]{2,1,0:T(8,128)(2,1)S(1)}, u32[]{:S(2)}, u32[]{:S(2)}) collective-permute-start(bf16[16,128,256]{2,1,0:T(8,128)(2,1)} %bitcast.46), channel_id=1, source_target_pairs={{0,1},{1,0},{2,3},{3,2},{4,5},{5,4},{6,7},{7,6},{8,9},{9,8},{10,11... | collective-permute-start | bytes 3145736 | tf_op jit(solution)/shard_map/ppermute | solution.py:330
  2.6 32.5 %copy-start.5 = (f32[512]{0:T(512)S(1)}, f32[512]{0:T(512)}, u32[]{:S(2)}) copy-start(f32[512]{0:T(512)} %param.15) | copy-start | bytes 6148
  4.1 10.8 %collective-permute-start = (bf16[288,128]{1,0:T(8,128)(2,1)S(1)}, bf16[288,128]{1,0:T(8,128)(2,1)S(1)}, u32[]{:S(2)}, u32[]{:S(2)}) collective-permute-start(bf16[288,128]{1,0:T(8,128)(2,1)S(1)} %get-tuple-element.23), channel_id=1, source_target_pairs={{0,8},{1,13},{4,12},{5,9},{8,0},{9,5},{12,4},{13,1},{2,10},{3,15},... | collective-permute-start | bytes 221192 | tf_op jit(solution)/shard_map/ppermute | solution.py:341
  7.8 8.5 %collective-permute-start.1 = (bf16[288,128]{1,0:T(8,128)(2,1)S(1)}, bf16[288,128]{1,0:T(8,128)(2,1)S(1)}, u32[]{:S(2)}, u32[]{:S(2)}) collective-permute-start(bf16[288,128]{1,0:T(8,128)(2,1)S(1)} %get-tuple-element.24), channel_id=1, source_target_pairs={{0,4},{1,5},{4,0},{5,1},{8,12},{9,13},{12,8},{13,9},{2,6},{3,7},{6... | collective-permute-start | bytes 221192 | tf_op jit(solution)/shard_map/ppermute | solution.py:341
  9.3 6.9 %collective-permute-start.2 = (bf16[288,128]{1,0:T(8,128)(2,1)S(1)}, bf16[288,128]{1,0:T(8,128)(2,1)S(1)}, u32[]{:S(2)}, u32[]{:S(2)}) collective-permute-start(bf16[288,128]{1,0:T(8,128)(2,1)S(1)} %get-tuple-element.25), channel_id=1, source_target_pairs={{0,12},{1,9},{4,8},{5,13},{8,4},{9,1},{12,0},{13,5},{2,14},{3,11},... | collective-permute-start | bytes 221192 | tf_op jit(solution)/shard_map/ppermute | solution.py:341
  10.4 9.0 %collective-permute-start.4 = (bf16[256,128]{1,0:T(8,128)(2,1)S(1)}, bf16[256,128]{1,0:T(8,128)(2,1)S(1)}, u32[]{:S(2)}, u32[]{:S(2)}) collective-permute-start(bf16[256,128]{1,0:T(8,128)(2,1)S(1)} %get-tuple-element.28), channel_id=1, source_target_pairs={{0,8},{1,13},{4,12},{5,9},{8,0},{9,5},{12,4},{13,1},{2,10},{3,15},... | collective-permute-start | bytes 196616 | tf_op jit(solution)/shard_map/ppermute | solution.py:341
  12.4 7.1 %collective-permute-start.5 = (bf16[256,128]{1,0:T(8,128)(2,1)S(1)}, bf16[256,128]{1,0:T(8,128)(2,1)S(1)}, u32[]{:S(2)}, u32[]{:S(2)}) collective-permute-start(bf16[256,128]{1,0:T(8,128)(2,1)S(1)} %get-tuple-element.29), channel_id=1, source_target_pairs={{0,4},{1,5},{4,0},{5,1},{8,12},{9,13},{12,8},{13,9},{2,6},{3,7},{6... | collective-permute-start | bytes 196616 | tf_op jit(solution)/shard_map/ppermute | solution.py:341
  14.9 6.2 %collective-permute-start.6 = (bf16[256,128]{1,0:T(8,128)(2,1)S(1)}, bf16[256,128]{1,0:T(8,128)(2,1)S(1)}, u32[]{:S(2)}, u32[]{:S(2)}) collective-permute-start(bf16[256,128]{1,0:T(8,128)(2,1)S(1)} %get-tuple-element.30), channel_id=1, source_target_pairs={{0,12},{1,9},{4,8},{5,13},{8,4},{9,1},{12,0},{13,5},{2,14},{3,11},... | collective-permute-start | bytes 196616 | tf_op jit(solution)/shard_map/ppermute | solution.py:341
  21.1 10.3 %collective-permute-start.10 = (bf16[528,128]{1,0:T(8,128)(2,1)S(1)}, bf16[528,128]{1,0:T(8,128)(2,1)S(1)}, u32[]{:S(2)}, u32[]{:S(2)}) collective-permute-start(bf16[528,128]{1,0:T(8,128)(2,1)S(1)} %get-tuple-element.32.refs_2_), channel_id=1, source_target_pairs={{0,8},{1,13},{4,12},{5,9},{8,0},{9,5},{12,4},{13,1},{2,10},{3,15},... | collective-permute-start | bytes 405512 | tf_op jit(solution)/shard_map/ppermute | solution.py:341
  23.5 9.3 %collective-permute-start.11 = (bf16[528,128]{1,0:T(8,128)(2,1)S(1)}, bf16[528,128]{1,0:T(8,128)(2,1)S(1)}, u32[]{:S(2)}, u32[]{:S(2)}) collective-permute-start(bf16[528,128]{1,0:T(8,128)(2,1)S(1)} %get-tuple-element.32.refs_2_), channel_id=1, source_target_pairs={{0,4},{1,5},{4,0},{5,1},{8,12},{9,13},{12,8},{13,9},{2,6},{3,7},{6... | collective-permute-start | bytes 405512 | tf_op jit(solution)/shard_map/ppermute | solution.py:341
  24.3 9.4 %collective-permute-start.7 = (bf16[528,128]{1,0:T(8,128)(2,1)S(1)}, bf16[528,128]{1,0:T(8,128)(2,1)S(1)}, u32[]{:S(2)}, u32[]{:S(2)}) collective-permute-start(bf16[528,128]{1,0:T(8,128)(2,1)S(1)} %get-tuple-element.32.refs_2_), channel_id=1, source_target_pairs={{0,12},{1,9},{4,8},{5,13},{8,4},{9,1},{12,0},{13,5},{2,14},{3,11},... | collective-permute-start | bytes 405512 | tf_op jit(solution)/shard_map/ppermute | solution.py:341
  25.6 1.2 %collective-permute-start.9 = (f32[4,8,128]{2,1,0:T(8,128)S(1)}, f32[4,8,128]{2,1,0:T(8,128)S(1)}, u32[]{:S(2)}, u32[]{:S(2)}) collective-permute-start(f32[4,8,128]{2,1,0:T(8,128)S(1)} %get-tuple-element.33.here_ref), channel_id=1, source_target_pairs={{0,1},{1,0},{2,3},{3,2},{4,5},{5,4},{6,7},{7,6},{8,9},{9,8},{10,11... | collective-permute-start | bytes 49160 | tf_op jit(solution)/shard_map/ppermute | solution.py:352
  25.6 8.2 %collective-permute-start.14 = (bf16[528,128]{1,0:T(8,128)(2,1)S(1)}, bf16[528,128]{1,0:T(8,128)(2,1)S(1)}, u32[]{:S(2)}, u32[]{:S(2)}) collective-permute-start(bf16[528,128]{1,0:T(8,128)(2,1)S(1)} %get-tuple-element.32.refs_2_), channel_id=1, source_target_pairs={{0,1},{1,0},{2,3},{3,2},{4,5},{5,4},{6,7},{7,6},{8,9},{9,8},{10,11... | collective-permute-start | bytes 405512 | tf_op jit(solution)/shard_map/ppermute | solution.py:352
  31.5 2.3 %collective-permute-start.12 = (bf16[528,128]{1,0:T(8,128)(2,1)S(1)}, bf16[528,128]{1,0:T(8,128)(2,1)S(1)}, u32[]{:S(2)}, u32[]{:S(2)}) collective-permute-start(bf16[528,128]{1,0:T(8,128)(2,1)S(1)} %collective-permute-done.10.refs_0_), channel_id=1, source_target_pairs={{0,1},{1,0},{2,3},{3,2},{4,5},{5,4},{6,7},{7,6},{8,9},{9,8},{10,11... | collective-permute-start | bytes 405512 | tf_op jit(solution)/shard_map/ppermute | solution.py:352
  32.9 1.4 %collective-permute-start.13 = (bf16[528,128]{1,0:T(8,128)(2,1)S(1)}, bf16[528,128]{1,0:T(8,128)(2,1)S(1)}, u32[]{:S(2)}, u32[]{:S(2)}) collective-permute-start(bf16[528,128]{1,0:T(8,128)(2,1)S(1)} %collective-permute-done.11.refs_1_), channel_id=1, source_target_pairs={{0,1},{1,0},{2,3},{3,2},{4,5},{5,4},{6,7},{7,6},{8,9},{9,8},{10,11... | collective-permute-start | bytes 405512 | tf_op jit(solution)/shard_map/ppermute | solution.py:352
  33.8 1.4 %collective-permute-start.8 = (bf16[528,128]{1,0:T(8,128)(2,1)S(1)}, bf16[528,128]{1,0:T(8,128)(2,1)S(1)}, u32[]{:S(2)}, u32[]{:S(2)}) collective-permute-start(bf16[528,128]{1,0:T(8,128)(2,1)S(1)} %collective-permute-done.7.refs_0_), channel_id=1, source_target_pairs={{0,1},{1,0},{2,3},{3,2},{4,5},{5,4},{6,7},{7,6},{8,9},{9,8},{10,11... | collective-permute-start | bytes 405512 | tf_op jit(solution)/shard_map/ppermute | solution.py:352
  36.5 3.1 %collective-permute-start.15 = (f32[1,512]{1,0:T(1,128)S(1)}, f32[1,512]{1,0:T(1,128)S(1)}, u32[]{:S(2)}, u32[]{:S(2)}) collective-permute-start(f32[1,512]{1,0:T(1,128)S(1)} %slice.50), channel_id=1, source_target_pairs={{0,3},{1,2},{2,1},{3,0},{4,7},{5,6},{6,5},{7,4},{8,11},{9,10},{10,... | collective-permute-start | bytes 6152 | tf_op jit(solution)/shard_map/ppermute | solution.py:349
  39.6 3.1 %collective-permute-start.16 = (f32[1,512]{1,0:T(1,128)S(1)}, f32[1,512]{1,0:T(1,128)S(1)}, u32[]{:S(2)}, u32[]{:S(2)}) collective-permute-start(f32[1,512]{1,0:T(1,128)S(1)} %fusion), channel_id=1, source_target_pairs={{0,3},{1,2},{2,1},{3,0},{4,7},{5,6},{6,5},{7,4},{8,11},{9,10},{10,... | collective-permute-start | bytes 6152 | tf_op jit(solution)/shard_map/ppermute | solution.py:349
